TPU v7x, 256 devices: a whole 4x4x8 slice. The times are simulated.
256 devices in a mesh: frames: 64 (over x, z, core), rows: 4 (over y).
Axes of the slice: x: 4, y: 4, z: 8, core: 2. Of those that a mesh axis runs over, the one named last changes fastest.
Arguments:
- fmap: bfloat16 [128, 12, 64, 128], P('frames', 'rows'), may hold values from -6 to 6
- context: bfloat16 [128, 12, 64, 128], P('frames', 'rows'), may hold values from -6 to 6
- pairs: int32 [256, 3], replicated, may hold values from 0 to 127, as said below
- w_corr: bfloat16 [49, 128], replicated, may hold values from -0.875 to 0.875
- w_zr: bfloat16 [256, 256], replicated, may hold values from -0.375 to 0.375
- w_q: bfloat16 [9, 256, 128], replicated, may hold values from -0.125 to 0.125
- w_msg: bfloat16 [128, 256], replicated, may hold values from -0.5 to 0.5
- w_res: bfloat16 [9, 128, 128], replicated, may hold values from -0.1875 to 0.1875
Outputs:
- state: bfloat16 [128, 12, 64, 128], P('frames', 'rows')
Inputs may be any that keep to these rules, and one draw needn't show every extreme that they name: Source and target differ. With dev(f) = f // 2, the source's dev, the target's dev and the owner differ pairwise by at most one. No owner holds more than 8 pairs, and some owner holds exactly 8.
All inputs are finite; a program needn't handle non-finite values.
Results may differ from a plain program's by a relative error of at most 0.01.
Values may be sent and summed in bfloat16 or wider, within the bound.
No kernel may reach another device: no remote copies, remote signals or barrier semaphores. Data moves between devices by JAX's collectives and lax.ppermute only.
A program may use at most 64 MiB of HBM per device.

v0:
```python
import jax
import jax.numpy as jnp
from jax import lax
from jax.sharding import PartitionSpec as P

RADIUS = 3
ROUNDS = 2
CAPACITY = 8


def with_halo(array, sides, width):
    for axis, dim in sides:
        size, length = (lax.axis_size(axis), array.shape[dim])
        up = [(i, (i + 1) % size) for i in range(size - 1)]
        down = [(j, i) for i, j in up]
        last = lax.slice_in_dim(array, length - width, length, axis=dim)
        leading = lax.slice_in_dim(array, 0, width, axis=dim)
        before = lax.ppermute(last, axis, up)
        after = lax.ppermute(leading, axis, down)
        array = jnp.concatenate([before, array, after], axis=dim)
    return array


def passed_along(block, axis, distance):
    devices = range(lax.axis_size(axis))
    route = [(i - distance, i) for i in devices if i - distance in devices]
    return lax.ppermute(block, axis, route)


def slot_table(pair_rows, owner_index):
    owners = pair_rows[:, 2]
    mine = (owners == owner_index).astype(jnp.int32)
    ranks = jnp.cumsum(mine) - mine
    levels = jnp.arange(CAPACITY, dtype=jnp.int32)
    picks = mine[None, :] * (ranks[None, :] == levels[:, None]).astype(jnp.int32)
    sources = jnp.sum(picks * pair_rows[None, :, 0], axis=1)
    targets = jnp.sum(picks * pair_rows[None, :, 1], axis=1)
    valid = jnp.sum(picks, axis=1)
    return (sources, targets, valid)


def dest_onehot(frame_ids, valid, start, count):
    relative = frame_ids - start
    inside = valid * (relative >= 0).astype(jnp.int32) * (relative < count).astype(jnp.int32)
    levels = jnp.arange(count, dtype=jnp.int32)
    hits = (relative[None, :] == levels[:, None]).astype(jnp.int32) * inside[None, :]
    return hits.astype(jnp.bfloat16)


def conv_taps(padded, kernel, height, width):
    count = padded.shape[0]
    cin = padded.shape[-1]
    total = None
    for row_off in range(3):
        for col_off in range(3):
            window = padded[:, row_off : row_off + height, col_off : col_off + width, :].reshape(
                -1, cin
            )
            term = jnp.dot(
                window, kernel[3 * row_off + col_off], preferred_element_type=jnp.float32
            )
            total = term if total is None else total + term
    return total.reshape(count, height, width, -1)


def pad_columns(field, amount):
    return jnp.pad(field, ((0, 0), (0, 0), (amount, amount), (0, 0)))


def spread_messages(messages, sources, targets, valid, start, count):
    chans = messages.shape[-1] // 2
    slots = messages.shape[0]
    first_half = messages[..., :chans].reshape(slots, -1)
    second_half = messages[..., chans:].reshape(slots, -1)
    to_source = dest_onehot(sources, valid, start, count)
    to_target = dest_onehot(targets, valid, start, count)
    return jnp.dot(to_source, first_half, preferred_element_type=jnp.float32) + jnp.dot(
        to_target, second_half, preferred_element_type=jnp.float32
    )


def local(fmap, context, pairs, w_corr, w_zr, w_q, w_msg, w_res):
    frame_dev, height, width, chans = fmap.shape
    own_index = lax.axis_index("frames")
    sources, targets, valid = slot_table(pairs, own_index)
    feat_window = with_halo(fmap, (("frames", 0),), frame_dev)
    window_start = (own_index - 1) * frame_dev
    limit = feat_window.shape[0] - 1
    src_index = jnp.clip(sources - window_start, 0, limit)
    tgt_index = jnp.clip(targets - window_start, 0, limit)
    src_feat = jnp.take(feat_window, src_index, axis=0)
    tgt_feat = jnp.take(feat_window, tgt_index, axis=0)
    tgt_rim = with_halo(tgt_feat, (("rows", 1),), RADIUS)
    tgt_rim = pad_columns(tgt_rim, RADIUS)
    span = 2 * RADIUS + 1
    columns = []
    for row_off in range(span):
        for col_off in range(span):
            moved = tgt_rim[:, row_off : row_off + height, col_off : col_off + width, :]
            columns.append(
                jnp.einsum("syxc,syxc->syx", src_feat, moved, preferred_element_type=jnp.float32)
            )
    scale = 1.0 / chans**0.5
    corr = (jnp.stack(columns, axis=-1) * scale).astype(jnp.bfloat16)
    motion = jax.nn.relu(
        jnp.dot(corr.reshape(-1, span * span), w_corr, preferred_element_type=jnp.float32)
    )
    motion = motion.astype(jnp.bfloat16).reshape(-1, height, width, chans)
    slots = motion.shape[0]
    state = context
    hidden = None
    for sweep in range(ROUNDS):
        state_window = with_halo(state, (("frames", 0),), frame_dev)
        ctx_src = jnp.take(state_window, src_index, axis=0).astype(jnp.float32)
        if sweep == 0:
            hidden = jnp.tanh(ctx_src)
        xin = (motion.astype(jnp.float32) + ctx_src).astype(jnp.bfloat16)
        joined = jnp.concatenate([hidden.astype(jnp.bfloat16), xin], axis=-1)
        gates = jax.nn.sigmoid(
            jnp.dot(joined.reshape(-1, 2 * chans), w_zr, preferred_element_type=jnp.float32)
        )
        gates = gates.reshape(slots, height, width, 2 * chans)
        update_gate = gates[..., :chans]
        reset_gate = gates[..., chans:]
        qin = jnp.concatenate([(reset_gate * hidden).astype(jnp.bfloat16), xin], axis=-1)
        qin_rim = pad_columns(with_halo(qin, (("rows", 1),), 1), 1)
        candidate = jnp.tanh(conv_taps(qin_rim, w_q, height, width))
        hidden = (1.0 - update_gate) * hidden + update_gate * candidate
        messages = jnp.dot(
            hidden.astype(jnp.bfloat16).reshape(-1, chans),
            w_msg,
            preferred_element_type=jnp.float32,
        )
        messages = messages.astype(jnp.bfloat16).reshape(slots, height, width, 2 * chans)
        partial_value = spread_messages(
            messages, sources, targets, valid, (own_index - 1) * frame_dev, 3 * frame_dev
        )
        incoming = partial_value[frame_dev : 2 * frame_dev]
        for offset, piece in ((-1, partial_value[:frame_dev]), (1, partial_value[2 * frame_dev :])):
            incoming = incoming + passed_along(piece.astype(jnp.bfloat16), "frames", offset).astype(
                piece.dtype
            )
        update = jax.nn.relu(incoming).reshape(frame_dev, height, width, chans).astype(jnp.bfloat16)
        update_rim = pad_columns(with_halo(update, (("rows", 1),), 1), 1)
        state = (state.astype(jnp.float32) + conv_taps(update_rim, w_res, height, width)).astype(
            jnp.bfloat16
        )
    return state


def solution(mesh):
    placed = (
        P("frames", "rows", None, None),
        P("frames", "rows", None, None),
        P(),
        P(),
        P(),
        P(),
        P(),
        P(),
    )
    return jax.shard_map(
        local,
        mesh=mesh,
        in_specs=placed,
        out_specs=P("frames", "rows", None, None),
        check_vma=False,
    )
```

profile of v0, /device:TPU:6, one launch (start us, length us, event | category | flops | bytes accessed | tf_op | source)
XLA Modules:
  0.0 142.2 jit_solution(16542106349841420477)
XLA Ops:
  0.0 7.6 %collective-permute-start.1 = (bf16[2,3,64,128]{3,2,1,0:T(8,128)(2,1)}, bf16[2,3,64,128]{3,2,1,0:T(8,128)(2,1)S(1)}, u32[]{:S(2)}, u32[]{:S(2)}) collective-permute-start(bf16[2,3,64,128]{3,2,1,0:T(8,128)(2,1)} %param.11), channel_id=1, source_target_pairs={{4,0},{8,4},{12,8},{16,12},{20,16},{24,20},{28,24},{32,28},{36,32}... | collective-permute-start | bytes 294920 | tf_op jit(solution)/shard_map/ppermute | solution.py:19
  7.6 1.9 %collective-permute-start = (bf16[2,3,64,128]{3,2,1,0:T(8,128)(2,1)}, bf16[2,3,64,128]{3,2,1,0:T(8,128)(2,1)S(1)}, u32[]{:S(2)}, u32[]{:S(2)}) collective-permute-start(bf16[2,3,64,128]{3,2,1,0:T(8,128)(2,1)} %param.11), channel_id=1, source_target_pairs={{0,4},{4,8},{8,12},{12,16},{16,20},{20,24},{24,28},{28,32},{32,36}... | collective-permute-start | bytes 294920 | tf_op jit(solution)/shard_map/ppermute | solution.py:18
  9.5 1.9 %collective-permute-start.2 = (bf16[2,3,64,128]{3,2,1,0:T(8,128)(2,1)}, bf16[2,3,64,128]{3,2,1,0:T(8,128)(2,1)S(1)}, u32[]{:S(2)}, u32[]{:S(2)}) collective-permute-start(bf16[2,3,64,128]{3,2,1,0:T(8,128)(2,1)} %param.10), channel_id=1, source_target_pairs={{0,4},{4,8},{8,12},{12,16},{16,20},{20,24},{24,28},{28,32},{32,36}... | collective-permute-start | bytes 294920 | tf_op jit(solution)/shard_map/ppermute | solution.py:18
  11.5 5.8 %collective-permute-start.3 = (bf16[2,3,64,128]{3,2,1,0:T(8,128)(2,1)}, bf16[2,3,64,128]{3,2,1,0:T(8,128)(2,1)S(1)}, u32[]{:S(2)}, u32[]{:S(2)}) collective-permute-start(bf16[2,3,64,128]{3,2,1,0:T(8,128)(2,1)} %param.10), channel_id=1, source_target_pairs={{4,0},{8,4},{12,8},{16,12},{20,16},{24,20},{28,24},{32,28},{36,32}... | collective-permute-start | bytes 294920 | tf_op jit(solution)/shard_map/ppermute | solution.py:19
  22.5 4.6 %collective-permute-start.4 = (bf16[8,3,64,128]{3,2,1,0:T(8,128)(2,1)S(1)}, bf16[8,3,64,128]{3,2,1,0:T(8,128)(2,1)S(1)}, u32[]{:S(2)}, u32[]{:S(2)}) collective-permute-start(bf16[8,3,64,128]{3,2,1,0:T(8,128)(2,1)S(1)} %broadcast_select_fusion), channel_id=1, source_target_pairs={{0,1},{1,2},{2,3},{4,5},{5,6},{6,7},{8,9},{9,10},{10,11},{12,13},{... | collective-permute-start | bytes 1179656 | tf_op jit(solution)/shard_map/ppermute | solution.py:18
  28.5 2.4 %collective-permute-done.5 = bf16[8,3,64,128]{3,2,1,0:T(8,128)(2,1)S(1)} collective-permute-done((bf16[8,3,64,128]{3,2,1,0:T(8,128)(2,1)S(1)}, bf16[8,3,64,128]{3,2,1,0:T(8,128)(2,1)S(1)}, u32[]{:S(2)}, u32[]{:S(2)}) %collective-permute-start.5) | collective-permute-done | bytes 393248 | tf_op jit(solution)/shard_map/ppermute | solution.py:19
  33.0 2.0 %fusion.38 = (f32[8,3,64]{2,1,0:T(4,128)S(1)}, f32[8,3,64]{2,1,0:T(4,128)S(1)}, f32[8,3,64]{2,1,0:T(4,128)S(1)}, f32[8,3,64]{2,1,0:T(4,128)S(1)}, f32[8,3,64]{2,...) fusion(bf16[8,9,70,128]{3,2,1,0:T(8,128)(2,1)S(1)} %fusion.20, ...), kind=kLoop, calls=%fused_computation.150 | loop fusion | flops 5099520 | bytes 3588104 | tf_op jit(solution)/shard_map/syxc,syxc->syx/dot_general | solution.py:101
  35.0 3.9 %fusion.58 = (f32[8,3,64]{2,1,0:T(4,128)S(1)}, f32[8,3,64]{2,1,0:T(4,128)S(1)}, f32[8,3,64]{2,1,0:T(4,128)S(1)}, f32[8,3,64]{2,1,0:T(4,128)S(1)}, f32[8,3,64]{2,...) fusion(bf16[8,9,70,128]{3,2,1,0:T(8,128)(2,1)S(1)} %fusion.20, ...), kind=kLoop, calls=%fused_computation.170 | loop fusion | flops 10394112 | bytes 7182344 | tf_op jit(solution)/shard_map/syxc,syxc->syx/dot_general | solution.py:101
  39.0 3.9 %fusion.78 = (f32[8,3,64]{2,1,0:T(4,128)S(1)}, f32[8,3,64]{2,1,0:T(4,128)S(1)}, f32[8,3,64]{2,1,0:T(4,128)S(1)}, f32[8,3,64]{2,1,0:T(4,128)S(1)}, f32[8,3,64]{2,...) fusion(bf16[8,9,70,128]{3,2,1,0:T(8,128)(2,1)S(1)} %fusion.20, ...), kind=kLoop, calls=%fused_computation.190 | loop fusion | flops 10394112 | bytes 7182344 | tf_op jit(solution)/shard_map/syxc,syxc->syx/dot_general | solution.py:101
  52.3 5.2 %collective-permute-start.6 = (bf16[8,1,64,256]{3,2,1,0:T(8,128)(2,1)S(1)}, bf16[8,1,64,256]{3,2,1,0:T(8,128)(2,1)S(1)}, u32[]{:S(2)}, u32[]{:S(2)}) collective-permute-start(bf16[8,1,64,256]{3,2,1,0:T(8,128)(2,1)S(1)} %get-tuple-element.94), channel_id=1, source_target_pairs={{0,1},{1,2},{2,3},{4,5},{5,6},{6,7},{8,9},{9,10},{10,11},{12,13},{... | collective-permute-start | bytes 786440 | tf_op jit(solution)/shard_map/ppermute | solution.py:18
  57.5 2.2 %collective-permute-done.7 = bf16[8,1,64,256]{3,2,1,0:T(8,128)(2,1)S(1)} collective-permute-done((bf16[8,1,64,256]{3,2,1,0:T(8,128)(2,1)S(1)}, bf16[8,1,64,256]{3,2,1,0:T(8,128)(2,1)S(1)}, u32[]{:S(2)}, u32[]{:S(2)}) %collective-permute-start.7) | collective-permute-done | bytes 262176 | tf_op jit(solution)/shard_map/ppermute | solution.py:19
  69.1 1.9 %collective-permute-start.9 = (bf16[2,24576]{1,0:T(2,128)(2,1)S(1)}, bf16[2,24576]{1,0:T(2,128)(2,1)S(1)}, u32[]{:S(2)}, u32[]{:S(2)}) collective-permute-start(bf16[2,24576]{1,0:T(2,128)(2,1)S(1)} %get-tuple-element.101), channel_id=1, source_target_pairs={{0,4},{4,8},{8,12},{12,16},{16,20},{20,24},{24,28},{28,32},{32,36}... | collective-permute-start | bytes 294920 | tf_op jit(solution)/shard_map/ppermute | solution.py:27
  71.0 7.1 %collective-permute-start.8 = (bf16[2,24576]{1,0:T(2,128)(2,1)S(1)}, bf16[2,24576]{1,0:T(2,128)(2,1)S(1)}, u32[]{:S(2)}, u32[]{:S(2)}) collective-permute-start(bf16[2,24576]{1,0:T(2,128)(2,1)S(1)} %get-tuple-element.100), channel_id=1, source_target_pairs={{4,0},{8,4},{12,8},{16,12},{20,16},{24,20},{28,24},{32,28},{36,32}... | collective-permute-start | bytes 294920 | tf_op jit(solution)/shard_map/ppermute | solution.py:27
  78.5 1.8 %collective-permute-done.8 = bf16[2,24576]{1,0:T(2,128)(2,1)S(1)} collective-permute-done((bf16[2,24576]{1,0:T(2,128)(2,1)S(1)}, bf16[2,24576]{1,0:T(2,128)(2,1)S(1)}, u32[]{:S(2)}, u32[]{:S(2)}) %collective-permute-start.8) | collective-permute-done | bytes 98336 | tf_op jit(solution)/shard_map/ppermute | solution.py:27
  81.9 4.7 %collective-permute-start.10 = (bf16[2,1,64,128]{3,2,1,0:T(8,128)(2,1)S(1)}, bf16[2,1,64,128]{3,2,1,0:T(8,128)(2,1)S(1)}, u32[]{:S(2)}, u32[]{:S(2)}) collective-permute-start(bf16[2,1,64,128]{3,2,1,0:T(8,128)(2,1)S(1)} %get-tuple-element.120), channel_id=1, source_target_pairs={{0,1},{1,2},{2,3},{4,5},{5,6},{6,7},{8,9},{9,10},{10,11},{12,13},{... | collective-permute-start | bytes 98312 | tf_op jit(solution)/shard_map/ppermute | solution.py:18
  90.0 5.0 %collective-permute-start.13 = (bf16[2,3,64,128]{3,2,1,0:T(8,128)(2,1)S(1)}, bf16[2,3,64,128]{3,2,1,0:T(8,128)(2,1)S(1)}, u32[]{:S(2)}, u32[]{:S(2)}) collective-permute-start(bf16[2,3,64,128]{3,2,1,0:T(8,128)(2,1)S(1)} %add_convert_fusion.2), channel_id=1, source_target_pairs={{4,0},{8,4},{12,8},{16,12},{20,16},{24,20},{28,24},{32,28},{36,32}... | collective-permute-start | bytes 294920 | tf_op jit(solution)/shard_map/ppermute | solution.py:19
  95.0 1.9 %collective-permute-start.12 = (bf16[2,3,64,128]{3,2,1,0:T(8,128)(2,1)S(1)}, bf16[2,3,64,128]{3,2,1,0:T(8,128)(2,1)S(1)}, u32[]{:S(2)}, u32[]{:S(2)}) collective-permute-start(bf16[2,3,64,128]{3,2,1,0:T(8,128)(2,1)S(1)} %add_convert_fusion.2), channel_id=1, source_target_pairs={{0,4},{4,8},{8,12},{12,16},{16,20},{20,24},{24,28},{28,32},{32,36}... | collective-permute-start | bytes 294920 | tf_op jit(solution)/shard_map/ppermute | solution.py:18
  97.1 5.9 %collective-permute-done.12 = bf16[2,3,64,128]{3,2,1,0:T(8,128)(2,1)S(1)} collective-permute-done((bf16[2,3,64,128]{3,2,1,0:T(8,128)(2,1)S(1)}, bf16[2,3,64,128]{3,2,1,0:T(8,128)(2,1)S(1)}, u32[]{:S(2)}, u32[]{:S(2)}) %collective-permute-start.12) | collective-permute-done | bytes 98336 | tf_op jit(solution)/shard_map/ppermute | solution.py:18
  106.1 4.8 %collective-permute-start.14 = (bf16[8,1,64,256]{3,2,1,0:T(8,128)(2,1)S(1)}, bf16[8,1,64,256]{3,2,1,0:T(8,128)(2,1)S(1)}, u32[]{:S(2)}, u32[]{:S(2)}) collective-permute-start(bf16[8,1,64,256]{3,2,1,0:T(8,128)(2,1)S(1)} %get-tuple-element.87), channel_id=1, source_target_pairs={{0,1},{1,2},{2,3},{4,5},{5,6},{6,7},{8,9},{9,10},{10,11},{12,13},{... | collective-permute-start | bytes 786440 | tf_op jit(solution)/shard_map/ppermute | solution.py:18
  110.9 2.2 %collective-permute-done.15 = bf16[8,1,64,256]{3,2,1,0:T(8,128)(2,1)S(1)} collective-permute-done((bf16[8,1,64,256]{3,2,1,0:T(8,128)(2,1)S(1)}, bf16[8,1,64,256]{3,2,1,0:T(8,128)(2,1)S(1)}, u32[]{:S(2)}, u32[]{:S(2)}) %collective-permute-start.15) | collective-permute-done | bytes 262176 | tf_op jit(solution)/shard_map/ppermute | solution.py:19
  121.9 1.9 %collective-permute-start.17 = (bf16[2,24576]{1,0:T(2,128)(2,1)S(1)}, bf16[2,24576]{1,0:T(2,128)(2,1)S(1)}, u32[]{:S(2)}, u32[]{:S(2)}) collective-permute-start(bf16[2,24576]{1,0:T(2,128)(2,1)S(1)} %get-tuple-element.99), channel_id=1, source_target_pairs={{0,4},{4,8},{8,12},{12,16},{16,20},{20,24},{24,28},{28,32},{32,36}... | collective-permute-start | bytes 294920 | tf_op jit(solution)/shard_map/ppermute | solution.py:27
  123.8 5.8 %collective-permute-start.16 = (bf16[2,24576]{1,0:T(2,128)(2,1)S(1)}, bf16[2,24576]{1,0:T(2,128)(2,1)S(1)}, u32[]{:S(2)}, u32[]{:S(2)}) collective-permute-start(bf16[2,24576]{1,0:T(2,128)(2,1)S(1)} %get-tuple-element.98), channel_id=1, source_target_pairs={{4,0},{8,4},{12,8},{16,12},{20,16},{24,20},{28,24},{32,28},{36,32}... | collective-permute-start | bytes 294920 | tf_op jit(solution)/shard_map/ppermute | solution.py:27
  129.9 1.8 %collective-permute-done.16 = bf16[2,24576]{1,0:T(2,128)(2,1)S(1)} collective-permute-done((bf16[2,24576]{1,0:T(2,128)(2,1)S(1)}, bf16[2,24576]{1,0:T(2,128)(2,1)S(1)}, u32[]{:S(2)}, u32[]{:S(2)}) %collective-permute-start.16) | collective-permute-done | bytes 98336 | tf_op jit(solution)/shard_map/ppermute | solution.py:27
  133.3 5.0 %collective-permute-start.18 = (bf16[2,1,64,128]{3,2,1,0:T(8,128)(2,1)S(1)}, bf16[2,1,64,128]{3,2,1,0:T(8,128)(2,1)S(1)}, u32[]{:S(2)}, u32[]{:S(2)}) collective-permute-start(bf16[2,1,64,128]{3,2,1,0:T(8,128)(2,1)S(1)} %get-tuple-element.116), channel_id=1, source_target_pairs={{0,1},{1,2},{2,3},{4,5},{5,6},{6,7},{8,9},{9,10},{10,11},{12,13},{... | collective-permute-start | bytes 98312 | tf_op jit(solution)/shard_map/ppermute | solution.py:18
  (197 shorter events, 50.1 us)
Async XLA Ops:
  0.0 50.1 %copy-start = (bf16[256,256]{1,0:T(8,128)(2,1)S(1)}, bf16[256,256]{1,0:T(8,128)(2,1)}, u32[]{:S(2)}) copy-start(bf16[256,256]{1,0:T(8,128)(2,1)} %param.14) | copy-start | bytes 393220
  0.0 27.8 %copy-start.3 = (bf16[2,3,64,128]{3,2,1,0:T(8,128)(2,1)S(1)}, bf16[2,3,64,128]{3,2,1,0:T(8,128)(2,1)}, u32[]{:S(2)}) copy-start(bf16[2,3,64,128]{3,2,1,0:T(8,128)(2,1)} %param.11) | copy-start | bytes 294916
  0.0 27.8 %collective-permute-start.1 = (bf16[2,3,64,128]{3,2,1,0:T(8,128)(2,1)}, bf16[2,3,64,128]{3,2,1,0:T(8,128)(2,1)S(1)}, u32[]{:S(2)}, u32[]{:S(2)}) collective-permute-start(bf16[2,3,64,128]{3,2,1,0:T(8,128)(2,1)} %param.11), channel_id=1, source_target_pairs={{4,0},{8,4},{12,8},{16,12},{20,16},{24,20},{28,24},{32,28},{36,32}... | collective-permute-start | bytes 294920 | tf_op jit(solution)/shard_map/ppermute | solution.py:19
  7.6 20.2 %collective-permute-start = (bf16[2,3,64,128]{3,2,1,0:T(8,128)(2,1)}, bf16[2,3,64,128]{3,2,1,0:T(8,128)(2,1)S(1)}, u32[]{:S(2)}, u32[]{:S(2)}) collective-permute-start(bf16[2,3,64,128]{3,2,1,0:T(8,128)(2,1)} %param.11), channel_id=1, source_target_pairs={{0,4},{4,8},{8,12},{12,16},{16,20},{20,24},{24,28},{28,32},{32,36}... | collective-permute-start | bytes 294920 | tf_op jit(solution)/shard_map/ppermute | solution.py:18
  9.5 10.0 %collective-permute-start.2 = (bf16[2,3,64,128]{3,2,1,0:T(8,128)(2,1)}, bf16[2,3,64,128]{3,2,1,0:T(8,128)(2,1)S(1)}, u32[]{:S(2)}, u32[]{:S(2)}) collective-permute-start(bf16[2,3,64,128]{3,2,1,0:T(8,128)(2,1)} %param.10), channel_id=1, source_target_pairs={{0,4},{4,8},{8,12},{12,16},{16,20},{20,24},{24,28},{28,32},{32,36}... | collective-permute-start | bytes 294920 | tf_op jit(solution)/shard_map/ppermute | solution.py:18
  11.5 9.0 %collective-permute-start.3 = (bf16[2,3,64,128]{3,2,1,0:T(8,128)(2,1)}, bf16[2,3,64,128]{3,2,1,0:T(8,128)(2,1)S(1)}, u32[]{:S(2)}, u32[]{:S(2)}) collective-permute-start(bf16[2,3,64,128]{3,2,1,0:T(8,128)(2,1)} %param.10), channel_id=1, source_target_pairs={{4,0},{8,4},{12,8},{16,12},{20,16},{24,20},{28,24},{32,28},{36,32}... | collective-permute-start | bytes 294920 | tf_op jit(solution)/shard_map/ppermute | solution.py:19
  19.5 49.1 %copy-start.7 = (s32[8]{0:T(128)}, s32[8]{0:T(128)S(1)}, u32[]{:S(2)}) copy-start(s32[8]{0:T(128)S(1)} %get-tuple-element.124) | copy-start | bytes 100
  19.5 49.1 %copy-start.9 = (s32[8]{0:T(128)}, s32[8]{0:T(128)S(1)}, u32[]{:S(2)}) copy-start(s32[8]{0:T(128)S(1)} %get-tuple-element.125) | copy-start | bytes 100
  21.2 9.7 %collective-permute-start.5 = (bf16[8,3,64,128]{3,2,1,0:T(8,128)(2,1)S(1)}, bf16[8,3,64,128]{3,2,1,0:T(8,128)(2,1)S(1)}, u32[]{:S(2)}, u32[]{:S(2)}) collective-permute-start(bf16[8,3,64,128]{3,2,1,0:T(8,128)(2,1)S(1)} %broadcast_select_fusion), channel_id=1, source_target_pairs={{1,0},{2,1},{3,2},{5,4},{6,5},{7,6},{9,8},{10,9},{11,10},{13,12},{... | collective-permute-start | bytes 1179656 | tf_op jit(solution)/shard_map/ppermute | solution.py:19
  22.5 9.8 %collective-permute-start.4 = (bf16[8,3,64,128]{3,2,1,0:T(8,128)(2,1)S(1)}, bf16[8,3,64,128]{3,2,1,0:T(8,128)(2,1)S(1)}, u32[]{:S(2)}, u32[]{:S(2)}) collective-permute-start(bf16[8,3,64,128]{3,2,1,0:T(8,128)(2,1)S(1)} %broadcast_select_fusion), channel_id=1, source_target_pairs={{0,1},{1,2},{2,3},{4,5},{5,6},{6,7},{8,9},{9,10},{10,11},{12,13},{... | collective-permute-start | bytes 1179656 | tf_op jit(solution)/shard_map/ppermute | solution.py:18
  51.0 8.7 %collective-permute-start.7 = (bf16[8,1,64,256]{3,2,1,0:T(8,128)(2,1)S(1)}, bf16[8,1,64,256]{3,2,1,0:T(8,128)(2,1)S(1)}, u32[]{:S(2)}, u32[]{:S(2)}) collective-permute-start(bf16[8,1,64,256]{3,2,1,0:T(8,128)(2,1)S(1)} %get-tuple-element.95), channel_id=1, source_target_pairs={{1,0},{2,1},{3,2},{5,4},{6,5},{7,6},{9,8},{10,9},{11,10},{13,12},{... | collective-permute-start | bytes 786440 | tf_op jit(solution)/shard_map/ppermute | solution.py:19
  52.3 8.9 %collective-permute-start.6 = (bf16[8,1,64,256]{3,2,1,0:T(8,128)(2,1)S(1)}, bf16[8,1,64,256]{3,2,1,0:T(8,128)(2,1)S(1)}, u32[]{:S(2)}, u32[]{:S(2)}) collective-permute-start(bf16[8,1,64,256]{3,2,1,0:T(8,128)(2,1)S(1)} %get-tuple-element.94), channel_id=1, source_target_pairs={{0,1},{1,2},{2,3},{4,5},{5,6},{6,7},{8,9},{9,10},{10,11},{12,13},{... | collective-permute-start | bytes 786440 | tf_op jit(solution)/shard_map/ppermute | solution.py:18
  69.1 9.4 %collective-permute-start.9 = (bf16[2,24576]{1,0:T(2,128)(2,1)S(1)}, bf16[2,24576]{1,0:T(2,128)(2,1)S(1)}, u32[]{:S(2)}, u32[]{:S(2)}) collective-permute-start(bf16[2,24576]{1,0:T(2,128)(2,1)S(1)} %get-tuple-element.101), channel_id=1, source_target_pairs={{0,4},{4,8},{8,12},{12,16},{16,20},{20,24},{24,28},{28,32},{32,36}... | collective-permute-start | bytes 294920 | tf_op jit(solution)/shard_map/ppermute | solution.py:27
  71.0 9.3 %collective-permute-start.8 = (bf16[2,24576]{1,0:T(2,128)(2,1)S(1)}, bf16[2,24576]{1,0:T(2,128)(2,1)S(1)}, u32[]{:S(2)}, u32[]{:S(2)}) collective-permute-start(bf16[2,24576]{1,0:T(2,128)(2,1)S(1)} %get-tuple-element.100), channel_id=1, source_target_pairs={{4,0},{8,4},{12,8},{16,12},{20,16},{24,20},{28,24},{32,28},{36,32}... | collective-permute-start | bytes 294920 | tf_op jit(solution)/shard_map/ppermute | solution.py:27
  80.6 6.8 %collective-permute-start.11 = (bf16[2,1,64,128]{3,2,1,0:T(8,128)(2,1)S(1)}, bf16[2,1,64,128]{3,2,1,0:T(8,128)(2,1)S(1)}, u32[]{:S(2)}, u32[]{:S(2)}) collective-permute-start(bf16[2,1,64,128]{3,2,1,0:T(8,128)(2,1)S(1)} %get-tuple-element.121), channel_id=1, source_target_pairs={{1,0},{2,1},{3,2},{5,4},{6,5},{7,6},{9,8},{10,9},{11,10},{13,12},{... | collective-permute-start | bytes 98312 | tf_op jit(solution)/shard_map/ppermute | solution.py:19
  81.9 6.3 %collective-permute-start.10 = (bf16[2,1,64,128]{3,2,1,0:T(8,128)(2,1)S(1)}, bf16[2,1,64,128]{3,2,1,0:T(8,128)(2,1)S(1)}, u32[]{:S(2)}, u32[]{:S(2)}) collective-permute-start(bf16[2,1,64,128]{3,2,1,0:T(8,128)(2,1)S(1)} %get-tuple-element.120), channel_id=1, source_target_pairs={{0,1},{1,2},{2,3},{4,5},{5,6},{6,7},{8,9},{9,10},{10,11},{12,13},{... | collective-permute-start | bytes 98312 | tf_op jit(solution)/shard_map/ppermute | solution.py:18
  90.0 7.2 %collective-permute-start.13 = (bf16[2,3,64,128]{3,2,1,0:T(8,128)(2,1)S(1)}, bf16[2,3,64,128]{3,2,1,0:T(8,128)(2,1)S(1)}, u32[]{:S(2)}, u32[]{:S(2)}) collective-permute-start(bf16[2,3,64,128]{3,2,1,0:T(8,128)(2,1)S(1)} %add_convert_fusion.2), channel_id=1, source_target_pairs={{4,0},{8,4},{12,8},{16,12},{20,16},{24,20},{28,24},{32,28},{36,32}... | collective-permute-start | bytes 294920 | tf_op jit(solution)/shard_map/ppermute | solution.py:19
  95.0 8.0 %collective-permute-start.12 = (bf16[2,3,64,128]{3,2,1,0:T(8,128)(2,1)S(1)}, bf16[2,3,64,128]{3,2,1,0:T(8,128)(2,1)S(1)}, u32[]{:S(2)}, u32[]{:S(2)}) collective-permute-start(bf16[2,3,64,128]{3,2,1,0:T(8,128)(2,1)S(1)} %add_convert_fusion.2), channel_id=1, source_target_pairs={{0,4},{4,8},{8,12},{12,16},{16,20},{20,24},{24,28},{28,32},{32,36}... | collective-permute-start | bytes 294920 | tf_op jit(solution)/shard_map/ppermute | solution.py:18
  104.8 8.3 %collective-permute-start.15 = (bf16[8,1,64,256]{3,2,1,0:T(8,128)(2,1)S(1)}, bf16[8,1,64,256]{3,2,1,0:T(8,128)(2,1)S(1)}, u32[]{:S(2)}, u32[]{:S(2)}) collective-permute-start(bf16[8,1,64,256]{3,2,1,0:T(8,128)(2,1)S(1)} %get-tuple-element.88), channel_id=1, source_target_pairs={{1,0},{2,1},{3,2},{5,4},{6,5},{7,6},{9,8},{10,9},{11,10},{13,12},{... | collective-permute-start | bytes 786440 | tf_op jit(solution)/shard_map/ppermute | solution.py:19
  106.1 8.4 %collective-permute-start.14 = (bf16[8,1,64,256]{3,2,1,0:T(8,128)(2,1)S(1)}, bf16[8,1,64,256]{3,2,1,0:T(8,128)(2,1)S(1)}, u32[]{:S(2)}, u32[]{:S(2)}) collective-permute-start(bf16[8,1,64,256]{3,2,1,0:T(8,128)(2,1)S(1)} %get-tuple-element.87), channel_id=1, source_target_pairs={{0,1},{1,2},{2,3},{4,5},{5,6},{6,7},{8,9},{9,10},{10,11},{12,13},{... | collective-permute-start | bytes 786440 | tf_op jit(solution)/shard_map/ppermute | solution.py:18
  121.9 8.0 %collective-permute-start.17 = (bf16[2,24576]{1,0:T(2,128)(2,1)S(1)}, bf16[2,24576]{1,0:T(2,128)(2,1)S(1)}, u32[]{:S(2)}, u32[]{:S(2)}) collective-permute-start(bf16[2,24576]{1,0:T(2,128)(2,1)S(1)} %get-tuple-element.99), channel_id=1, source_target_pairs={{0,4},{4,8},{8,12},{12,16},{16,20},{20,24},{24,28},{28,32},{32,36}... | collective-permute-start | bytes 294920 | tf_op jit(solution)/shard_map/ppermute | solution.py:27
  123.8 8.0 %collective-permute-start.16 = (bf16[2,24576]{1,0:T(2,128)(2,1)S(1)}, bf16[2,24576]{1,0:T(2,128)(2,1)S(1)}, u32[]{:S(2)}, u32[]{:S(2)}) collective-permute-start(bf16[2,24576]{1,0:T(2,128)(2,1)S(1)} %get-tuple-element.98), channel_id=1, source_target_pairs={{4,0},{8,4},{12,8},{16,12},{20,16},{24,20},{28,24},{32,28},{36,32}... | collective-permute-start | bytes 294920 | tf_op jit(solution)/shard_map/ppermute | solution.py:27
  132.0 6.4 %collective-permute-start.19 = (bf16[2,1,64,128]{3,2,1,0:T(8,128)(2,1)S(1)}, bf16[2,1,64,128]{3,2,1,0:T(8,128)(2,1)S(1)}, u32[]{:S(2)}, u32[]{:S(2)}) collective-permute-start(bf16[2,1,64,128]{3,2,1,0:T(8,128)(2,1)S(1)} %get-tuple-element.117), channel_id=1, source_target_pairs={{1,0},{2,1},{3,2},{5,4},{6,5},{7,6},{9,8},{10,9},{11,10},{13,12},{... | collective-permute-start | bytes 98312 | tf_op jit(solution)/shard_map/ppermute | solution.py:19
  133.3 6.6 %collective-permute-start.18 = (bf16[2,1,64,128]{3,2,1,0:T(8,128)(2,1)S(1)}, bf16[2,1,64,128]{3,2,1,0:T(8,128)(2,1)S(1)}, u32[]{:S(2)}, u32[]{:S(2)}) collective-permute-start(bf16[2,1,64,128]{3,2,1,0:T(8,128)(2,1)S(1)} %get-tuple-element.116), channel_id=1, source_target_pairs={{0,1},{1,2},{2,3},{4,5},{5,6},{6,7},{8,9},{9,10},{10,11},{12,13},{... | collective-permute-start | bytes 98312 | tf_op jit(solution)/shard_map/ppermute | solution.py:18
  (7 other events, 29.9 us)
where the time goes:
time: 145 us; the launch traced here: 142 us
  starting transfers between devices  71.6 us (49%)
  waiting for transfers between devices  24 us (17%)
  other arithmetic  19 us (13%)
  local copies, waits for them, and re-layouts  13.7 us (9%)
  matrix products  13 us (9%)
    ppermute x8, starting transfers between devices, with_halo(): before = lax.ppermute(last, axis, up)  30 us
    ppermute x8, starting transfers between devices, with_halo(): after = lax.ppermute(leading, axis, down)  24.8 us
    ppermute x4, starting transfers between devices, passed_along(): return lax.ppermute(block, axis, route)  16.7 us
    ppermute x8, waiting for transfers between devices, with_halo(): before = lax.ppermute(last, axis, up)  12.6 us
    dot_general x4, other arithmetic, local(): jnp.einsum('syxc,syxc->syx', src_feat, moved, preferred_element_type=jnp....  11.5 us
    dot_general x36, matrix products, conv_taps(): jnp.dot(window, kernel[3 * row_off + col_off], preferred_element_type=jnp...  9.54 us
    ppermute x8, waiting for transfers between devices, with_halo(): after = lax.ppermute(leading, axis, down)  7.09 us
    another operation x50, local copies, waits for them, and re-layouts, local(): corr = (jnp.stack(columns, axis=-1) * scale).astype(jnp.bfloat16)  4.8 us
  transfers between devices with their start and end apart: 20, of which 14 were waited for; matrix products, arithmetic and copies ran while one was open for 4% of the time, Pallas kernels for 0%

commit v1 on v0

v1 whole, which is shorter than its diff:
```python
import jax
import jax.numpy as jnp
from jax import lax
from jax.experimental import pallas as pl
from jax.experimental.pallas import tpu as pltpu
from jax.sharding import PartitionSpec as P

SLOTS = 8
ROWS = 3
WIDTH = 64
CHANS = 128
SPAN = 7
WIDE = 5 * WIDTH
OWN = ROWS * WIDTH
F32 = jnp.float32
BF16 = jnp.bfloat16


def dot(a, b):
    return lax.dot_general(a, b, (((1,), (0,)), ((), ())), preferred_element_type=F32)


def dot_t(a, b):
    return lax.dot_general(a, b, (((1,), (1,)), ((), ())), preferred_element_type=F32)


def sigmoid(x):
    return 0.5 * jnp.tanh(0.5 * x) + 0.5


def conv_rows(field, weights, rows):
    size = rows * WIDTH
    taps = [field[k * WIDTH : k * WIDTH + size] for k in range(3)]
    out = dot(jnp.concatenate(taps, axis=1), weights)
    column = lax.broadcasted_iota(jnp.int32, (size, CHANS), 0) % WIDTH
    left = jnp.where(column == 0, 0.0, pltpu.roll(out[:, :CHANS], 1, 0))
    right = jnp.where(column == WIDTH - 1, 0.0, pltpu.roll(out[:, 2 * CHANS :], size - 1, 0))
    return out[:, CHANS : 2 * CHANS] + left + right


def gru(hidden, xin, w_zr, w_q):
    joined = jnp.concatenate([hidden.astype(BF16), xin], axis=1)
    reset = sigmoid(dot(joined, w_zr[:, CHANS:]))
    update = sigmoid(dot(joined[WIDTH : WIDTH + OWN], w_zr[:, :CHANS]))
    qin = jnp.concatenate([(reset * hidden).astype(BF16), xin], axis=1)
    candidate = jnp.tanh(conv_rows(qin, w_q, ROWS))
    own = hidden[WIDTH : WIDTH + OWN]
    return own + update * (candidate - own)


def band_mask(group):
    column = WIDTH - 1 - lax.broadcasted_iota(jnp.int32, (WIDTH, CHANS), 0)
    lane = lax.broadcasted_iota(jnp.int32, (WIDTH, CHANS), 1)
    high = lane >= WIDTH
    tap = jnp.where(high, lane - WIDTH, lane) - 8 * group - 4
    at = column + tap - 3
    keep = (tap >= 0) & (tap < SPAN) & (at >= 0) & (at < WIDTH)
    if group == 3:
        keep = keep & high
    return keep


def add_messages(acc, hidden, w_msg, source, target):
    messages = dot(hidden.astype(BF16), w_msg)
    acc[source] += messages[:, :CHANS]
    acc[target] += messages[:, CHANS:]


def first_kernel(
    idx, p0, p1, p2, p3, w_corr, w_zr, w_q, w_msg, part, hid, motion_out, feat, rim, ctx, acc
):
    pieces = (p0, p1, p2, p3)
    ends = [lax.broadcasted_iota(jnp.int32, (WIDTH, WIDTH), k) for k in range(2)]
    flip = jnp.where(ends[0] + ends[1] == WIDTH - 1, 1.0, 0.0).astype(BF16)
    acc[...] = jnp.zeros_like(acc)

    def body(s, carry):
        source, target = idx[s], idx[SLOTS + s]
        for k, piece in enumerate(pieces):

            @pl.when(source // 2 == k)
            def _():
                feat[...] = piece[source % 2, 3:8]
                ctx[...] = piece[source % 2, 11:16]

            @pl.when(target // 2 == k)
            def _():
                rim[...] = piece[target % 2, 0:11]

        rows = feat[...]
        turned = dot(flip, jnp.concatenate([rows[y] for y in range(5)], axis=1)).astype(BF16)
        corr = []
        for y in range(5):
            near = turned[:, y * CHANS : (y + 1) * CHANS]
            far = rim[y : y + SPAN].reshape(SPAN * WIDTH, CHANS)
            total = jnp.zeros((WIDTH, CHANS), F32)
            for g in range(4):
                start = 2 * WIDTH * g if g < 3 else 5 * WIDTH
                table = dot_t(near, far[start : start + 2 * WIDTH])
                moved = pltpu.roll(table, 8 * g + 72, 1, stride=1, stride_axis=0)
                total = jnp.where(band_mask(g), moved, total)
            corr.append((total * (1.0 / CHANS**0.5)).astype(BF16))
        turned = dot(flip, jnp.concatenate(corr, axis=1)).astype(BF16)
        corr = [turned[:, y * CHANS : (y + 1) * CHANS] for y in range(5)]
        motion = jnp.maximum(dot(jnp.concatenate(corr, axis=0), w_corr[...]), 0.0).astype(BF16)
        motion_out[s] = motion
        state = ctx[...].reshape(WIDE, CHANS).astype(F32)
        xin = (motion.astype(F32) + state).astype(BF16)
        hidden = gru(jnp.tanh(state), xin, w_zr[...], w_q[...])
        hid[s] = hidden
        add_messages(acc, hidden, w_msg[...], source, target)
        return carry

    lax.fori_loop(0, idx[2 * SLOTS], body, 0)
    part[...] = acc[...].astype(BF16)


def second_kernel(idx, s0, s1, motion, hid, above, below, w_zr, w_q, w_msg, part, state_buf, acc):
    acc[...] = jnp.zeros_like(acc)

    def body(s, carry):
        source, target = idx[s], idx[SLOTS + s]
        for k, piece in enumerate((s0, s1)):

            @pl.when(source // 4 == k)
            def _():
                state_buf[...] = piece[source % 4]

        state = state_buf[...].reshape(WIDE, CHANS).astype(F32)
        xin = (motion[s].astype(F32) + state).astype(BF16)
        hidden = jnp.concatenate([above[s].astype(F32), hid[s], below[s].astype(F32)], axis=0)
        hidden = gru(hidden, xin, w_zr[...], w_q[...])
        add_messages(acc, hidden, w_msg[...], source, target)
        return carry

    lax.fori_loop(0, idx[2 * SLOTS], body, 0)
    part[...] = acc[...].astype(BF16)


def state_kernel(idx, own, near, upd, above, below, w_res, out):
    row = idx[2 * SLOTS + 1]
    for frame in range(4):
        piece = own if frame < 2 else near
        field = jnp.concatenate(
            [above[frame].reshape(2 * WIDTH, CHANS), upd[frame].reshape(OWN, CHANS), below[frame].reshape(2 * WIDTH, CHANS)],
            axis=0,
        )
        base = piece[frame % 2, 11:16].reshape(WIDE, CHANS).astype(F32)
        new = (base + conv_rows(field, w_res[...], 5)).astype(BF16).reshape(5, WIDTH, CHANS)
        out[frame, 1:4] = new[1:4]
        out[frame, 0] = jnp.where(row > 0, new[0], jnp.zeros_like(new[0]))
        out[frame, 4] = jnp.where(row < 3, new[4], jnp.zeros_like(new[4]))


def last_kernel(state, upd, above, below, w_res, out):
    for frame in range(2):
        field = jnp.concatenate(
            [above[frame].reshape(WIDTH, CHANS), upd[frame].reshape(OWN, CHANS), below[frame].reshape(WIDTH, CHANS)], axis=0
        )
        base = state[frame, 1:4].reshape(OWN, CHANS).astype(F32)
        out[frame] = (base + conv_rows(field, w_res[...], ROWS)).astype(BF16).reshape(ROWS, WIDTH, CHANS)


VM = pl.BlockSpec(memory_space=pltpu.VMEM)
SM = pl.BlockSpec(memory_space=pltpu.SMEM)


def call(kernel, outs, scratch, flops, *args):
    specs = [SM if a.dtype == jnp.int32 else VM for a in args]
    size = sum(a.size * a.dtype.itemsize for a in args)
    return pl.pallas_call(
        kernel,
        out_shape=outs,
        in_specs=specs,
        out_specs=[VM] * len(outs),
        scratch_shapes=scratch,
        compiler_params=pltpu.CompilerParams(vmem_limit_bytes=24 * 2**20),
        cost_estimate=pl.CostEstimate(flops=flops, bytes_accessed=size, transcendentals=0),
    )(*args)


def slot_table(pairs, index, row):
    chip, core = index // 2, index % 2
    sources, targets, owners = (pairs[:, k] for k in range(3))

    def place(frame):
        dev = frame // 2 - 2 * chip
        other = (dev >= 1).astype(jnp.int32) != core
        beyond = (dev < 0) | (dev > 1)
        return 4 * other.astype(jnp.int32) + 2 * beyond.astype(jnp.int32) + frame % 2

    mine = (owners // 2 == chip).astype(jnp.int32)
    order = jnp.arange(pairs.shape[0], dtype=jnp.int32)
    ranks = jnp.sum(jnp.where(order[None, :] < order[:, None], mine[None, :], 0), axis=1)
    codes = place(sources) * SLOTS + place(targets)
    levels = 2 * jnp.arange(SLOTS, dtype=jnp.int32) + core
    picked = jnp.sum(jnp.where((ranks[None, :] == levels[:, None]) & (mine[None, :] == 1), codes[None, :], 0), axis=1)
    count = (jnp.sum(mine) - core + 1) // 2
    return jnp.concatenate([picked // SLOTS, picked % SLOTS, jnp.stack([count, row])])


def local(fmap, context, pairs, w_corr, w_zr, w_q, w_msg, w_res):
    index, row = lax.axis_index("frames"), lax.axis_index("rows")
    n_frames, n_rows = lax.axis_size("frames"), lax.axis_size("rows")
    up = [(i, i + 1) for i in range(n_rows - 1)]
    down = [(i + 1, i) for i in range(n_rows - 1)]
    across = [(i, (i + 2) % 4) for i in range(n_rows)]
    core_swap = [(i, i ^ 1) for i in range(n_frames)]
    chip_swap = [(i, ((i - 1) ^ 1) + 1) for i in range(1, n_frames - 1)]

    def swap_core(x):
        return lax.ppermute(x, "frames", core_swap)

    def swap_chip(x):
        return lax.ppermute(x, "frames", chip_swap)

    idx = slot_table(pairs, index, row)
    taps = w_corr.reshape(SPAN, SPAN, CHANS)
    order = (taps[0], taps[2], taps[4], jnp.zeros_like(taps[0]), taps[1], taps[3], taps[5], taps[6])
    wc = jnp.pad(jnp.stack(order), ((0, 0), (0, 1), (0, 0))).reshape(2, 32, CHANS)
    wc = jnp.pad(wc, ((0, 0), (4, 28), (0, 0))).reshape(2 * WIDTH, CHANS)
    wq = w_q.reshape(3, 3, 256, CHANS).transpose(0, 2, 1, 3).reshape(768, 384)
    wr = w_res.reshape(3, 3, CHANS, CHANS).transpose(0, 2, 1, 3).reshape(384, 384)

    with jax.named_scope("feature_rows"):
        from_above = lax.ppermute(jnp.concatenate([fmap, context[:, 2:]], axis=1), "rows", up)
        from_below = lax.ppermute(jnp.concatenate([fmap, context[:, :1]], axis=1), "rows", down)
        far = lax.ppermute(jnp.where(row < 2, fmap[:, 2:], fmap[:, :1]), "rows", across)
        none = jnp.zeros_like(far)
        own = jnp.concatenate(
            [
                jnp.where(row < 2, none, far),
                from_above[:, :3],
                fmap,
                from_below[:, :3],
                jnp.where(row < 2, far, none),
                from_above[:, 3:],
                context,
                from_below[:, 3:],
            ],
            axis=1,
        )
    with jax.named_scope("feature_window"):
        near = swap_chip(own)
        own_other = swap_core(own)
        near_other = swap_core(near)

    with jax.named_scope("first_iteration"):
        part, hid, motion = call(
            first_kernel,
            [
                jax.ShapeDtypeStruct((SLOTS, OWN, CHANS), BF16),
                jax.ShapeDtypeStruct((SLOTS, OWN, CHANS), F32),
                jax.ShapeDtypeStruct((SLOTS, WIDE, CHANS), BF16),
            ],
            [
                pltpu.VMEM((5, WIDTH, CHANS), BF16),
                pltpu.VMEM((11, WIDTH, CHANS), BF16),
                pltpu.VMEM((5, WIDTH, CHANS), BF16),
                pltpu.VMEM((SLOTS, OWN, CHANS), F32),
            ],
            2_000_000_000,
            idx, own, near, own_other, near_other, wc, w_zr, wq, w_msg,
        )

    def half_sum(part):
        return part[:4].astype(F32) + swap_core(part[4:]).astype(F32)

    with jax.named_scope("first_sums"):
        mine = half_sum(part)
        arrived = swap_chip(mine.astype(BF16)).astype(F32)
        total = mine + jnp.concatenate([arrived[2:], arrived[:2]])
        upd = jnp.maximum(total, 0.0).astype(BF16).reshape(4, ROWS, WIDTH, CHANS)
    with jax.named_scope("update_rows"):
        hid_last = hid[:, 2 * WIDTH :].astype(BF16)
        hid_first = hid[:, :WIDTH].astype(BF16)
        got_above = lax.ppermute(
            jnp.concatenate([upd[:, 1:].reshape(8, WIDTH, CHANS), hid_last]), "rows", up
        )
        got_below = lax.ppermute(
            jnp.concatenate([upd[:, :2].reshape(8, WIDTH, CHANS), hid_first]), "rows", down
        )
    with jax.named_scope("first_state"):
        [state] = call(
            state_kernel,
            [jax.ShapeDtypeStruct((4, 5, WIDTH, CHANS), BF16)],
            [],
            400_000_000,
            idx, own, near, upd, got_above[:8].reshape(4, 2, WIDTH, CHANS), got_below[:8].reshape(4, 2, WIDTH, CHANS), wr,
        )
        state_other = swap_core(state)
    with jax.named_scope("second_iteration"):
        [part] = call(
            second_kernel,
            [jax.ShapeDtypeStruct((SLOTS, OWN, CHANS), BF16)],
            [pltpu.VMEM((5, WIDTH, CHANS), BF16), pltpu.VMEM((SLOTS, OWN, CHANS), F32)],
            1_500_000_000,
            idx, state, state_other, motion, hid, got_above[8:], got_below[8:], w_zr, wq, w_msg,
        )
    with jax.named_scope("second_sums"):
        mine = half_sum(part)
        arrived = swap_chip(mine[2:].astype(BF16)).astype(F32)
        upd = jnp.maximum(mine[:2] + arrived, 0.0).astype(BF16).reshape(2, ROWS, WIDTH, CHANS)
        above = lax.ppermute(upd[:, 2:], "rows", up)
        below = lax.ppermute(upd[:, :1], "rows", down)
    with jax.named_scope("last_state"):
        [out] = call(
            last_kernel,
            [jax.ShapeDtypeStruct((2, ROWS, WIDTH, CHANS), BF16)],
            [],
            120_000_000,
            state, upd, above, below, wr,
        )
    return out


def solution(mesh):
    placed = (
        P("frames", "rows", None, None),
        P("frames", "rows", None, None),
        P(),
        P(),
        P(),
        P(),
        P(),
        P(),
    )
    return jax.shard_map(
        local,
        mesh=mesh,
        in_specs=placed,
        out_specs=P("frames", "rows", None, None),
        check_vma=False,
    )
```

time: 145 us -> 87 us (0.60); the launches traced: 142 us -> 86 us
  starting transfers between devices: 71.6 us -> 38.3 us
  other arithmetic: 19 us -> 2.38 us
  matrix products: 13 us -> 0 us
  Pallas kernels: 0 us -> 12.6 us
  local copies, waits for them, and re-layouts: 13.7 us -> 6.11 us
    ppermute x20 -> x15, starting transfers between devices: 71.6 us -> 38.3 us  [the longest x3 18.8 us: swap_chip(): return lax.ppermute(x, 'frames', chip_swap)]
    dot_general x45 -> x0, matrix products: 13 us -> none  [the longest x36 9.54 us: conv_taps(): jnp.dot(window, kernel[3 * row_off + col_off], preferred_element_type=jnp...]
    pallas_call x0 -> x4, Pallas kernels: none -> 12.6 us  [call(): pl.pallas_call(kernel, out_shape=outs, in_specs=specs, out_specs=[VM] * l...]
    dot_general x4 -> x0, other arithmetic: 11.5 us -> none  [local(): jnp.einsum('syxc,syxc->syx', src_feat, moved, preferred_element_type=jnp....]
    another operation x51 -> x1, local copies, waits for them, and re-layouts: 4.92 us -> 0.7 us  [local(): jnp.stack(order)]
    slice x12 -> x11, local copies, waits for them, and re-layouts: 3.82 us -> 0.18 us  [the longest x1 0.03 us: local(): upd[:, :2].reshape(8, WIDTH, CHANS)]
    concatenate x15 -> x4, other arithmetic: 3.67 us -> 0.16 us  [the longest x1 0.08 us: slot_table(): jnp.concatenate([picked // SLOTS, picked % SLOTS, jnp.stack([count, row])])]
    convert_element_type x11 -> x3, other arithmetic: 3.12 us -> 0.17 us  [the longest x1 0.09 us: local(): upd = jnp.maximum(total, 0.0).astype(BF16).reshape(4, ROWS, WIDTH, CHANS)]
  transfers between devices with their start and end apart: 20 -> 15, of which waited for: 14 -> 11; matrix products, arithmetic and copies ran while one was open for 4% -> 8% of each run, Pallas kernels for 0% -> 0%
where the time goes in v1:
time: 87 us; the launch traced here: 86 us
  starting transfers between devices  38.3 us (44%)
  waiting for transfers between devices  25.4 us (29%)
  Pallas kernels  12.6 us (14%)
  local copies, waits for them, and re-layouts  6.11 us (7%)
  other arithmetic  2.38 us (3%)
  between operations  1.17 us (1%)
    ppermute x3, starting transfers between devices, swap_chip(): return lax.ppermute(x, 'frames', chip_swap)  18.8 us
    pallas_call x4, Pallas kernels, call(): pl.pallas_call(kernel, out_shape=outs, in_specs=specs, out_specs=[VM] * l...  12.6 us
    ppermute x3, waiting for transfers between devices, swap_chip(): return lax.ppermute(x, 'frames', chip_swap)  11.5 us
    ppermute x5, waiting for transfers between devices, swap_core(): return lax.ppermute(x, 'frames', core_swap)  5.77 us
    ppermute x1, starting transfers between devices, local(): lax.ppermute(jnp.concatenate([upd[:, 1:].reshape(8, WIDTH, CHANS), hid_la...  4.92 us
    unnamed x28, local copies, waits for them, and re-layouts  4.43 us
    ppermute x1, waiting for transfers between devices, local(): below = lax.ppermute(upd[:, :1], 'rows', down)  4.23 us
    ppermute x1, starting transfers between devices, local(): above = lax.ppermute(upd[:, 2:], 'rows', up)  4.12 us
  transfers between devices with their start and end apart: 15, of which 11 were waited for; matrix products, arithmetic and copies ran while one was open for 8% of the time, Pallas kernels for 0%

profile of v1, /device:TPU:6, one launch (start us, length us, event | category | flops | bytes accessed | tf_op | source)
XLA Modules:
  0.0 86.0 jit_solution(4935054128299006318)
XLA Ops:
  0.9 3.2 %collective-permute-start = (bf16[2,1,64,128]{3,2,1,0:T(8,128)(2,1)S(1)}, bf16[2,1,64,128]{3,2,1,0:T(8,128)(2,1)S(1)}, u32[]{:S(2)}, u32[]{:S(2)}) collective-permute-start(bf16[2,1,64,128]{3,2,1,0:T(8,128)(2,1)S(1)} %slice_select_fusion), channel_id=1, source_target_pairs={{0,2},{1,3},{2,0},{3,1},{4,6},{5,7},{6,4},{7,5},{8,10},{9,11},{10,... | collective-permute-start | bytes 98312 | tf_op jit(solution)/shard_map/feature_rows/ppermute | solution.py:228
  4.1 2.6 %collective-permute-start.1 = (bf16[2,4,64,128]{3,2,1,0:T(8,128)(2,1)S(1)}, bf16[2,4,64,128]{3,2,1,0:T(8,128)(2,1)S(1)}, u32[]{:S(2)}, u32[]{:S(2)}) collective-permute-start(bf16[2,4,64,128]{3,2,1,0:T(8,128)(2,1)S(1)} %get-tuple-element.26), channel_id=1, source_target_pairs={{0,1},{1,2},{2,3},{4,5},{5,6},{6,7},{8,9},{9,10},{10,11},{12,13},{... | collective-permute-start | bytes 393224 | tf_op jit(solution)/shard_map/feature_rows/ppermute | solution.py:226
  6.7 1.3 %collective-permute-start.2 = (bf16[2,4,64,128]{3,2,1,0:T(8,128)(2,1)S(1)}, bf16[2,4,64,128]{3,2,1,0:T(8,128)(2,1)S(1)}, u32[]{:S(2)}, u32[]{:S(2)}) collective-permute-start(bf16[2,4,64,128]{3,2,1,0:T(8,128)(2,1)S(1)} %get-tuple-element.25), channel_id=1, source_target_pairs={{1,0},{2,1},{3,2},{5,4},{6,5},{7,6},{9,8},{10,9},{11,10},{13,12},{... | collective-permute-start | bytes 393224 | tf_op jit(solution)/shard_map/feature_rows/ppermute | solution.py:227
  14.5 7.0 %collective-permute-start.3 = (bf16[2,16,64,128]{3,2,1,0:T(8,128)(2,1)S(1)}, bf16[2,16,64,128]{3,2,1,0:T(8,128)(2,1)S(1)}, u32[]{:S(2)}, u32[]{:S(2)}) collective-permute-start(bf16[2,16,64,128]{3,2,1,0:T(8,128)(2,1)S(1)} %constant_dynamic-update-slice_fusion.p0.own), channel_id=1, source_target_pairs={{4,8},{8,4},{12,16},{16,12},{20,24},{24,20},{28,32},{32,28},{36,40... | collective-permute-start | bytes 1572872 | tf_op jit(solution)/shard_map/feature_window/ppermute | solution.py:215
  22.6 5.9 %collective-permute-done.3.p1.near = bf16[2,16,64,128]{3,2,1,0:T(8,128)(2,1)S(1)} collective-permute-done((bf16[2,16,64,128]{3,2,1,0:T(8,128)(2,1)S(1)}, bf16[2,16,64,128]{3,2,1,0:T(8,128)(2,1)S(1)}, u32[]{:S(2)}, u32[]{:S(2)}) %collective-permute-start.3) | collective-permute-done | bytes 524320 | tf_op jit(solution)/shard_map/feature_window/ppermute | solution.py:215
  28.7 1.6 %collective-permute-done.5.p3 = bf16[2,16,64,128]{3,2,1,0:T(8,128)(2,1)S(1)} collective-permute-done((bf16[2,16,64,128]{3,2,1,0:T(8,128)(2,1)S(1)}, bf16[2,16,64,128]{3,2,1,0:T(8,128)(2,1)S(1)}, u32[]{:S(2)}, u32[]{:S(2)}) %collective-permute-start.5) | collective-permute-done | bytes 524320 | tf_op jit(solution)/shard_map/feature_window/ppermute | solution.py:212
  30.4 7.0 %first_iteration.1 = (bf16[8,192,128]{2,1,0:T(8,128)(2,1)S(1)}, f32[8,192,128]{2,1,0:T(8,128)S(1)}, bf16[8,320,128]{2,1,0:T(8,128)(2,1)S(1)}) custom-call(s32[18]{0:T(128)S(1)} %pad_add_fusion.idx, bf16[2,16,64,128]{3,2,1,0:T(8,128)(2,1)S(1)} %constant_dynamic-update-slice_fusion.p0.own, bf16[2,16,64,128]{3,2,1,0:T(8,128)(2,1)S(1)} %collective-permute-done.3.p1.near, ...), custom_call_target="tpu_custom_call" | custom-call | flops 2000000000 | bytes 2916424 | tf_op jit(solution)/shard_map/first_iteration/pallas_call | solution.py:171
  37.7 1.2 %collective-permute-done.6 = bf16[4,192,128]{2,1,0:T(8,128)(2,1)S(1)} collective-permute-done((bf16[4,192,128]{2,1,0:T(8,128)(2,1)S(1)}, bf16[4,192,128]{2,1,0:T(8,128)(2,1)S(1)}, u32[]{:S(2)}, u32[]{:S(2)}) %collective-permute-start.6) | collective-permute-done | bytes 196640 | tf_op jit(solution)/shard_map/first_sums/ppermute | solution.py:212
  39.0 5.7 %collective-permute-start.7 = (bf16[4,192,128]{2,1,0:T(8,128)(2,1)S(1)}, bf16[4,192,128]{2,1,0:T(8,128)(2,1)S(1)}, u32[]{:S(2)}, u32[]{:S(2)}) collective-permute-start(bf16[4,192,128]{2,1,0:T(8,128)(2,1)S(1)} %fusion.2), channel_id=1, source_target_pairs={{4,8},{8,4},{12,16},{16,12},{20,24},{24,20},{28,32},{32,28},{36,40... | collective-permute-start | bytes 589832 | tf_op jit(solution)/shard_map/first_sums/ppermute | solution.py:215
  44.8 3.3 %collective-permute-done.7 = bf16[4,192,128]{2,1,0:T(8,128)(2,1)S(1)} collective-permute-done((bf16[4,192,128]{2,1,0:T(8,128)(2,1)S(1)}, bf16[4,192,128]{2,1,0:T(8,128)(2,1)S(1)}, u32[]{:S(2)}, u32[]{:S(2)}) %collective-permute-start.7) | collective-permute-done | bytes 196640 | tf_op jit(solution)/shard_map/first_sums/ppermute | solution.py:215
  48.3 1.4 %collective-permute-start.9 = (bf16[16,64,128]{2,1,0:T(8,128)(2,1)S(1)}, bf16[16,64,128]{2,1,0:T(8,128)(2,1)S(1)}, u32[]{:S(2)}, u32[]{:S(2)}) collective-permute-start(bf16[16,64,128]{2,1,0:T(8,128)(2,1)S(1)} %pad_maximum_fusion.1), channel_id=1, source_target_pairs={{1,0},{2,1},{3,2},{5,4},{6,5},{7,6},{9,8},{10,9},{11,10},{13,12},{... | collective-permute-start | bytes 786440 | tf_op jit(solution)/shard_map/update_rows/ppermute | solution.py:280
  49.8 4.9 %collective-permute-start.8 = (bf16[16,64,128]{2,1,0:T(8,128)(2,1)S(1)}, bf16[16,64,128]{2,1,0:T(8,128)(2,1)S(1)}, u32[]{:S(2)}, u32[]{:S(2)}) collective-permute-start(bf16[16,64,128]{2,1,0:T(8,128)(2,1)S(1)} %pad_maximum_fusion), channel_id=1, source_target_pairs={{0,1},{1,2},{2,3},{4,5},{5,6},{6,7},{8,9},{9,10},{10,11},{12,13},{... | collective-permute-start | bytes 786440 | tf_op jit(solution)/shard_map/update_rows/ppermute | solution.py:277
  55.0 2.5 %collective-permute-done.9 = bf16[16,64,128]{2,1,0:T(8,128)(2,1)S(1)} collective-permute-done((bf16[16,64,128]{2,1,0:T(8,128)(2,1)S(1)}, bf16[16,64,128]{2,1,0:T(8,128)(2,1)S(1)}, u32[]{:S(2)}, u32[]{:S(2)}) %collective-permute-start.9) | collective-permute-done | bytes 262176 | tf_op jit(solution)/shard_map/update_rows/ppermute | solution.py:280
  57.5 1.2 %collective-permute-done.8 = bf16[16,64,128]{2,1,0:T(8,128)(2,1)S(1)} collective-permute-done((bf16[16,64,128]{2,1,0:T(8,128)(2,1)S(1)}, bf16[16,64,128]{2,1,0:T(8,128)(2,1)S(1)}, u32[]{:S(2)}, u32[]{:S(2)}) %collective-permute-start.8) | collective-permute-done | bytes 262176 | tf_op jit(solution)/shard_map/update_rows/ppermute | solution.py:277
  58.7 1.3 %first_state.1.s0.state = bf16[4,5,64,128]{3,2,1,0:T(8,128)(2,1)S(1)} custom-call(s32[18]{0:T(128)S(1)} %pad_add_fusion.idx, bf16[2,16,64,128]{3,2,1,0:T(8,128)(2,1)S(1)} %constant_dynamic-update-slice_fusion.p0.own, bf16[2,16,64,128]{3,2,1,0:T(8,128)(2,1)S(1)} %collective-permute-done.3.p1.near, bf16[4,3,64,128]{3,2,1,0:T(8,128)(2,1)S(1)} %bitcast.44, ...), custom_call_target="tpu_custom_call" | custom-call | flops 400000000 | bytes 1802312 | tf_op jit(solution)/shard_map/first_state/pallas_call | solution.py:171
  60.2 1.6 %collective-permute-done.10.s1 = bf16[4,5,64,128]{3,2,1,0:T(8,128)(2,1)S(1)} collective-permute-done((bf16[4,5,64,128]{3,2,1,0:T(8,128)(2,1)S(1)}, bf16[4,5,64,128]{3,2,1,0:T(8,128)(2,1)S(1)}, u32[]{:S(2)}, u32[]{:S(2)}) %collective-permute-start.10) | collective-permute-done | bytes 327712 | tf_op jit(solution)/shard_map/first_state/ppermute | solution.py:212
  61.8 3.3 %second_iteration.1 = bf16[8,192,128]{2,1,0:T(8,128)(2,1)S(1)} custom-call(s32[18]{0:T(128)S(1)} %pad_add_fusion.idx, bf16[4,5,64,128]{3,2,1,0:T(8,128)(2,1)S(1)} %first_state.1.s0.state, bf16[4,5,64,128]{3,2,1,0:T(8,128)(2,1)S(1)} %collective-permute-done.10.s1, bf16[8,320,128]{2,1,0:T(8,128)(2,1)S(1)} %get-tuple-element.10.motion, ...), custom_call_target="tpu_custom_call" | custom-call | flops 1500000000 | bytes 3145800 | tf_op jit(solution)/shard_map/second_iteration/pallas_call | solution.py:171
  65.3 1.3 %collective-permute-done.11 = bf16[4,192,128]{2,1,0:T(8,128)(2,1)S(1)} collective-permute-done((bf16[4,192,128]{2,1,0:T(8,128)(2,1)S(1)}, bf16[4,192,128]{2,1,0:T(8,128)(2,1)S(1)}, u32[]{:S(2)}, u32[]{:S(2)}) %collective-permute-start.11) | collective-permute-done | bytes 196640 | tf_op jit(solution)/shard_map/second_sums/ppermute | solution.py:212
  66.7 6.0 %collective-permute-start.12 = (bf16[2,192,128]{2,1,0:T(8,128)(2,1)S(1)}, bf16[2,192,128]{2,1,0:T(8,128)(2,1)S(1)}, u32[]{:S(2)}, u32[]{:S(2)}) collective-permute-start(bf16[2,192,128]{2,1,0:T(8,128)(2,1)S(1)} %slice.217), channel_id=1, source_target_pairs={{4,8},{8,4},{12,16},{16,12},{20,24},{24,20},{28,32},{32,28},{36,40... | collective-permute-start | bytes 294920 | tf_op jit(solution)/shard_map/second_sums/ppermute | solution.py:215
  72.7 2.3 %collective-permute-done.12 = bf16[2,192,128]{2,1,0:T(8,128)(2,1)S(1)} collective-permute-done((bf16[2,192,128]{2,1,0:T(8,128)(2,1)S(1)}, bf16[2,192,128]{2,1,0:T(8,128)(2,1)S(1)}, u32[]{:S(2)}, u32[]{:S(2)}) %collective-permute-start.12) | collective-permute-done | bytes 98336 | tf_op jit(solution)/shard_map/second_sums/ppermute | solution.py:215
  75.1 4.1 %collective-permute-start.13 = (bf16[2,1,64,128]{3,2,1,0:T(8,128)(2,1)S(1)}, bf16[2,1,64,128]{3,2,1,0:T(8,128)(2,1)S(1)}, u32[]{:S(2)}, u32[]{:S(2)}) collective-permute-start(bf16[2,1,64,128]{3,2,1,0:T(8,128)(2,1)S(1)} %get-tuple-element.24), channel_id=1, source_target_pairs={{0,1},{1,2},{2,3},{4,5},{5,6},{6,7},{8,9},{9,10},{10,11},{12,13},{... | collective-permute-start | bytes 98312 | tf_op jit(solution)/shard_map/second_sums/ppermute | solution.py:304
  79.2 1.3 %collective-permute-start.14 = (bf16[2,1,64,128]{3,2,1,0:T(8,128)(2,1)S(1)}, bf16[2,1,64,128]{3,2,1,0:T(8,128)(2,1)S(1)}, u32[]{:S(2)}, u32[]{:S(2)}) collective-permute-start(bf16[2,1,64,128]{3,2,1,0:T(8,128)(2,1)S(1)} %get-tuple-element.23), channel_id=1, source_target_pairs={{1,0},{2,1},{3,2},{5,4},{6,5},{7,6},{9,8},{10,9},{11,10},{13,12},{... | collective-permute-start | bytes 98312 | tf_op jit(solution)/shard_map/second_sums/ppermute | solution.py:305
  80.8 4.2 %collective-permute-done.14.below = bf16[2,1,64,128]{3,2,1,0:T(8,128)(2,1)S(1)} collective-permute-done((bf16[2,1,64,128]{3,2,1,0:T(8,128)(2,1)S(1)}, bf16[2,1,64,128]{3,2,1,0:T(8,128)(2,1)S(1)}, u32[]{:S(2)}, u32[]{:S(2)}) %collective-permute-start.14) | collective-permute-done | bytes 32800 | tf_op jit(solution)/shard_map/second_sums/ppermute | solution.py:305
  85.0 1.0 %last_state.1 = bf16[2,3,64,128]{3,2,1,0:T(8,128)(2,1)} custom-call(bf16[4,5,64,128]{3,2,1,0:T(8,128)(2,1)S(1)} %first_state.1.s0.state, bf16[2,3,64,128]{3,2,1,0:T(8,128)(2,1)S(1)} %bitcast.46, bf16[2,1,64,128]{3,2,1,0:T(8,128)(2,1)S(1)} %collective-permute-done.13.above, bf16[2,1,64,128]{3,2,1,0:T(8,128)(2,1)S(1)} %collective-permute-done.14.below, ...), custom_call_target="tpu_custom_call" | custom-call | flops 120000000 | bytes 786432 | tf_op jit(solution)/shard_map/last_state/pallas_call | solution.py:171
  (74 shorter events, 9.4 us)
Async XLA Ops:
  0.0 4.1 %copy-start.5 = (bf16[2,3,64,128]{3,2,1,0:T(8,128)(2,1)S(1)}, bf16[2,3,64,128]{3,2,1,0:T(8,128)(2,1)}, u32[]{:S(2)}) copy-start(bf16[2,3,64,128]{3,2,1,0:T(8,128)(2,1)} %param.9) | copy-start | bytes 294916
  0.0 8.0 %copy-start.6 = (s32[256,3]{0,1:T(4,128)S(1)}, s32[256,3]{0,1:T(4,128)}, u32[]{:S(2)}) copy-start(s32[256,3]{0,1:T(4,128)} %param.10) | copy-start | bytes 9220
  0.0 4.1 %copy-start.2 = (bf16[2,3,64,128]{3,2,1,0:T(8,128)(2,1)S(1)}, bf16[2,3,64,128]{3,2,1,0:T(8,128)(2,1)}, u32[]{:S(2)}) copy-start(bf16[2,3,64,128]{3,2,1,0:T(8,128)(2,1)} %param.8) | copy-start | bytes 294916
  0.0 13.7 %copy-start.3 = (bf16[9,256,128]{2,1,0:T(8,128)(2,1)S(1)}, bf16[9,256,128]{2,1,0:T(8,128)(2,1)}, u32[]{:S(2)}) copy-start(bf16[9,256,128]{2,1,0:T(8,128)(2,1)} %param.13) | copy-start | bytes 1769476
  0.9 13.4 %collective-permute-start = (bf16[2,1,64,128]{3,2,1,0:T(8,128)(2,1)S(1)}, bf16[2,1,64,128]{3,2,1,0:T(8,128)(2,1)S(1)}, u32[]{:S(2)}, u32[]{:S(2)}) collective-permute-start(bf16[2,1,64,128]{3,2,1,0:T(8,128)(2,1)S(1)} %slice_select_fusion), channel_id=1, source_target_pairs={{0,2},{1,3},{2,0},{3,1},{4,6},{5,7},{6,4},{7,5},{8,10},{9,11},{10,... | collective-permute-start | bytes 98312 | tf_op jit(solution)/shard_map/feature_rows/ppermute | solution.py:228
  4.1 10.2 %collective-permute-start.1 = (bf16[2,4,64,128]{3,2,1,0:T(8,128)(2,1)S(1)}, bf16[2,4,64,128]{3,2,1,0:T(8,128)(2,1)S(1)}, u32[]{:S(2)}, u32[]{:S(2)}) collective-permute-start(bf16[2,4,64,128]{3,2,1,0:T(8,128)(2,1)S(1)} %get-tuple-element.26), channel_id=1, source_target_pairs={{0,1},{1,2},{2,3},{4,5},{5,6},{6,7},{8,9},{9,10},{10,11},{12,13},{... | collective-permute-start | bytes 393224 | tf_op jit(solution)/shard_map/feature_rows/ppermute | solution.py:226
  6.7 7.7 %collective-permute-start.2 = (bf16[2,4,64,128]{3,2,1,0:T(8,128)(2,1)S(1)}, bf16[2,4,64,128]{3,2,1,0:T(8,128)(2,1)S(1)}, u32[]{:S(2)}, u32[]{:S(2)}) collective-permute-start(bf16[2,4,64,128]{3,2,1,0:T(8,128)(2,1)S(1)} %get-tuple-element.25), channel_id=1, source_target_pairs={{1,0},{2,1},{3,2},{5,4},{6,5},{7,6},{9,8},{10,9},{11,10},{13,12},{... | collective-permute-start | bytes 393224 | tf_op jit(solution)/shard_map/feature_rows/ppermute | solution.py:227
  14.5 15.9 %copy-start.1 = (bf16[128,256]{1,0:T(8,128)(2,1)S(1)}, bf16[128,256]{1,0:T(8,128)(2,1)}, u32[]{:S(2)}) copy-start(bf16[128,256]{1,0:T(8,128)(2,1)} %w_msg.3) | copy-start | bytes 196612
  14.5 15.8 %copy-start = (bf16[256,256]{1,0:T(8,128)(2,1)S(1)}, bf16[256,256]{1,0:T(8,128)(2,1)}, u32[]{:S(2)}) copy-start(bf16[256,256]{1,0:T(8,128)(2,1)} %w_zr.3) | copy-start | bytes 393220
  14.5 13.9 %collective-permute-start.3 = (bf16[2,16,64,128]{3,2,1,0:T(8,128)(2,1)S(1)}, bf16[2,16,64,128]{3,2,1,0:T(8,128)(2,1)S(1)}, u32[]{:S(2)}, u32[]{:S(2)}) collective-permute-start(bf16[2,16,64,128]{3,2,1,0:T(8,128)(2,1)S(1)} %constant_dynamic-update-slice_fusion.p0.own), channel_id=1, source_target_pairs={{4,8},{8,4},{12,16},{16,12},{20,24},{24,20},{28,32},{32,28},{36,40... | collective-permute-start | bytes 1572872 | tf_op jit(solution)/shard_map/feature_window/ppermute | solution.py:215
  22.5 6.3 %collective-permute-start.4 = (bf16[2,16,64,128]{3,2,1,0:T(8,128)(2,1)S(1)}, bf16[2,16,64,128]{3,2,1,0:T(8,128)(2,1)S(1)}, u32[]{:S(2)}, u32[]{:S(2)}) collective-permute-start(bf16[2,16,64,128]{3,2,1,0:T(8,128)(2,1)S(1)} %constant_dynamic-update-slice_fusion.p0.own), channel_id=1, source_target_pairs={{0,4},{4,0},{8,12},{12,8},{16,20},{20,16},{24,28},{28,24},{32,36},... | collective-permute-start | bytes 1572872 | tf_op jit(solution)/shard_map/feature_window/ppermute | solution.py:212
  28.4 1.9 %collective-permute-start.5 = (bf16[2,16,64,128]{3,2,1,0:T(8,128)(2,1)S(1)}, bf16[2,16,64,128]{3,2,1,0:T(8,128)(2,1)S(1)}, u32[]{:S(2)}, u32[]{:S(2)}) collective-permute-start(bf16[2,16,64,128]{3,2,1,0:T(8,128)(2,1)S(1)} %collective-permute-done.3.p1.near), channel_id=1, source_target_pairs={{0,4},{4,0},{8,12},{12,8},{16,20},{20,16},{24,28},{28,24},{32,36},... | collective-permute-start | bytes 1572872 | tf_op jit(solution)/shard_map/feature_window/ppermute | solution.py:212
  37.4 1.5 %collective-permute-start.6 = (bf16[4,192,128]{2,1,0:T(8,128)(2,1)S(1)}, bf16[4,192,128]{2,1,0:T(8,128)(2,1)S(1)}, u32[]{:S(2)}, u32[]{:S(2)}) collective-permute-start(bf16[4,192,128]{2,1,0:T(8,128)(2,1)S(1)} %slice.158), channel_id=1, source_target_pairs={{0,4},{4,0},{8,12},{12,8},{16,20},{20,16},{24,28},{28,24},{32,36},... | collective-permute-start | bytes 589832 | tf_op jit(solution)/shard_map/first_sums/ppermute | solution.py:212
  39.0 9.1 %collective-permute-start.7 = (bf16[4,192,128]{2,1,0:T(8,128)(2,1)S(1)}, bf16[4,192,128]{2,1,0:T(8,128)(2,1)S(1)}, u32[]{:S(2)}, u32[]{:S(2)}) collective-permute-start(bf16[4,192,128]{2,1,0:T(8,128)(2,1)S(1)} %fusion.2), channel_id=1, source_target_pairs={{4,8},{8,4},{12,16},{16,12},{20,24},{24,20},{28,32},{32,28},{36,40... | collective-permute-start | bytes 589832 | tf_op jit(solution)/shard_map/first_sums/ppermute | solution.py:215
  48.3 6.4 %copy-start.4 = (bf16[9,128,128]{2,1,0:T(8,128)(2,1)S(1)}, bf16[9,128,128]{2,1,0:T(8,128)(2,1)}, u32[]{:S(2)}) copy-start(bf16[9,128,128]{2,1,0:T(8,128)(2,1)} %param.15) | copy-start | bytes 884740
  48.3 9.2 %collective-permute-start.9 = (bf16[16,64,128]{2,1,0:T(8,128)(2,1)S(1)}, bf16[16,64,128]{2,1,0:T(8,128)(2,1)S(1)}, u32[]{:S(2)}, u32[]{:S(2)}) collective-permute-start(bf16[16,64,128]{2,1,0:T(8,128)(2,1)S(1)} %pad_maximum_fusion.1), channel_id=1, source_target_pairs={{1,0},{2,1},{3,2},{5,4},{6,5},{7,6},{9,8},{10,9},{11,10},{13,12},{... | collective-permute-start | bytes 786440 | tf_op jit(solution)/shard_map/update_rows/ppermute | solution.py:280
  49.8 8.9 %collective-permute-start.8 = (bf16[16,64,128]{2,1,0:T(8,128)(2,1)S(1)}, bf16[16,64,128]{2,1,0:T(8,128)(2,1)S(1)}, u32[]{:S(2)}, u32[]{:S(2)}) collective-permute-start(bf16[16,64,128]{2,1,0:T(8,128)(2,1)S(1)} %pad_maximum_fusion), channel_id=1, source_target_pairs={{0,1},{1,2},{2,3},{4,5},{5,6},{6,7},{8,9},{9,10},{10,11},{12,13},{... | collective-permute-start | bytes 786440 | tf_op jit(solution)/shard_map/update_rows/ppermute | solution.py:277
  60.1 1.7 %collective-permute-start.10 = (bf16[4,5,64,128]{3,2,1,0:T(8,128)(2,1)S(1)}, bf16[4,5,64,128]{3,2,1,0:T(8,128)(2,1)S(1)}, u32[]{:S(2)}, u32[]{:S(2)}) collective-permute-start(bf16[4,5,64,128]{3,2,1,0:T(8,128)(2,1)S(1)} %first_state.1.s0.state), channel_id=1, source_target_pairs={{0,4},{4,0},{8,12},{12,8},{16,20},{20,16},{24,28},{28,24},{32,36},... | collective-permute-start | bytes 983048 | tf_op jit(solution)/shard_map/first_state/ppermute | solution.py:212
  65.1 1.5 %collective-permute-start.11 = (bf16[4,192,128]{2,1,0:T(8,128)(2,1)S(1)}, bf16[4,192,128]{2,1,0:T(8,128)(2,1)S(1)}, u32[]{:S(2)}, u32[]{:S(2)}) collective-permute-start(bf16[4,192,128]{2,1,0:T(8,128)(2,1)S(1)} %slice.190), channel_id=1, source_target_pairs={{0,4},{4,0},{8,12},{12,8},{16,20},{20,16},{24,28},{28,24},{32,36},... | collective-permute-start | bytes 589832 | tf_op jit(solution)/shard_map/second_sums/ppermute | solution.py:212
  66.7 8.3 %collective-permute-start.12 = (bf16[2,192,128]{2,1,0:T(8,128)(2,1)S(1)}, bf16[2,192,128]{2,1,0:T(8,128)(2,1)S(1)}, u32[]{:S(2)}, u32[]{:S(2)}) collective-permute-start(bf16[2,192,128]{2,1,0:T(8,128)(2,1)S(1)} %slice.217), channel_id=1, source_target_pairs={{4,8},{8,4},{12,16},{16,12},{20,24},{24,20},{28,32},{32,28},{36,40... | collective-permute-start | bytes 294920 | tf_op jit(solution)/shard_map/second_sums/ppermute | solution.py:215
  75.1 5.7 %collective-permute-start.13 = (bf16[2,1,64,128]{3,2,1,0:T(8,128)(2,1)S(1)}, bf16[2,1,64,128]{3,2,1,0:T(8,128)(2,1)S(1)}, u32[]{:S(2)}, u32[]{:S(2)}) collective-permute-start(bf16[2,1,64,128]{3,2,1,0:T(8,128)(2,1)S(1)} %get-tuple-element.24), channel_id=1, source_target_pairs={{0,1},{1,2},{2,3},{4,5},{5,6},{6,7},{8,9},{9,10},{10,11},{12,13},{... | collective-permute-start | bytes 98312 | tf_op jit(solution)/shard_map/second_sums/ppermute | solution.py:304
  79.2 5.8 %collective-permute-start.14 = (bf16[2,1,64,128]{3,2,1,0:T(8,128)(2,1)S(1)}, bf16[2,1,64,128]{3,2,1,0:T(8,128)(2,1)S(1)}, u32[]{:S(2)}, u32[]{:S(2)}) collective-permute-start(bf16[2,1,64,128]{3,2,1,0:T(8,128)(2,1)S(1)} %get-tuple-element.23), channel_id=1, source_target_pairs={{1,0},{2,1},{3,2},{5,4},{6,5},{7,6},{9,8},{10,9},{11,10},{13,12},{... | collective-permute-start | bytes 98312 | tf_op jit(solution)/shard_map/second_sums/ppermute | solution.py:305

commit v2 on v1

--- a/solution.py
+++ b/solution.py
@@ -28,6 +28,11 @@
     return 0.5 * jnp.tanh(0.5 * x) + 0.5
 
 
+def side_by_side(weights):
+    rows = [jnp.concatenate([weights[3 * k + j] for j in range(3)], axis=1) for k in range(3)]
+    return jnp.concatenate(rows, axis=0)
+
+
 def conv_rows(field, weights, rows):
     size = rows * WIDTH
     taps = [field[k * WIDTH : k * WIDTH + size] for k in range(3)]
@@ -46,6 +51,13 @@
     candidate = jnp.tanh(conv_rows(qin, w_q, ROWS))
     own = hidden[WIDTH : WIDTH + OWN]
     return own + update * (candidate - own)
+
+
+def filled(idx):
+    count = 0
+    for s in range(SLOTS):
+        count += jnp.where(idx[s] >= 0, 1, 0)
+    return count
 
 
 def band_mask(group):
@@ -71,11 +83,16 @@
 ):
     pieces = (p0, p1, p2, p3)
     ends = [lax.broadcasted_iota(jnp.int32, (WIDTH, WIDTH), k) for k in range(2)]
+    lane, tap = [lax.broadcasted_iota(jnp.int32, (CHANS, SPAN * SPAN), k) for k in range(2)]
+    place = lane % WIDTH - 4
+    shift = jnp.where(lane < WIDTH, 2 * (place // 8), jnp.minimum(2 * (place // 8) + 1, SPAN - 1))
+    wanted = (place >= 0) & (place < 32) & (place % 8 < SPAN) & (tap == SPAN * shift + place % 8)
+    spread = dot(jnp.where(wanted, 1.0, 0.0).astype(BF16), w_corr[...]).astype(BF16)
     flip = jnp.where(ends[0] + ends[1] == WIDTH - 1, 1.0, 0.0).astype(BF16)
     acc[...] = jnp.zeros_like(acc)
 
     def body(s, carry):
-        source, target = idx[s], idx[SLOTS + s]
+        source, target = idx[s] // SLOTS, idx[s] % SLOTS
         for k, piece in enumerate(pieces):
 
             @pl.when(source // 2 == k)
@@ -102,16 +119,16 @@
             corr.append((total * (1.0 / CHANS**0.5)).astype(BF16))
         turned = dot(flip, jnp.concatenate(corr, axis=1)).astype(BF16)
         corr = [turned[:, y * CHANS : (y + 1) * CHANS] for y in range(5)]
-        motion = jnp.maximum(dot(jnp.concatenate(corr, axis=0), w_corr[...]), 0.0).astype(BF16)
+        motion = jnp.maximum(dot(jnp.concatenate(corr, axis=0), spread), 0.0).astype(BF16)
         motion_out[s] = motion
         state = ctx[...].reshape(WIDE, CHANS).astype(F32)
         xin = (motion.astype(F32) + state).astype(BF16)
-        hidden = gru(jnp.tanh(state), xin, w_zr[...], w_q[...])
+        hidden = gru(jnp.tanh(state), xin, w_zr[...], side_by_side(w_q))
         hid[s] = hidden
         add_messages(acc, hidden, w_msg[...], source, target)
         return carry
 
-    lax.fori_loop(0, idx[2 * SLOTS], body, 0)
+    lax.fori_loop(0, filled(idx), body, 0)
     part[...] = acc[...].astype(BF16)
 
 
@@ -119,7 +136,7 @@
     acc[...] = jnp.zeros_like(acc)
 
     def body(s, carry):
-        source, target = idx[s], idx[SLOTS + s]
+        source, target = idx[s] // SLOTS, idx[s] % SLOTS
         for k, piece in enumerate((s0, s1)):
 
             @pl.when(source // 4 == k)
@@ -128,37 +145,54 @@
 
         state = state_buf[...].reshape(WIDE, CHANS).astype(F32)
         xin = (motion[s].astype(F32) + state).astype(BF16)
-        hidden = jnp.concatenate([above[s].astype(F32), hid[s], below[s].astype(F32)], axis=0)
-        hidden = gru(hidden, xin, w_zr[...], w_q[...])
+        row = idx[SLOTS]
+        first = kept(row > 0, above[s].astype(F32))
+        last = kept(row < 3, below[s].astype(F32))
+        hidden = jnp.concatenate([first, hid[s], last], axis=0)
+        hidden = gru(hidden, xin, w_zr[...], side_by_side(w_q))
         add_messages(acc, hidden, w_msg[...], source, target)
         return carry
 
-    lax.fori_loop(0, idx[2 * SLOTS], body, 0)
+    lax.fori_loop(0, filled(idx), body, 0)
     part[...] = acc[...].astype(BF16)
 
 
+def kept(keep, block):
+    return jnp.where(keep, block, jnp.zeros_like(block))
+
+
 def state_kernel(idx, own, near, upd, above, below, w_res, out):
-    row = idx[2 * SLOTS + 1]
+    row = idx[SLOTS]
     for frame in range(4):
         piece = own if frame < 2 else near
         field = jnp.concatenate(
-            [above[frame].reshape(2 * WIDTH, CHANS), upd[frame].reshape(OWN, CHANS), below[frame].reshape(2 * WIDTH, CHANS)],
+            [
+                kept(row > 0, above[frame].reshape(2 * WIDTH, CHANS)),
+                upd[frame].reshape(OWN, CHANS),
+                kept(row < 3, below[frame].reshape(2 * WIDTH, CHANS)),
+            ],
             axis=0,
         )
         base = piece[frame % 2, 11:16].reshape(WIDE, CHANS).astype(F32)
-        new = (base + conv_rows(field, w_res[...], 5)).astype(BF16).reshape(5, WIDTH, CHANS)
+        new = (base + conv_rows(field, side_by_side(w_res), 5)).astype(BF16).reshape(5, WIDTH, CHANS)
         out[frame, 1:4] = new[1:4]
-        out[frame, 0] = jnp.where(row > 0, new[0], jnp.zeros_like(new[0]))
-        out[frame, 4] = jnp.where(row < 3, new[4], jnp.zeros_like(new[4]))
-
-
-def last_kernel(state, upd, above, below, w_res, out):
+        out[frame, 0] = kept(row > 0, new[0])
+        out[frame, 4] = kept(row < 3, new[4])
+
+
+def last_kernel(idx, state, upd, above, below, w_res, out):
+    row = idx[SLOTS]
     for frame in range(2):
         field = jnp.concatenate(
-            [above[frame].reshape(WIDTH, CHANS), upd[frame].reshape(OWN, CHANS), below[frame].reshape(WIDTH, CHANS)], axis=0
+            [
+                kept(row > 0, above[frame].reshape(WIDTH, CHANS)),
+                upd[frame].reshape(OWN, CHANS),
+                kept(row < 3, below[frame].reshape(WIDTH, CHANS)),
+            ],
+            axis=0,
         )
         base = state[frame, 1:4].reshape(OWN, CHANS).astype(F32)
-        out[frame] = (base + conv_rows(field, w_res[...], ROWS)).astype(BF16).reshape(ROWS, WIDTH, CHANS)
+        out[frame] = (base + conv_rows(field, side_by_side(w_res), ROWS)).astype(BF16).reshape(ROWS, WIDTH, CHANS)
 
 
 VM = pl.BlockSpec(memory_space=pltpu.VMEM)
@@ -180,53 +214,46 @@
 
 
 def slot_table(pairs, index, row):
-    chip, core = index // 2, index % 2
+    chip, core = index >> 1, index & 1
     sources, targets, owners = (pairs[:, k] for k in range(3))
 
     def place(frame):
-        dev = frame // 2 - 2 * chip
-        other = (dev >= 1).astype(jnp.int32) != core
-        beyond = (dev < 0) | (dev > 1)
-        return 4 * other.astype(jnp.int32) + 2 * beyond.astype(jnp.int32) + frame % 2
-
-    mine = (owners // 2 == chip).astype(jnp.int32)
+        dev = (frame >> 1) - 2 * chip
+        other = jnp.where((dev >= 1) != (core == 1), 4, 0)
+        return other + jnp.where((dev < 0) | (dev > 1), 2, 0) + (frame & 1)
+
+    mine = (owners >> 1) == chip
     order = jnp.arange(pairs.shape[0], dtype=jnp.int32)
-    ranks = jnp.sum(jnp.where(order[None, :] < order[:, None], mine[None, :], 0), axis=1)
+    ranks = jnp.sum(jnp.where((order[None, :] < order[:, None]) & mine[None, :], 1, 0), axis=1)
     codes = place(sources) * SLOTS + place(targets)
     levels = 2 * jnp.arange(SLOTS, dtype=jnp.int32) + core
-    picked = jnp.sum(jnp.where((ranks[None, :] == levels[:, None]) & (mine[None, :] == 1), codes[None, :], 0), axis=1)
-    count = (jnp.sum(mine) - core + 1) // 2
-    return jnp.concatenate([picked // SLOTS, picked % SLOTS, jnp.stack([count, row])])
+    picked = jnp.where((ranks[None, :] == levels[:, None]) & mine[None, :], codes[None, :] + 1, 0)
+    picked = jnp.sum(picked, axis=1) - 1
+    return jnp.concatenate([picked, row[None]])
 
 
 def local(fmap, context, pairs, w_corr, w_zr, w_q, w_msg, w_res):
     index, row = lax.axis_index("frames"), lax.axis_index("rows")
     n_frames, n_rows = lax.axis_size("frames"), lax.axis_size("rows")
-    up = [(i, i + 1) for i in range(n_rows - 1)]
-    down = [(i + 1, i) for i in range(n_rows - 1)]
+    up = [(i, (i + 1) % n_rows) for i in range(n_rows)]
+    down = [(j, i) for i, j in up]
     across = [(i, (i + 2) % 4) for i in range(n_rows)]
     core_swap = [(i, i ^ 1) for i in range(n_frames)]
-    chip_swap = [(i, ((i - 1) ^ 1) + 1) for i in range(1, n_frames - 1)]
+    chip_swap = [(i, (i + 1 if i % 2 else i - 1) % n_frames) for i in range(n_frames)]
 
     def swap_core(x):
         return lax.ppermute(x, "frames", core_swap)
 
     def swap_chip(x):
         return lax.ppermute(x, "frames", chip_swap)
-
-    idx = slot_table(pairs, index, row)
-    taps = w_corr.reshape(SPAN, SPAN, CHANS)
-    order = (taps[0], taps[2], taps[4], jnp.zeros_like(taps[0]), taps[1], taps[3], taps[5], taps[6])
-    wc = jnp.pad(jnp.stack(order), ((0, 0), (0, 1), (0, 0))).reshape(2, 32, CHANS)
-    wc = jnp.pad(wc, ((0, 0), (4, 28), (0, 0))).reshape(2 * WIDTH, CHANS)
-    wq = w_q.reshape(3, 3, 256, CHANS).transpose(0, 2, 1, 3).reshape(768, 384)
-    wr = w_res.reshape(3, 3, CHANS, CHANS).transpose(0, 2, 1, 3).reshape(384, 384)
 
     with jax.named_scope("feature_rows"):
         from_above = lax.ppermute(jnp.concatenate([fmap, context[:, 2:]], axis=1), "rows", up)
         from_below = lax.ppermute(jnp.concatenate([fmap, context[:, :1]], axis=1), "rows", down)
         far = lax.ppermute(jnp.where(row < 2, fmap[:, 2:], fmap[:, :1]), "rows", across)
         none = jnp.zeros_like(far)
+        from_above = jnp.where(row > 0, from_above, jnp.zeros_like(from_above))
+        from_below = jnp.where(row < n_rows - 1, from_below, jnp.zeros_like(from_below))
         own = jnp.concatenate(
             [
                 jnp.where(row < 2, none, far),
@@ -240,6 +267,8 @@
             ],
             axis=1,
         )
+    own, pairs = lax.optimization_barrier((own, pairs))
+    idx = slot_table(pairs, index, row)
     with jax.named_scope("feature_window"):
         near = swap_chip(own)
         own_other = swap_core(own)
@@ -260,7 +289,7 @@
                 pltpu.VMEM((SLOTS, OWN, CHANS), F32),
             ],
             2_000_000_000,
-            idx, own, near, own_other, near_other, wc, w_zr, wq, w_msg,
+            idx, own, near, own_other, near_other, w_corr, w_zr, w_q, w_msg,
         )
 
     def half_sum(part):
@@ -286,7 +315,7 @@
             [jax.ShapeDtypeStruct((4, 5, WIDTH, CHANS), BF16)],
             [],
             400_000_000,
-            idx, own, near, upd, got_above[:8].reshape(4, 2, WIDTH, CHANS), got_below[:8].reshape(4, 2, WIDTH, CHANS), wr,
+            idx, own, near, upd, got_above[:8].reshape(4, 2, WIDTH, CHANS), got_below[:8].reshape(4, 2, WIDTH, CHANS), w_res,
         )
         state_other = swap_core(state)
     with jax.named_scope("second_iteration"):
@@ -295,7 +324,7 @@
             [jax.ShapeDtypeStruct((SLOTS, OWN, CHANS), BF16)],
             [pltpu.VMEM((5, WIDTH, CHANS), BF16), pltpu.VMEM((SLOTS, OWN, CHANS), F32)],
             1_500_000_000,
-            idx, state, state_other, motion, hid, got_above[8:], got_below[8:], w_zr, wq, w_msg,
+            idx, state, state_other, motion, hid, got_above[8:], got_below[8:], w_zr, w_q, w_msg,
         )
     with jax.named_scope("second_sums"):
         mine = half_sum(part)
@@ -309,7 +338,7 @@
             [jax.ShapeDtypeStruct((2, ROWS, WIDTH, CHANS), BF16)],
             [],
             120_000_000,
-            state, upd, above, below, wr,
+            idx, state, upd, above, below, w_res,
         )
     return out
 

time: 87 us -> 75.4 us (0.87)
  the two profiles are of different devices: /device:TPU:6 before, /device:TPU:0 now
where the time goes in v2:
time: 75.4 us; the launch traced here: 75.3 us
  waiting for transfers between devices  33.7 us (45%)
  starting transfers between devices  25.1 us (33%)
  Pallas kernels  13.3 us (18%)
  other arithmetic  1.66 us (2%)
  local copies, waits for them, and re-layouts  1.22 us (2%)
    ppermute x3, starting transfers between devices, swap_chip(): return lax.ppermute(x, 'frames', chip_swap)  15.1 us
    ppermute x3, waiting for transfers between devices, swap_chip(): return lax.ppermute(x, 'frames', chip_swap)  13.5 us
    pallas_call x4, Pallas kernels, call(): pl.pallas_call(kernel, out_shape=outs, in_specs=specs, out_specs=[VM] * l...  13.3 us
    ppermute x5, waiting for transfers between devices, swap_core(): return lax.ppermute(x, 'frames', core_swap)  5.68 us
    ppermute x1, waiting for transfers between devices, local(): lax.ppermute(jnp.concatenate([upd[:, 1:].reshape(8, WIDTH, CHANS), hid_la...  4.24 us
    ppermute x1, waiting for transfers between devices, local(): above = lax.ppermute(upd[:, 2:], 'rows', up)  3.53 us
    ppermute x1, starting transfers between devices, local(): lax.ppermute(jnp.concatenate([upd[:, :2].reshape(8, WIDTH, CHANS), hid_fi...  3.26 us
    ppermute x1, waiting for transfers between devices, local(): lax.ppermute(jnp.concatenate([fmap, context[:, 2:]], axis=1), 'rows', up)  3.09 us
  transfers between devices with their start and end apart: 15, of which 12 were waited for; matrix products, arithmetic and copies ran while one was open for 1% of the time, Pallas kernels for 0%

profile of v2, /device:TPU:0, one launch (start us, length us, event | category | flops | bytes accessed | tf_op | source)
XLA Modules:
  0.0 75.3 jit_solution(16901353285648445386)
XLA Ops:
  0.8 1.5 %collective-permute-start = (bf16[2,1,64,128]{3,2,1,0:T(8,128)(2,1)S(1)}, bf16[2,1,64,128]{3,2,1,0:T(8,128)(2,1)S(1)}, u32[]{:S(2)}, u32[]{:S(2)}) collective-permute-start(bf16[2,1,64,128]{3,2,1,0:T(8,128)(2,1)S(1)} %slice_select_fusion), channel_id=1, source_target_pairs={{0,2},{1,3},{2,0},{3,1},{4,6},{5,7},{6,4},{7,5},{8,10},{9,11},{10,... | collective-permute-start | bytes 98312 | tf_op jit(solution)/shard_map/feature_rows/ppermute | solution.py:253
  2.4 1.1 %collective-permute-start.2 = (bf16[2,4,64,128]{3,2,1,0:T(8,128)(2,1)S(1)}, bf16[2,4,64,128]{3,2,1,0:T(8,128)(2,1)S(1)}, u32[]{:S(2)}, u32[]{:S(2)}) collective-permute-start(bf16[2,4,64,128]{3,2,1,0:T(8,128)(2,1)S(1)} %get-tuple-element.27), channel_id=1, source_target_pairs={{1,0},{2,1},{3,2},{0,3},{5,4},{6,5},{7,6},{4,7},{9,8},{10,9},{11,1... | collective-permute-start | bytes 393224 | tf_op jit(solution)/shard_map/feature_rows/ppermute | solution.py:252
  3.5 1.0 %collective-permute-start.1 = (bf16[2,4,64,128]{3,2,1,0:T(8,128)(2,1)S(1)}, bf16[2,4,64,128]{3,2,1,0:T(8,128)(2,1)S(1)}, u32[]{:S(2)}, u32[]{:S(2)}) collective-permute-start(bf16[2,4,64,128]{3,2,1,0:T(8,128)(2,1)S(1)} %get-tuple-element.28), channel_id=1, source_target_pairs={{0,1},{1,2},{2,3},{3,0},{4,5},{5,6},{6,7},{7,4},{8,9},{9,10},{10,1... | collective-permute-start | bytes 393224 | tf_op jit(solution)/shard_map/feature_rows/ppermute | solution.py:251
  4.5 2.1 %collective-permute-done = bf16[2,1,64,128]{3,2,1,0:T(8,128)(2,1)S(1)} collective-permute-done((bf16[2,1,64,128]{3,2,1,0:T(8,128)(2,1)S(1)}, bf16[2,1,64,128]{3,2,1,0:T(8,128)(2,1)S(1)}, u32[]{:S(2)}, u32[]{:S(2)}) %collective-permute-start) | collective-permute-done | bytes 32800 | tf_op jit(solution)/shard_map/feature_rows/ppermute | solution.py:253
  6.6 3.1 %collective-permute-done.1 = bf16[2,4,64,128]{3,2,1,0:T(8,128)(2,1)S(1)} collective-permute-done((bf16[2,4,64,128]{3,2,1,0:T(8,128)(2,1)S(1)}, bf16[2,4,64,128]{3,2,1,0:T(8,128)(2,1)S(1)}, u32[]{:S(2)}, u32[]{:S(2)}) %collective-permute-start.1) | collective-permute-done | bytes 131104 | tf_op jit(solution)/shard_map/feature_rows/ppermute | solution.py:251
  9.9 5.9 %collective-permute-start.3 = (bf16[2,16,64,128]{3,2,1,0:T(8,128)(2,1)S(1)}, bf16[2,16,64,128]{3,2,1,0:T(8,128)(2,1)S(1)}, u32[]{:S(2)}, u32[]{:S(2)}) collective-permute-start(bf16[2,16,64,128]{3,2,1,0:T(8,128)(2,1)S(1)} %slice_dynamic-update-slice_fusion.2.p0.own), channel_id=1, source_target_pairs={{0,252},{4,8},{8,4},{12,16},{16,12},{20,24},{24,20},{28,32},{32,28... | collective-permute-start | bytes 1572872 | tf_op jit(solution)/shard_map/feature_window/ppermute | solution.py:248
  15.8 6.8 %collective-permute-done.3.p1.near = bf16[2,16,64,128]{3,2,1,0:T(8,128)(2,1)S(1)} collective-permute-done((bf16[2,16,64,128]{3,2,1,0:T(8,128)(2,1)S(1)}, bf16[2,16,64,128]{3,2,1,0:T(8,128)(2,1)S(1)}, u32[]{:S(2)}, u32[]{:S(2)}) %collective-permute-start.3) | collective-permute-done | bytes 524320 | tf_op jit(solution)/shard_map/feature_window/ppermute | solution.py:248
  23.0 1.5 %collective-permute-done.5.p3 = bf16[2,16,64,128]{3,2,1,0:T(8,128)(2,1)S(1)} collective-permute-done((bf16[2,16,64,128]{3,2,1,0:T(8,128)(2,1)S(1)}, bf16[2,16,64,128]{3,2,1,0:T(8,128)(2,1)S(1)}, u32[]{:S(2)}, u32[]{:S(2)}) %collective-permute-start.5) | collective-permute-done | bytes 524320 | tf_op jit(solution)/shard_map/feature_window/ppermute | solution.py:245
  24.6 7.1 %first_iteration.1 = (bf16[8,192,128]{2,1,0:T(8,128)(2,1)S(1)}, f32[8,192,128]{2,1,0:T(8,128)S(1)}, bf16[8,320,128]{2,1,0:T(8,128)(2,1)S(1)}) custom-call(s32[9]{0:T(128)S(1)} %pad_add_fusion.idx, bf16[2,16,64,128]{3,2,1,0:T(8,128)(2,1)S(1)} %slice_dynamic-update-slice_fusion.2.p0.own, bf16[2,16,64,128]{3,2,1,0:T(8,128)(2,1)S(1)} %collective-permute-done.3.p1.near, ...), custom_call_target="tpu_custom_call" | custom-call | flops 2000000000 | bytes 2896164 | tf_op jit(solution)/shard_map/first_iteration/pallas_call | solution.py:205
  32.0 1.2 %collective-permute-done.6 = bf16[4,192,128]{2,1,0:T(8,128)(2,1)S(1)} collective-permute-done((bf16[4,192,128]{2,1,0:T(8,128)(2,1)S(1)}, bf16[4,192,128]{2,1,0:T(8,128)(2,1)S(1)}, u32[]{:S(2)}, u32[]{:S(2)}) %collective-permute-start.6) | collective-permute-done | bytes 196640 | tf_op jit(solution)/shard_map/first_sums/ppermute | solution.py:245
  33.3 5.2 %collective-permute-start.7 = (bf16[4,192,128]{2,1,0:T(8,128)(2,1)S(1)}, bf16[4,192,128]{2,1,0:T(8,128)(2,1)S(1)}, u32[]{:S(2)}, u32[]{:S(2)}) collective-permute-start(bf16[4,192,128]{2,1,0:T(8,128)(2,1)S(1)} %fusion.2), channel_id=1, source_target_pairs={{0,252},{4,8},{8,4},{12,16},{16,12},{20,24},{24,20},{28,32},{32,28... | collective-permute-start | bytes 589832 | tf_op jit(solution)/shard_map/first_sums/ppermute | solution.py:248
  38.5 3.3 %collective-permute-done.7 = bf16[4,192,128]{2,1,0:T(8,128)(2,1)S(1)} collective-permute-done((bf16[4,192,128]{2,1,0:T(8,128)(2,1)S(1)}, bf16[4,192,128]{2,1,0:T(8,128)(2,1)S(1)}, u32[]{:S(2)}, u32[]{:S(2)}) %collective-permute-start.7) | collective-permute-done | bytes 196640 | tf_op jit(solution)/shard_map/first_sums/ppermute | solution.py:248
  42.2 3.3 %collective-permute-start.9 = (bf16[16,64,128]{2,1,0:T(8,128)(2,1)S(1)}, bf16[16,64,128]{2,1,0:T(8,128)(2,1)S(1)}, u32[]{:S(2)}, u32[]{:S(2)}) collective-permute-start(bf16[16,64,128]{2,1,0:T(8,128)(2,1)S(1)} %pad_maximum_fusion.1), channel_id=1, source_target_pairs={{1,0},{2,1},{3,2},{0,3},{5,4},{6,5},{7,6},{4,7},{9,8},{10,9},{11,1... | collective-permute-start | bytes 786440 | tf_op jit(solution)/shard_map/update_rows/ppermute | solution.py:309
  45.4 4.2 %collective-permute-done.8 = bf16[16,64,128]{2,1,0:T(8,128)(2,1)S(1)} collective-permute-done((bf16[16,64,128]{2,1,0:T(8,128)(2,1)S(1)}, bf16[16,64,128]{2,1,0:T(8,128)(2,1)S(1)}, u32[]{:S(2)}, u32[]{:S(2)}) %collective-permute-start.8) | collective-permute-done | bytes 262176 | tf_op jit(solution)/shard_map/update_rows/ppermute | solution.py:306
  50.7 1.3 %first_state.1.s0.state = bf16[4,5,64,128]{3,2,1,0:T(8,128)(2,1)S(1)} custom-call(s32[9]{0:T(128)S(1)} %pad_add_fusion.idx, bf16[2,16,64,128]{3,2,1,0:T(8,128)(2,1)S(1)} %slice_dynamic-update-slice_fusion.2.p0.own, bf16[2,16,64,128]{3,2,1,0:T(8,128)(2,1)S(1)} %collective-permute-done.3.p1.near, bf16[4,3,64,128]{3,2,1,0:T(8,128)(2,1)S(1)} %bitcast.9, ...), custom_call_target="tpu_custom_call" | custom-call | flops 400000000 | bytes 1802276 | tf_op jit(solution)/shard_map/first_state/pallas_call | solution.py:205
  52.1 1.6 %collective-permute-done.10.s1 = bf16[4,5,64,128]{3,2,1,0:T(8,128)(2,1)S(1)} collective-permute-done((bf16[4,5,64,128]{3,2,1,0:T(8,128)(2,1)S(1)}, bf16[4,5,64,128]{3,2,1,0:T(8,128)(2,1)S(1)}, u32[]{:S(2)}, u32[]{:S(2)}) %collective-permute-start.10) | collective-permute-done | bytes 327712 | tf_op jit(solution)/shard_map/first_state/ppermute | solution.py:245
  53.7 3.3 %second_iteration.1 = bf16[8,192,128]{2,1,0:T(8,128)(2,1)S(1)} custom-call(s32[9]{0:T(128)S(1)} %pad_add_fusion.idx, bf16[4,5,64,128]{3,2,1,0:T(8,128)(2,1)S(1)} %first_state.1.s0.state, bf16[4,5,64,128]{3,2,1,0:T(8,128)(2,1)S(1)} %collective-permute-done.10.s1, bf16[8,320,128]{2,1,0:T(8,128)(2,1)S(1)} %get-tuple-element.14.motion, ...), custom_call_target="tpu_custom_call" | custom-call | flops 1500000000 | bytes 3145764 | tf_op jit(solution)/shard_map/second_iteration/pallas_call | solution.py:205
  57.3 1.3 %collective-permute-done.11 = bf16[4,192,128]{2,1,0:T(8,128)(2,1)S(1)} collective-permute-done((bf16[4,192,128]{2,1,0:T(8,128)(2,1)S(1)}, bf16[4,192,128]{2,1,0:T(8,128)(2,1)S(1)}, u32[]{:S(2)}, u32[]{:S(2)}) %collective-permute-start.11) | collective-permute-done | bytes 196640 | tf_op jit(solution)/shard_map/second_sums/ppermute | solution.py:245
  58.7 4.1 %collective-permute-start.12 = (bf16[2,192,128]{2,1,0:T(8,128)(2,1)S(1)}, bf16[2,192,128]{2,1,0:T(8,128)(2,1)S(1)}, u32[]{:S(2)}, u32[]{:S(2)}) collective-permute-start(bf16[2,192,128]{2,1,0:T(8,128)(2,1)S(1)} %slice.157), channel_id=1, source_target_pairs={{0,252},{4,8},{8,4},{12,16},{16,12},{20,24},{24,20},{28,32},{32,28... | collective-permute-start | bytes 294920 | tf_op jit(solution)/shard_map/second_sums/ppermute | solution.py:248
  62.8 3.4 %collective-permute-done.12 = bf16[2,192,128]{2,1,0:T(8,128)(2,1)S(1)} collective-permute-done((bf16[2,192,128]{2,1,0:T(8,128)(2,1)S(1)}, bf16[2,192,128]{2,1,0:T(8,128)(2,1)S(1)}, u32[]{:S(2)}, u32[]{:S(2)}) %collective-permute-start.12) | collective-permute-done | bytes 98336 | tf_op jit(solution)/shard_map/second_sums/ppermute | solution.py:248
  66.2 2.5 %collective-permute-start.14 = (bf16[2,1,64,128]{3,2,1,0:T(8,128)(2,1)S(1)}, bf16[2,1,64,128]{3,2,1,0:T(8,128)(2,1)S(1)}, u32[]{:S(2)}, u32[]{:S(2)}) collective-permute-start(bf16[2,1,64,128]{3,2,1,0:T(8,128)(2,1)S(1)} %get-tuple-element.25), channel_id=1, source_target_pairs={{1,0},{2,1},{3,2},{0,3},{5,4},{6,5},{7,6},{4,7},{9,8},{10,9},{11,1... | collective-permute-start | bytes 98312 | tf_op jit(solution)/shard_map/second_sums/ppermute | solution.py:334
  68.7 1.6 %collective-permute-done.14.below = bf16[2,1,64,128]{3,2,1,0:T(8,128)(2,1)S(1)} collective-permute-done((bf16[2,1,64,128]{3,2,1,0:T(8,128)(2,1)S(1)}, bf16[2,1,64,128]{3,2,1,0:T(8,128)(2,1)S(1)}, u32[]{:S(2)}, u32[]{:S(2)}) %collective-permute-start.14) | collective-permute-done | bytes 32800 | tf_op jit(solution)/shard_map/second_sums/ppermute | solution.py:334
  70.3 3.5 %collective-permute-done.13.above = bf16[2,1,64,128]{3,2,1,0:T(8,128)(2,1)S(1)} collective-permute-done((bf16[2,1,64,128]{3,2,1,0:T(8,128)(2,1)S(1)}, bf16[2,1,64,128]{3,2,1,0:T(8,128)(2,1)S(1)}, u32[]{:S(2)}, u32[]{:S(2)}) %collective-permute-start.13) | collective-permute-done | bytes 32800 | tf_op jit(solution)/shard_map/second_sums/ppermute | solution.py:333
  73.8 1.5 %last_state.1 = bf16[2,3,64,128]{3,2,1,0:T(8,128)(2,1)} custom-call(s32[9]{0:T(128)S(1)} %pad_add_fusion.idx, bf16[4,5,64,128]{3,2,1,0:T(8,128)(2,1)S(1)} %first_state.1.s0.state, bf16[2,3,64,128]{3,2,1,0:T(8,128)(2,1)S(1)} %bitcast.11, bf16[2,1,64,128]{3,2,1,0:T(8,128)(2,1)S(1)} %collective-permute-done.13.above, ...), custom_call_target="tpu_custom_call" | custom-call | flops 120000000 | bytes 786468 | tf_op jit(solution)/shard_map/last_state/pallas_call | solution.py:205
  (62 shorter events, 3.6 us)
Async XLA Ops:
  0.0 2.3 %copy-start.6 = (bf16[2,3,64,128]{3,2,1,0:T(8,128)(2,1)S(1)}, bf16[2,3,64,128]{3,2,1,0:T(8,128)(2,1)}, u32[]{:S(2)}) copy-start(bf16[2,3,64,128]{3,2,1,0:T(8,128)(2,1)} %param.9) | copy-start | bytes 294916
  0.0 2.3 %copy-start.5 = (bf16[2,3,64,128]{3,2,1,0:T(8,128)(2,1)S(1)}, bf16[2,3,64,128]{3,2,1,0:T(8,128)(2,1)}, u32[]{:S(2)}) copy-start(bf16[2,3,64,128]{3,2,1,0:T(8,128)(2,1)} %param.8) | copy-start | bytes 294916
  0.8 5.7 %collective-permute-start = (bf16[2,1,64,128]{3,2,1,0:T(8,128)(2,1)S(1)}, bf16[2,1,64,128]{3,2,1,0:T(8,128)(2,1)S(1)}, u32[]{:S(2)}, u32[]{:S(2)}) collective-permute-start(bf16[2,1,64,128]{3,2,1,0:T(8,128)(2,1)S(1)} %slice_select_fusion), channel_id=1, source_target_pairs={{0,2},{1,3},{2,0},{3,1},{4,6},{5,7},{6,4},{7,5},{8,10},{9,11},{10,... | collective-permute-start | bytes 98312 | tf_op jit(solution)/shard_map/feature_rows/ppermute | solution.py:253
  2.4 7.4 %collective-permute-start.2 = (bf16[2,4,64,128]{3,2,1,0:T(8,128)(2,1)S(1)}, bf16[2,4,64,128]{3,2,1,0:T(8,128)(2,1)S(1)}, u32[]{:S(2)}, u32[]{:S(2)}) collective-permute-start(bf16[2,4,64,128]{3,2,1,0:T(8,128)(2,1)S(1)} %get-tuple-element.27), channel_id=1, source_target_pairs={{1,0},{2,1},{3,2},{0,3},{5,4},{6,5},{7,6},{4,7},{9,8},{10,9},{11,1... | collective-permute-start | bytes 393224 | tf_op jit(solution)/shard_map/feature_rows/ppermute | solution.py:252
  3.5 6.2 %collective-permute-start.1 = (bf16[2,4,64,128]{3,2,1,0:T(8,128)(2,1)S(1)}, bf16[2,4,64,128]{3,2,1,0:T(8,128)(2,1)S(1)}, u32[]{:S(2)}, u32[]{:S(2)}) collective-permute-start(bf16[2,4,64,128]{3,2,1,0:T(8,128)(2,1)S(1)} %get-tuple-element.28), channel_id=1, source_target_pairs={{0,1},{1,2},{2,3},{3,0},{4,5},{5,6},{6,7},{7,4},{8,9},{9,10},{10,1... | collective-permute-start | bytes 393224 | tf_op jit(solution)/shard_map/feature_rows/ppermute | solution.py:251
  9.7 14.9 %copy-start.1 = (bf16[9,256,128]{2,1,0:T(8,128)(2,1)S(1)}, bf16[9,256,128]{2,1,0:T(8,128)(2,1)}, u32[]{:S(2)}) copy-start(bf16[9,256,128]{2,1,0:T(8,128)(2,1)} %w_q.3) | copy-start | bytes 1769476
  9.8 14.7 %copy-start.2 = (bf16[256,256]{1,0:T(8,128)(2,1)S(1)}, bf16[256,256]{1,0:T(8,128)(2,1)}, u32[]{:S(2)}) copy-start(bf16[256,256]{1,0:T(8,128)(2,1)} %w_zr.3) | copy-start | bytes 393220
  9.9 5.9 %copy-start.7 = (s32[256,3]{0,1:T(4,128)S(1)}, s32[256,3]{0,1:T(4,128)}, u32[]{:S(2)}) copy-start(s32[256,3]{0,1:T(4,128)} %param.10) | copy-start | bytes 9220
  9.9 14.7 %copy-start.3 = (bf16[128,256]{1,0:T(8,128)(2,1)S(1)}, bf16[128,256]{1,0:T(8,128)(2,1)}, u32[]{:S(2)}) copy-start(bf16[128,256]{1,0:T(8,128)(2,1)} %w_msg.3) | copy-start | bytes 196612
  9.9 12.7 %collective-permute-start.3 = (bf16[2,16,64,128]{3,2,1,0:T(8,128)(2,1)S(1)}, bf16[2,16,64,128]{3,2,1,0:T(8,128)(2,1)S(1)}, u32[]{:S(2)}, u32[]{:S(2)}) collective-permute-start(bf16[2,16,64,128]{3,2,1,0:T(8,128)(2,1)S(1)} %slice_dynamic-update-slice_fusion.2.p0.own), channel_id=1, source_target_pairs={{0,252},{4,8},{8,4},{12,16},{16,12},{20,24},{24,20},{28,32},{32,28... | collective-permute-start | bytes 1572872 | tf_op jit(solution)/shard_map/feature_window/ppermute | solution.py:248
  15.8 8.8 %copy-start.4 = (bf16[49,128]{1,0:T(8,128)(2,1)S(1)}, bf16[49,128]{1,0:T(8,128)(2,1)}, u32[]{:S(2)}) copy-start(bf16[49,128]{1,0:T(8,128)(2,1)} %w_corr.1) | copy-start | bytes 37636
  15.8 7.3 %collective-permute-start.4 = (bf16[2,16,64,128]{3,2,1,0:T(8,128)(2,1)S(1)}, bf16[2,16,64,128]{3,2,1,0:T(8,128)(2,1)S(1)}, u32[]{:S(2)}, u32[]{:S(2)}) collective-permute-start(bf16[2,16,64,128]{3,2,1,0:T(8,128)(2,1)S(1)} %slice_dynamic-update-slice_fusion.2.p0.own), channel_id=1, source_target_pairs={{0,4},{4,0},{8,12},{12,8},{16,20},{20,16},{24,28},{28,24},{32,36},... | collective-permute-start | bytes 1572872 | tf_op jit(solution)/shard_map/feature_window/ppermute | solution.py:245
  22.6 1.9 %collective-permute-start.5 = (bf16[2,16,64,128]{3,2,1,0:T(8,128)(2,1)S(1)}, bf16[2,16,64,128]{3,2,1,0:T(8,128)(2,1)S(1)}, u32[]{:S(2)}, u32[]{:S(2)}) collective-permute-start(bf16[2,16,64,128]{3,2,1,0:T(8,128)(2,1)S(1)} %collective-permute-done.3.p1.near), channel_id=1, source_target_pairs={{0,4},{4,0},{8,12},{12,8},{16,20},{20,16},{24,28},{28,24},{32,36},... | collective-permute-start | bytes 1572872 | tf_op jit(solution)/shard_map/feature_window/ppermute | solution.py:245
  31.7 1.5 %collective-permute-start.6 = (bf16[4,192,128]{2,1,0:T(8,128)(2,1)S(1)}, bf16[4,192,128]{2,1,0:T(8,128)(2,1)S(1)}, u32[]{:S(2)}, u32[]{:S(2)}) collective-permute-start(bf16[4,192,128]{2,1,0:T(8,128)(2,1)S(1)} %slice.102), channel_id=1, source_target_pairs={{0,4},{4,0},{8,12},{12,8},{16,20},{20,16},{24,28},{28,24},{32,36},... | collective-permute-start | bytes 589832 | tf_op jit(solution)/shard_map/first_sums/ppermute | solution.py:245
  33.3 8.5 %collective-permute-start.7 = (bf16[4,192,128]{2,1,0:T(8,128)(2,1)S(1)}, bf16[4,192,128]{2,1,0:T(8,128)(2,1)S(1)}, u32[]{:S(2)}, u32[]{:S(2)}) collective-permute-start(bf16[4,192,128]{2,1,0:T(8,128)(2,1)S(1)} %fusion.2), channel_id=1, source_target_pairs={{0,252},{4,8},{8,4},{12,16},{16,12},{20,24},{24,20},{28,32},{32,28... | collective-permute-start | bytes 589832 | tf_op jit(solution)/shard_map/first_sums/ppermute | solution.py:248
  42.0 7.7 %collective-permute-start.8 = (bf16[16,64,128]{2,1,0:T(8,128)(2,1)S(1)}, bf16[16,64,128]{2,1,0:T(8,128)(2,1)S(1)}, u32[]{:S(2)}, u32[]{:S(2)}) collective-permute-start(bf16[16,64,128]{2,1,0:T(8,128)(2,1)S(1)} %pad_maximum_fusion), channel_id=1, source_target_pairs={{0,1},{1,2},{2,3},{3,0},{4,5},{5,6},{6,7},{7,4},{8,9},{9,10},{10,1... | collective-permute-start | bytes 786440 | tf_op jit(solution)/shard_map/update_rows/ppermute | solution.py:306
  42.2 7.5 %collective-permute-start.9 = (bf16[16,64,128]{2,1,0:T(8,128)(2,1)S(1)}, bf16[16,64,128]{2,1,0:T(8,128)(2,1)S(1)}, u32[]{:S(2)}, u32[]{:S(2)}) collective-permute-start(bf16[16,64,128]{2,1,0:T(8,128)(2,1)S(1)} %pad_maximum_fusion.1), channel_id=1, source_target_pairs={{1,0},{2,1},{3,2},{0,3},{5,4},{6,5},{7,6},{4,7},{9,8},{10,9},{11,1... | collective-permute-start | bytes 786440 | tf_op jit(solution)/shard_map/update_rows/ppermute | solution.py:309
  49.7 1.0 %copy-start = (bf16[9,128,128]{2,1,0:T(8,128)(2,1)S(1)}, bf16[9,128,128]{2,1,0:T(8,128)(2,1)}, u32[]{:S(2)}) copy-start(bf16[9,128,128]{2,1,0:T(8,128)(2,1)} %w_res.3) | copy-start | bytes 884740
  52.0 1.7 %collective-permute-start.10 = (bf16[4,5,64,128]{3,2,1,0:T(8,128)(2,1)S(1)}, bf16[4,5,64,128]{3,2,1,0:T(8,128)(2,1)S(1)}, u32[]{:S(2)}, u32[]{:S(2)}) collective-permute-start(bf16[4,5,64,128]{3,2,1,0:T(8,128)(2,1)S(1)} %first_state.1.s0.state), channel_id=1, source_target_pairs={{0,4},{4,0},{8,12},{12,8},{16,20},{20,16},{24,28},{28,24},{32,36},... | collective-permute-start | bytes 983048 | tf_op jit(solution)/shard_map/first_state/ppermute | solution.py:245
  57.1 1.5 %collective-permute-start.11 = (bf16[4,192,128]{2,1,0:T(8,128)(2,1)S(1)}, bf16[4,192,128]{2,1,0:T(8,128)(2,1)S(1)}, u32[]{:S(2)}, u32[]{:S(2)}) collective-permute-start(bf16[4,192,128]{2,1,0:T(8,128)(2,1)S(1)} %slice.134), channel_id=1, source_target_pairs={{0,4},{4,0},{8,12},{12,8},{16,20},{20,16},{24,28},{28,24},{32,36},... | collective-permute-start | bytes 589832 | tf_op jit(solution)/shard_map/second_sums/ppermute | solution.py:245
  58.7 7.4 %collective-permute-start.12 = (bf16[2,192,128]{2,1,0:T(8,128)(2,1)S(1)}, bf16[2,192,128]{2,1,0:T(8,128)(2,1)S(1)}, u32[]{:S(2)}, u32[]{:S(2)}) collective-permute-start(bf16[2,192,128]{2,1,0:T(8,128)(2,1)S(1)} %slice.157), channel_id=1, source_target_pairs={{0,252},{4,8},{8,4},{12,16},{16,12},{20,24},{24,20},{28,32},{32,28... | collective-permute-start | bytes 294920 | tf_op jit(solution)/shard_map/second_sums/ppermute | solution.py:248
  66.2 4.1 %collective-permute-start.14 = (bf16[2,1,64,128]{3,2,1,0:T(8,128)(2,1)S(1)}, bf16[2,1,64,128]{3,2,1,0:T(8,128)(2,1)S(1)}, u32[]{:S(2)}, u32[]{:S(2)}) collective-permute-start(bf16[2,1,64,128]{3,2,1,0:T(8,128)(2,1)S(1)} %get-tuple-element.25), channel_id=1, source_target_pairs={{1,0},{2,1},{3,2},{0,3},{5,4},{6,5},{7,6},{4,7},{9,8},{10,9},{11,1... | collective-permute-start | bytes 98312 | tf_op jit(solution)/shard_map/second_sums/ppermute | solution.py:334
  68.7 5.1 %collective-permute-start.13 = (bf16[2,1,64,128]{3,2,1,0:T(8,128)(2,1)S(1)}, bf16[2,1,64,128]{3,2,1,0:T(8,128)(2,1)S(1)}, u32[]{:S(2)}, u32[]{:S(2)}) collective-permute-start(bf16[2,1,64,128]{3,2,1,0:T(8,128)(2,1)S(1)} %get-tuple-element.26), channel_id=1, source_target_pairs={{0,1},{1,2},{2,3},{3,0},{4,5},{5,6},{6,7},{7,4},{8,9},{9,10},{10,1... | collective-permute-start | bytes 98312 | tf_op jit(solution)/shard_map/second_sums/ppermute | solution.py:333

commit v3 on v2

v3 whole, which is shorter than its diff:
```python
import jax
import jax.numpy as jnp
from jax import lax
from jax.experimental import pallas as pl
from jax.experimental.pallas import tpu as pltpu
from jax.sharding import PartitionSpec as P

SLOTS = 8
ROWS = 3
WIDTH = 64
CHANS = 128
SPAN = 7
WIDE = 5 * WIDTH
OWN = ROWS * WIDTH
F32 = jnp.float32
BF16 = jnp.bfloat16


def dot(a, b):
    return lax.dot_general(a, b, (((1,), (0,)), ((), ())), preferred_element_type=F32)


def dot_t(a, b):
    return lax.dot_general(a, b, (((1,), (1,)), ((), ())), preferred_element_type=F32)


def sigmoid(x):
    return 0.5 * jnp.tanh(0.5 * x) + 0.5


def side_by_side(weights):
    rows = [jnp.concatenate([weights[3 * k + j] for j in range(3)], axis=1) for k in range(3)]
    return jnp.concatenate(rows, axis=0)


def conv_rows(fields, weights, rows):
    size = rows * WIDTH
    taps = [
        jnp.concatenate([field[k * WIDTH : k * WIDTH + size] for k in range(3)], axis=1) for field in fields
    ]
    out = dot(jnp.concatenate(taps), weights)
    size *= len(fields)
    column = lax.broadcasted_iota(jnp.int32, (size, CHANS), 0) & (WIDTH - 1)
    left = jnp.where(column == 0, 0.0, pltpu.roll(out[:, :CHANS], 1, 0))
    right = jnp.where(column == WIDTH - 1, 0.0, pltpu.roll(out[:, 2 * CHANS :], size - 1, 0))
    return out[:, CHANS : 2 * CHANS] + left + right


def gru(hidden, xin, w_zr, w_q):
    joined = [jnp.concatenate([h.astype(BF16), x], axis=1) for h, x in zip(hidden, xin)]
    own = slice(WIDTH, WIDTH + OWN)
    reset = sigmoid(dot(jnp.concatenate(joined), w_zr[:, CHANS:]))
    update = sigmoid(dot(jnp.concatenate([j[own] for j in joined]), w_zr[:, :CHANS]))
    gated = (reset * jnp.concatenate(hidden)).astype(BF16)
    fields = [jnp.concatenate([gated[k * WIDE : (k + 1) * WIDE], x], axis=1) for k, x in enumerate(xin)]
    candidate = jnp.tanh(conv_rows(fields, w_q, ROWS))
    old = jnp.concatenate([h[own] for h in hidden])
    new = old + update * (candidate - old)
    return [new[k * OWN : (k + 1) * OWN] for k in range(len(xin))]


def filled(idx):
    count = 0
    for s in range(SLOTS):
        count += jnp.where(idx[s] >= 0, 1, 0)
    return count


def add_messages(acc, idx, slots, hidden, w_msg):
    messages = dot(jnp.concatenate(hidden).astype(BF16), w_msg)
    for k, s in enumerate(slots):

        @pl.when(idx[s] >= 0)
        def _():
            acc[idx[s] // SLOTS] += messages[k * OWN : (k + 1) * OWN, :CHANS]
            acc[idx[s] % SLOTS] += messages[k * OWN : (k + 1) * OWN, CHANS:]


def give_sums(acc, part, part_other):
    part[...] = acc[:4].astype(BF16)
    part_other[...] = acc[4:].astype(BF16)


def first_kernel(
    idx, p0, p1, p2, p3, w_corr, w_zr, w_q, w_msg,
    part, part_other, hid, hid_first, hid_last, motion_out,
    feat, rim, ctx, acc, flip, spread, edge,
):
    pieces = (p0, p1, p2, p3)
    acc[...] = jnp.zeros_like(acc)
    ends = [lax.broadcasted_iota(jnp.int32, (WIDTH, WIDTH), k) for k in range(2)]
    flip[...] = jnp.where(ends[0] + ends[1] == WIDTH - 1, 1.0, 0.0).astype(BF16)
    lane, tap = [lax.broadcasted_iota(jnp.int32, (CHANS, SPAN * SPAN), k) for k in range(2)]
    place = (lane & (WIDTH - 1)) - 4
    shift = jnp.where(lane < WIDTH, 2 * (place >> 3), jnp.minimum(2 * (place >> 3) + 1, SPAN - 1))
    wanted = (place >= 0) & (place < 32) & ((place & 7) < SPAN) & (tap == SPAN * shift + (place & 7))
    spread[...] = dot(jnp.where(wanted, 1.0, 0.0).astype(BF16), w_corr[...]).astype(BF16)
    column = WIDTH - 1 - lax.broadcasted_iota(jnp.int32, (WIDTH, CHANS), 0)
    lane = lax.broadcasted_iota(jnp.int32, (WIDTH, CHANS), 1)
    place = (lane & (WIDTH - 1)) - 4
    at = column + (place & 7) - 3
    inside = (place >= 0) & (place < 32) & ((place & 7) < SPAN) & (at >= 0) & (at < WIDTH)
    inside = inside & ((place < 24) | (lane >= WIDTH))
    edge[...] = jnp.where(inside, 1.0 / CHANS**0.5, 0.0)
    place = (lax.broadcasted_iota(jnp.int32, (WIDTH, CHANS), 1) & (WIDTH - 1)) - 4

    def body(i, carry):
        slots = [2 * i + j for j in range(2)]
        for j, s in enumerate(slots):
            code = jnp.maximum(idx[s], 0)
            source, target = code // SLOTS, code % SLOTS
            for k, piece in enumerate(pieces):

                @pl.when(source // 2 == k)
                def _():
                    feat[j] = piece[source % 2, 3:8]
                    ctx[j] = piece[source % 2, 11:16]

                @pl.when(target // 2 == k)
                def _():
                    rim[j] = piece[target % 2, 0:11]

        rows = [(j, y) for j in range(2) for y in range(5)]
        turned = dot(flip[...], jnp.concatenate([feat[j, y] for j, y in rows], axis=1)).astype(BF16)
        corr = []
        for k, (j, y) in enumerate(rows):
            near = turned[:, k * CHANS : (k + 1) * CHANS]
            far = rim[j, y : y + SPAN].reshape(SPAN * WIDTH, CHANS)
            total = None
            for g in range(4):
                start = 2 * WIDTH * g if g < 3 else 5 * WIDTH
                table = dot_t(near, far[start : start + 2 * WIDTH])
                moved = pltpu.roll(table, 8 * g + 72, 1, stride=1, stride_axis=0)
                total = moved if g == 0 else jnp.where(place < 8 * g, total, moved)
            corr.append((total * edge[...]).astype(BF16))
        turned = dot(flip[...], jnp.concatenate(corr, axis=1)).astype(BF16)
        corr = jnp.concatenate([turned[:, k * CHANS : (k + 1) * CHANS] for k in range(len(rows))])
        motion = jnp.maximum(dot(corr, spread[...]), 0.0).astype(BF16)
        motion = [motion[j * WIDE : (j + 1) * WIDE] for j in range(2)]
        state = [ctx[j].reshape(WIDE, CHANS).astype(F32) for j in range(2)]
        xin = [(m.astype(F32) + c).astype(BF16) for m, c in zip(motion, state)]
        hidden = gru([jnp.tanh(c) for c in state], xin, w_zr[...], side_by_side(w_q))
        for s, m, h in zip(slots, motion, hidden):
            motion_out[s] = m
            hid[s] = h
            hid_first[s] = h[:WIDTH].astype(BF16)
            hid_last[s] = h[2 * WIDTH :].astype(BF16)
        add_messages(acc, idx, slots, hidden, w_msg[...])
        return carry

    lax.fori_loop(0, (filled(idx) + 1) // 2, body, 0)
    give_sums(acc, part, part_other)


def second_kernel(
    idx, s0, s1, motion, hid, above, below, w_zr, w_q, w_msg, part, part_other, state_buf, acc
):
    acc[...] = jnp.zeros_like(acc)
    row = idx[SLOTS]

    def body(i, carry):
        slots = [2 * i + j for j in range(2)]
        for j, s in enumerate(slots):
            source = jnp.maximum(idx[s], 0) // SLOTS
            for k, piece in enumerate((s0, s1)):

                @pl.when(source // 4 == k)
                def _():
                    state_buf[j] = piece[source % 4]

        state = [state_buf[j].reshape(WIDE, CHANS).astype(F32) for j in range(2)]
        xin = [(motion[s].astype(F32) + c).astype(BF16) for s, c in zip(slots, state)]
        hidden = [
            jnp.concatenate(
                [kept(row > 0, above[s].astype(F32)), hid[s], kept(row < 3, below[s].astype(F32))]
            )
            for s in slots
        ]
        hidden = gru(hidden, xin, w_zr[...], side_by_side(w_q))
        add_messages(acc, idx, slots, hidden, w_msg[...])
        return carry

    lax.fori_loop(0, (filled(idx) + 1) // 2, body, 0)
    give_sums(acc, part, part_other)


def kept(keep, block):
    return jnp.where(keep, block, jnp.zeros_like(block))


def state_kernel(idx, own, near, upd, above, below, w_res, out):
    row = idx[SLOTS]
    for frame in range(4):
        piece = own if frame < 2 else near
        field = jnp.concatenate(
            [
                kept(row > 0, above[frame].reshape(2 * WIDTH, CHANS)),
                upd[frame].reshape(OWN, CHANS),
                kept(row < 3, below[frame].reshape(2 * WIDTH, CHANS)),
            ],
            axis=0,
        )
        base = piece[frame % 2, 11:16].reshape(WIDE, CHANS).astype(F32)
        new = (base + conv_rows([field], side_by_side(w_res), 5)).astype(BF16).reshape(5, WIDTH, CHANS)
        out[frame, 1:4] = new[1:4]
        out[frame, 0] = kept(row > 0, new[0])
        out[frame, 4] = kept(row < 3, new[4])


def last_kernel(idx, state, upd, above, below, w_res, out):
    row = idx[SLOTS]
    for frame in range(2):
        field = jnp.concatenate(
            [
                kept(row > 0, above[frame].reshape(WIDTH, CHANS)),
                upd[frame].reshape(OWN, CHANS),
                kept(row < 3, below[frame].reshape(WIDTH, CHANS)),
            ],
            axis=0,
        )
        base = state[frame, 1:4].reshape(OWN, CHANS).astype(F32)
        out[frame] = (base + conv_rows([field], side_by_side(w_res), ROWS)).astype(BF16).reshape(ROWS, WIDTH, CHANS)


VM = pl.BlockSpec(memory_space=pltpu.VMEM)
SM = pl.BlockSpec(memory_space=pltpu.SMEM)


def call(kernel, outs, scratch, flops, *args):
    specs = [SM if a.dtype == jnp.int32 else VM for a in args]
    size = sum(a.size * a.dtype.itemsize for a in args)
    return pl.pallas_call(
        kernel,
        out_shape=outs,
        in_specs=specs,
        out_specs=[VM] * len(outs),
        scratch_shapes=scratch,
        compiler_params=pltpu.CompilerParams(vmem_limit_bytes=24 * 2**20),
        cost_estimate=pl.CostEstimate(flops=flops, bytes_accessed=size, transcendentals=0),
    )(*args)


def slot_table(pairs, index, row):
    chip, core = index >> 1, index & 1
    sources, targets, owners = (pairs[:, k] for k in range(3))

    def place(frame):
        dev = (frame >> 1) - 2 * chip
        other = jnp.where((dev >= 1) != (core == 1), 4, 0)
        return other + jnp.where((dev < 0) | (dev > 1), 2, 0) + (frame & 1)

    mine = (owners >> 1) == chip
    order = jnp.arange(pairs.shape[0], dtype=jnp.int32)
    ranks = jnp.sum(jnp.where((order[None, :] < order[:, None]) & mine[None, :], 1, 0), axis=1)
    codes = place(sources) * SLOTS + place(targets)
    levels = 2 * jnp.arange(SLOTS, dtype=jnp.int32) + core
    picked = jnp.where((ranks[None, :] == levels[:, None]) & mine[None, :], codes[None, :] + 1, 0)
    picked = jnp.sum(picked, axis=1) - 1
    return jnp.concatenate([picked, row[None]])


def local(fmap, context, pairs, w_corr, w_zr, w_q, w_msg, w_res):
    index, row = lax.axis_index("frames"), lax.axis_index("rows")
    n_frames, n_rows = lax.axis_size("frames"), lax.axis_size("rows")
    up = [(i, (i + 1) % n_rows) for i in range(n_rows)]
    down = [(j, i) for i, j in up]
    across = [(i, (i + 2) % 4) for i in range(n_rows)]
    core_swap = [(i, i ^ 1) for i in range(n_frames)]
    partner = {i: i + 1 if i % 2 else i - 1 for i in range(1, n_frames - 1)}
    chip_swap = [
        (i * n_rows + j, partner[i] * n_rows + j if i in partner else i * n_rows + (j ^ 1))
        for i in range(n_frames)
        for j in range(n_rows)
    ]

    def swap_core(x):
        return lax.ppermute(x, "frames", core_swap)

    def swap_chip(x):
        return lax.ppermute(x, ("frames", "rows"), chip_swap)

    with jax.named_scope("feature_rows"):
        from_above = lax.ppermute(jnp.concatenate([fmap, context[:, 2:]], axis=1), "rows", up)
        from_below = lax.ppermute(jnp.concatenate([fmap, context[:, :1]], axis=1), "rows", down)
        far = lax.ppermute(jnp.where(row < 2, fmap[:, 2:], fmap[:, :1]), "rows", across)
        none = jnp.zeros_like(far)
        from_above = jnp.where(row > 0, from_above, jnp.zeros_like(from_above))
        from_below = jnp.where(row < n_rows - 1, from_below, jnp.zeros_like(from_below))
        own = jnp.concatenate(
            [
                jnp.where(row < 2, none, far),
                from_above[:, :3],
                fmap,
                from_below[:, :3],
                jnp.where(row < 2, far, none),
                from_above[:, 3:],
                context,
                from_below[:, 3:],
            ],
            axis=1,
        )
    own, pairs = lax.optimization_barrier((own, pairs))
    idx = slot_table(pairs, index, row)
    with jax.named_scope("feature_window"):
        near = swap_chip(own)
        own_other = swap_core(own)
        near_other = swap_core(near)

    with jax.named_scope("first_iteration"):
        sums = [jax.ShapeDtypeStruct((4, OWN, CHANS), BF16)] * 2
        edge_rows = [jax.ShapeDtypeStruct((SLOTS, WIDTH, CHANS), BF16)] * 2
        part, part_other, hid, hid_first, hid_last, motion = call(
            first_kernel,
            [
                *sums,
                jax.ShapeDtypeStruct((SLOTS, OWN, CHANS), F32),
                *edge_rows,
                jax.ShapeDtypeStruct((SLOTS, WIDE, CHANS), BF16),
            ],
            [
                pltpu.VMEM((2, 5, WIDTH, CHANS), BF16),
                pltpu.VMEM((2, 11, WIDTH, CHANS), BF16),
                pltpu.VMEM((2, 5, WIDTH, CHANS), BF16),
                pltpu.VMEM((SLOTS, OWN, CHANS), F32),
                pltpu.VMEM((WIDTH, WIDTH), BF16),
                pltpu.VMEM((CHANS, CHANS), BF16),
                pltpu.VMEM((WIDTH, CHANS), F32),
            ],
            2_000_000_000,
            idx, own, near, own_other, near_other, w_corr, w_zr, w_q, w_msg,
        )

    with jax.named_scope("first_sums"):
        mine = part.astype(F32) + swap_core(part_other).astype(F32)
        sent = mine.astype(BF16)
        arrived = swap_chip(sent).astype(F32)
        total = mine + jnp.concatenate([arrived[2:], arrived[:2]])
        upd = jnp.maximum(total, 0.0).astype(BF16).reshape(4, ROWS, WIDTH, CHANS)
    with jax.named_scope("update_rows"):
        above = lax.ppermute(jnp.concatenate([upd[:, 1:].reshape(8, WIDTH, CHANS), hid_last]), "rows", up)
        below = lax.ppermute(jnp.concatenate([upd[:, :2].reshape(8, WIDTH, CHANS), hid_first]), "rows", down)
        upd_above, hid_above = above[:8].reshape(4, 2, WIDTH, CHANS), above[8:]
        upd_below, hid_below = below[:8].reshape(4, 2, WIDTH, CHANS), below[8:]
    with jax.named_scope("first_state"):
        [state] = call(
            state_kernel,
            [jax.ShapeDtypeStruct((4, 5, WIDTH, CHANS), BF16)],
            [],
            400_000_000,
            idx, own, near, upd, upd_above, upd_below, w_res,
        )
        state_other = swap_core(state)
    with jax.named_scope("second_iteration"):
        part, part_other = call(
            second_kernel,
            sums,
            [pltpu.VMEM((2, 5, WIDTH, CHANS), BF16), pltpu.VMEM((SLOTS, OWN, CHANS), F32)],
            1_500_000_000,
            idx, state, state_other, motion, hid, hid_above, hid_below, w_zr, w_q, w_msg,
        )
    with jax.named_scope("second_sums"):
        mine = part.astype(F32) + swap_core(part_other).astype(F32)
        arrived = swap_chip(mine[2:].astype(BF16)).astype(F32)
        upd = jnp.maximum(mine[:2] + arrived, 0.0).astype(BF16).reshape(2, ROWS, WIDTH, CHANS)
        above = lax.ppermute(upd[:, 2:], "rows", up)
        below = lax.ppermute(upd[:, :1], "rows", down)
    with jax.named_scope("last_state"):
        [out] = call(
            last_kernel,
            [jax.ShapeDtypeStruct((2, ROWS, WIDTH, CHANS), BF16)],
            [],
            120_000_000,
            idx, state, upd, above, below, w_res,
        )
    return out


def solution(mesh):
    placed = (
        P("frames", "rows", None, None),
        P("frames", "rows", None, None),
        P(),
        P(),
        P(),
        P(),
        P(),
        P(),
    )
    return jax.shard_map(
        local,
        mesh=mesh,
        in_specs=placed,
        out_specs=P("frames", "rows", None, None),
        check_vma=False,
    )
```

time: 75.4 us -> 70.5 us (0.935)
  the two profiles are of different devices: /device:TPU:0 before, /device:TPU:6 now
where the time goes in v3:
time: 70.5 us; the launch traced here: 70.4 us
  waiting for transfers between devices  32.9 us (47%)
  starting transfers between devices  23.6 us (33%)
  Pallas kernels  10.8 us (15%)
  other arithmetic  1.61 us (2%)
  local copies, waits for them, and re-layouts  1.17 us (2%)
    ppermute x3, waiting for transfers between devices, swap_chip(): return lax.ppermute(x, ('frames', 'rows'), chip_swap)  12.5 us
    ppermute x3, starting transfers between devices, swap_chip(): return lax.ppermute(x, ('frames', 'rows'), chip_swap)  11.9 us
    pallas_call x4, Pallas kernels, call(): pl.pallas_call(kernel, out_shape=outs, in_specs=specs, out_specs=[VM] * l...  10.8 us
    ppermute x5, waiting for transfers between devices, swap_core(): return lax.ppermute(x, 'frames', core_swap)  5.75 us
    ppermute x1, waiting for transfers between devices, local(): lax.ppermute(jnp.concatenate([fmap, context[:, 2:]], axis=1), 'rows', up)  5.12 us
    ppermute x1, waiting for transfers between devices, local(): lax.ppermute(jnp.concatenate([upd[:, 1:].reshape(8, WIDTH, CHANS), hid_la...  4.4 us
    ppermute x1, waiting for transfers between devices, local(): above = lax.ppermute(upd[:, 2:], 'rows', up)  3.53 us
    ppermute x1, starting transfers between devices, local(): lax.ppermute(jnp.concatenate([upd[:, :2].reshape(8, WIDTH, CHANS), hid_fi...  3.26 us
  transfers between devices with their start and end apart: 15, of which 12 were waited for; matrix products, arithmetic and copies ran while one was open for 1% of the time, Pallas kernels for 0%

profile of v3, /device:TPU:6, one launch (start us, length us, event | category | flops | bytes accessed | tf_op | source)
XLA Modules:
  0.0 70.4 jit_solution(134903580690759038)
XLA Ops:
  0.8 3.2 %collective-permute-start = (bf16[2,1,64,128]{3,2,1,0:T(8,128)(2,1)S(1)}, bf16[2,1,64,128]{3,2,1,0:T(8,128)(2,1)S(1)}, u32[]{:S(2)}, u32[]{:S(2)}) collective-permute-start(bf16[2,1,64,128]{3,2,1,0:T(8,128)(2,1)S(1)} %slice_select_fusion), channel_id=1, source_target_pairs={{0,2},{1,3},{2,0},{3,1},{4,6},{5,7},{6,4},{7,5},{8,10},{9,11},{10,... | collective-permute-start | bytes 98312 | tf_op jit(solution)/shard_map/feature_rows/ppermute | solution.py:285
  4.1 1.1 %collective-permute-start.2 = (bf16[2,4,64,128]{3,2,1,0:T(8,128)(2,1)S(1)}, bf16[2,4,64,128]{3,2,1,0:T(8,128)(2,1)S(1)}, u32[]{:S(2)}, u32[]{:S(2)}) collective-permute-start(bf16[2,4,64,128]{3,2,1,0:T(8,128)(2,1)S(1)} %get-tuple-element.35), channel_id=1, source_target_pairs={{1,0},{2,1},{3,2},{0,3},{5,4},{6,5},{7,6},{4,7},{9,8},{10,9},{11,1... | collective-permute-start | bytes 393224 | tf_op jit(solution)/shard_map/feature_rows/ppermute | solution.py:284
  5.2 1.0 %collective-permute-start.1 = (bf16[2,4,64,128]{3,2,1,0:T(8,128)(2,1)S(1)}, bf16[2,4,64,128]{3,2,1,0:T(8,128)(2,1)S(1)}, u32[]{:S(2)}, u32[]{:S(2)}) collective-permute-start(bf16[2,4,64,128]{3,2,1,0:T(8,128)(2,1)S(1)} %get-tuple-element.36), channel_id=1, source_target_pairs={{0,1},{1,2},{2,3},{3,0},{4,5},{5,6},{6,7},{7,4},{8,9},{9,10},{10,1... | collective-permute-start | bytes 393224 | tf_op jit(solution)/shard_map/feature_rows/ppermute | solution.py:283
  6.3 5.1 %collective-permute-done.1 = bf16[2,4,64,128]{3,2,1,0:T(8,128)(2,1)S(1)} collective-permute-done((bf16[2,4,64,128]{3,2,1,0:T(8,128)(2,1)S(1)}, bf16[2,4,64,128]{3,2,1,0:T(8,128)(2,1)S(1)}, u32[]{:S(2)}, u32[]{:S(2)}) %collective-permute-start.1) | collective-permute-done | bytes 131104 | tf_op jit(solution)/shard_map/feature_rows/ppermute | solution.py:283
  11.6 3.9 %collective-permute-start.3 = (bf16[2,16,64,128]{3,2,1,0:T(8,128)(2,1)S(1)}, bf16[2,16,64,128]{3,2,1,0:T(8,128)(2,1)S(1)}, u32[]{:S(2)}, u32[]{:S(2)}) collective-permute-start(bf16[2,16,64,128]{3,2,1,0:T(8,128)(2,1)S(1)} %slice_dynamic-update-slice_fusion.2.p0.own), channel_id=1, source_target_pairs={{0,1},{1,0},{2,3},{3,2},{4,8},{5,9},{6,10},{7,11},{8,4},{9,5},{10,... | collective-permute-start | bytes 1572872 | tf_op jit(solution)/shard_map/feature_window/ppermute | solution.py:280
  15.7 6.8 %collective-permute-done.3.p1.near = bf16[2,16,64,128]{3,2,1,0:T(8,128)(2,1)S(1)} collective-permute-done((bf16[2,16,64,128]{3,2,1,0:T(8,128)(2,1)S(1)}, bf16[2,16,64,128]{3,2,1,0:T(8,128)(2,1)S(1)}, u32[]{:S(2)}, u32[]{:S(2)}) %collective-permute-start.3) | collective-permute-done | bytes 524320 | tf_op jit(solution)/shard_map/feature_window/ppermute | solution.py:280
  22.8 1.5 %collective-permute-done.5.p3 = bf16[2,16,64,128]{3,2,1,0:T(8,128)(2,1)S(1)} collective-permute-done((bf16[2,16,64,128]{3,2,1,0:T(8,128)(2,1)S(1)}, bf16[2,16,64,128]{3,2,1,0:T(8,128)(2,1)S(1)}, u32[]{:S(2)}, u32[]{:S(2)}) %collective-permute-start.5) | collective-permute-done | bytes 524320 | tf_op jit(solution)/shard_map/feature_window/ppermute | solution.py:277
  24.4 5.5 %first_iteration.1 = (bf16[4,192,128]{2,1,0:T(8,128)(2,1)S(1)}, bf16[4,192,128]{2,1,0:T(8,128)(2,1)S(1)}, f32[8,192,128]{2,1,0:T(8,128)S(1)}, bf16[8,64,128]{2,1...) custom-call(s32[9]{0:T(128)S(1)} %pad_add_fusion.idx, ...), custom_call_target="tpu_custom_call" | custom-call | flops 2000000000 | bytes 2896164 | tf_op jit(solution)/shard_map/first_iteration/pallas_call | solution.py:232
  30.1 1.3 %collective-permute-done.6 = bf16[4,192,128]{2,1,0:T(8,128)(2,1)S(1)} collective-permute-done((bf16[4,192,128]{2,1,0:T(8,128)(2,1)S(1)}, bf16[4,192,128]{2,1,0:T(8,128)(2,1)S(1)}, u32[]{:S(2)}, u32[]{:S(2)}) %collective-permute-start.6) | collective-permute-done | bytes 196640 | tf_op jit(solution)/shard_map/first_sums/ppermute | solution.py:277
  31.5 3.9 %collective-permute-start.7 = (bf16[4,192,128]{2,1,0:T(8,128)(2,1)S(1)}, bf16[4,192,128]{2,1,0:T(8,128)(2,1)S(1)}, u32[]{:S(2)}, u32[]{:S(2)}) collective-permute-start(bf16[4,192,128]{2,1,0:T(8,128)(2,1)S(1)} %fusion.2), channel_id=1, source_target_pairs={{0,1},{1,0},{2,3},{3,2},{4,8},{5,9},{6,10},{7,11},{8,4},{9,5},{10,... | collective-permute-start | bytes 589832 | tf_op jit(solution)/shard_map/first_sums/ppermute | solution.py:280
  35.4 3.4 %collective-permute-done.7 = bf16[4,192,128]{2,1,0:T(8,128)(2,1)S(1)} collective-permute-done((bf16[4,192,128]{2,1,0:T(8,128)(2,1)S(1)}, bf16[4,192,128]{2,1,0:T(8,128)(2,1)S(1)}, u32[]{:S(2)}, u32[]{:S(2)}) %collective-permute-start.7) | collective-permute-done | bytes 196640 | tf_op jit(solution)/shard_map/first_sums/ppermute | solution.py:280
  39.2 3.3 %collective-permute-start.9 = (bf16[16,64,128]{2,1,0:T(8,128)(2,1)S(1)}, bf16[16,64,128]{2,1,0:T(8,128)(2,1)S(1)}, u32[]{:S(2)}, u32[]{:S(2)}) collective-permute-start(bf16[16,64,128]{2,1,0:T(8,128)(2,1)S(1)} %pad_maximum_fusion.1), channel_id=1, source_target_pairs={{1,0},{2,1},{3,2},{0,3},{5,4},{6,5},{7,6},{4,7},{9,8},{10,9},{11,1... | collective-permute-start | bytes 786440 | tf_op jit(solution)/shard_map/update_rows/ppermute | solution.py:341
  42.4 4.4 %collective-permute-done.8 = bf16[16,64,128]{2,1,0:T(8,128)(2,1)S(1)} collective-permute-done((bf16[16,64,128]{2,1,0:T(8,128)(2,1)S(1)}, bf16[16,64,128]{2,1,0:T(8,128)(2,1)S(1)}, u32[]{:S(2)}, u32[]{:S(2)}) %collective-permute-start.8) | collective-permute-done | bytes 262176 | tf_op jit(solution)/shard_map/update_rows/ppermute | solution.py:340
  46.9 0.9 %copy-done = bf16[9,128,128]{2,1,0:T(8,128)(2,1)S(1)} copy-done((bf16[9,128,128]{2,1,0:T(8,128)(2,1)S(1)}, bf16[9,128,128]{2,1,0:T(8,128)(2,1)}, u32[]{:S(2)}) %copy-start) | copy-done | bytes 294936
  47.8 1.3 %first_state.1.s0.state = bf16[4,5,64,128]{3,2,1,0:T(8,128)(2,1)S(1)} custom-call(s32[9]{0:T(128)S(1)} %pad_add_fusion.idx, bf16[2,16,64,128]{3,2,1,0:T(8,128)(2,1)S(1)} %slice_dynamic-update-slice_fusion.2.p0.own, bf16[2,16,64,128]{3,2,1,0:T(8,128)(2,1)S(1)} %collective-permute-done.3.p1.near, bf16[4,3,64,128]{3,2,1,0:T(8,128)(2,1)S(1)} %bitcast.9, ...), custom_call_target="tpu_custom_call" | custom-call | flops 400000000 | bytes 1802276 | tf_op jit(solution)/shard_map/first_state/pallas_call | solution.py:232
  49.2 1.6 %collective-permute-done.10.s1 = bf16[4,5,64,128]{3,2,1,0:T(8,128)(2,1)S(1)} collective-permute-done((bf16[4,5,64,128]{3,2,1,0:T(8,128)(2,1)S(1)}, bf16[4,5,64,128]{3,2,1,0:T(8,128)(2,1)S(1)}, u32[]{:S(2)}, u32[]{:S(2)}) %collective-permute-start.10) | collective-permute-done | bytes 327712 | tf_op jit(solution)/shard_map/first_state/ppermute | solution.py:277
  50.8 2.4 %second_iteration.1 = (bf16[4,192,128]{2,1,0:T(8,128)(2,1)S(1)}, bf16[4,192,128]{2,1,0:T(8,128)(2,1)S(1)}) custom-call(s32[9]{0:T(128)S(1)} %pad_add_fusion.idx, bf16[4,5,64,128]{3,2,1,0:T(8,128)(2,1)S(1)} %first_state.1.s0.state, bf16[4,5,64,128]{3,2,1,0:T(8,128)(2,1)S(1)} %collective-permute-done.10.s1, bf16[8,320,128]{2,1,0:T(8,128)(2,1)S(1)} %get-tuple-element.21.motion, ...), custom_call_target="tpu_custom_call" | custom-call | flops 1500000000 | bytes 3145764 | tf_op jit(solution)/shard_map/second_iteration/pallas_call | solution.py:232
  53.5 1.3 %collective-permute-done.11 = bf16[4,192,128]{2,1,0:T(8,128)(2,1)S(1)} collective-permute-done((bf16[4,192,128]{2,1,0:T(8,128)(2,1)S(1)}, bf16[4,192,128]{2,1,0:T(8,128)(2,1)S(1)}, u32[]{:S(2)}, u32[]{:S(2)}) %collective-permute-start.11) | collective-permute-done | bytes 196640 | tf_op jit(solution)/shard_map/second_sums/ppermute | solution.py:277
  54.9 4.0 %collective-permute-start.12 = (bf16[2,192,128]{2,1,0:T(8,128)(2,1)S(1)}, bf16[2,192,128]{2,1,0:T(8,128)(2,1)S(1)}, u32[]{:S(2)}, u32[]{:S(2)}) collective-permute-start(bf16[2,192,128]{2,1,0:T(8,128)(2,1)S(1)} %slice.124), channel_id=1, source_target_pairs={{0,1},{1,0},{2,3},{3,2},{4,8},{5,9},{6,10},{7,11},{8,4},{9,5},{10,... | collective-permute-start | bytes 294920 | tf_op jit(solution)/shard_map/second_sums/ppermute | solution.py:280
  58.9 2.3 %collective-permute-done.12 = bf16[2,192,128]{2,1,0:T(8,128)(2,1)S(1)} collective-permute-done((bf16[2,192,128]{2,1,0:T(8,128)(2,1)S(1)}, bf16[2,192,128]{2,1,0:T(8,128)(2,1)S(1)}, u32[]{:S(2)}, u32[]{:S(2)}) %collective-permute-start.12) | collective-permute-done | bytes 98336 | tf_op jit(solution)/shard_map/second_sums/ppermute | solution.py:280
  61.3 2.5 %collective-permute-start.14 = (bf16[2,1,64,128]{3,2,1,0:T(8,128)(2,1)S(1)}, bf16[2,1,64,128]{3,2,1,0:T(8,128)(2,1)S(1)}, u32[]{:S(2)}, u32[]{:S(2)}) collective-permute-start(bf16[2,1,64,128]{3,2,1,0:T(8,128)(2,1)S(1)} %get-tuple-element.33), channel_id=1, source_target_pairs={{1,0},{2,1},{3,2},{0,3},{5,4},{6,5},{7,6},{4,7},{9,8},{10,9},{11,1... | collective-permute-start | bytes 98312 | tf_op jit(solution)/shard_map/second_sums/ppermute | solution.py:366
  63.8 1.6 %collective-permute-done.14.below = bf16[2,1,64,128]{3,2,1,0:T(8,128)(2,1)S(1)} collective-permute-done((bf16[2,1,64,128]{3,2,1,0:T(8,128)(2,1)S(1)}, bf16[2,1,64,128]{3,2,1,0:T(8,128)(2,1)S(1)}, u32[]{:S(2)}, u32[]{:S(2)}) %collective-permute-start.14) | collective-permute-done | bytes 32800 | tf_op jit(solution)/shard_map/second_sums/ppermute | solution.py:366
  65.3 3.5 %collective-permute-done.13.above = bf16[2,1,64,128]{3,2,1,0:T(8,128)(2,1)S(1)} collective-permute-done((bf16[2,1,64,128]{3,2,1,0:T(8,128)(2,1)S(1)}, bf16[2,1,64,128]{3,2,1,0:T(8,128)(2,1)S(1)}, u32[]{:S(2)}, u32[]{:S(2)}) %collective-permute-start.13) | collective-permute-done | bytes 32800 | tf_op jit(solution)/shard_map/second_sums/ppermute | solution.py:365
  68.9 1.5 %last_state.1 = bf16[2,3,64,128]{3,2,1,0:T(8,128)(2,1)} custom-call(s32[9]{0:T(128)S(1)} %pad_add_fusion.idx, bf16[4,5,64,128]{3,2,1,0:T(8,128)(2,1)S(1)} %first_state.1.s0.state, bf16[2,3,64,128]{3,2,1,0:T(8,128)(2,1)S(1)} %bitcast.11, bf16[2,1,64,128]{3,2,1,0:T(8,128)(2,1)S(1)} %collective-permute-done.13.above, ...), custom_call_target="tpu_custom_call" | custom-call | flops 120000000 | bytes 786468 | tf_op jit(solution)/shard_map/last_state/pallas_call | solution.py:232
  (58 shorter events, 2.6 us)
Async XLA Ops:
  0.0 4.0 %copy-start.6 = (bf16[2,3,64,128]{3,2,1,0:T(8,128)(2,1)S(1)}, bf16[2,3,64,128]{3,2,1,0:T(8,128)(2,1)}, u32[]{:S(2)}) copy-start(bf16[2,3,64,128]{3,2,1,0:T(8,128)(2,1)} %param.9) | copy-start | bytes 294916
  0.0 4.0 %copy-start.5 = (bf16[2,3,64,128]{3,2,1,0:T(8,128)(2,1)S(1)}, bf16[2,3,64,128]{3,2,1,0:T(8,128)(2,1)}, u32[]{:S(2)}) copy-start(bf16[2,3,64,128]{3,2,1,0:T(8,128)(2,1)} %param.8) | copy-start | bytes 294916
  0.8 5.4 %collective-permute-start = (bf16[2,1,64,128]{3,2,1,0:T(8,128)(2,1)S(1)}, bf16[2,1,64,128]{3,2,1,0:T(8,128)(2,1)S(1)}, u32[]{:S(2)}, u32[]{:S(2)}) collective-permute-start(bf16[2,1,64,128]{3,2,1,0:T(8,128)(2,1)S(1)} %slice_select_fusion), channel_id=1, source_target_pairs={{0,2},{1,3},{2,0},{3,1},{4,6},{5,7},{6,4},{7,5},{8,10},{9,11},{10,... | collective-permute-start | bytes 98312 | tf_op jit(solution)/shard_map/feature_rows/ppermute | solution.py:285
  4.1 7.4 %collective-permute-start.2 = (bf16[2,4,64,128]{3,2,1,0:T(8,128)(2,1)S(1)}, bf16[2,4,64,128]{3,2,1,0:T(8,128)(2,1)S(1)}, u32[]{:S(2)}, u32[]{:S(2)}) collective-permute-start(bf16[2,4,64,128]{3,2,1,0:T(8,128)(2,1)S(1)} %get-tuple-element.35), channel_id=1, source_target_pairs={{1,0},{2,1},{3,2},{0,3},{5,4},{6,5},{7,6},{4,7},{9,8},{10,9},{11,1... | collective-permute-start | bytes 393224 | tf_op jit(solution)/shard_map/feature_rows/ppermute | solution.py:284
  5.2 6.2 %collective-permute-start.1 = (bf16[2,4,64,128]{3,2,1,0:T(8,128)(2,1)S(1)}, bf16[2,4,64,128]{3,2,1,0:T(8,128)(2,1)S(1)}, u32[]{:S(2)}, u32[]{:S(2)}) collective-permute-start(bf16[2,4,64,128]{3,2,1,0:T(8,128)(2,1)S(1)} %get-tuple-element.36), channel_id=1, source_target_pairs={{0,1},{1,2},{2,3},{3,0},{4,5},{5,6},{6,7},{7,4},{8,9},{9,10},{10,1... | collective-permute-start | bytes 393224 | tf_op jit(solution)/shard_map/feature_rows/ppermute | solution.py:283
  11.4 12.9 %copy-start.1 = (bf16[9,256,128]{2,1,0:T(8,128)(2,1)S(1)}, bf16[9,256,128]{2,1,0:T(8,128)(2,1)}, u32[]{:S(2)}) copy-start(bf16[9,256,128]{2,1,0:T(8,128)(2,1)} %w_q.3) | copy-start | bytes 1769476
  11.6 12.8 %copy-start.2 = (bf16[256,256]{1,0:T(8,128)(2,1)S(1)}, bf16[256,256]{1,0:T(8,128)(2,1)}, u32[]{:S(2)}) copy-start(bf16[256,256]{1,0:T(8,128)(2,1)} %w_zr.3) | copy-start | bytes 393220
  11.6 4.0 %copy-start.7 = (s32[256,3]{0,1:T(4,128)S(1)}, s32[256,3]{0,1:T(4,128)}, u32[]{:S(2)}) copy-start(s32[256,3]{0,1:T(4,128)} %param.10) | copy-start | bytes 9220
  11.6 12.8 %copy-start.3 = (bf16[128,256]{1,0:T(8,128)(2,1)S(1)}, bf16[128,256]{1,0:T(8,128)(2,1)}, u32[]{:S(2)}) copy-start(bf16[128,256]{1,0:T(8,128)(2,1)} %w_msg.3) | copy-start | bytes 196612
  11.6 10.8 %collective-permute-start.3 = (bf16[2,16,64,128]{3,2,1,0:T(8,128)(2,1)S(1)}, bf16[2,16,64,128]{3,2,1,0:T(8,128)(2,1)S(1)}, u32[]{:S(2)}, u32[]{:S(2)}) collective-permute-start(bf16[2,16,64,128]{3,2,1,0:T(8,128)(2,1)S(1)} %slice_dynamic-update-slice_fusion.2.p0.own), channel_id=1, source_target_pairs={{0,1},{1,0},{2,3},{3,2},{4,8},{5,9},{6,10},{7,11},{8,4},{9,5},{10,... | collective-permute-start | bytes 1572872 | tf_op jit(solution)/shard_map/feature_window/ppermute | solution.py:280
  15.6 8.8 %copy-start.4 = (bf16[49,128]{1,0:T(8,128)(2,1)S(1)}, bf16[49,128]{1,0:T(8,128)(2,1)}, u32[]{:S(2)}) copy-start(bf16[49,128]{1,0:T(8,128)(2,1)} %w_corr.1) | copy-start | bytes 37636
  15.6 7.3 %collective-permute-start.4 = (bf16[2,16,64,128]{3,2,1,0:T(8,128)(2,1)S(1)}, bf16[2,16,64,128]{3,2,1,0:T(8,128)(2,1)S(1)}, u32[]{:S(2)}, u32[]{:S(2)}) collective-permute-start(bf16[2,16,64,128]{3,2,1,0:T(8,128)(2,1)S(1)} %slice_dynamic-update-slice_fusion.2.p0.own), channel_id=1, source_target_pairs={{0,4},{4,0},{8,12},{12,8},{16,20},{20,16},{24,28},{28,24},{32,36},... | collective-permute-start | bytes 1572872 | tf_op jit(solution)/shard_map/feature_window/ppermute | solution.py:277
  22.4 1.9 %collective-permute-start.5 = (bf16[2,16,64,128]{3,2,1,0:T(8,128)(2,1)S(1)}, bf16[2,16,64,128]{3,2,1,0:T(8,128)(2,1)S(1)}, u32[]{:S(2)}, u32[]{:S(2)}) collective-permute-start(bf16[2,16,64,128]{3,2,1,0:T(8,128)(2,1)S(1)} %collective-permute-done.3.p1.near), channel_id=1, source_target_pairs={{0,4},{4,0},{8,12},{12,8},{16,20},{20,16},{24,28},{28,24},{32,36},... | collective-permute-start | bytes 1572872 | tf_op jit(solution)/shard_map/feature_window/ppermute | solution.py:277
  29.9 1.5 %collective-permute-start.6 = (bf16[4,192,128]{2,1,0:T(8,128)(2,1)S(1)}, bf16[4,192,128]{2,1,0:T(8,128)(2,1)S(1)}, u32[]{:S(2)}, u32[]{:S(2)}) collective-permute-start(bf16[4,192,128]{2,1,0:T(8,128)(2,1)S(1)} %get-tuple-element.18), channel_id=1, source_target_pairs={{0,4},{4,0},{8,12},{12,8},{16,20},{20,16},{24,28},{28,24},{32,36},... | collective-permute-start | bytes 589832 | tf_op jit(solution)/shard_map/first_sums/ppermute | solution.py:277
  31.5 7.3 %collective-permute-start.7 = (bf16[4,192,128]{2,1,0:T(8,128)(2,1)S(1)}, bf16[4,192,128]{2,1,0:T(8,128)(2,1)S(1)}, u32[]{:S(2)}, u32[]{:S(2)}) collective-permute-start(bf16[4,192,128]{2,1,0:T(8,128)(2,1)S(1)} %fusion.2), channel_id=1, source_target_pairs={{0,1},{1,0},{2,3},{3,2},{4,8},{5,9},{6,10},{7,11},{8,4},{9,5},{10,... | collective-permute-start | bytes 589832 | tf_op jit(solution)/shard_map/first_sums/ppermute | solution.py:280
  39.0 7.8 %collective-permute-start.8 = (bf16[16,64,128]{2,1,0:T(8,128)(2,1)S(1)}, bf16[16,64,128]{2,1,0:T(8,128)(2,1)S(1)}, u32[]{:S(2)}, u32[]{:S(2)}) collective-permute-start(bf16[16,64,128]{2,1,0:T(8,128)(2,1)S(1)} %pad_maximum_fusion), channel_id=1, source_target_pairs={{0,1},{1,2},{2,3},{3,0},{4,5},{5,6},{6,7},{7,4},{8,9},{9,10},{10,1... | collective-permute-start | bytes 786440 | tf_op jit(solution)/shard_map/update_rows/ppermute | solution.py:340
  39.2 7.7 %collective-permute-start.9 = (bf16[16,64,128]{2,1,0:T(8,128)(2,1)S(1)}, bf16[16,64,128]{2,1,0:T(8,128)(2,1)S(1)}, u32[]{:S(2)}, u32[]{:S(2)}) collective-permute-start(bf16[16,64,128]{2,1,0:T(8,128)(2,1)S(1)} %pad_maximum_fusion.1), channel_id=1, source_target_pairs={{1,0},{2,1},{3,2},{0,3},{5,4},{6,5},{7,6},{4,7},{9,8},{10,9},{11,1... | collective-permute-start | bytes 786440 | tf_op jit(solution)/shard_map/update_rows/ppermute | solution.py:341
  46.8 1.0 %copy-start = (bf16[9,128,128]{2,1,0:T(8,128)(2,1)S(1)}, bf16[9,128,128]{2,1,0:T(8,128)(2,1)}, u32[]{:S(2)}) copy-start(bf16[9,128,128]{2,1,0:T(8,128)(2,1)} %w_res.3) | copy-start | bytes 884740
  49.1 1.7 %collective-permute-start.10 = (bf16[4,5,64,128]{3,2,1,0:T(8,128)(2,1)S(1)}, bf16[4,5,64,128]{3,2,1,0:T(8,128)(2,1)S(1)}, u32[]{:S(2)}, u32[]{:S(2)}) collective-permute-start(bf16[4,5,64,128]{3,2,1,0:T(8,128)(2,1)S(1)} %first_state.1.s0.state), channel_id=1, source_target_pairs={{0,4},{4,0},{8,12},{12,8},{16,20},{20,16},{24,28},{28,24},{32,36},... | collective-permute-start | bytes 983048 | tf_op jit(solution)/shard_map/first_state/ppermute | solution.py:277
  53.3 1.5 %collective-permute-start.11 = (bf16[4,192,128]{2,1,0:T(8,128)(2,1)S(1)}, bf16[4,192,128]{2,1,0:T(8,128)(2,1)S(1)}, u32[]{:S(2)}, u32[]{:S(2)}) collective-permute-start(bf16[4,192,128]{2,1,0:T(8,128)(2,1)S(1)} %get-tuple-element.24), channel_id=1, source_target_pairs={{0,4},{4,0},{8,12},{12,8},{16,20},{20,16},{24,28},{28,24},{32,36},... | collective-permute-start | bytes 589832 | tf_op jit(solution)/shard_map/second_sums/ppermute | solution.py:277
  54.9 6.4 %collective-permute-start.12 = (bf16[2,192,128]{2,1,0:T(8,128)(2,1)S(1)}, bf16[2,192,128]{2,1,0:T(8,128)(2,1)S(1)}, u32[]{:S(2)}, u32[]{:S(2)}) collective-permute-start(bf16[2,192,128]{2,1,0:T(8,128)(2,1)S(1)} %slice.124), channel_id=1, source_target_pairs={{0,1},{1,0},{2,3},{3,2},{4,8},{5,9},{6,10},{7,11},{8,4},{9,5},{10,... | collective-permute-start | bytes 294920 | tf_op jit(solution)/shard_map/second_sums/ppermute | solution.py:280
  61.3 4.1 %collective-permute-start.14 = (bf16[2,1,64,128]{3,2,1,0:T(8,128)(2,1)S(1)}, bf16[2,1,64,128]{3,2,1,0:T(8,128)(2,1)S(1)}, u32[]{:S(2)}, u32[]{:S(2)}) collective-permute-start(bf16[2,1,64,128]{3,2,1,0:T(8,128)(2,1)S(1)} %get-tuple-element.33), channel_id=1, source_target_pairs={{1,0},{2,1},{3,2},{0,3},{5,4},{6,5},{7,6},{4,7},{9,8},{10,9},{11,1... | collective-permute-start | bytes 98312 | tf_op jit(solution)/shard_map/second_sums/ppermute | solution.py:366
  63.7 5.1 %collective-permute-start.13 = (bf16[2,1,64,128]{3,2,1,0:T(8,128)(2,1)S(1)}, bf16[2,1,64,128]{3,2,1,0:T(8,128)(2,1)S(1)}, u32[]{:S(2)}, u32[]{:S(2)}) collective-permute-start(bf16[2,1,64,128]{3,2,1,0:T(8,128)(2,1)S(1)} %get-tuple-element.34), channel_id=1, source_target_pairs={{0,1},{1,2},{2,3},{3,0},{4,5},{5,6},{6,7},{7,4},{8,9},{9,10},{10,1... | collective-permute-start | bytes 98312 | tf_op jit(solution)/shard_map/second_sums/ppermute | solution.py:365

commit v4 on v3

--- a/solution.py
+++ b/solution.py
@@ -123,16 +123,19 @@
         rows = [(j, y) for j in range(2) for y in range(5)]
         turned = dot(flip[...], jnp.concatenate([feat[j, y] for j, y in rows], axis=1)).astype(BF16)
         corr = []
-        for k, (j, y) in enumerate(rows):
-            near = turned[:, k * CHANS : (k + 1) * CHANS]
-            far = rim[j, y : y + SPAN].reshape(SPAN * WIDTH, CHANS)
-            total = None
-            for g in range(4):
-                start = 2 * WIDTH * g if g < 3 else 5 * WIDTH
-                table = dot_t(near, far[start : start + 2 * WIDTH])
-                moved = pltpu.roll(table, 8 * g + 72, 1, stride=1, stride_axis=0)
-                total = moved if g == 0 else jnp.where(place < 8 * g, total, moved)
-            corr.append((total * edge[...]).astype(BF16))
+        for j in range(2):
+            near = [turned[:, (5 * j + y) * CHANS : (5 * j + y + 1) * CHANS] for y in range(5)]
+            totals = [None] * 5
+            for t in range(10):
+                far = rim[j, t : t + 2].reshape(2 * WIDTH, CHANS)
+                uses = [(t - 2 * g, g) for g in range(3) if 0 <= t - 2 * g < 5]
+                uses += [(t - 5, 3)] if t >= 5 else []
+                table = dot_t(jnp.concatenate([near[y] for y, _ in uses]), far)
+                for k, (y, g) in enumerate(uses):
+                    part_table = table[k * WIDTH : (k + 1) * WIDTH]
+                    moved = pltpu.roll(part_table, 8 * g + 72, 1, stride=1, stride_axis=0)
+                    totals[y] = moved if g == 0 else jnp.where(place < 8 * g, totals[y], moved)
+            corr += [(total * edge[...]).astype(BF16) for total in totals]
         turned = dot(flip[...], jnp.concatenate(corr, axis=1)).astype(BF16)
         corr = jnp.concatenate([turned[:, k * CHANS : (k + 1) * CHANS] for k in range(len(rows))])
         motion = jnp.maximum(dot(corr, spread[...]), 0.0).astype(BF16)
@@ -153,7 +156,7 @@
 
 
 def second_kernel(
-    idx, s0, s1, motion, hid, above, below, w_zr, w_q, w_msg, part, part_other, state_buf, acc
+    idx, s0, s1, motion, hid, first, second, w_zr, w_q, w_msg, part, part_other, state_buf, acc
 ):
     acc[...] = jnp.zeros_like(acc)
     row = idx[SLOTS]
@@ -170,12 +173,10 @@
 
         state = [state_buf[j].reshape(WIDE, CHANS).astype(F32) for j in range(2)]
         xin = [(motion[s].astype(F32) + c).astype(BF16) for s, c in zip(slots, state)]
-        hidden = [
-            jnp.concatenate(
-                [kept(row > 0, above[s].astype(F32)), hid[s], kept(row < 3, below[s].astype(F32))]
-            )
-            for s in slots
-        ]
+        hidden = []
+        for s in slots:
+            above, below = arrived(row, first[SLOTS + s].astype(F32), second[SLOTS + s].astype(F32))
+            hidden.append(jnp.concatenate([above, hid[s], below]))
         hidden = gru(hidden, xin, w_zr[...], side_by_side(w_q))
         add_messages(acc, idx, slots, hidden, w_msg[...])
         return carry
@@ -188,38 +189,36 @@
     return jnp.where(keep, block, jnp.zeros_like(block))
 
 
-def state_kernel(idx, own, near, upd, above, below, w_res, out):
+def arrived(row, first, second):
+    odd = row % 2 == 1
+    above = kept(row > 0, jnp.where(odd, first, second))
+    below = kept(row < 3, jnp.where(odd, second, first))
+    return above, below
+
+
+def state_kernel(idx, own, near, upd, first, second, w_res, out):
     row = idx[SLOTS]
-    for frame in range(4):
-        piece = own if frame < 2 else near
-        field = jnp.concatenate(
-            [
-                kept(row > 0, above[frame].reshape(2 * WIDTH, CHANS)),
-                upd[frame].reshape(OWN, CHANS),
-                kept(row < 3, below[frame].reshape(2 * WIDTH, CHANS)),
-            ],
-            axis=0,
-        )
-        base = piece[frame % 2, 11:16].reshape(WIDE, CHANS).astype(F32)
-        new = (base + conv_rows([field], side_by_side(w_res), 5)).astype(BF16).reshape(5, WIDTH, CHANS)
-        out[frame, 1:4] = new[1:4]
-        out[frame, 0] = kept(row > 0, new[0])
-        out[frame, 4] = kept(row < 3, new[4])
-
-
-def last_kernel(idx, state, upd, above, below, w_res, out):
+    for half, piece in enumerate((own, near)):
+        fields = []
+        for frame in (2 * half, 2 * half + 1):
+            rows = pl.ds(2 * frame, 2)
+            above, below = arrived(row, first[rows].reshape(2 * WIDTH, CHANS), second[rows].reshape(2 * WIDTH, CHANS))
+            fields.append(jnp.concatenate([above, upd[frame].reshape(OWN, CHANS), below]))
+        new = conv_rows(fields, side_by_side(w_res), 5).reshape(2, 5, WIDTH, CHANS)
+        new = (piece[:, 11:16].astype(F32) + new).astype(BF16)
+        out[2 * half : 2 * half + 2, 1:4] = new[:, 1:4]
+        out[2 * half : 2 * half + 2, 0] = kept(row > 0, new[:, 0])
+        out[2 * half : 2 * half + 2, 4] = kept(row < 3, new[:, 4])
+
+
+def last_kernel(idx, state, upd, first, second, w_res, out):
     row = idx[SLOTS]
+    fields = []
     for frame in range(2):
-        field = jnp.concatenate(
-            [
-                kept(row > 0, above[frame].reshape(WIDTH, CHANS)),
-                upd[frame].reshape(OWN, CHANS),
-                kept(row < 3, below[frame].reshape(WIDTH, CHANS)),
-            ],
-            axis=0,
-        )
-        base = state[frame, 1:4].reshape(OWN, CHANS).astype(F32)
-        out[frame] = (base + conv_rows([field], side_by_side(w_res), ROWS)).astype(BF16).reshape(ROWS, WIDTH, CHANS)
+        above, below = arrived(row, first[frame, 0], second[frame, 0])
+        fields.append(jnp.concatenate([above, upd[frame].reshape(OWN, CHANS), below]))
+    new = conv_rows(fields, side_by_side(w_res), ROWS).reshape(2, ROWS, WIDTH, CHANS)
+    out[...] = (state[:2, 1:4].astype(F32) + new).astype(BF16)
 
 
 VM = pl.BlockSpec(memory_space=pltpu.VMEM)
@@ -262,8 +261,9 @@
 def local(fmap, context, pairs, w_corr, w_zr, w_q, w_msg, w_res):
     index, row = lax.axis_index("frames"), lax.axis_index("rows")
     n_frames, n_rows = lax.axis_size("frames"), lax.axis_size("rows")
-    up = [(i, (i + 1) % n_rows) for i in range(n_rows)]
-    down = [(j, i) for i, j in up]
+    even_swap = [(i, i ^ 1) for i in range(n_rows)]
+    odd_swap = [(i, n_rows - 1 - i) for i in range(n_rows)]
+    odd = row % 2 == 1
     across = [(i, (i + 2) % 4) for i in range(n_rows)]
     core_swap = [(i, i ^ 1) for i in range(n_frames)]
     partner = {i: i + 1 if i % 2 else i - 1 for i in range(1, n_frames - 1)}
@@ -273,6 +273,11 @@
         for j in range(n_rows)
     ]
 
+    def rows_swaps(to_above, to_below):
+        first = lax.ppermute(jnp.where(odd, to_above, to_below), "rows", even_swap)
+        second = lax.ppermute(jnp.where(odd, to_below, to_above), "rows", odd_swap)
+        return first, second
+
     def swap_core(x):
         return lax.ppermute(x, "frames", core_swap)
 
@@ -280,12 +285,14 @@
         return lax.ppermute(x, ("frames", "rows"), chip_swap)
 
     with jax.named_scope("feature_rows"):
-        from_above = lax.ppermute(jnp.concatenate([fmap, context[:, 2:]], axis=1), "rows", up)
-        from_below = lax.ppermute(jnp.concatenate([fmap, context[:, :1]], axis=1), "rows", down)
         far = lax.ppermute(jnp.where(row < 2, fmap[:, 2:], fmap[:, :1]), "rows", across)
+        first, second = rows_swaps(
+            jnp.concatenate([fmap, context[:, :1]], axis=1), jnp.concatenate([fmap, context[:, 2:]], axis=1)
+        )
         none = jnp.zeros_like(far)
-        from_above = jnp.where(row > 0, from_above, jnp.zeros_like(from_above))
-        from_below = jnp.where(row < n_rows - 1, from_below, jnp.zeros_like(from_below))
+        blank = jnp.zeros_like(first)
+        from_above = jnp.where(row > 0, jnp.where(odd, first, second), blank)
+        from_below = jnp.where(row < n_rows - 1, jnp.where(odd, second, first), blank)
         own = jnp.concatenate(
             [
                 jnp.where(row < 2, none, far),
@@ -337,17 +344,17 @@
         total = mine + jnp.concatenate([arrived[2:], arrived[:2]])
         upd = jnp.maximum(total, 0.0).astype(BF16).reshape(4, ROWS, WIDTH, CHANS)
     with jax.named_scope("update_rows"):
-        above = lax.ppermute(jnp.concatenate([upd[:, 1:].reshape(8, WIDTH, CHANS), hid_last]), "rows", up)
-        below = lax.ppermute(jnp.concatenate([upd[:, :2].reshape(8, WIDTH, CHANS), hid_first]), "rows", down)
-        upd_above, hid_above = above[:8].reshape(4, 2, WIDTH, CHANS), above[8:]
-        upd_below, hid_below = below[:8].reshape(4, 2, WIDTH, CHANS), below[8:]
+        first, second = rows_swaps(
+            jnp.concatenate([upd[:, :2].reshape(8, WIDTH, CHANS), hid_first]),
+            jnp.concatenate([upd[:, 1:].reshape(8, WIDTH, CHANS), hid_last]),
+        )
     with jax.named_scope("first_state"):
         [state] = call(
             state_kernel,
             [jax.ShapeDtypeStruct((4, 5, WIDTH, CHANS), BF16)],
             [],
             400_000_000,
-            idx, own, near, upd, upd_above, upd_below, w_res,
+            idx, own, near, upd, first, second, w_res,
         )
         state_other = swap_core(state)
     with jax.named_scope("second_iteration"):
@@ -356,21 +363,20 @@
             sums,
             [pltpu.VMEM((2, 5, WIDTH, CHANS), BF16), pltpu.VMEM((SLOTS, OWN, CHANS), F32)],
             1_500_000_000,
-            idx, state, state_other, motion, hid, hid_above, hid_below, w_zr, w_q, w_msg,
+            idx, state, state_other, motion, hid, first, second, w_zr, w_q, w_msg,
         )
     with jax.named_scope("second_sums"):
         mine = part.astype(F32) + swap_core(part_other).astype(F32)
         arrived = swap_chip(mine[2:].astype(BF16)).astype(F32)
         upd = jnp.maximum(mine[:2] + arrived, 0.0).astype(BF16).reshape(2, ROWS, WIDTH, CHANS)
-        above = lax.ppermute(upd[:, 2:], "rows", up)
-        below = lax.ppermute(upd[:, :1], "rows", down)
+        first, second = rows_swaps(upd[:, :1], upd[:, 2:])
     with jax.named_scope("last_state"):
         [out] = call(
             last_kernel,
             [jax.ShapeDtypeStruct((2, ROWS, WIDTH, CHANS), BF16)],
             [],
             120_000_000,
-            idx, state, upd, above, below, w_res,
+            idx, state, upd, first, second, w_res,
         )
     return out
 

time: 70.5 us -> 66.3 us (0.940)
  starting transfers between devices: 23.6 us -> 20.6 us
  local copies, waits for them, and re-layouts: 1.17 us -> 0.21 us
  Pallas kernels: 10.8 us -> 9.91 us
    ppermute x6, starting transfers between devices: 7.97 us -> 4.59 us  [the longest x3 4.58 us: rows_swaps(): second = lax.ppermute(jnp.where(odd, to_below, to_above), 'rows', odd_swap)]
    ppermute x1, waiting for transfers between devices: 0.07 us -> 1.03 us  [local(): lax.ppermute(jnp.where(row < 2, fmap[:, 2:], fmap[:, :1]), 'rows', across)]
    unnamed x21, local copies, waits for them, and re-layouts: 1.03 us -> 0.12 us
    pallas_call x4, Pallas kernels: 10.8 us -> 9.91 us  [call(): pl.pallas_call(kernel, out_shape=outs, in_specs=specs, out_specs=[VM] * l...]
where the time goes in v4:
time: 66.3 us; the launch traced here: 66.2 us
  waiting for transfers between devices  33.6 us (51%)
  starting transfers between devices  20.6 us (31%)
  Pallas kernels  9.91 us (15%)
  other arithmetic  1.6 us (2%)
    ppermute x3, waiting for transfers between devices, rows_swaps(): second = lax.ppermute(jnp.where(odd, to_below, to_above), 'rows', odd_swap)  13.7 us
    ppermute x3, waiting for transfers between devices, swap_chip(): return lax.ppermute(x, ('frames', 'rows'), chip_swap)  12.5 us
    ppermute x3, starting transfers between devices, swap_chip(): return lax.ppermute(x, ('frames', 'rows'), chip_swap)  12.2 us
    pallas_call x4, Pallas kernels, call(): pl.pallas_call(kernel, out_shape=outs, in_specs=specs, out_specs=[VM] * l...  9.91 us
    ppermute x5, waiting for transfers between devices, swap_core(): return lax.ppermute(x, 'frames', core_swap)  5.74 us
    ppermute x3, starting transfers between devices, rows_swaps(): second = lax.ppermute(jnp.where(odd, to_below, to_above), 'rows', odd_swap)  4.58 us
    ppermute x1, starting transfers between devices, local(): lax.ppermute(jnp.where(row < 2, fmap[:, 2:], fmap[:, :1]), 'rows', across)  3.27 us
  transfers between devices with their start and end apart: 15, of which 12 were waited for; matrix products, arithmetic and copies ran while one was open for 1% of the time, Pallas kernels for 0%

profile of v4, /device:TPU:6, one launch (start us, length us, event | category | flops | bytes accessed | tf_op | source)
XLA Modules:
  0.0 66.2 jit_solution(7869336808659642311)
XLA Ops:
  0.0 0.8 %slice_select_fusion = bf16[2,1,64,128]{3,2,1,0:T(8,128)(2,1)S(1)} fusion(bf16[2,3,64,128]{3,2,1,0:T(8,128)(2,1)} %param.8, pred[]{:T(512)S(6)} %lt.46), kind=kLoop, calls=%fused_computation.29 | loop fusion | flops 16384 | bytes 98305 | tf_op jit(solution)/shard_map/feature_rows/jit(_where)/select_n | solution.py:288
  0.8 3.3 %collective-permute-start = (bf16[2,1,64,128]{3,2,1,0:T(8,128)(2,1)S(1)}, bf16[2,1,64,128]{3,2,1,0:T(8,128)(2,1)S(1)}, u32[]{:S(2)}, u32[]{:S(2)}) collective-permute-start(bf16[2,1,64,128]{3,2,1,0:T(8,128)(2,1)S(1)} %slice_select_fusion), channel_id=1, source_target_pairs={{0,2},{1,3},{2,0},{3,1},{4,6},{5,7},{6,4},{7,5},{8,10},{9,11},{10,... | collective-permute-start | bytes 98312 | tf_op jit(solution)/shard_map/feature_rows/ppermute | solution.py:288
  4.1 1.1 %collective-permute-start.2 = (bf16[2,4,64,128]{3,2,1,0:T(8,128)(2,1)S(1)}, bf16[2,4,64,128]{3,2,1,0:T(8,128)(2,1)S(1)}, u32[]{:S(2)}, u32[]{:S(2)}) collective-permute-start(bf16[2,4,64,128]{3,2,1,0:T(8,128)(2,1)S(1)} %get-tuple-element.33), channel_id=1, source_target_pairs={{0,3},{1,2},{2,1},{3,0},{4,7},{5,6},{6,5},{7,4},{8,11},{9,10},{10,... | collective-permute-start | bytes 393224 | tf_op jit(solution)/shard_map/feature_rows/ppermute | solution.py:278
  5.3 1.0 %collective-permute-done = bf16[2,1,64,128]{3,2,1,0:T(8,128)(2,1)S(1)} collective-permute-done((bf16[2,1,64,128]{3,2,1,0:T(8,128)(2,1)S(1)}, bf16[2,1,64,128]{3,2,1,0:T(8,128)(2,1)S(1)}, u32[]{:S(2)}, u32[]{:S(2)}) %collective-permute-start) | collective-permute-done | bytes 32800 | tf_op jit(solution)/shard_map/feature_rows/ppermute | solution.py:288
  6.3 4.1 %collective-permute-done.2 = bf16[2,4,64,128]{3,2,1,0:T(8,128)(2,1)S(1)} collective-permute-done((bf16[2,4,64,128]{3,2,1,0:T(8,128)(2,1)S(1)}, bf16[2,4,64,128]{3,2,1,0:T(8,128)(2,1)S(1)}, u32[]{:S(2)}, u32[]{:S(2)}) %collective-permute-start.2) | collective-permute-done | bytes 131104 | tf_op jit(solution)/shard_map/feature_rows/ppermute | solution.py:278
  10.6 4.2 %collective-permute-start.3 = (bf16[2,16,64,128]{3,2,1,0:T(8,128)(2,1)S(1)}, bf16[2,16,64,128]{3,2,1,0:T(8,128)(2,1)S(1)}, u32[]{:S(2)}, u32[]{:S(2)}) collective-permute-start(bf16[2,16,64,128]{3,2,1,0:T(8,128)(2,1)S(1)} %slice_dynamic-update-slice_fusion.2.p0.own), channel_id=1, source_target_pairs={{0,1},{1,0},{2,3},{3,2},{4,8},{5,9},{6,10},{7,11},{8,4},{9,5},{10,... | collective-permute-start | bytes 1572872 | tf_op jit(solution)/shard_map/feature_window/ppermute | solution.py:285
  14.9 6.8 %collective-permute-done.3.p1.near = bf16[2,16,64,128]{3,2,1,0:T(8,128)(2,1)S(1)} collective-permute-done((bf16[2,16,64,128]{3,2,1,0:T(8,128)(2,1)S(1)}, bf16[2,16,64,128]{3,2,1,0:T(8,128)(2,1)S(1)}, u32[]{:S(2)}, u32[]{:S(2)}) %collective-permute-start.3) | collective-permute-done | bytes 524320 | tf_op jit(solution)/shard_map/feature_window/ppermute | solution.py:285
  22.1 1.5 %collective-permute-done.5.p3 = bf16[2,16,64,128]{3,2,1,0:T(8,128)(2,1)S(1)} collective-permute-done((bf16[2,16,64,128]{3,2,1,0:T(8,128)(2,1)S(1)}, bf16[2,16,64,128]{3,2,1,0:T(8,128)(2,1)S(1)}, u32[]{:S(2)}, u32[]{:S(2)}) %collective-permute-start.5) | collective-permute-done | bytes 524320 | tf_op jit(solution)/shard_map/feature_window/ppermute | solution.py:282
  23.7 4.6 %first_iteration.1 = (bf16[4,192,128]{2,1,0:T(8,128)(2,1)S(1)}, bf16[4,192,128]{2,1,0:T(8,128)(2,1)S(1)}, f32[8,192,128]{2,1,0:T(8,128)S(1)}, bf16[8,64,128]{2,1...) custom-call(s32[9]{0:T(128)S(1)} %pad_add_fusion.idx, ...), custom_call_target="tpu_custom_call" | custom-call | flops 2000000000 | bytes 2896164 | tf_op jit(solution)/shard_map/first_iteration/pallas_call | solution.py:231
  28.5 1.3 %collective-permute-done.6 = bf16[4,192,128]{2,1,0:T(8,128)(2,1)S(1)} collective-permute-done((bf16[4,192,128]{2,1,0:T(8,128)(2,1)S(1)}, bf16[4,192,128]{2,1,0:T(8,128)(2,1)S(1)}, u32[]{:S(2)}, u32[]{:S(2)}) %collective-permute-start.6) | collective-permute-done | bytes 196640 | tf_op jit(solution)/shard_map/first_sums/ppermute | solution.py:282
  29.9 3.9 %collective-permute-start.7 = (bf16[4,192,128]{2,1,0:T(8,128)(2,1)S(1)}, bf16[4,192,128]{2,1,0:T(8,128)(2,1)S(1)}, u32[]{:S(2)}, u32[]{:S(2)}) collective-permute-start(bf16[4,192,128]{2,1,0:T(8,128)(2,1)S(1)} %fusion.2), channel_id=1, source_target_pairs={{0,1},{1,0},{2,3},{3,2},{4,8},{5,9},{6,10},{7,11},{8,4},{9,5},{10,... | collective-permute-start | bytes 589832 | tf_op jit(solution)/shard_map/first_sums/ppermute | solution.py:285
  33.8 3.4 %collective-permute-done.7 = bf16[4,192,128]{2,1,0:T(8,128)(2,1)S(1)} collective-permute-done((bf16[4,192,128]{2,1,0:T(8,128)(2,1)S(1)}, bf16[4,192,128]{2,1,0:T(8,128)(2,1)S(1)}, u32[]{:S(2)}, u32[]{:S(2)}) %collective-permute-start.7) | collective-permute-done | bytes 196640 | tf_op jit(solution)/shard_map/first_sums/ppermute | solution.py:285
  37.4 2.1 %collective-permute-start.9 = (bf16[16,64,128]{2,1,0:T(8,128)(2,1)S(1)}, bf16[16,64,128]{2,1,0:T(8,128)(2,1)S(1)}, u32[]{:S(2)}, u32[]{:S(2)}) collective-permute-start(bf16[16,64,128]{2,1,0:T(8,128)(2,1)S(1)} %get-tuple-element.25), channel_id=1, source_target_pairs={{0,3},{1,2},{2,1},{3,0},{4,7},{5,6},{6,5},{7,4},{8,11},{9,10},{10,... | collective-permute-start | bytes 786440 | tf_op jit(solution)/shard_map/update_rows/ppermute | solution.py:278
  39.5 5.7 %collective-permute-done.9.second = bf16[16,64,128]{2,1,0:T(8,128)(2,1)S(1)} collective-permute-done((bf16[16,64,128]{2,1,0:T(8,128)(2,1)S(1)}, bf16[16,64,128]{2,1,0:T(8,128)(2,1)S(1)}, u32[]{:S(2)}, u32[]{:S(2)}) %collective-permute-start.9) | collective-permute-done | bytes 262176 | tf_op jit(solution)/shard_map/update_rows/ppermute | solution.py:278
  45.2 0.7 %collective-permute-done.8.first = bf16[16,64,128]{2,1,0:T(8,128)(2,1)S(1)} collective-permute-done((bf16[16,64,128]{2,1,0:T(8,128)(2,1)S(1)}, bf16[16,64,128]{2,1,0:T(8,128)(2,1)S(1)}, u32[]{:S(2)}, u32[]{:S(2)}) %collective-permute-start.8) | collective-permute-done | bytes 262176 | tf_op jit(solution)/shard_map/update_rows/ppermute | solution.py:277
  45.9 1.3 %first_state.1.s0.state = bf16[4,5,64,128]{3,2,1,0:T(8,128)(2,1)S(1)} custom-call(s32[9]{0:T(128)S(1)} %pad_add_fusion.idx, bf16[2,16,64,128]{3,2,1,0:T(8,128)(2,1)S(1)} %slice_dynamic-update-slice_fusion.2.p0.own, bf16[2,16,64,128]{3,2,1,0:T(8,128)(2,1)S(1)} %collective-permute-done.3.p1.near, bf16[4,3,64,128]{3,2,1,0:T(8,128)(2,1)S(1)} %bitcast.7, ...), custom_call_target="tpu_custom_call" | custom-call | flops 400000000 | bytes 2064420 | tf_op jit(solution)/shard_map/first_state/pallas_call | solution.py:231
  47.3 1.6 %collective-permute-done.10.s1 = bf16[4,5,64,128]{3,2,1,0:T(8,128)(2,1)S(1)} collective-permute-done((bf16[4,5,64,128]{3,2,1,0:T(8,128)(2,1)S(1)}, bf16[4,5,64,128]{3,2,1,0:T(8,128)(2,1)S(1)}, u32[]{:S(2)}, u32[]{:S(2)}) %collective-permute-start.10) | collective-permute-done | bytes 327712 | tf_op jit(solution)/shard_map/first_state/ppermute | solution.py:282
  49.0 2.4 %second_iteration.1 = (bf16[4,192,128]{2,1,0:T(8,128)(2,1)S(1)}, bf16[4,192,128]{2,1,0:T(8,128)(2,1)S(1)}) custom-call(s32[9]{0:T(128)S(1)} %pad_add_fusion.idx, bf16[4,5,64,128]{3,2,1,0:T(8,128)(2,1)S(1)} %first_state.1.s0.state, bf16[4,5,64,128]{3,2,1,0:T(8,128)(2,1)S(1)} %collective-permute-done.10.s1, bf16[8,320,128]{2,1,0:T(8,128)(2,1)S(1)} %get-tuple-element.21.motion, ...), custom_call_target="tpu_custom_call" | custom-call | flops 1500000000 | bytes 3407908 | tf_op jit(solution)/shard_map/second_iteration/pallas_call | solution.py:231
  51.6 1.3 %collective-permute-done.11 = bf16[4,192,128]{2,1,0:T(8,128)(2,1)S(1)} collective-permute-done((bf16[4,192,128]{2,1,0:T(8,128)(2,1)S(1)}, bf16[4,192,128]{2,1,0:T(8,128)(2,1)S(1)}, u32[]{:S(2)}, u32[]{:S(2)}) %collective-permute-start.11) | collective-permute-done | bytes 196640 | tf_op jit(solution)/shard_map/second_sums/ppermute | solution.py:282
  53.0 4.1 %collective-permute-start.12 = (bf16[2,192,128]{2,1,0:T(8,128)(2,1)S(1)}, bf16[2,192,128]{2,1,0:T(8,128)(2,1)S(1)}, u32[]{:S(2)}, u32[]{:S(2)}) collective-permute-start(bf16[2,192,128]{2,1,0:T(8,128)(2,1)S(1)} %slice.108), channel_id=1, source_target_pairs={{0,1},{1,0},{2,3},{3,2},{4,8},{5,9},{6,10},{7,11},{8,4},{9,5},{10,... | collective-permute-start | bytes 294920 | tf_op jit(solution)/shard_map/second_sums/ppermute | solution.py:285
  57.1 2.3 %collective-permute-done.12 = bf16[2,192,128]{2,1,0:T(8,128)(2,1)S(1)} collective-permute-done((bf16[2,192,128]{2,1,0:T(8,128)(2,1)S(1)}, bf16[2,192,128]{2,1,0:T(8,128)(2,1)S(1)}, u32[]{:S(2)}, u32[]{:S(2)}) %collective-permute-start.12) | collective-permute-done | bytes 98336 | tf_op jit(solution)/shard_map/second_sums/ppermute | solution.py:285
  59.4 1.3 %collective-permute-start.14 = (bf16[2,1,64,128]{3,2,1,0:T(8,128)(2,1)S(1)}, bf16[2,1,64,128]{3,2,1,0:T(8,128)(2,1)S(1)}, u32[]{:S(2)}, u32[]{:S(2)}) collective-permute-start(bf16[2,1,64,128]{3,2,1,0:T(8,128)(2,1)S(1)} %get-tuple-element.35), channel_id=1, source_target_pairs={{0,3},{1,2},{2,1},{3,0},{4,7},{5,6},{6,5},{7,4},{8,11},{9,10},{10,... | collective-permute-start | bytes 98312 | tf_op jit(solution)/shard_map/second_sums/ppermute | solution.py:278
  60.7 3.9 %collective-permute-done.14.second = bf16[2,1,64,128]{3,2,1,0:T(8,128)(2,1)S(1)} collective-permute-done((bf16[2,1,64,128]{3,2,1,0:T(8,128)(2,1)S(1)}, bf16[2,1,64,128]{3,2,1,0:T(8,128)(2,1)S(1)}, u32[]{:S(2)}, u32[]{:S(2)}) %collective-permute-start.14) | collective-permute-done | bytes 32800 | tf_op jit(solution)/shard_map/second_sums/ppermute | solution.py:278
  64.7 1.5 %last_state.1 = bf16[2,3,64,128]{3,2,1,0:T(8,128)(2,1)} custom-call(s32[9]{0:T(128)S(1)} %pad_add_fusion.idx, bf16[4,5,64,128]{3,2,1,0:T(8,128)(2,1)S(1)} %first_state.1.s0.state, bf16[2,3,64,128]{3,2,1,0:T(8,128)(2,1)S(1)} %bitcast.9, bf16[2,1,64,128]{3,2,1,0:T(8,128)(2,1)S(1)} %collective-permute-done.13.first, ...), custom_call_target="tpu_custom_call" | custom-call | flops 120000000 | bytes 786468 | tf_op jit(solution)/shard_map/last_state/pallas_call | solution.py:231
  (54 shorter events, 1.6 us)
Async XLA Ops:
  0.0 4.1 %copy-start.6 = (bf16[2,3,64,128]{3,2,1,0:T(8,128)(2,1)S(1)}, bf16[2,3,64,128]{3,2,1,0:T(8,128)(2,1)}, u32[]{:S(2)}) copy-start(bf16[2,3,64,128]{3,2,1,0:T(8,128)(2,1)} %param.9) | copy-start | bytes 294916
  0.8 3.3 %copy-start.5 = (bf16[2,3,64,128]{3,2,1,0:T(8,128)(2,1)S(1)}, bf16[2,3,64,128]{3,2,1,0:T(8,128)(2,1)}, u32[]{:S(2)}) copy-start(bf16[2,3,64,128]{3,2,1,0:T(8,128)(2,1)} %param.8) | copy-start | bytes 294916
  0.8 5.5 %collective-permute-start = (bf16[2,1,64,128]{3,2,1,0:T(8,128)(2,1)S(1)}, bf16[2,1,64,128]{3,2,1,0:T(8,128)(2,1)S(1)}, u32[]{:S(2)}, u32[]{:S(2)}) collective-permute-start(bf16[2,1,64,128]{3,2,1,0:T(8,128)(2,1)S(1)} %slice_select_fusion), channel_id=1, source_target_pairs={{0,2},{1,3},{2,0},{3,1},{4,6},{5,7},{6,4},{7,5},{8,10},{9,11},{10,... | collective-permute-start | bytes 98312 | tf_op jit(solution)/shard_map/feature_rows/ppermute | solution.py:288
  4.1 6.3 %collective-permute-start.2 = (bf16[2,4,64,128]{3,2,1,0:T(8,128)(2,1)S(1)}, bf16[2,4,64,128]{3,2,1,0:T(8,128)(2,1)S(1)}, u32[]{:S(2)}, u32[]{:S(2)}) collective-permute-start(bf16[2,4,64,128]{3,2,1,0:T(8,128)(2,1)S(1)} %get-tuple-element.33), channel_id=1, source_target_pairs={{0,3},{1,2},{2,1},{3,0},{4,7},{5,6},{6,5},{7,4},{8,11},{9,10},{10,... | collective-permute-start | bytes 393224 | tf_op jit(solution)/shard_map/feature_rows/ppermute | solution.py:278
  5.3 5.1 %collective-permute-start.1 = (bf16[2,4,64,128]{3,2,1,0:T(8,128)(2,1)S(1)}, bf16[2,4,64,128]{3,2,1,0:T(8,128)(2,1)S(1)}, u32[]{:S(2)}, u32[]{:S(2)}) collective-permute-start(bf16[2,4,64,128]{3,2,1,0:T(8,128)(2,1)S(1)} %get-tuple-element.34), channel_id=1, source_target_pairs={{0,1},{1,0},{2,3},{3,2},{4,5},{5,4},{6,7},{7,6},{8,9},{9,8},{10,11... | collective-permute-start | bytes 393224 | tf_op jit(solution)/shard_map/feature_rows/ppermute | solution.py:277
  10.4 13.2 %copy-start.1 = (bf16[9,256,128]{2,1,0:T(8,128)(2,1)S(1)}, bf16[9,256,128]{2,1,0:T(8,128)(2,1)}, u32[]{:S(2)}) copy-start(bf16[9,256,128]{2,1,0:T(8,128)(2,1)} %w_q.3) | copy-start | bytes 1769476
  10.6 13.1 %copy-start.2 = (bf16[256,256]{1,0:T(8,128)(2,1)S(1)}, bf16[256,256]{1,0:T(8,128)(2,1)}, u32[]{:S(2)}) copy-start(bf16[256,256]{1,0:T(8,128)(2,1)} %w_zr.3) | copy-start | bytes 393220
  10.6 4.3 %copy-start.7 = (s32[256,3]{0,1:T(4,128)S(1)}, s32[256,3]{0,1:T(4,128)}, u32[]{:S(2)}) copy-start(s32[256,3]{0,1:T(4,128)} %param.10) | copy-start | bytes 9220
  10.6 13.0 %copy-start.3 = (bf16[128,256]{1,0:T(8,128)(2,1)S(1)}, bf16[128,256]{1,0:T(8,128)(2,1)}, u32[]{:S(2)}) copy-start(bf16[128,256]{1,0:T(8,128)(2,1)} %w_msg.3) | copy-start | bytes 196612
  10.6 11.1 %collective-permute-start.3 = (bf16[2,16,64,128]{3,2,1,0:T(8,128)(2,1)S(1)}, bf16[2,16,64,128]{3,2,1,0:T(8,128)(2,1)S(1)}, u32[]{:S(2)}, u32[]{:S(2)}) collective-permute-start(bf16[2,16,64,128]{3,2,1,0:T(8,128)(2,1)S(1)} %slice_dynamic-update-slice_fusion.2.p0.own), channel_id=1, source_target_pairs={{0,1},{1,0},{2,3},{3,2},{4,8},{5,9},{6,10},{7,11},{8,4},{9,5},{10,... | collective-permute-start | bytes 1572872 | tf_op jit(solution)/shard_map/feature_window/ppermute | solution.py:285
  14.9 8.8 %copy-start.4 = (bf16[49,128]{1,0:T(8,128)(2,1)S(1)}, bf16[49,128]{1,0:T(8,128)(2,1)}, u32[]{:S(2)}) copy-start(bf16[49,128]{1,0:T(8,128)(2,1)} %w_corr.1) | copy-start | bytes 37636
  14.9 7.3 %collective-permute-start.4 = (bf16[2,16,64,128]{3,2,1,0:T(8,128)(2,1)S(1)}, bf16[2,16,64,128]{3,2,1,0:T(8,128)(2,1)S(1)}, u32[]{:S(2)}, u32[]{:S(2)}) collective-permute-start(bf16[2,16,64,128]{3,2,1,0:T(8,128)(2,1)S(1)} %slice_dynamic-update-slice_fusion.2.p0.own), channel_id=1, source_target_pairs={{0,4},{4,0},{8,12},{12,8},{16,20},{20,16},{24,28},{28,24},{32,36},... | collective-permute-start | bytes 1572872 | tf_op jit(solution)/shard_map/feature_window/ppermute | solution.py:282
  21.7 1.9 %collective-permute-start.5 = (bf16[2,16,64,128]{3,2,1,0:T(8,128)(2,1)S(1)}, bf16[2,16,64,128]{3,2,1,0:T(8,128)(2,1)S(1)}, u32[]{:S(2)}, u32[]{:S(2)}) collective-permute-start(bf16[2,16,64,128]{3,2,1,0:T(8,128)(2,1)S(1)} %collective-permute-done.3.p1.near), channel_id=1, source_target_pairs={{0,4},{4,0},{8,12},{12,8},{16,20},{20,16},{24,28},{28,24},{32,36},... | collective-permute-start | bytes 1572872 | tf_op jit(solution)/shard_map/feature_window/ppermute | solution.py:282
  28.3 1.5 %collective-permute-start.6 = (bf16[4,192,128]{2,1,0:T(8,128)(2,1)S(1)}, bf16[4,192,128]{2,1,0:T(8,128)(2,1)S(1)}, u32[]{:S(2)}, u32[]{:S(2)}) collective-permute-start(bf16[4,192,128]{2,1,0:T(8,128)(2,1)S(1)} %get-tuple-element.18), channel_id=1, source_target_pairs={{0,4},{4,0},{8,12},{12,8},{16,20},{20,16},{24,28},{28,24},{32,36},... | collective-permute-start | bytes 589832 | tf_op jit(solution)/shard_map/first_sums/ppermute | solution.py:282
  29.9 7.3 %collective-permute-start.7 = (bf16[4,192,128]{2,1,0:T(8,128)(2,1)S(1)}, bf16[4,192,128]{2,1,0:T(8,128)(2,1)S(1)}, u32[]{:S(2)}, u32[]{:S(2)}) collective-permute-start(bf16[4,192,128]{2,1,0:T(8,128)(2,1)S(1)} %fusion.2), channel_id=1, source_target_pairs={{0,1},{1,0},{2,3},{3,2},{4,8},{5,9},{6,10},{7,11},{8,4},{9,5},{10,... | collective-permute-start | bytes 589832 | tf_op jit(solution)/shard_map/first_sums/ppermute | solution.py:285
  37.3 8.6 %copy-start = (bf16[9,128,128]{2,1,0:T(8,128)(2,1)S(1)}, bf16[9,128,128]{2,1,0:T(8,128)(2,1)}, u32[]{:S(2)}) copy-start(bf16[9,128,128]{2,1,0:T(8,128)(2,1)} %w_res.3) | copy-start | bytes 884740
  37.4 7.8 %collective-permute-start.9 = (bf16[16,64,128]{2,1,0:T(8,128)(2,1)S(1)}, bf16[16,64,128]{2,1,0:T(8,128)(2,1)S(1)}, u32[]{:S(2)}, u32[]{:S(2)}) collective-permute-start(bf16[16,64,128]{2,1,0:T(8,128)(2,1)S(1)} %get-tuple-element.25), channel_id=1, source_target_pairs={{0,3},{1,2},{2,1},{3,0},{4,7},{5,6},{6,5},{7,4},{8,11},{9,10},{10,... | collective-permute-start | bytes 786440 | tf_op jit(solution)/shard_map/update_rows/ppermute | solution.py:278
  39.5 6.4 %collective-permute-start.8 = (bf16[16,64,128]{2,1,0:T(8,128)(2,1)S(1)}, bf16[16,64,128]{2,1,0:T(8,128)(2,1)S(1)}, u32[]{:S(2)}, u32[]{:S(2)}) collective-permute-start(bf16[16,64,128]{2,1,0:T(8,128)(2,1)S(1)} %get-tuple-element.26), channel_id=1, source_target_pairs={{0,1},{1,0},{2,3},{3,2},{4,5},{5,4},{6,7},{7,6},{8,9},{9,8},{10,11... | collective-permute-start | bytes 786440 | tf_op jit(solution)/shard_map/update_rows/ppermute | solution.py:277
  47.2 1.7 %collective-permute-start.10 = (bf16[4,5,64,128]{3,2,1,0:T(8,128)(2,1)S(1)}, bf16[4,5,64,128]{3,2,1,0:T(8,128)(2,1)S(1)}, u32[]{:S(2)}, u32[]{:S(2)}) collective-permute-start(bf16[4,5,64,128]{3,2,1,0:T(8,128)(2,1)S(1)} %first_state.1.s0.state), channel_id=1, source_target_pairs={{0,4},{4,0},{8,12},{12,8},{16,20},{20,16},{24,28},{28,24},{32,36},... | collective-permute-start | bytes 983048 | tf_op jit(solution)/shard_map/first_state/ppermute | solution.py:282
  51.4 1.5 %collective-permute-start.11 = (bf16[4,192,128]{2,1,0:T(8,128)(2,1)S(1)}, bf16[4,192,128]{2,1,0:T(8,128)(2,1)S(1)}, u32[]{:S(2)}, u32[]{:S(2)}) collective-permute-start(bf16[4,192,128]{2,1,0:T(8,128)(2,1)S(1)} %get-tuple-element.24), channel_id=1, source_target_pairs={{0,4},{4,0},{8,12},{12,8},{16,20},{20,16},{24,28},{28,24},{32,36},... | collective-permute-start | bytes 589832 | tf_op jit(solution)/shard_map/second_sums/ppermute | solution.py:282
  53.0 6.4 %collective-permute-start.12 = (bf16[2,192,128]{2,1,0:T(8,128)(2,1)S(1)}, bf16[2,192,128]{2,1,0:T(8,128)(2,1)S(1)}, u32[]{:S(2)}, u32[]{:S(2)}) collective-permute-start(bf16[2,192,128]{2,1,0:T(8,128)(2,1)S(1)} %slice.108), channel_id=1, source_target_pairs={{0,1},{1,0},{2,3},{3,2},{4,8},{5,9},{6,10},{7,11},{8,4},{9,5},{10,... | collective-permute-start | bytes 294920 | tf_op jit(solution)/shard_map/second_sums/ppermute | solution.py:285
  59.4 5.2 %collective-permute-start.14 = (bf16[2,1,64,128]{3,2,1,0:T(8,128)(2,1)S(1)}, bf16[2,1,64,128]{3,2,1,0:T(8,128)(2,1)S(1)}, u32[]{:S(2)}, u32[]{:S(2)}) collective-permute-start(bf16[2,1,64,128]{3,2,1,0:T(8,128)(2,1)S(1)} %get-tuple-element.35), channel_id=1, source_target_pairs={{0,3},{1,2},{2,1},{3,0},{4,7},{5,6},{6,5},{7,4},{8,11},{9,10},{10,... | collective-permute-start | bytes 98312 | tf_op jit(solution)/shard_map/second_sums/ppermute | solution.py:278
  60.7 3.9 %collective-permute-start.13 = (bf16[2,1,64,128]{3,2,1,0:T(8,128)(2,1)S(1)}, bf16[2,1,64,128]{3,2,1,0:T(8,128)(2,1)S(1)}, u32[]{:S(2)}, u32[]{:S(2)}) collective-permute-start(bf16[2,1,64,128]{3,2,1,0:T(8,128)(2,1)S(1)} %get-tuple-element.36), channel_id=1, source_target_pairs={{0,1},{1,0},{2,3},{3,2},{4,5},{5,4},{6,7},{7,6},{8,9},{9,8},{10,11... | collective-permute-start | bytes 98312 | tf_op jit(solution)/shard_map/second_sums/ppermute | solution.py:277

commit v5 on v4

--- a/solution.py
+++ b/solution.py
@@ -59,10 +59,12 @@
     return [new[k * OWN : (k + 1) * OWN] for k in range(len(xin))]
 
 
-def filled(idx):
+def read_table(table, idx):
     count = 0
     for s in range(SLOTS):
-        count += jnp.where(idx[s] >= 0, 1, 0)
+        code = table[0, s]
+        idx[s] = code
+        count += jnp.where(code >= 0, 1, 0)
     return count
 
 
@@ -82,11 +84,12 @@
 
 
 def first_kernel(
-    idx, p0, p1, p2, p3, w_corr, w_zr, w_q, w_msg,
+    table, p0, p1, p2, p3, w_corr, w_zr, w_q, w_msg,
     part, part_other, hid, hid_first, hid_last, motion_out,
-    feat, rim, ctx, acc, flip, spread, edge,
+    feat, rim, ctx, acc, flip, spread, edge, idx,
 ):
     pieces = (p0, p1, p2, p3)
+    count = read_table(table, idx)
     acc[...] = jnp.zeros_like(acc)
     ends = [lax.broadcasted_iota(jnp.int32, (WIDTH, WIDTH), k) for k in range(2)]
     flip[...] = jnp.where(ends[0] + ends[1] == WIDTH - 1, 1.0, 0.0).astype(BF16)
@@ -151,15 +154,16 @@
         add_messages(acc, idx, slots, hidden, w_msg[...])
         return carry
 
-    lax.fori_loop(0, (filled(idx) + 1) // 2, body, 0)
+    lax.fori_loop(0, (count + 1) // 2, body, 0)
     give_sums(acc, part, part_other)
 
 
 def second_kernel(
-    idx, s0, s1, motion, hid, first, second, w_zr, w_q, w_msg, part, part_other, state_buf, acc
+    table, flags, s0, s1, motion, hid, first, second, w_zr, w_q, w_msg,
+    part, part_other, state_buf, acc, idx,
 ):
+    count = read_table(table, idx)
     acc[...] = jnp.zeros_like(acc)
-    row = idx[SLOTS]
 
     def body(i, carry):
         slots = [2 * i + j for j in range(2)]
@@ -175,71 +179,61 @@
         xin = [(motion[s].astype(F32) + c).astype(BF16) for s, c in zip(slots, state)]
         hidden = []
         for s in slots:
-            above, below = arrived(row, first[SLOTS + s].astype(F32), second[SLOTS + s].astype(F32))
+            above, below = arrived(flags, first[SLOTS + s].astype(F32), second[SLOTS + s].astype(F32))
             hidden.append(jnp.concatenate([above, hid[s], below]))
         hidden = gru(hidden, xin, w_zr[...], side_by_side(w_q))
         add_messages(acc, idx, slots, hidden, w_msg[...])
         return carry
 
-    lax.fori_loop(0, (filled(idx) + 1) // 2, body, 0)
+    lax.fori_loop(0, (count + 1) // 2, body, 0)
     give_sums(acc, part, part_other)
 
 
-def kept(keep, block):
-    return jnp.where(keep, block, jnp.zeros_like(block))
-
-
-def arrived(row, first, second):
-    odd = row % 2 == 1
-    above = kept(row > 0, jnp.where(odd, first, second))
-    below = kept(row < 3, jnp.where(odd, second, first))
-    return above, below
-
-
-def state_kernel(idx, own, near, upd, first, second, w_res, out):
-    row = idx[SLOTS]
+def arrived(flags, first, second):
+    weight = [flags[k : k + 1].astype(first.dtype) for k in range(4)]
+    return first * weight[0] + second * weight[1], first * weight[2] + second * weight[3]
+
+
+def state_kernel(flags, own, near, upd, first, second, w_res, out):
     for half, piece in enumerate((own, near)):
         fields = []
         for frame in (2 * half, 2 * half + 1):
             rows = pl.ds(2 * frame, 2)
-            above, below = arrived(row, first[rows].reshape(2 * WIDTH, CHANS), second[rows].reshape(2 * WIDTH, CHANS))
+            above, below = arrived(flags, first[rows].reshape(2 * WIDTH, CHANS), second[rows].reshape(2 * WIDTH, CHANS))
             fields.append(jnp.concatenate([above, upd[frame].reshape(OWN, CHANS), below]))
         new = conv_rows(fields, side_by_side(w_res), 5).reshape(2, 5, WIDTH, CHANS)
         new = (piece[:, 11:16].astype(F32) + new).astype(BF16)
         out[2 * half : 2 * half + 2, 1:4] = new[:, 1:4]
-        out[2 * half : 2 * half + 2, 0] = kept(row > 0, new[:, 0])
-        out[2 * half : 2 * half + 2, 4] = kept(row < 3, new[:, 4])
-
-
-def last_kernel(idx, state, upd, first, second, w_res, out):
-    row = idx[SLOTS]
+        out[2 * half : 2 * half + 2, 0] = new[:, 0] * flags[4:5].astype(BF16)
+        out[2 * half : 2 * half + 2, 4] = new[:, 4] * flags[5:6].astype(BF16)
+
+
+def last_kernel(flags, state, upd, first, second, w_res, out):
     fields = []
     for frame in range(2):
-        above, below = arrived(row, first[frame, 0], second[frame, 0])
+        above, below = arrived(flags, first[frame, 0], second[frame, 0])
         fields.append(jnp.concatenate([above, upd[frame].reshape(OWN, CHANS), below]))
     new = conv_rows(fields, side_by_side(w_res), ROWS).reshape(2, ROWS, WIDTH, CHANS)
     out[...] = (state[:2, 1:4].astype(F32) + new).astype(BF16)
 
 
 VM = pl.BlockSpec(memory_space=pltpu.VMEM)
-SM = pl.BlockSpec(memory_space=pltpu.SMEM)
 
 
 def call(kernel, outs, scratch, flops, *args):
-    specs = [SM if a.dtype == jnp.int32 else VM for a in args]
     size = sum(a.size * a.dtype.itemsize for a in args)
     return pl.pallas_call(
         kernel,
         out_shape=outs,
-        in_specs=specs,
+        in_specs=[VM] * len(args),
         out_specs=[VM] * len(outs),
         scratch_shapes=scratch,
-        compiler_params=pltpu.CompilerParams(vmem_limit_bytes=24 * 2**20),
+        compiler_params=pltpu.CompilerParams(vmem_limit_bytes=14 * 2**20),
         cost_estimate=pl.CostEstimate(flops=flops, bytes_accessed=size, transcendentals=0),
     )(*args)
 
 
-def slot_table(pairs, index, row):
+def slot_table(pairs, index):
     chip, core = index >> 1, index & 1
     sources, targets, owners = (pairs[:, k] for k in range(3))
 
@@ -255,7 +249,15 @@
     levels = 2 * jnp.arange(SLOTS, dtype=jnp.int32) + core
     picked = jnp.where((ranks[None, :] == levels[:, None]) & mine[None, :], codes[None, :] + 1, 0)
     picked = jnp.sum(picked, axis=1) - 1
-    return jnp.concatenate([picked, row[None]])
+    return picked[None]
+
+
+def row_flags(row):
+    line = lax.broadcasted_iota(jnp.int32, (8, CHANS), 0)
+    odd, up, down = row % 2 == 1, row > 0, row < 3
+    flags = ((line == 0) & (up & odd)) | ((line == 1) & (up & ~odd)) | ((line == 2) & (down & ~odd))
+    flags = flags | ((line == 3) & (down & odd)) | ((line == 4) & up) | ((line == 5) & down)
+    return flags.astype(F32)
 
 
 def local(fmap, context, pairs, w_corr, w_zr, w_q, w_msg, w_res):
@@ -307,7 +309,7 @@
             axis=1,
         )
     own, pairs = lax.optimization_barrier((own, pairs))
-    idx = slot_table(pairs, index, row)
+    idx, flags = slot_table(pairs, index), row_flags(row)
     with jax.named_scope("feature_window"):
         near = swap_chip(own)
         own_other = swap_core(own)
@@ -332,6 +334,7 @@
                 pltpu.VMEM((WIDTH, WIDTH), BF16),
                 pltpu.VMEM((CHANS, CHANS), BF16),
                 pltpu.VMEM((WIDTH, CHANS), F32),
+                pltpu.SMEM((SLOTS,), jnp.int32),
             ],
             2_000_000_000,
             idx, own, near, own_other, near_other, w_corr, w_zr, w_q, w_msg,
@@ -354,16 +357,20 @@
             [jax.ShapeDtypeStruct((4, 5, WIDTH, CHANS), BF16)],
             [],
             400_000_000,
-            idx, own, near, upd, first, second, w_res,
+            flags, own, near, upd, first, second, w_res,
         )
         state_other = swap_core(state)
     with jax.named_scope("second_iteration"):
         part, part_other = call(
             second_kernel,
             sums,
-            [pltpu.VMEM((2, 5, WIDTH, CHANS), BF16), pltpu.VMEM((SLOTS, OWN, CHANS), F32)],
+            [
+                pltpu.VMEM((2, 5, WIDTH, CHANS), BF16),
+                pltpu.VMEM((SLOTS, OWN, CHANS), F32),
+                pltpu.SMEM((SLOTS,), jnp.int32),
+            ],
             1_500_000_000,
-            idx, state, state_other, motion, hid, first, second, w_zr, w_q, w_msg,
+            idx, flags, state, state_other, motion, hid, first, second, w_zr, w_q, w_msg,
         )
     with jax.named_scope("second_sums"):
         mine = part.astype(F32) + swap_core(part_other).astype(F32)
@@ -376,7 +383,7 @@
             [jax.ShapeDtypeStruct((2, ROWS, WIDTH, CHANS), BF16)],
             [],
             120_000_000,
-            idx, state, upd, first, second, w_res,
+            flags, state, upd, first, second, w_res,
         )
     return out
 

time: 66.3 us -> 65.8 us (level)
  Pallas kernels: 9.91 us -> 7.82 us
  starting transfers between devices: 20.6 us -> 21.4 us
  other arithmetic: 1.6 us -> 2.36 us
    ppermute x3, waiting for transfers between devices: 0.69 us -> 9.65 us  [rows_swaps(): first = lax.ppermute(jnp.where(odd, to_above, to_below), 'rows', even_swap)]
    ppermute x3, waiting for transfers between devices: 13.7 us -> 4.82 us  [rows_swaps(): second = lax.ppermute(jnp.where(odd, to_below, to_above), 'rows', odd_swap)]
    pallas_call x4, Pallas kernels: 9.91 us -> 7.82 us  [call(): pl.pallas_call(kernel, out_shape=outs, in_specs=[VM] * len(args), out_spe...]
    ppermute x3, starting transfers between devices: 0.01 us -> 1.8 us  [rows_swaps(): first = lax.ppermute(jnp.where(odd, to_above, to_below), 'rows', even_swap)]
    select_n x3, other arithmetic: 0.09 us -> 0.91 us  [rows_swaps(): second = lax.ppermute(jnp.where(odd, to_below, to_above), 'rows', odd_swap)]
    ppermute x3, starting transfers between devices: 4.58 us -> 3.87 us  [rows_swaps(): second = lax.ppermute(jnp.where(odd, to_below, to_above), 'rows', odd_swap)]
  transfers between devices with their start and end apart: 15 -> 15, of which waited for: 12 -> 14; matrix products, arithmetic and copies ran while one was open for 1% -> 1% of each run, Pallas kernels for 0% -> 0%
where the time goes in v5:
time: 65.8 us; the launch traced here: 65.6 us
  waiting for transfers between devices  33.5 us (51%)
  starting transfers between devices  21.4 us (33%)
  Pallas kernels  7.82 us (12%)
  other arithmetic  2.36 us (4%)
    ppermute x3, waiting for transfers between devices, swap_chip(): return lax.ppermute(x, ('frames', 'rows'), chip_swap)  12.4 us
    ppermute x3, starting transfers between devices, swap_chip(): return lax.ppermute(x, ('frames', 'rows'), chip_swap)  12 us
    ppermute x3, waiting for transfers between devices, rows_swaps(): first = lax.ppermute(jnp.where(odd, to_above, to_below), 'rows', even_swap)  9.65 us
    pallas_call x4, Pallas kernels, call(): pl.pallas_call(kernel, out_shape=outs, in_specs=[VM] * len(args), out_spe...  7.82 us
    ppermute x5, waiting for transfers between devices, swap_core(): return lax.ppermute(x, 'frames', core_swap)  5.93 us
    ppermute x3, waiting for transfers between devices, rows_swaps(): second = lax.ppermute(jnp.where(odd, to_below, to_above), 'rows', odd_swap)  4.82 us
    ppermute x3, starting transfers between devices, rows_swaps(): second = lax.ppermute(jnp.where(odd, to_below, to_above), 'rows', odd_swap)  3.87 us
    ppermute x1, starting transfers between devices, local(): lax.ppermute(jnp.where(row < 2, fmap[:, 2:], fmap[:, :1]), 'rows', across)  3.27 us
  transfers between devices with their start and end apart: 15, of which 14 were waited for; matrix products, arithmetic and copies ran while one was open for 1% of the time, Pallas kernels for 0%

profile of v5, /device:TPU:6, one launch (start us, length us, event | category | flops | bytes accessed | tf_op | source)
XLA Modules:
  0.0 65.6 jit_solution(18137215943690277726)
XLA Ops:
  0.0 0.8 %slice_select_fusion = bf16[2,1,64,128]{3,2,1,0:T(8,128)(2,1)S(1)} fusion(bf16[2,3,64,128]{3,2,1,0:T(8,128)(2,1)} %param.8, pred[]{:T(512)S(6)} %lt.48), kind=kLoop, calls=%fused_computation.29 | loop fusion | flops 16384 | bytes 98305 | tf_op jit(solution)/shard_map/feature_rows/jit(_where)/select_n | solution.py:290
  0.8 3.3 %collective-permute-start = (bf16[2,1,64,128]{3,2,1,0:T(8,128)(2,1)S(1)}, bf16[2,1,64,128]{3,2,1,0:T(8,128)(2,1)S(1)}, u32[]{:S(2)}, u32[]{:S(2)}) collective-permute-start(bf16[2,1,64,128]{3,2,1,0:T(8,128)(2,1)S(1)} %slice_select_fusion), channel_id=1, source_target_pairs={{0,2},{1,3},{2,0},{3,1},{4,6},{5,7},{6,4},{7,5},{8,10},{9,11},{10,... | collective-permute-start | bytes 98312 | tf_op jit(solution)/shard_map/feature_rows/ppermute | solution.py:290
  6.3 3.1 %collective-permute-done.1 = bf16[2,4,64,128]{3,2,1,0:T(8,128)(2,1)S(1)} collective-permute-done((bf16[2,4,64,128]{3,2,1,0:T(8,128)(2,1)S(1)}, bf16[2,4,64,128]{3,2,1,0:T(8,128)(2,1)S(1)}, u32[]{:S(2)}, u32[]{:S(2)}) %collective-permute-start.1) | collective-permute-done | bytes 131104 | tf_op jit(solution)/shard_map/feature_rows/ppermute | solution.py:279
  9.5 1.6 %collective-permute-done.2 = bf16[2,4,64,128]{3,2,1,0:T(8,128)(2,1)S(1)} collective-permute-done((bf16[2,4,64,128]{3,2,1,0:T(8,128)(2,1)S(1)}, bf16[2,4,64,128]{3,2,1,0:T(8,128)(2,1)S(1)}, u32[]{:S(2)}, u32[]{:S(2)}) %collective-permute-start.2) | collective-permute-done | bytes 131104 | tf_op jit(solution)/shard_map/feature_rows/ppermute | solution.py:280
  11.3 3.9 %collective-permute-start.3 = (bf16[2,16,64,128]{3,2,1,0:T(8,128)(2,1)S(1)}, bf16[2,16,64,128]{3,2,1,0:T(8,128)(2,1)S(1)}, u32[]{:S(2)}, u32[]{:S(2)}) collective-permute-start(bf16[2,16,64,128]{3,2,1,0:T(8,128)(2,1)S(1)} %slice_dynamic-update-slice_fusion.2.p0.own), channel_id=1, source_target_pairs={{0,1},{1,0},{2,3},{3,2},{4,8},{5,9},{6,10},{7,11},{8,4},{9,5},{10,... | collective-permute-start | bytes 1572872 | tf_op jit(solution)/shard_map/feature_window/ppermute | solution.py:287
  15.4 6.7 %collective-permute-done.3.p1.near = bf16[2,16,64,128]{3,2,1,0:T(8,128)(2,1)S(1)} collective-permute-done((bf16[2,16,64,128]{3,2,1,0:T(8,128)(2,1)S(1)}, bf16[2,16,64,128]{3,2,1,0:T(8,128)(2,1)S(1)}, u32[]{:S(2)}, u32[]{:S(2)}) %collective-permute-start.3) | collective-permute-done | bytes 524320 | tf_op jit(solution)/shard_map/feature_window/ppermute | solution.py:287
  22.3 1.7 %collective-permute-done.5.p3 = bf16[2,16,64,128]{3,2,1,0:T(8,128)(2,1)S(1)} collective-permute-done((bf16[2,16,64,128]{3,2,1,0:T(8,128)(2,1)S(1)}, bf16[2,16,64,128]{3,2,1,0:T(8,128)(2,1)S(1)}, u32[]{:S(2)}, u32[]{:S(2)}) %collective-permute-start.5) | collective-permute-done | bytes 524320 | tf_op jit(solution)/shard_map/feature_window/ppermute | solution.py:284
  24.0 4.1 %first_iteration.1 = (bf16[4,192,128]{2,1,0:T(8,128)(2,1)S(1)}, bf16[4,192,128]{2,1,0:T(8,128)(2,1)S(1)}, f32[8,192,128]{2,1,0:T(8,128)S(1)}, bf16[8,64,128]{2,1...) custom-call(s32[1,8]{1,0:T(1,128)S(1)} %add_bitcast_fusion.table, ...), custom_call_target="tpu_custom_call" | custom-call | flops 2000000000 | bytes 2896160 | tf_op jit(solution)/shard_map/first_iteration/pallas_call | solution.py:225
  28.4 1.3 %collective-permute-done.6 = bf16[4,192,128]{2,1,0:T(8,128)(2,1)S(1)} collective-permute-done((bf16[4,192,128]{2,1,0:T(8,128)(2,1)S(1)}, bf16[4,192,128]{2,1,0:T(8,128)(2,1)S(1)}, u32[]{:S(2)}, u32[]{:S(2)}) %collective-permute-start.6) | collective-permute-done | bytes 196640 | tf_op jit(solution)/shard_map/first_sums/ppermute | solution.py:284
  29.8 3.9 %collective-permute-start.7 = (bf16[4,192,128]{2,1,0:T(8,128)(2,1)S(1)}, bf16[4,192,128]{2,1,0:T(8,128)(2,1)S(1)}, u32[]{:S(2)}, u32[]{:S(2)}) collective-permute-start(bf16[4,192,128]{2,1,0:T(8,128)(2,1)S(1)} %fusion.2), channel_id=1, source_target_pairs={{0,1},{1,0},{2,3},{3,2},{4,8},{5,9},{6,10},{7,11},{8,4},{9,5},{10,... | collective-permute-start | bytes 589832 | tf_op jit(solution)/shard_map/first_sums/ppermute | solution.py:287
  33.7 3.4 %collective-permute-done.7 = bf16[4,192,128]{2,1,0:T(8,128)(2,1)S(1)} collective-permute-done((bf16[4,192,128]{2,1,0:T(8,128)(2,1)S(1)}, bf16[4,192,128]{2,1,0:T(8,128)(2,1)S(1)}, u32[]{:S(2)}, u32[]{:S(2)}) %collective-permute-start.7) | collective-permute-done | bytes 196640 | tf_op jit(solution)/shard_map/first_sums/ppermute | solution.py:287
  37.2 0.9 %broadcast_select_fusion = (bf16[16,64,128]{2,1,0:T(8,128)(2,1)}, bf16[16,64,128]{2,1,0:T(8,128)(2,1)}) fusion(pred[]{:T(512)S(6)} %eq.81, bf16[8,64,128]{2,1,0:T(8,128)(2,1)S(1)} %get-tuple-element.20, bf16[8,64,128]{2,1,0:T(8,128)(2,1)S(1)} %bitcast.12, bf16[8,64,128]{2,1,0:T(8,128)(2,1)S(1)} %get-tuple-element.19, bf16[8,64,128]{2,1,0:T(8,128)(2,1)S(1)} %bitcast.11), kind=kLoop, calls=%fused_computation.11 | loop fusion | flops 524288 | bytes 1048577 | tf_op jit(solution)/shard_map/update_rows/jit(_where)/select_n | solution.py:280
  38.6 1.4 %collective-permute-start.9 = (bf16[16,64,128]{2,1,0:T(8,128)(2,1)}, bf16[16,64,128]{2,1,0:T(8,128)(2,1)S(1)}, u32[]{:S(2)}, u32[]{:S(2)}) collective-permute-start(bf16[16,64,128]{2,1,0:T(8,128)(2,1)} %get-tuple-element.25), channel_id=1, source_target_pairs={{0,3},{1,2},{2,1},{3,0},{4,7},{5,6},{6,5},{7,4},{8,11},{9,10},{10,... | collective-permute-start | bytes 786440 | tf_op jit(solution)/shard_map/update_rows/ppermute | solution.py:280
  40.0 4.8 %collective-permute-done.8.first = bf16[16,64,128]{2,1,0:T(8,128)(2,1)S(1)} collective-permute-done((bf16[16,64,128]{2,1,0:T(8,128)(2,1)}, bf16[16,64,128]{2,1,0:T(8,128)(2,1)S(1)}, u32[]{:S(2)}, u32[]{:S(2)}) %collective-permute-start.8) | collective-permute-done | bytes 262176 | tf_op jit(solution)/shard_map/update_rows/ppermute | solution.py:279
  44.9 1.5 %collective-permute-done.9.second = bf16[16,64,128]{2,1,0:T(8,128)(2,1)S(1)} collective-permute-done((bf16[16,64,128]{2,1,0:T(8,128)(2,1)}, bf16[16,64,128]{2,1,0:T(8,128)(2,1)S(1)}, u32[]{:S(2)}, u32[]{:S(2)}) %collective-permute-start.9) | collective-permute-done | bytes 262176 | tf_op jit(solution)/shard_map/update_rows/ppermute | solution.py:280
  47.3 1.6 %collective-permute-done.10.s1 = bf16[4,5,64,128]{3,2,1,0:T(8,128)(2,1)S(1)} collective-permute-done((bf16[4,5,64,128]{3,2,1,0:T(8,128)(2,1)S(1)}, bf16[4,5,64,128]{3,2,1,0:T(8,128)(2,1)S(1)}, u32[]{:S(2)}, u32[]{:S(2)}) %collective-permute-start.10) | collective-permute-done | bytes 327712 | tf_op jit(solution)/shard_map/first_state/ppermute | solution.py:284
  49.0 2.0 %second_iteration.1 = (bf16[4,192,128]{2,1,0:T(8,128)(2,1)S(1)}, bf16[4,192,128]{2,1,0:T(8,128)(2,1)S(1)}) custom-call(s32[1,8]{1,0:T(1,128)S(1)} %add_bitcast_fusion.table, f32[8,128]{1,0:T(8,128)S(1)} %iota.34.flags, bf16[4,5,64,128]{3,2,1,0:T(8,128)(2,1)S(1)} %first_state.1.s0.state, bf16[4,5,64,128]{3,2,1,0:T(8,128)(2,1)S(1)} %collective-permute-done.10.s1, ...), custom_call_target="tpu_custom_call" | custom-call | flops 1500000000 | bytes 3412000 | tf_op jit(solution)/shard_map/second_iteration/pallas_call | solution.py:225
  51.2 1.3 %collective-permute-done.11 = bf16[4,192,128]{2,1,0:T(8,128)(2,1)S(1)} collective-permute-done((bf16[4,192,128]{2,1,0:T(8,128)(2,1)S(1)}, bf16[4,192,128]{2,1,0:T(8,128)(2,1)S(1)}, u32[]{:S(2)}, u32[]{:S(2)}) %collective-permute-start.11) | collective-permute-done | bytes 196640 | tf_op jit(solution)/shard_map/second_sums/ppermute | solution.py:284
  52.5 4.1 %collective-permute-start.12 = (bf16[2,192,128]{2,1,0:T(8,128)(2,1)S(1)}, bf16[2,192,128]{2,1,0:T(8,128)(2,1)S(1)}, u32[]{:S(2)}, u32[]{:S(2)}) collective-permute-start(bf16[2,192,128]{2,1,0:T(8,128)(2,1)S(1)} %slice.108), channel_id=1, source_target_pairs={{0,1},{1,0},{2,3},{3,2},{4,8},{5,9},{6,10},{7,11},{8,4},{9,5},{10,... | collective-permute-start | bytes 294920 | tf_op jit(solution)/shard_map/second_sums/ppermute | solution.py:287
  56.6 2.3 %collective-permute-done.12 = bf16[2,192,128]{2,1,0:T(8,128)(2,1)S(1)} collective-permute-done((bf16[2,192,128]{2,1,0:T(8,128)(2,1)S(1)}, bf16[2,192,128]{2,1,0:T(8,128)(2,1)S(1)}, u32[]{:S(2)}, u32[]{:S(2)}) %collective-permute-start.12) | collective-permute-done | bytes 98336 | tf_op jit(solution)/shard_map/second_sums/ppermute | solution.py:287
  59.5 1.8 %collective-permute-start.14 = (bf16[2,1,64,128]{3,2,1,0:T(8,128)(2,1)S(1)}, bf16[2,1,64,128]{3,2,1,0:T(8,128)(2,1)S(1)}, u32[]{:S(2)}, u32[]{:S(2)}) collective-permute-start(bf16[2,1,64,128]{3,2,1,0:T(8,128)(2,1)S(1)} %get-tuple-element.35), channel_id=1, source_target_pairs={{0,3},{1,2},{2,1},{3,0},{4,7},{5,6},{6,5},{7,4},{8,11},{9,10},{10,... | collective-permute-start | bytes 98312 | tf_op jit(solution)/shard_map/second_sums/ppermute | solution.py:280
  61.3 1.7 %collective-permute-done.13.first = bf16[2,1,64,128]{3,2,1,0:T(8,128)(2,1)S(1)} collective-permute-done((bf16[2,1,64,128]{3,2,1,0:T(8,128)(2,1)S(1)}, bf16[2,1,64,128]{3,2,1,0:T(8,128)(2,1)S(1)}, u32[]{:S(2)}, u32[]{:S(2)}) %collective-permute-start.13) | collective-permute-done | bytes 32800 | tf_op jit(solution)/shard_map/second_sums/ppermute | solution.py:279
  63.0 1.7 %collective-permute-done.14.second = bf16[2,1,64,128]{3,2,1,0:T(8,128)(2,1)S(1)} collective-permute-done((bf16[2,1,64,128]{3,2,1,0:T(8,128)(2,1)S(1)}, bf16[2,1,64,128]{3,2,1,0:T(8,128)(2,1)S(1)}, u32[]{:S(2)}, u32[]{:S(2)}) %collective-permute-start.14) | collective-permute-done | bytes 32800 | tf_op jit(solution)/shard_map/second_sums/ppermute | solution.py:280
  64.6 1.0 %last_state.1 = bf16[2,3,64,128]{3,2,1,0:T(8,128)(2,1)} custom-call(f32[8,128]{1,0:T(8,128)S(1)} %iota.34.flags, bf16[4,5,64,128]{3,2,1,0:T(8,128)(2,1)S(1)} %first_state.1.s0.state, bf16[2,3,64,128]{3,2,1,0:T(8,128)(2,1)S(1)} %bitcast.10, bf16[2,1,64,128]{3,2,1,0:T(8,128)(2,1)S(1)} %collective-permute-done.13.first, ...), custom_call_target="tpu_custom_call" | custom-call | flops 120000000 | bytes 790528 | tf_op jit(solution)/shard_map/last_state/pallas_call | solution.py:225
  (59 shorter events, 5.5 us)
Async XLA Ops:
  0.0 4.1 %copy-start.8 = (bf16[2,3,64,128]{3,2,1,0:T(8,128)(2,1)S(1)}, bf16[2,3,64,128]{3,2,1,0:T(8,128)(2,1)}, u32[]{:S(2)}) copy-start(bf16[2,3,64,128]{3,2,1,0:T(8,128)(2,1)} %param.9) | copy-start | bytes 294916
  0.8 3.3 %copy-start.7 = (bf16[2,3,64,128]{3,2,1,0:T(8,128)(2,1)S(1)}, bf16[2,3,64,128]{3,2,1,0:T(8,128)(2,1)}, u32[]{:S(2)}) copy-start(bf16[2,3,64,128]{3,2,1,0:T(8,128)(2,1)} %param.8) | copy-start | bytes 294916
  0.8 5.5 %collective-permute-start = (bf16[2,1,64,128]{3,2,1,0:T(8,128)(2,1)S(1)}, bf16[2,1,64,128]{3,2,1,0:T(8,128)(2,1)S(1)}, u32[]{:S(2)}, u32[]{:S(2)}) collective-permute-start(bf16[2,1,64,128]{3,2,1,0:T(8,128)(2,1)S(1)} %slice_select_fusion), channel_id=1, source_target_pairs={{0,2},{1,3},{2,0},{3,1},{4,6},{5,7},{6,4},{7,5},{8,10},{9,11},{10,... | collective-permute-start | bytes 98312 | tf_op jit(solution)/shard_map/feature_rows/ppermute | solution.py:290
  4.1 5.3 %collective-permute-start.1 = (bf16[2,4,64,128]{3,2,1,0:T(8,128)(2,1)S(1)}, bf16[2,4,64,128]{3,2,1,0:T(8,128)(2,1)S(1)}, u32[]{:S(2)}, u32[]{:S(2)}) collective-permute-start(bf16[2,4,64,128]{3,2,1,0:T(8,128)(2,1)S(1)} %get-tuple-element.34), channel_id=1, source_target_pairs={{0,1},{1,0},{2,3},{3,2},{4,5},{5,4},{6,7},{7,6},{8,9},{9,8},{10,11... | collective-permute-start | bytes 393224 | tf_op jit(solution)/shard_map/feature_rows/ppermute | solution.py:279
  4.9 6.2 %collective-permute-start.2 = (bf16[2,4,64,128]{3,2,1,0:T(8,128)(2,1)S(1)}, bf16[2,4,64,128]{3,2,1,0:T(8,128)(2,1)S(1)}, u32[]{:S(2)}, u32[]{:S(2)}) collective-permute-start(bf16[2,4,64,128]{3,2,1,0:T(8,128)(2,1)S(1)} %get-tuple-element.33), channel_id=1, source_target_pairs={{0,3},{1,2},{2,1},{3,0},{4,7},{5,6},{6,5},{7,4},{8,11},{9,10},{10,... | collective-permute-start | bytes 393224 | tf_op jit(solution)/shard_map/feature_rows/ppermute | solution.py:280
  11.1 12.9 %copy-start.1 = (bf16[9,256,128]{2,1,0:T(8,128)(2,1)S(1)}, bf16[9,256,128]{2,1,0:T(8,128)(2,1)}, u32[]{:S(2)}) copy-start(bf16[9,256,128]{2,1,0:T(8,128)(2,1)} %w_q.3) | copy-start | bytes 1769476
  11.2 12.8 %copy-start.2 = (bf16[256,256]{1,0:T(8,128)(2,1)S(1)}, bf16[256,256]{1,0:T(8,128)(2,1)}, u32[]{:S(2)}) copy-start(bf16[256,256]{1,0:T(8,128)(2,1)} %w_zr.3) | copy-start | bytes 393220
  11.3 4.0 %copy-start.9 = (s32[256,3]{0,1:T(4,128)S(1)}, s32[256,3]{0,1:T(4,128)}, u32[]{:S(2)}) copy-start(s32[256,3]{0,1:T(4,128)} %param.10) | copy-start | bytes 9220
  11.3 12.8 %copy-start.3 = (bf16[128,256]{1,0:T(8,128)(2,1)S(1)}, bf16[128,256]{1,0:T(8,128)(2,1)}, u32[]{:S(2)}) copy-start(bf16[128,256]{1,0:T(8,128)(2,1)} %w_msg.3) | copy-start | bytes 196612
  11.3 10.8 %collective-permute-start.3 = (bf16[2,16,64,128]{3,2,1,0:T(8,128)(2,1)S(1)}, bf16[2,16,64,128]{3,2,1,0:T(8,128)(2,1)S(1)}, u32[]{:S(2)}, u32[]{:S(2)}) collective-permute-start(bf16[2,16,64,128]{3,2,1,0:T(8,128)(2,1)S(1)} %slice_dynamic-update-slice_fusion.2.p0.own), channel_id=1, source_target_pairs={{0,1},{1,0},{2,3},{3,2},{4,8},{5,9},{6,10},{7,11},{8,4},{9,5},{10,... | collective-permute-start | bytes 1572872 | tf_op jit(solution)/shard_map/feature_window/ppermute | solution.py:287
  15.2 8.8 %copy-start.4 = (bf16[49,128]{1,0:T(8,128)(2,1)S(1)}, bf16[49,128]{1,0:T(8,128)(2,1)}, u32[]{:S(2)}) copy-start(bf16[49,128]{1,0:T(8,128)(2,1)} %w_corr.1) | copy-start | bytes 37636
  15.3 7.1 %collective-permute-start.4 = (bf16[2,16,64,128]{3,2,1,0:T(8,128)(2,1)S(1)}, bf16[2,16,64,128]{3,2,1,0:T(8,128)(2,1)S(1)}, u32[]{:S(2)}, u32[]{:S(2)}) collective-permute-start(bf16[2,16,64,128]{3,2,1,0:T(8,128)(2,1)S(1)} %slice_dynamic-update-slice_fusion.2.p0.own), channel_id=1, source_target_pairs={{0,4},{4,0},{8,12},{12,8},{16,20},{20,16},{24,28},{28,24},{32,36},... | collective-permute-start | bytes 1572872 | tf_op jit(solution)/shard_map/feature_window/ppermute | solution.py:284
  22.1 1.9 %collective-permute-start.5 = (bf16[2,16,64,128]{3,2,1,0:T(8,128)(2,1)S(1)}, bf16[2,16,64,128]{3,2,1,0:T(8,128)(2,1)S(1)}, u32[]{:S(2)}, u32[]{:S(2)}) collective-permute-start(bf16[2,16,64,128]{3,2,1,0:T(8,128)(2,1)S(1)} %collective-permute-done.3.p1.near), channel_id=1, source_target_pairs={{0,4},{4,0},{8,12},{12,8},{16,20},{20,16},{24,28},{28,24},{32,36},... | collective-permute-start | bytes 1572872 | tf_op jit(solution)/shard_map/feature_window/ppermute | solution.py:284
  28.2 9.0 %copy-start.5 = (f32[8,192,128]{2,1,0:T(8,128)}, f32[8,192,128]{2,1,0:T(8,128)S(1)}, u32[]{:S(2)}) copy-start(f32[8,192,128]{2,1,0:T(8,128)S(1)} %get-tuple-element.22.hid) | copy-start | bytes 2359300
  28.2 1.5 %collective-permute-start.6 = (bf16[4,192,128]{2,1,0:T(8,128)(2,1)S(1)}, bf16[4,192,128]{2,1,0:T(8,128)(2,1)S(1)}, u32[]{:S(2)}, u32[]{:S(2)}) collective-permute-start(bf16[4,192,128]{2,1,0:T(8,128)(2,1)S(1)} %get-tuple-element.18), channel_id=1, source_target_pairs={{0,4},{4,0},{8,12},{12,8},{16,20},{20,16},{24,28},{28,24},{32,36},... | collective-permute-start | bytes 589832 | tf_op jit(solution)/shard_map/first_sums/ppermute | solution.py:284
  29.8 7.3 %collective-permute-start.7 = (bf16[4,192,128]{2,1,0:T(8,128)(2,1)S(1)}, bf16[4,192,128]{2,1,0:T(8,128)(2,1)S(1)}, u32[]{:S(2)}, u32[]{:S(2)}) collective-permute-start(bf16[4,192,128]{2,1,0:T(8,128)(2,1)S(1)} %fusion.2), channel_id=1, source_target_pairs={{0,1},{1,0},{2,3},{3,2},{4,8},{5,9},{6,10},{7,11},{8,4},{9,5},{10,... | collective-permute-start | bytes 589832 | tf_op jit(solution)/shard_map/first_sums/ppermute | solution.py:287
  37.2 9.2 %copy-start = (bf16[9,128,128]{2,1,0:T(8,128)(2,1)S(1)}, bf16[9,128,128]{2,1,0:T(8,128)(2,1)}, u32[]{:S(2)}) copy-start(bf16[9,128,128]{2,1,0:T(8,128)(2,1)} %w_res.3) | copy-start | bytes 884740
  38.1 6.7 %collective-permute-start.8 = (bf16[16,64,128]{2,1,0:T(8,128)(2,1)}, bf16[16,64,128]{2,1,0:T(8,128)(2,1)S(1)}, u32[]{:S(2)}, u32[]{:S(2)}) collective-permute-start(bf16[16,64,128]{2,1,0:T(8,128)(2,1)} %get-tuple-element.26), channel_id=1, source_target_pairs={{0,1},{1,0},{2,3},{3,2},{4,5},{5,4},{6,7},{7,6},{8,9},{9,8},{10,11... | collective-permute-start | bytes 786440 | tf_op jit(solution)/shard_map/update_rows/ppermute | solution.py:279
  38.6 7.8 %collective-permute-start.9 = (bf16[16,64,128]{2,1,0:T(8,128)(2,1)}, bf16[16,64,128]{2,1,0:T(8,128)(2,1)S(1)}, u32[]{:S(2)}, u32[]{:S(2)}) collective-permute-start(bf16[16,64,128]{2,1,0:T(8,128)(2,1)} %get-tuple-element.25), channel_id=1, source_target_pairs={{0,3},{1,2},{2,1},{3,0},{4,7},{5,6},{6,5},{7,4},{8,11},{9,10},{10,... | collective-permute-start | bytes 786440 | tf_op jit(solution)/shard_map/update_rows/ppermute | solution.py:280
  47.2 1.7 %collective-permute-start.10 = (bf16[4,5,64,128]{3,2,1,0:T(8,128)(2,1)S(1)}, bf16[4,5,64,128]{3,2,1,0:T(8,128)(2,1)S(1)}, u32[]{:S(2)}, u32[]{:S(2)}) collective-permute-start(bf16[4,5,64,128]{3,2,1,0:T(8,128)(2,1)S(1)} %first_state.1.s0.state), channel_id=1, source_target_pairs={{0,4},{4,0},{8,12},{12,8},{16,20},{20,16},{24,28},{28,24},{32,36},... | collective-permute-start | bytes 983048 | tf_op jit(solution)/shard_map/first_state/ppermute | solution.py:284
  50.9 1.5 %collective-permute-start.11 = (bf16[4,192,128]{2,1,0:T(8,128)(2,1)S(1)}, bf16[4,192,128]{2,1,0:T(8,128)(2,1)S(1)}, u32[]{:S(2)}, u32[]{:S(2)}) collective-permute-start(bf16[4,192,128]{2,1,0:T(8,128)(2,1)S(1)} %get-tuple-element.24), channel_id=1, source_target_pairs={{0,4},{4,0},{8,12},{12,8},{16,20},{20,16},{24,28},{28,24},{32,36},... | collective-permute-start | bytes 589832 | tf_op jit(solution)/shard_map/second_sums/ppermute | solution.py:284
  52.5 6.4 %collective-permute-start.12 = (bf16[2,192,128]{2,1,0:T(8,128)(2,1)S(1)}, bf16[2,192,128]{2,1,0:T(8,128)(2,1)S(1)}, u32[]{:S(2)}, u32[]{:S(2)}) collective-permute-start(bf16[2,192,128]{2,1,0:T(8,128)(2,1)S(1)} %slice.108), channel_id=1, source_target_pairs={{0,1},{1,0},{2,3},{3,2},{4,8},{5,9},{6,10},{7,11},{8,4},{9,5},{10,... | collective-permute-start | bytes 294920 | tf_op jit(solution)/shard_map/second_sums/ppermute | solution.py:287
  59.0 4.0 %collective-permute-start.13 = (bf16[2,1,64,128]{3,2,1,0:T(8,128)(2,1)S(1)}, bf16[2,1,64,128]{3,2,1,0:T(8,128)(2,1)S(1)}, u32[]{:S(2)}, u32[]{:S(2)}) collective-permute-start(bf16[2,1,64,128]{3,2,1,0:T(8,128)(2,1)S(1)} %get-tuple-element.36), channel_id=1, source_target_pairs={{0,1},{1,0},{2,3},{3,2},{4,5},{5,4},{6,7},{7,6},{8,9},{9,8},{10,11... | collective-permute-start | bytes 98312 | tf_op jit(solution)/shard_map/second_sums/ppermute | solution.py:279
  59.5 5.1 %collective-permute-start.14 = (bf16[2,1,64,128]{3,2,1,0:T(8,128)(2,1)S(1)}, bf16[2,1,64,128]{3,2,1,0:T(8,128)(2,1)S(1)}, u32[]{:S(2)}, u32[]{:S(2)}) collective-permute-start(bf16[2,1,64,128]{3,2,1,0:T(8,128)(2,1)S(1)} %get-tuple-element.35), channel_id=1, source_target_pairs={{0,3},{1,2},{2,1},{3,0},{4,7},{5,6},{6,5},{7,4},{8,11},{9,10},{10,... | collective-permute-start | bytes 98312 | tf_op jit(solution)/shard_map/second_sums/ppermute | solution.py:280
  (1 other events, 2.5 us)

commit v6 on v5

--- a/solution.py
+++ b/solution.py
@@ -84,11 +84,11 @@
 
 
 def first_kernel(
-    table, p0, p1, p2, p3, w_corr, w_zr, w_q, w_msg,
+    table, c0, c1, c23, h0, h1, h2, h3, w_corr, w_zr, w_q, w_msg,
     part, part_other, hid, hid_first, hid_last, motion_out,
     feat, rim, ctx, acc, flip, spread, edge, idx,
 ):
-    pieces = (p0, p1, p2, p3)
+    pieces = ((c0, 0, h0), (c1, 0, h1), (c23, 0, h2), (c23, 2, h3))
     count = read_table(table, idx)
     acc[...] = jnp.zeros_like(acc)
     ends = [lax.broadcasted_iota(jnp.int32, (WIDTH, WIDTH), k) for k in range(2)]
@@ -112,16 +112,21 @@
         for j, s in enumerate(slots):
             code = jnp.maximum(idx[s], 0)
             source, target = code // SLOTS, code % SLOTS
-            for k, piece in enumerate(pieces):
+            for k, (center, first, halo) in enumerate(pieces):
 
                 @pl.when(source // 2 == k)
                 def _():
-                    feat[j] = piece[source % 2, 3:8]
-                    ctx[j] = piece[source % 2, 11:16]
+                    frame = source % 2
+                    feat[j, 0], ctx[j, 0] = halo[frame, 3], halo[frame, 8]
+                    feat[j, 1:4], ctx[j, 1:4] = center[first + frame, 0:3], center[first + frame, 3:6]
+                    feat[j, 4], ctx[j, 4] = halo[frame, 4], halo[frame, 9]
 
                 @pl.when(target // 2 == k)
                 def _():
-                    rim[j] = piece[target % 2, 0:11]
+                    frame = target % 2
+                    rim[j, 0:4] = halo[frame, 0:4]
+                    rim[j, 4:7] = center[first + frame, 0:3]
+                    rim[j, 7:11] = halo[frame, 4:8]
 
         rows = [(j, y) for j in range(2) for y in range(5)]
         turned = dot(flip[...], jnp.concatenate([feat[j, y] for j, y in rows], axis=1)).astype(BF16)
@@ -194,15 +199,16 @@
     return first * weight[0] + second * weight[1], first * weight[2] + second * weight[3]
 
 
-def state_kernel(flags, own, near, upd, first, second, w_res, out):
-    for half, piece in enumerate((own, near)):
+def state_kernel(flags, c0, c1, h0, h1, upd, first, second, w_res, out):
+    for half, (center, halo) in enumerate(((c0, h0), (c1, h1))):
         fields = []
         for frame in (2 * half, 2 * half + 1):
             rows = pl.ds(2 * frame, 2)
             above, below = arrived(flags, first[rows].reshape(2 * WIDTH, CHANS), second[rows].reshape(2 * WIDTH, CHANS))
             fields.append(jnp.concatenate([above, upd[frame].reshape(OWN, CHANS), below]))
         new = conv_rows(fields, side_by_side(w_res), 5).reshape(2, 5, WIDTH, CHANS)
-        new = (piece[:, 11:16].astype(F32) + new).astype(BF16)
+        base = jnp.concatenate([halo[:, 8:9], center[:, 3:6], halo[:, 9:10]], axis=1)
+        new = (base.astype(F32) + new).astype(BF16)
         out[2 * half : 2 * half + 2, 1:4] = new[:, 1:4]
         out[2 * half : 2 * half + 2, 0] = new[:, 0] * flags[4:5].astype(BF16)
         out[2 * half : 2 * half + 2, 4] = new[:, 4] * flags[5:6].astype(BF16)
@@ -287,6 +293,8 @@
         return lax.ppermute(x, ("frames", "rows"), chip_swap)
 
     with jax.named_scope("feature_rows"):
+        center = jnp.concatenate([fmap, context], axis=1)
+        near_center = swap_chip(center)
         far = lax.ppermute(jnp.where(row < 2, fmap[:, 2:], fmap[:, :1]), "rows", across)
         first, second = rows_swaps(
             jnp.concatenate([fmap, context[:, :1]], axis=1), jnp.concatenate([fmap, context[:, 2:]], axis=1)
@@ -295,25 +303,24 @@
         blank = jnp.zeros_like(first)
         from_above = jnp.where(row > 0, jnp.where(odd, first, second), blank)
         from_below = jnp.where(row < n_rows - 1, jnp.where(odd, second, first), blank)
-        own = jnp.concatenate(
+        halo = jnp.concatenate(
             [
                 jnp.where(row < 2, none, far),
                 from_above[:, :3],
-                fmap,
                 from_below[:, :3],
                 jnp.where(row < 2, far, none),
                 from_above[:, 3:],
-                context,
                 from_below[:, 3:],
             ],
             axis=1,
         )
-    own, pairs = lax.optimization_barrier((own, pairs))
+    halo, pairs = lax.optimization_barrier((halo, pairs))
     idx, flags = slot_table(pairs, index), row_flags(row)
     with jax.named_scope("feature_window"):
-        near = swap_chip(own)
-        own_other = swap_core(own)
-        near_other = swap_core(near)
+        near_halo = swap_chip(halo)
+        halo_other = swap_core(halo)
+        center_other = swap_core(jnp.concatenate([center, near_center]))
+        near_halo_other = swap_core(near_halo)
 
     with jax.named_scope("first_iteration"):
         sums = [jax.ShapeDtypeStruct((4, OWN, CHANS), BF16)] * 2
@@ -337,7 +344,7 @@
                 pltpu.SMEM((SLOTS,), jnp.int32),
             ],
             2_000_000_000,
-            idx, own, near, own_other, near_other, w_corr, w_zr, w_q, w_msg,
+            idx, center, near_center, center_other, halo, near_halo, halo_other, near_halo_other, w_corr, w_zr, w_q, w_msg,
         )
 
     with jax.named_scope("first_sums"):
@@ -357,7 +364,7 @@
             [jax.ShapeDtypeStruct((4, 5, WIDTH, CHANS), BF16)],
             [],
             400_000_000,
-            flags, own, near, upd, first, second, w_res,
+            flags, center, near_center, halo, near_halo, upd, first, second, w_res,
         )
         state_other = swap_core(state)
     with jax.named_scope("second_iteration"):

time: 65.8 us -> 62.9 us (0.956)
  waiting for transfers between devices: 33.5 us -> 24.4 us
  starting transfers between devices: 21.4 us -> 27.4 us
  local copies, waits for them, and re-layouts: 0.29 us -> 1.25 us
  other arithmetic: 2.36 us -> 1.58 us
    ppermute x3 -> x4, starting transfers between devices: 12 us -> 16.3 us  [swap_chip(): return lax.ppermute(x, ('frames', 'rows'), chip_swap)]
    ppermute x3, waiting for transfers between devices: 9.65 us -> 5.34 us  [rows_swaps(): first = lax.ppermute(jnp.where(odd, to_above, to_below), 'rows', even_swap)]
    ppermute x3, starting transfers between devices: 3.87 us -> 6.62 us  [rows_swaps(): second = lax.ppermute(jnp.where(odd, to_below, to_above), 'rows', odd_swap)]
    ppermute x1, starting transfers between devices: 3.27 us -> 0.82 us  [local(): lax.ppermute(jnp.where(row < 2, fmap[:, 2:], fmap[:, :1]), 'rows', across)]
    ppermute x3 -> x4, waiting for transfers between devices: 12.4 us -> 10.2 us  [swap_chip(): return lax.ppermute(x, ('frames', 'rows'), chip_swap)]
    ppermute x3, waiting for transfers between devices: 4.82 us -> 3.21 us  [rows_swaps(): second = lax.ppermute(jnp.where(odd, to_below, to_above), 'rows', odd_swap)]
    ppermute x3, starting transfers between devices: 1.8 us -> 2.61 us  [rows_swaps(): first = lax.ppermute(jnp.where(odd, to_above, to_below), 'rows', even_swap)]
    slice x1, local copies, waits for them, and re-layouts: 0.01 us -> 0.81 us  [local(): context[:, 2:]]
  transfers between devices with their start and end apart: 15 -> 17, of which waited for: 14 -> 11; matrix products, arithmetic and copies ran while one was open for 1% -> 1% of each run, Pallas kernels for 0% -> 0%
where the time goes in v6:
time: 62.9 us; the launch traced here: 62.8 us
  starting transfers between devices  27.4 us (44%)
  waiting for transfers between devices  24.4 us (39%)
  Pallas kernels  7.83 us (12%)
  other arithmetic  1.58 us (3%)
  local copies, waits for them, and re-layouts  1.25 us (2%)
    ppermute x4, starting transfers between devices, swap_chip(): return lax.ppermute(x, ('frames', 'rows'), chip_swap)  16.3 us
    ppermute x4, waiting for transfers between devices, swap_chip(): return lax.ppermute(x, ('frames', 'rows'), chip_swap)  10.2 us
    pallas_call x4, Pallas kernels, call(): pl.pallas_call(kernel, out_shape=outs, in_specs=[VM] * len(args), out_spe...  7.83 us
    ppermute x3, starting transfers between devices, rows_swaps(): second = lax.ppermute(jnp.where(odd, to_below, to_above), 'rows', odd_swap)  6.62 us
    ppermute x6, waiting for transfers between devices, swap_core(): return lax.ppermute(x, 'frames', core_swap)  5.66 us
    ppermute x3, waiting for transfers between devices, rows_swaps(): first = lax.ppermute(jnp.where(odd, to_above, to_below), 'rows', even_swap)  5.34 us
    ppermute x3, waiting for transfers between devices, rows_swaps(): second = lax.ppermute(jnp.where(odd, to_below, to_above), 'rows', odd_swap)  3.21 us
    ppermute x3, starting transfers between devices, rows_swaps(): first = lax.ppermute(jnp.where(odd, to_above, to_below), 'rows', even_swap)  2.61 us
  transfers between devices with their start and end apart: 17, of which 11 were waited for; matrix products, arithmetic and copies ran while one was open for 1% of the time, Pallas kernels for 0%

profile of v6, /device:TPU:6, one launch (start us, length us, event | category | flops | bytes accessed | tf_op | source)
XLA Modules:
  0.0 62.8 jit_solution(8681953133526002680)
XLA Ops:
  0.9 1.7 %collective-permute-start.2 = (bf16[2,4,64,128]{3,2,1,0:T(8,128)(2,1)S(1)}, bf16[2,4,64,128]{3,2,1,0:T(8,128)(2,1)S(1)}, u32[]{:S(2)}, u32[]{:S(2)}) collective-permute-start(bf16[2,4,64,128]{3,2,1,0:T(8,128)(2,1)S(1)} %get-tuple-element.34), channel_id=1, source_target_pairs={{0,1},{1,0},{2,3},{3,2},{4,5},{5,4},{6,7},{7,6},{8,9},{9,8},{10,11... | collective-permute-start | bytes 393224 | tf_op jit(solution)/shard_map/feature_rows/ppermute | solution.py:285
  2.6 2.2 %collective-permute-start.3 = (bf16[2,4,64,128]{3,2,1,0:T(8,128)(2,1)S(1)}, bf16[2,4,64,128]{3,2,1,0:T(8,128)(2,1)S(1)}, u32[]{:S(2)}, u32[]{:S(2)}) collective-permute-start(bf16[2,4,64,128]{3,2,1,0:T(8,128)(2,1)S(1)} %get-tuple-element.33), channel_id=1, source_target_pairs={{0,3},{1,2},{2,1},{3,0},{4,7},{5,6},{6,5},{7,4},{8,11},{9,10},{10,... | collective-permute-start | bytes 393224 | tf_op jit(solution)/shard_map/feature_rows/ppermute | solution.py:286
  5.7 5.1 %collective-permute-start = (bf16[2,6,64,128]{3,2,1,0:T(8,128)(2,1)S(1)}, bf16[2,6,64,128]{3,2,1,0:T(8,128)(2,1)S(1)}, u32[]{:S(2)}, u32[]{:S(2)}) collective-permute-start(bf16[2,6,64,128]{3,2,1,0:T(8,128)(2,1)S(1)} %constant_dynamic-update-slice_fusion.c0), channel_id=1, source_target_pairs={{0,1},{1,0},{2,3},{3,2},{4,8},{5,9},{6,10},{7,11},{8,4},{9,5},{10,... | collective-permute-start | bytes 589832 | tf_op jit(solution)/shard_map/feature_rows/ppermute | solution.py:293
  11.0 3.8 %collective-permute-start.4 = (bf16[2,10,64,128]{3,2,1,0:T(8,128)(2,1)S(1)}, bf16[2,10,64,128]{3,2,1,0:T(8,128)(2,1)S(1)}, u32[]{:S(2)}, u32[]{:S(2)}) collective-permute-start(bf16[2,10,64,128]{3,2,1,0:T(8,128)(2,1)S(1)} %slice_dynamic-update-slice_fusion.2.h0), channel_id=1, source_target_pairs={{0,1},{1,0},{2,3},{3,2},{4,8},{5,9},{6,10},{7,11},{8,4},{9,5},{10,... | collective-permute-start | bytes 983048 | tf_op jit(solution)/shard_map/feature_window/ppermute | solution.py:293
  15.7 4.0 %collective-permute-done.4.h1 = bf16[2,10,64,128]{3,2,1,0:T(8,128)(2,1)S(1)} collective-permute-done((bf16[2,10,64,128]{3,2,1,0:T(8,128)(2,1)S(1)}, bf16[2,10,64,128]{3,2,1,0:T(8,128)(2,1)S(1)}, u32[]{:S(2)}, u32[]{:S(2)}) %collective-permute-start.4) | collective-permute-done | bytes 327712 | tf_op jit(solution)/shard_map/feature_window/ppermute | solution.py:293
  19.9 1.4 %collective-permute-done.7.h3 = bf16[2,10,64,128]{3,2,1,0:T(8,128)(2,1)S(1)} collective-permute-done((bf16[2,10,64,128]{3,2,1,0:T(8,128)(2,1)S(1)}, bf16[2,10,64,128]{3,2,1,0:T(8,128)(2,1)S(1)}, u32[]{:S(2)}, u32[]{:S(2)}) %collective-permute-start.7) | collective-permute-done | bytes 327712 | tf_op jit(solution)/shard_map/feature_window/ppermute | solution.py:290
  21.3 4.1 %first_iteration.1 = (bf16[4,192,128]{2,1,0:T(8,128)(2,1)S(1)}, bf16[4,192,128]{2,1,0:T(8,128)(2,1)S(1)}, f32[8,192,128]{2,1,0:T(8,128)S(1)}, bf16[8,64,128]{2,1...) custom-call(s32[1,8]{1,0:T(1,128)S(1)} %add_bitcast_fusion.table, ...), custom_call_target="tpu_custom_call" | custom-call | flops 2000000000 | bytes 2896160 | tf_op jit(solution)/shard_map/first_iteration/pallas_call | solution.py:231
  25.7 1.3 %collective-permute-done.8 = bf16[4,192,128]{2,1,0:T(8,128)(2,1)S(1)} collective-permute-done((bf16[4,192,128]{2,1,0:T(8,128)(2,1)S(1)}, bf16[4,192,128]{2,1,0:T(8,128)(2,1)S(1)}, u32[]{:S(2)}, u32[]{:S(2)}) %collective-permute-start.8) | collective-permute-done | bytes 196640 | tf_op jit(solution)/shard_map/first_sums/ppermute | solution.py:290
  27.1 3.8 %collective-permute-start.9 = (bf16[4,192,128]{2,1,0:T(8,128)(2,1)S(1)}, bf16[4,192,128]{2,1,0:T(8,128)(2,1)S(1)}, u32[]{:S(2)}, u32[]{:S(2)}) collective-permute-start(bf16[4,192,128]{2,1,0:T(8,128)(2,1)S(1)} %fusion.2), channel_id=1, source_target_pairs={{0,1},{1,0},{2,3},{3,2},{4,8},{5,9},{6,10},{7,11},{8,4},{9,5},{10,... | collective-permute-start | bytes 589832 | tf_op jit(solution)/shard_map/first_sums/ppermute | solution.py:293
  30.9 3.5 %collective-permute-done.9 = bf16[4,192,128]{2,1,0:T(8,128)(2,1)S(1)} collective-permute-done((bf16[4,192,128]{2,1,0:T(8,128)(2,1)S(1)}, bf16[4,192,128]{2,1,0:T(8,128)(2,1)S(1)}, u32[]{:S(2)}, u32[]{:S(2)}) %collective-permute-start.9) | collective-permute-done | bytes 196640 | tf_op jit(solution)/shard_map/first_sums/ppermute | solution.py:293
  34.5 0.9 %broadcast_select_fusion = (bf16[16,64,128]{2,1,0:T(8,128)(2,1)}, bf16[16,64,128]{2,1,0:T(8,128)(2,1)}) fusion(pred[]{:T(512)S(6)} %eq.81, bf16[8,64,128]{2,1,0:T(8,128)(2,1)S(1)} %get-tuple-element.20, bf16[8,64,128]{2,1,0:T(8,128)(2,1)S(1)} %bitcast.12, bf16[8,64,128]{2,1,0:T(8,128)(2,1)S(1)} %get-tuple-element.19, bf16[8,64,128]{2,1,0:T(8,128)(2,1)S(1)} %bitcast.11), kind=kLoop, calls=%fused_computation.12 | loop fusion | flops 524288 | bytes 1048577 | tf_op jit(solution)/shard_map/update_rows/jit(_where)/select_n | solution.py:286
  35.4 0.9 %collective-permute-start.10 = (bf16[16,64,128]{2,1,0:T(8,128)(2,1)}, bf16[16,64,128]{2,1,0:T(8,128)(2,1)S(1)}, u32[]{:S(2)}, u32[]{:S(2)}) collective-permute-start(bf16[16,64,128]{2,1,0:T(8,128)(2,1)} %get-tuple-element.26), channel_id=1, source_target_pairs={{0,1},{1,0},{2,3},{3,2},{4,5},{5,4},{6,7},{7,6},{8,9},{9,8},{10,11... | collective-permute-start | bytes 786440 | tf_op jit(solution)/shard_map/update_rows/ppermute | solution.py:285
  36.3 2.2 %collective-permute-start.11 = (bf16[16,64,128]{2,1,0:T(8,128)(2,1)}, bf16[16,64,128]{2,1,0:T(8,128)(2,1)S(1)}, u32[]{:S(2)}, u32[]{:S(2)}) collective-permute-start(bf16[16,64,128]{2,1,0:T(8,128)(2,1)} %get-tuple-element.25), channel_id=1, source_target_pairs={{0,3},{1,2},{2,1},{3,0},{4,7},{5,6},{6,5},{7,4},{8,11},{9,10},{10,... | collective-permute-start | bytes 786440 | tf_op jit(solution)/shard_map/update_rows/ppermute | solution.py:286
  38.5 3.7 %collective-permute-done.10.first = bf16[16,64,128]{2,1,0:T(8,128)(2,1)S(1)} collective-permute-done((bf16[16,64,128]{2,1,0:T(8,128)(2,1)}, bf16[16,64,128]{2,1,0:T(8,128)(2,1)S(1)}, u32[]{:S(2)}, u32[]{:S(2)}) %collective-permute-start.10) | collective-permute-done | bytes 262176 | tf_op jit(solution)/shard_map/update_rows/ppermute | solution.py:285
  42.2 1.9 %collective-permute-done.11.second = bf16[16,64,128]{2,1,0:T(8,128)(2,1)S(1)} collective-permute-done((bf16[16,64,128]{2,1,0:T(8,128)(2,1)}, bf16[16,64,128]{2,1,0:T(8,128)(2,1)S(1)}, u32[]{:S(2)}, u32[]{:S(2)}) %collective-permute-start.11) | collective-permute-done | bytes 262176 | tf_op jit(solution)/shard_map/update_rows/ppermute | solution.py:286
  45.0 1.6 %collective-permute-done.12.s1 = bf16[4,5,64,128]{3,2,1,0:T(8,128)(2,1)S(1)} collective-permute-done((bf16[4,5,64,128]{3,2,1,0:T(8,128)(2,1)S(1)}, bf16[4,5,64,128]{3,2,1,0:T(8,128)(2,1)S(1)}, u32[]{:S(2)}, u32[]{:S(2)}) %collective-permute-start.12) | collective-permute-done | bytes 327712 | tf_op jit(solution)/shard_map/first_state/ppermute | solution.py:290
  46.6 2.0 %second_iteration.1 = (bf16[4,192,128]{2,1,0:T(8,128)(2,1)S(1)}, bf16[4,192,128]{2,1,0:T(8,128)(2,1)S(1)}) custom-call(s32[1,8]{1,0:T(1,128)S(1)} %add_bitcast_fusion.table, f32[8,128]{1,0:T(8,128)S(1)} %iota.34.flags, bf16[4,5,64,128]{3,2,1,0:T(8,128)(2,1)S(1)} %first_state.1.s0.state, bf16[4,5,64,128]{3,2,1,0:T(8,128)(2,1)S(1)} %collective-permute-done.12.s1, ...), custom_call_target="tpu_custom_call" | custom-call | flops 1500000000 | bytes 3412000 | tf_op jit(solution)/shard_map/second_iteration/pallas_call | solution.py:231
  48.8 1.3 %collective-permute-done.13 = bf16[4,192,128]{2,1,0:T(8,128)(2,1)S(1)} collective-permute-done((bf16[4,192,128]{2,1,0:T(8,128)(2,1)S(1)}, bf16[4,192,128]{2,1,0:T(8,128)(2,1)S(1)}, u32[]{:S(2)}, u32[]{:S(2)}) %collective-permute-start.13) | collective-permute-done | bytes 196640 | tf_op jit(solution)/shard_map/second_sums/ppermute | solution.py:290
  50.2 3.6 %collective-permute-start.14 = (bf16[2,192,128]{2,1,0:T(8,128)(2,1)S(1)}, bf16[2,192,128]{2,1,0:T(8,128)(2,1)S(1)}, u32[]{:S(2)}, u32[]{:S(2)}) collective-permute-start(bf16[2,192,128]{2,1,0:T(8,128)(2,1)S(1)} %slice.108), channel_id=1, source_target_pairs={{0,1},{1,0},{2,3},{3,2},{4,8},{5,9},{6,10},{7,11},{8,4},{9,5},{10,... | collective-permute-start | bytes 294920 | tf_op jit(solution)/shard_map/second_sums/ppermute | solution.py:293
  53.8 2.7 %collective-permute-done.14 = bf16[2,192,128]{2,1,0:T(8,128)(2,1)S(1)} collective-permute-done((bf16[2,192,128]{2,1,0:T(8,128)(2,1)S(1)}, bf16[2,192,128]{2,1,0:T(8,128)(2,1)S(1)}, u32[]{:S(2)}, u32[]{:S(2)}) %collective-permute-start.14) | collective-permute-done | bytes 98336 | tf_op jit(solution)/shard_map/second_sums/ppermute | solution.py:293
  56.6 2.3 %collective-permute-start.16 = (bf16[2,1,64,128]{3,2,1,0:T(8,128)(2,1)S(1)}, bf16[2,1,64,128]{3,2,1,0:T(8,128)(2,1)S(1)}, u32[]{:S(2)}, u32[]{:S(2)}) collective-permute-start(bf16[2,1,64,128]{3,2,1,0:T(8,128)(2,1)S(1)} %get-tuple-element.35), channel_id=1, source_target_pairs={{0,3},{1,2},{2,1},{3,0},{4,7},{5,6},{6,5},{7,4},{8,11},{9,10},{10,... | collective-permute-start | bytes 98312 | tf_op jit(solution)/shard_map/second_sums/ppermute | solution.py:286
  58.9 1.6 %collective-permute-done.15.first = bf16[2,1,64,128]{3,2,1,0:T(8,128)(2,1)S(1)} collective-permute-done((bf16[2,1,64,128]{3,2,1,0:T(8,128)(2,1)S(1)}, bf16[2,1,64,128]{3,2,1,0:T(8,128)(2,1)S(1)}, u32[]{:S(2)}, u32[]{:S(2)}) %collective-permute-start.15) | collective-permute-done | bytes 32800 | tf_op jit(solution)/shard_map/second_sums/ppermute | solution.py:285
  60.5 1.3 %collective-permute-done.16.second = bf16[2,1,64,128]{3,2,1,0:T(8,128)(2,1)S(1)} collective-permute-done((bf16[2,1,64,128]{3,2,1,0:T(8,128)(2,1)S(1)}, bf16[2,1,64,128]{3,2,1,0:T(8,128)(2,1)S(1)}, u32[]{:S(2)}, u32[]{:S(2)}) %collective-permute-start.16) | collective-permute-done | bytes 32800 | tf_op jit(solution)/shard_map/second_sums/ppermute | solution.py:286
  61.8 1.0 %last_state.1 = bf16[2,3,64,128]{3,2,1,0:T(8,128)(2,1)} custom-call(f32[8,128]{1,0:T(8,128)S(1)} %iota.34.flags, bf16[4,5,64,128]{3,2,1,0:T(8,128)(2,1)S(1)} %first_state.1.s0.state, bf16[2,3,64,128]{3,2,1,0:T(8,128)(2,1)S(1)} %bitcast.10, bf16[2,1,64,128]{3,2,1,0:T(8,128)(2,1)S(1)} %collective-permute-done.15.first, ...), custom_call_target="tpu_custom_call" | custom-call | flops 120000000 | bytes 790528 | tf_op jit(solution)/shard_map/last_state/pallas_call | solution.py:231
  (64 shorter events, 4.8 us)
Async XLA Ops:
  0.9 9.9 %collective-permute-start.2 = (bf16[2,4,64,128]{3,2,1,0:T(8,128)(2,1)S(1)}, bf16[2,4,64,128]{3,2,1,0:T(8,128)(2,1)S(1)}, u32[]{:S(2)}, u32[]{:S(2)}) collective-permute-start(bf16[2,4,64,128]{3,2,1,0:T(8,128)(2,1)S(1)} %get-tuple-element.34), channel_id=1, source_target_pairs={{0,1},{1,0},{2,3},{3,2},{4,5},{5,4},{6,7},{7,6},{8,9},{9,8},{10,11... | collective-permute-start | bytes 393224 | tf_op jit(solution)/shard_map/feature_rows/ppermute | solution.py:285
  2.6 8.2 %collective-permute-start.3 = (bf16[2,4,64,128]{3,2,1,0:T(8,128)(2,1)S(1)}, bf16[2,4,64,128]{3,2,1,0:T(8,128)(2,1)S(1)}, u32[]{:S(2)}, u32[]{:S(2)}) collective-permute-start(bf16[2,4,64,128]{3,2,1,0:T(8,128)(2,1)S(1)} %get-tuple-element.33), channel_id=1, source_target_pairs={{0,3},{1,2},{2,1},{3,0},{4,7},{5,6},{6,5},{7,4},{8,11},{9,10},{10,... | collective-permute-start | bytes 393224 | tf_op jit(solution)/shard_map/feature_rows/ppermute | solution.py:286
  4.8 6.0 %collective-permute-start.1 = (bf16[2,1,64,128]{3,2,1,0:T(8,128)(2,1)S(1)}, bf16[2,1,64,128]{3,2,1,0:T(8,128)(2,1)S(1)}, u32[]{:S(2)}, u32[]{:S(2)}) collective-permute-start(bf16[2,1,64,128]{3,2,1,0:T(8,128)(2,1)S(1)} %slice_select_fusion), channel_id=1, source_target_pairs={{0,2},{1,3},{2,0},{3,1},{4,6},{5,7},{6,4},{7,5},{8,10},{9,11},{10,... | collective-permute-start | bytes 98312 | tf_op jit(solution)/shard_map/feature_rows/ppermute | solution.py:298
  5.7 9.2 %collective-permute-start = (bf16[2,6,64,128]{3,2,1,0:T(8,128)(2,1)S(1)}, bf16[2,6,64,128]{3,2,1,0:T(8,128)(2,1)S(1)}, u32[]{:S(2)}, u32[]{:S(2)}) collective-permute-start(bf16[2,6,64,128]{3,2,1,0:T(8,128)(2,1)S(1)} %constant_dynamic-update-slice_fusion.c0), channel_id=1, source_target_pairs={{0,1},{1,0},{2,3},{3,2},{4,8},{5,9},{6,10},{7,11},{8,4},{9,5},{10,... | collective-permute-start | bytes 589832 | tf_op jit(solution)/shard_map/feature_rows/ppermute | solution.py:293
  10.9 4.0 %copy-start.9 = (s32[256,3]{0,1:T(4,128)S(1)}, s32[256,3]{0,1:T(4,128)}, u32[]{:S(2)}) copy-start(s32[256,3]{0,1:T(4,128)} %param.10) | copy-start | bytes 9220
  10.9 10.4 %copy-start.1 = (bf16[9,256,128]{2,1,0:T(8,128)(2,1)S(1)}, bf16[9,256,128]{2,1,0:T(8,128)(2,1)}, u32[]{:S(2)}) copy-start(bf16[9,256,128]{2,1,0:T(8,128)(2,1)} %w_q.3) | copy-start | bytes 1769476
  11.0 8.7 %collective-permute-start.4 = (bf16[2,10,64,128]{3,2,1,0:T(8,128)(2,1)S(1)}, bf16[2,10,64,128]{3,2,1,0:T(8,128)(2,1)S(1)}, u32[]{:S(2)}, u32[]{:S(2)}) collective-permute-start(bf16[2,10,64,128]{3,2,1,0:T(8,128)(2,1)S(1)} %slice_dynamic-update-slice_fusion.2.h0), channel_id=1, source_target_pairs={{0,1},{1,0},{2,3},{3,2},{4,8},{5,9},{6,10},{7,11},{8,4},{9,5},{10,... | collective-permute-start | bytes 983048 | tf_op jit(solution)/shard_map/feature_window/ppermute | solution.py:293
  14.8 5.1 %collective-permute-start.6 = (bf16[2,10,64,128]{3,2,1,0:T(8,128)(2,1)S(1)}, bf16[2,10,64,128]{3,2,1,0:T(8,128)(2,1)S(1)}, u32[]{:S(2)}, u32[]{:S(2)}) collective-permute-start(bf16[2,10,64,128]{3,2,1,0:T(8,128)(2,1)S(1)} %slice_dynamic-update-slice_fusion.2.h0), channel_id=1, source_target_pairs={{0,4},{4,0},{8,12},{12,8},{16,20},{20,16},{24,28},{28,24},{32,36},... | collective-permute-start | bytes 983048 | tf_op jit(solution)/shard_map/feature_window/ppermute | solution.py:290
  14.9 6.5 %copy-start.2 = (bf16[256,256]{1,0:T(8,128)(2,1)S(1)}, bf16[256,256]{1,0:T(8,128)(2,1)}, u32[]{:S(2)}) copy-start(bf16[256,256]{1,0:T(8,128)(2,1)} %w_zr.3) | copy-start | bytes 393220
  14.9 6.5 %copy-start.3 = (bf16[128,256]{1,0:T(8,128)(2,1)S(1)}, bf16[128,256]{1,0:T(8,128)(2,1)}, u32[]{:S(2)}) copy-start(bf16[128,256]{1,0:T(8,128)(2,1)} %w_msg.3) | copy-start | bytes 196612
  14.9 6.4 %copy-start.4 = (bf16[49,128]{1,0:T(8,128)(2,1)S(1)}, bf16[49,128]{1,0:T(8,128)(2,1)}, u32[]{:S(2)}) copy-start(bf16[49,128]{1,0:T(8,128)(2,1)} %w_corr.1) | copy-start | bytes 37636
  15.0 4.9 %collective-permute-start.5 = (bf16[4,6,64,128]{3,2,1,0:T(8,128)(2,1)S(1)}, bf16[4,6,64,128]{3,2,1,0:T(8,128)(2,1)S(1)}, u32[]{:S(2)}, u32[]{:S(2)}) collective-permute-start(bf16[4,6,64,128]{3,2,1,0:T(8,128)(2,1)S(1)} %pad_maximum_fusion), channel_id=1, source_target_pairs={{0,4},{4,0},{8,12},{12,8},{16,20},{20,16},{24,28},{28,24},{32,36},... | collective-permute-start | bytes 1179656 | tf_op jit(solution)/shard_map/feature_window/ppermute | solution.py:290
  19.7 1.6 %collective-permute-start.7 = (bf16[2,10,64,128]{3,2,1,0:T(8,128)(2,1)S(1)}, bf16[2,10,64,128]{3,2,1,0:T(8,128)(2,1)S(1)}, u32[]{:S(2)}, u32[]{:S(2)}) collective-permute-start(bf16[2,10,64,128]{3,2,1,0:T(8,128)(2,1)S(1)} %collective-permute-done.4.h1), channel_id=1, source_target_pairs={{0,4},{4,0},{8,12},{12,8},{16,20},{20,16},{24,28},{28,24},{32,36},... | collective-permute-start | bytes 983048 | tf_op jit(solution)/shard_map/feature_window/ppermute | solution.py:290
  25.5 9.0 %copy-start.5 = (f32[8,192,128]{2,1,0:T(8,128)}, f32[8,192,128]{2,1,0:T(8,128)S(1)}, u32[]{:S(2)}) copy-start(f32[8,192,128]{2,1,0:T(8,128)S(1)} %get-tuple-element.22.hid) | copy-start | bytes 2359300
  25.5 1.5 %collective-permute-start.8 = (bf16[4,192,128]{2,1,0:T(8,128)(2,1)S(1)}, bf16[4,192,128]{2,1,0:T(8,128)(2,1)S(1)}, u32[]{:S(2)}, u32[]{:S(2)}) collective-permute-start(bf16[4,192,128]{2,1,0:T(8,128)(2,1)S(1)} %get-tuple-element.18), channel_id=1, source_target_pairs={{0,4},{4,0},{8,12},{12,8},{16,20},{20,16},{24,28},{28,24},{32,36},... | collective-permute-start | bytes 589832 | tf_op jit(solution)/shard_map/first_sums/ppermute | solution.py:290
  27.1 7.3 %collective-permute-start.9 = (bf16[4,192,128]{2,1,0:T(8,128)(2,1)S(1)}, bf16[4,192,128]{2,1,0:T(8,128)(2,1)S(1)}, u32[]{:S(2)}, u32[]{:S(2)}) collective-permute-start(bf16[4,192,128]{2,1,0:T(8,128)(2,1)S(1)} %fusion.2), channel_id=1, source_target_pairs={{0,1},{1,0},{2,3},{3,2},{4,8},{5,9},{6,10},{7,11},{8,4},{9,5},{10,... | collective-permute-start | bytes 589832 | tf_op jit(solution)/shard_map/first_sums/ppermute | solution.py:293
  34.5 9.6 %copy-start = (bf16[9,128,128]{2,1,0:T(8,128)(2,1)S(1)}, bf16[9,128,128]{2,1,0:T(8,128)(2,1)}, u32[]{:S(2)}) copy-start(bf16[9,128,128]{2,1,0:T(8,128)(2,1)} %w_res.3) | copy-start | bytes 884740
  35.4 6.7 %collective-permute-start.10 = (bf16[16,64,128]{2,1,0:T(8,128)(2,1)}, bf16[16,64,128]{2,1,0:T(8,128)(2,1)S(1)}, u32[]{:S(2)}, u32[]{:S(2)}) collective-permute-start(bf16[16,64,128]{2,1,0:T(8,128)(2,1)} %get-tuple-element.26), channel_id=1, source_target_pairs={{0,1},{1,0},{2,3},{3,2},{4,5},{5,4},{6,7},{7,6},{8,9},{9,8},{10,11... | collective-permute-start | bytes 786440 | tf_op jit(solution)/shard_map/update_rows/ppermute | solution.py:285
  36.3 7.8 %collective-permute-start.11 = (bf16[16,64,128]{2,1,0:T(8,128)(2,1)}, bf16[16,64,128]{2,1,0:T(8,128)(2,1)S(1)}, u32[]{:S(2)}, u32[]{:S(2)}) collective-permute-start(bf16[16,64,128]{2,1,0:T(8,128)(2,1)} %get-tuple-element.25), channel_id=1, source_target_pairs={{0,3},{1,2},{2,1},{3,0},{4,7},{5,6},{6,5},{7,4},{8,11},{9,10},{10,... | collective-permute-start | bytes 786440 | tf_op jit(solution)/shard_map/update_rows/ppermute | solution.py:286
  44.9 1.7 %collective-permute-start.12 = (bf16[4,5,64,128]{3,2,1,0:T(8,128)(2,1)S(1)}, bf16[4,5,64,128]{3,2,1,0:T(8,128)(2,1)S(1)}, u32[]{:S(2)}, u32[]{:S(2)}) collective-permute-start(bf16[4,5,64,128]{3,2,1,0:T(8,128)(2,1)S(1)} %first_state.1.s0.state), channel_id=1, source_target_pairs={{0,4},{4,0},{8,12},{12,8},{16,20},{20,16},{24,28},{28,24},{32,36},... | collective-permute-start | bytes 983048 | tf_op jit(solution)/shard_map/first_state/ppermute | solution.py:290
  48.6 1.5 %collective-permute-start.13 = (bf16[4,192,128]{2,1,0:T(8,128)(2,1)S(1)}, bf16[4,192,128]{2,1,0:T(8,128)(2,1)S(1)}, u32[]{:S(2)}, u32[]{:S(2)}) collective-permute-start(bf16[4,192,128]{2,1,0:T(8,128)(2,1)S(1)} %get-tuple-element.24), channel_id=1, source_target_pairs={{0,4},{4,0},{8,12},{12,8},{16,20},{20,16},{24,28},{28,24},{32,36},... | collective-permute-start | bytes 589832 | tf_op jit(solution)/shard_map/second_sums/ppermute | solution.py:290
  50.2 6.2 %collective-permute-start.14 = (bf16[2,192,128]{2,1,0:T(8,128)(2,1)S(1)}, bf16[2,192,128]{2,1,0:T(8,128)(2,1)S(1)}, u32[]{:S(2)}, u32[]{:S(2)}) collective-permute-start(bf16[2,192,128]{2,1,0:T(8,128)(2,1)S(1)} %slice.108), channel_id=1, source_target_pairs={{0,1},{1,0},{2,3},{3,2},{4,8},{5,9},{6,10},{7,11},{8,4},{9,5},{10,... | collective-permute-start | bytes 294920 | tf_op jit(solution)/shard_map/second_sums/ppermute | solution.py:293
  56.5 4.0 %collective-permute-start.15 = (bf16[2,1,64,128]{3,2,1,0:T(8,128)(2,1)S(1)}, bf16[2,1,64,128]{3,2,1,0:T(8,128)(2,1)S(1)}, u32[]{:S(2)}, u32[]{:S(2)}) collective-permute-start(bf16[2,1,64,128]{3,2,1,0:T(8,128)(2,1)S(1)} %get-tuple-element.36), channel_id=1, source_target_pairs={{0,1},{1,0},{2,3},{3,2},{4,5},{5,4},{6,7},{7,6},{8,9},{9,8},{10,11... | collective-permute-start | bytes 98312 | tf_op jit(solution)/shard_map/second_sums/ppermute | solution.py:285
  56.6 5.2 %collective-permute-start.16 = (bf16[2,1,64,128]{3,2,1,0:T(8,128)(2,1)S(1)}, bf16[2,1,64,128]{3,2,1,0:T(8,128)(2,1)S(1)}, u32[]{:S(2)}, u32[]{:S(2)}) collective-permute-start(bf16[2,1,64,128]{3,2,1,0:T(8,128)(2,1)S(1)} %get-tuple-element.35), channel_id=1, source_target_pairs={{0,3},{1,2},{2,1},{3,0},{4,7},{5,6},{6,5},{7,4},{8,11},{9,10},{10,... | collective-permute-start | bytes 98312 | tf_op jit(solution)/shard_map/second_sums/ppermute | solution.py:286
  (3 other events, 4.3 us)

commit v7 on v6

--- a/solution.py
+++ b/solution.py
@@ -85,12 +85,15 @@
 
 def first_kernel(
     table, c0, c1, c23, h0, h1, h2, h3, w_corr, w_zr, w_q, w_msg,
-    part, part_other, hid, hid_first, hid_last, motion_out,
+    part, part_other, hid, hid_first, hid_last, motion_out, base,
     feat, rim, ctx, acc, flip, spread, edge, idx,
 ):
     pieces = ((c0, 0, h0), (c1, 0, h1), (c23, 0, h2), (c23, 2, h3))
     count = read_table(table, idx)
     acc[...] = jnp.zeros_like(acc)
+    for half, (center, _, halo) in enumerate(pieces[:2]):
+        frames = pl.ds(2 * half, 2)
+        base[frames, 0], base[frames, 1:4], base[frames, 4] = halo[:, 8], center[:, 3:6], halo[:, 9]
     ends = [lax.broadcasted_iota(jnp.int32, (WIDTH, WIDTH), k) for k in range(2)]
     flip[...] = jnp.where(ends[0] + ends[1] == WIDTH - 1, 1.0, 0.0).astype(BF16)
     lane, tap = [lax.broadcasted_iota(jnp.int32, (CHANS, SPAN * SPAN), k) for k in range(2)]
@@ -199,16 +202,15 @@
     return first * weight[0] + second * weight[1], first * weight[2] + second * weight[3]
 
 
-def state_kernel(flags, c0, c1, h0, h1, upd, first, second, w_res, out):
-    for half, (center, halo) in enumerate(((c0, h0), (c1, h1))):
+def state_kernel(flags, base, upd, first, second, w_res, out):
+    for half in range(2):
         fields = []
         for frame in (2 * half, 2 * half + 1):
             rows = pl.ds(2 * frame, 2)
             above, below = arrived(flags, first[rows].reshape(2 * WIDTH, CHANS), second[rows].reshape(2 * WIDTH, CHANS))
             fields.append(jnp.concatenate([above, upd[frame].reshape(OWN, CHANS), below]))
         new = conv_rows(fields, side_by_side(w_res), 5).reshape(2, 5, WIDTH, CHANS)
-        base = jnp.concatenate([halo[:, 8:9], center[:, 3:6], halo[:, 9:10]], axis=1)
-        new = (base.astype(F32) + new).astype(BF16)
+        new = (base[2 * half : 2 * half + 2].astype(F32) + new).astype(BF16)
         out[2 * half : 2 * half + 2, 1:4] = new[:, 1:4]
         out[2 * half : 2 * half + 2, 0] = new[:, 0] * flags[4:5].astype(BF16)
         out[2 * half : 2 * half + 2, 4] = new[:, 4] * flags[5:6].astype(BF16)
@@ -325,13 +327,14 @@
     with jax.named_scope("first_iteration"):
         sums = [jax.ShapeDtypeStruct((4, OWN, CHANS), BF16)] * 2
         edge_rows = [jax.ShapeDtypeStruct((SLOTS, WIDTH, CHANS), BF16)] * 2
-        part, part_other, hid, hid_first, hid_last, motion = call(
+        part, part_other, hid, hid_first, hid_last, motion, base = call(
             first_kernel,
             [
                 *sums,
                 jax.ShapeDtypeStruct((SLOTS, OWN, CHANS), F32),
                 *edge_rows,
                 jax.ShapeDtypeStruct((SLOTS, WIDE, CHANS), BF16),
+                jax.ShapeDtypeStruct((4, 5, WIDTH, CHANS), BF16),
             ],
             [
                 pltpu.VMEM((2, 5, WIDTH, CHANS), BF16),
@@ -364,7 +367,7 @@
             [jax.ShapeDtypeStruct((4, 5, WIDTH, CHANS), BF16)],
             [],
             400_000_000,
-            flags, center, near_center, halo, near_halo, upd, first, second, w_res,
+            flags, base, upd, first, second, w_res,
         )
         state_other = swap_core(state)
     with jax.named_scope("second_iteration"):

time: 62.9 us -> 62 us (0.986)
  other arithmetic: 1.58 us -> 0.76 us
    select_n x3, other arithmetic: 0.9 us -> 0.08 us  [rows_swaps(): second = lax.ppermute(jnp.where(odd, to_below, to_above), 'rows', odd_swap)]
where the time goes in v7:
time: 62 us; the launch traced here: 61.9 us
  starting transfers between devices  27.6 us (45%)
  waiting for transfers between devices  24.2 us (39%)
  Pallas kernels  7.84 us (13%)
  local copies, waits for them, and re-layouts  1.25 us (2%)
  other arithmetic  0.76 us (1%)
    ppermute x4, starting transfers between devices, swap_chip(): return lax.ppermute(x, ('frames', 'rows'), chip_swap)  16.3 us
    ppermute x4, waiting for transfers between devices, swap_chip(): return lax.ppermute(x, ('frames', 'rows'), chip_swap)  10.2 us
    pallas_call x4, Pallas kernels, call(): pl.pallas_call(kernel, out_shape=outs, in_specs=[VM] * len(args), out_spe...  7.84 us
    ppermute x3, starting transfers between devices, rows_swaps(): second = lax.ppermute(jnp.where(odd, to_below, to_above), 'rows', odd_swap)  6.63 us
    ppermute x6, waiting for transfers between devices, swap_core(): return lax.ppermute(x, 'frames', core_swap)  5.65 us
    ppermute x3, waiting for transfers between devices, rows_swaps(): first = lax.ppermute(jnp.where(odd, to_above, to_below), 'rows', even_swap)  5.12 us
    ppermute x3, waiting for transfers between devices, rows_swaps(): second = lax.ppermute(jnp.where(odd, to_below, to_above), 'rows', odd_swap)  3.21 us
    ppermute x3, starting transfers between devices, rows_swaps(): first = lax.ppermute(jnp.where(odd, to_above, to_below), 'rows', even_swap)  2.7 us
  transfers between devices with their start and end apart: 17, of which 11 were waited for; matrix products, arithmetic and copies ran while one was open for 1% of the time, Pallas kernels for 0%

profile of v7, /device:TPU:6, one launch (start us, length us, event | category | flops | bytes accessed | tf_op | source)
XLA Modules:
  0.0 61.9 jit_solution(8702816075854569563)
XLA Ops:
  0.9 1.7 %collective-permute-start.1 = (bf16[2,4,64,128]{3,2,1,0:T(8,128)(2,1)S(1)}, bf16[2,4,64,128]{3,2,1,0:T(8,128)(2,1)S(1)}, u32[]{:S(2)}, u32[]{:S(2)}) collective-permute-start(bf16[2,4,64,128]{3,2,1,0:T(8,128)(2,1)S(1)} %get-tuple-element.36), channel_id=1, source_target_pairs={{0,1},{1,0},{2,3},{3,2},{4,5},{5,4},{6,7},{7,6},{8,9},{9,8},{10,11... | collective-permute-start | bytes 393224 | tf_op jit(solution)/shard_map/feature_rows/ppermute | solution.py:287
  2.6 2.2 %collective-permute-start.2 = (bf16[2,4,64,128]{3,2,1,0:T(8,128)(2,1)S(1)}, bf16[2,4,64,128]{3,2,1,0:T(8,128)(2,1)S(1)}, u32[]{:S(2)}, u32[]{:S(2)}) collective-permute-start(bf16[2,4,64,128]{3,2,1,0:T(8,128)(2,1)S(1)} %get-tuple-element.35), channel_id=1, source_target_pairs={{0,3},{1,2},{2,1},{3,0},{4,7},{5,6},{6,5},{7,4},{8,11},{9,10},{10,... | collective-permute-start | bytes 393224 | tf_op jit(solution)/shard_map/feature_rows/ppermute | solution.py:288
  4.8 0.8 %collective-permute-start = (bf16[2,1,64,128]{3,2,1,0:T(8,128)(2,1)S(1)}, bf16[2,1,64,128]{3,2,1,0:T(8,128)(2,1)S(1)}, u32[]{:S(2)}, u32[]{:S(2)}) collective-permute-start(bf16[2,1,64,128]{3,2,1,0:T(8,128)(2,1)S(1)} %slice_select_fusion), channel_id=1, source_target_pairs={{0,2},{1,3},{2,0},{3,1},{4,6},{5,7},{6,4},{7,5},{8,10},{9,11},{10,... | collective-permute-start | bytes 98312 | tf_op jit(solution)/shard_map/feature_rows/ppermute | solution.py:300
  5.7 5.1 %collective-permute-start.3 = (bf16[2,6,64,128]{3,2,1,0:T(8,128)(2,1)S(1)}, bf16[2,6,64,128]{3,2,1,0:T(8,128)(2,1)S(1)}, u32[]{:S(2)}, u32[]{:S(2)}) collective-permute-start(bf16[2,6,64,128]{3,2,1,0:T(8,128)(2,1)S(1)} %constant_dynamic-update-slice_fusion.c0), channel_id=1, source_target_pairs={{0,1},{1,0},{2,3},{3,2},{4,8},{5,9},{6,10},{7,11},{8,4},{9,5},{10,... | collective-permute-start | bytes 589832 | tf_op jit(solution)/shard_map/feature_rows/ppermute | solution.py:295
  11.0 3.8 %collective-permute-start.5 = (bf16[2,10,64,128]{3,2,1,0:T(8,128)(2,1)S(1)}, bf16[2,10,64,128]{3,2,1,0:T(8,128)(2,1)S(1)}, u32[]{:S(2)}, u32[]{:S(2)}) collective-permute-start(bf16[2,10,64,128]{3,2,1,0:T(8,128)(2,1)S(1)} %slice_dynamic-update-slice_fusion.2.h0), channel_id=1, source_target_pairs={{0,1},{1,0},{2,3},{3,2},{4,8},{5,9},{6,10},{7,11},{8,4},{9,5},{10,... | collective-permute-start | bytes 983048 | tf_op jit(solution)/shard_map/feature_window/ppermute | solution.py:295
  15.7 4.0 %collective-permute-done.5.h1 = bf16[2,10,64,128]{3,2,1,0:T(8,128)(2,1)S(1)} collective-permute-done((bf16[2,10,64,128]{3,2,1,0:T(8,128)(2,1)S(1)}, bf16[2,10,64,128]{3,2,1,0:T(8,128)(2,1)S(1)}, u32[]{:S(2)}, u32[]{:S(2)}) %collective-permute-start.5) | collective-permute-done | bytes 327712 | tf_op jit(solution)/shard_map/feature_window/ppermute | solution.py:295
  19.9 1.4 %collective-permute-done.7.h3 = bf16[2,10,64,128]{3,2,1,0:T(8,128)(2,1)S(1)} collective-permute-done((bf16[2,10,64,128]{3,2,1,0:T(8,128)(2,1)S(1)}, bf16[2,10,64,128]{3,2,1,0:T(8,128)(2,1)S(1)}, u32[]{:S(2)}, u32[]{:S(2)}) %collective-permute-start.7) | collective-permute-done | bytes 327712 | tf_op jit(solution)/shard_map/feature_window/ppermute | solution.py:292
  21.3 4.1 %first_iteration.1 = (bf16[4,192,128]{2,1,0:T(8,128)(2,1)S(1)}, bf16[4,192,128]{2,1,0:T(8,128)(2,1)S(1)}, f32[8,192,128]{2,1,0:T(8,128)S(1)}, bf16[8,64,128]{2,1...) custom-call(s32[1,8]{1,0:T(1,128)S(1)} %add_bitcast_fusion.table, ...), custom_call_target="tpu_custom_call" | custom-call | flops 2000000000 | bytes 2896160 | tf_op jit(solution)/shard_map/first_iteration/pallas_call | solution.py:233
  25.7 1.3 %collective-permute-done.8 = bf16[4,192,128]{2,1,0:T(8,128)(2,1)S(1)} collective-permute-done((bf16[4,192,128]{2,1,0:T(8,128)(2,1)S(1)}, bf16[4,192,128]{2,1,0:T(8,128)(2,1)S(1)}, u32[]{:S(2)}, u32[]{:S(2)}) %collective-permute-start.8) | collective-permute-done | bytes 196640 | tf_op jit(solution)/shard_map/first_sums/ppermute | solution.py:292
  27.1 3.8 %collective-permute-start.9 = (bf16[4,192,128]{2,1,0:T(8,128)(2,1)S(1)}, bf16[4,192,128]{2,1,0:T(8,128)(2,1)S(1)}, u32[]{:S(2)}, u32[]{:S(2)}) collective-permute-start(bf16[4,192,128]{2,1,0:T(8,128)(2,1)S(1)} %fusion.2), channel_id=1, source_target_pairs={{0,1},{1,0},{2,3},{3,2},{4,8},{5,9},{6,10},{7,11},{8,4},{9,5},{10,... | collective-permute-start | bytes 589832 | tf_op jit(solution)/shard_map/first_sums/ppermute | solution.py:295
  30.9 3.5 %collective-permute-done.9 = bf16[4,192,128]{2,1,0:T(8,128)(2,1)S(1)} collective-permute-done((bf16[4,192,128]{2,1,0:T(8,128)(2,1)S(1)}, bf16[4,192,128]{2,1,0:T(8,128)(2,1)S(1)}, u32[]{:S(2)}, u32[]{:S(2)}) %collective-permute-start.9) | collective-permute-done | bytes 196640 | tf_op jit(solution)/shard_map/first_sums/ppermute | solution.py:295
  34.6 0.9 %collective-permute-start.10 = (bf16[16,64,128]{2,1,0:T(8,128)(2,1)S(1)}, bf16[16,64,128]{2,1,0:T(8,128)(2,1)S(1)}, u32[]{:S(2)}, u32[]{:S(2)}) collective-permute-start(bf16[16,64,128]{2,1,0:T(8,128)(2,1)S(1)} %get-tuple-element.28), channel_id=1, source_target_pairs={{0,1},{1,0},{2,3},{3,2},{4,5},{5,4},{6,7},{7,6},{8,9},{9,8},{10,11... | collective-permute-start | bytes 786440 | tf_op jit(solution)/shard_map/update_rows/ppermute | solution.py:287
  35.5 2.2 %collective-permute-start.11 = (bf16[16,64,128]{2,1,0:T(8,128)(2,1)S(1)}, bf16[16,64,128]{2,1,0:T(8,128)(2,1)S(1)}, u32[]{:S(2)}, u32[]{:S(2)}) collective-permute-start(bf16[16,64,128]{2,1,0:T(8,128)(2,1)S(1)} %get-tuple-element.27), channel_id=1, source_target_pairs={{0,3},{1,2},{2,1},{3,0},{4,7},{5,6},{6,5},{7,4},{8,11},{9,10},{10,... | collective-permute-start | bytes 786440 | tf_op jit(solution)/shard_map/update_rows/ppermute | solution.py:288
  37.7 3.5 %collective-permute-done.10.first = bf16[16,64,128]{2,1,0:T(8,128)(2,1)S(1)} collective-permute-done((bf16[16,64,128]{2,1,0:T(8,128)(2,1)S(1)}, bf16[16,64,128]{2,1,0:T(8,128)(2,1)S(1)}, u32[]{:S(2)}, u32[]{:S(2)}) %collective-permute-start.10) | collective-permute-done | bytes 262176 | tf_op jit(solution)/shard_map/update_rows/ppermute | solution.py:287
  41.2 1.9 %collective-permute-done.11.second = bf16[16,64,128]{2,1,0:T(8,128)(2,1)S(1)} collective-permute-done((bf16[16,64,128]{2,1,0:T(8,128)(2,1)S(1)}, bf16[16,64,128]{2,1,0:T(8,128)(2,1)S(1)}, u32[]{:S(2)}, u32[]{:S(2)}) %collective-permute-start.11) | collective-permute-done | bytes 262176 | tf_op jit(solution)/shard_map/update_rows/ppermute | solution.py:288
  44.1 1.6 %collective-permute-done.12.s1 = bf16[4,5,64,128]{3,2,1,0:T(8,128)(2,1)S(1)} collective-permute-done((bf16[4,5,64,128]{3,2,1,0:T(8,128)(2,1)S(1)}, bf16[4,5,64,128]{3,2,1,0:T(8,128)(2,1)S(1)}, u32[]{:S(2)}, u32[]{:S(2)}) %collective-permute-start.12) | collective-permute-done | bytes 327712 | tf_op jit(solution)/shard_map/first_state/ppermute | solution.py:292
  45.7 2.0 %second_iteration.1 = (bf16[4,192,128]{2,1,0:T(8,128)(2,1)S(1)}, bf16[4,192,128]{2,1,0:T(8,128)(2,1)S(1)}) custom-call(s32[1,8]{1,0:T(1,128)S(1)} %add_bitcast_fusion.table, f32[8,128]{1,0:T(8,128)S(1)} %iota.34.flags, bf16[4,5,64,128]{3,2,1,0:T(8,128)(2,1)S(1)} %first_state.1.s0.state, bf16[4,5,64,128]{3,2,1,0:T(8,128)(2,1)S(1)} %collective-permute-done.12.s1, ...), custom_call_target="tpu_custom_call" | custom-call | flops 1500000000 | bytes 3412000 | tf_op jit(solution)/shard_map/second_iteration/pallas_call | solution.py:233
  47.9 1.3 %collective-permute-done.13 = bf16[4,192,128]{2,1,0:T(8,128)(2,1)S(1)} collective-permute-done((bf16[4,192,128]{2,1,0:T(8,128)(2,1)S(1)}, bf16[4,192,128]{2,1,0:T(8,128)(2,1)S(1)}, u32[]{:S(2)}, u32[]{:S(2)}) %collective-permute-start.13) | collective-permute-done | bytes 196640 | tf_op jit(solution)/shard_map/second_sums/ppermute | solution.py:292
  49.3 3.6 %collective-permute-start.14 = (bf16[2,192,128]{2,1,0:T(8,128)(2,1)S(1)}, bf16[2,192,128]{2,1,0:T(8,128)(2,1)S(1)}, u32[]{:S(2)}, u32[]{:S(2)}) collective-permute-start(bf16[2,192,128]{2,1,0:T(8,128)(2,1)S(1)} %slice.108), channel_id=1, source_target_pairs={{0,1},{1,0},{2,3},{3,2},{4,8},{5,9},{6,10},{7,11},{8,4},{9,5},{10,... | collective-permute-start | bytes 294920 | tf_op jit(solution)/shard_map/second_sums/ppermute | solution.py:295
  52.8 2.7 %collective-permute-done.14 = bf16[2,192,128]{2,1,0:T(8,128)(2,1)S(1)} collective-permute-done((bf16[2,192,128]{2,1,0:T(8,128)(2,1)S(1)}, bf16[2,192,128]{2,1,0:T(8,128)(2,1)S(1)}, u32[]{:S(2)}, u32[]{:S(2)}) %collective-permute-start.14) | collective-permute-done | bytes 98336 | tf_op jit(solution)/shard_map/second_sums/ppermute | solution.py:295
  55.7 2.3 %collective-permute-start.16 = (bf16[2,1,64,128]{3,2,1,0:T(8,128)(2,1)S(1)}, bf16[2,1,64,128]{3,2,1,0:T(8,128)(2,1)S(1)}, u32[]{:S(2)}, u32[]{:S(2)}) collective-permute-start(bf16[2,1,64,128]{3,2,1,0:T(8,128)(2,1)S(1)} %get-tuple-element.37), channel_id=1, source_target_pairs={{0,3},{1,2},{2,1},{3,0},{4,7},{5,6},{6,5},{7,4},{8,11},{9,10},{10,... | collective-permute-start | bytes 98312 | tf_op jit(solution)/shard_map/second_sums/ppermute | solution.py:288
  57.9 1.6 %collective-permute-done.15.first = bf16[2,1,64,128]{3,2,1,0:T(8,128)(2,1)S(1)} collective-permute-done((bf16[2,1,64,128]{3,2,1,0:T(8,128)(2,1)S(1)}, bf16[2,1,64,128]{3,2,1,0:T(8,128)(2,1)S(1)}, u32[]{:S(2)}, u32[]{:S(2)}) %collective-permute-start.15) | collective-permute-done | bytes 32800 | tf_op jit(solution)/shard_map/second_sums/ppermute | solution.py:287
  59.6 1.3 %collective-permute-done.16.second = bf16[2,1,64,128]{3,2,1,0:T(8,128)(2,1)S(1)} collective-permute-done((bf16[2,1,64,128]{3,2,1,0:T(8,128)(2,1)S(1)}, bf16[2,1,64,128]{3,2,1,0:T(8,128)(2,1)S(1)}, u32[]{:S(2)}, u32[]{:S(2)}) %collective-permute-start.16) | collective-permute-done | bytes 32800 | tf_op jit(solution)/shard_map/second_sums/ppermute | solution.py:288
  60.9 1.0 %last_state.1 = bf16[2,3,64,128]{3,2,1,0:T(8,128)(2,1)} custom-call(f32[8,128]{1,0:T(8,128)S(1)} %iota.34.flags, bf16[4,5,64,128]{3,2,1,0:T(8,128)(2,1)S(1)} %first_state.1.s0.state, bf16[2,3,64,128]{3,2,1,0:T(8,128)(2,1)S(1)} %bitcast.10, bf16[2,1,64,128]{3,2,1,0:T(8,128)(2,1)S(1)} %collective-permute-done.15.first, ...), custom_call_target="tpu_custom_call" | custom-call | flops 120000000 | bytes 790528 | tf_op jit(solution)/shard_map/last_state/pallas_call | solution.py:233
  (64 shorter events, 4.0 us)
Async XLA Ops:
  0.9 9.9 %collective-permute-start.1 = (bf16[2,4,64,128]{3,2,1,0:T(8,128)(2,1)S(1)}, bf16[2,4,64,128]{3,2,1,0:T(8,128)(2,1)S(1)}, u32[]{:S(2)}, u32[]{:S(2)}) collective-permute-start(bf16[2,4,64,128]{3,2,1,0:T(8,128)(2,1)S(1)} %get-tuple-element.36), channel_id=1, source_target_pairs={{0,1},{1,0},{2,3},{3,2},{4,5},{5,4},{6,7},{7,6},{8,9},{9,8},{10,11... | collective-permute-start | bytes 393224 | tf_op jit(solution)/shard_map/feature_rows/ppermute | solution.py:287
  2.6 8.2 %collective-permute-start.2 = (bf16[2,4,64,128]{3,2,1,0:T(8,128)(2,1)S(1)}, bf16[2,4,64,128]{3,2,1,0:T(8,128)(2,1)S(1)}, u32[]{:S(2)}, u32[]{:S(2)}) collective-permute-start(bf16[2,4,64,128]{3,2,1,0:T(8,128)(2,1)S(1)} %get-tuple-element.35), channel_id=1, source_target_pairs={{0,3},{1,2},{2,1},{3,0},{4,7},{5,6},{6,5},{7,4},{8,11},{9,10},{10,... | collective-permute-start | bytes 393224 | tf_op jit(solution)/shard_map/feature_rows/ppermute | solution.py:288
  4.8 6.0 %collective-permute-start = (bf16[2,1,64,128]{3,2,1,0:T(8,128)(2,1)S(1)}, bf16[2,1,64,128]{3,2,1,0:T(8,128)(2,1)S(1)}, u32[]{:S(2)}, u32[]{:S(2)}) collective-permute-start(bf16[2,1,64,128]{3,2,1,0:T(8,128)(2,1)S(1)} %slice_select_fusion), channel_id=1, source_target_pairs={{0,2},{1,3},{2,0},{3,1},{4,6},{5,7},{6,4},{7,5},{8,10},{9,11},{10,... | collective-permute-start | bytes 98312 | tf_op jit(solution)/shard_map/feature_rows/ppermute | solution.py:300
  5.7 9.2 %collective-permute-start.3 = (bf16[2,6,64,128]{3,2,1,0:T(8,128)(2,1)S(1)}, bf16[2,6,64,128]{3,2,1,0:T(8,128)(2,1)S(1)}, u32[]{:S(2)}, u32[]{:S(2)}) collective-permute-start(bf16[2,6,64,128]{3,2,1,0:T(8,128)(2,1)S(1)} %constant_dynamic-update-slice_fusion.c0), channel_id=1, source_target_pairs={{0,1},{1,0},{2,3},{3,2},{4,8},{5,9},{6,10},{7,11},{8,4},{9,5},{10,... | collective-permute-start | bytes 589832 | tf_op jit(solution)/shard_map/feature_rows/ppermute | solution.py:295
  10.9 4.0 %copy-start.9 = (s32[256,3]{0,1:T(4,128)S(1)}, s32[256,3]{0,1:T(4,128)}, u32[]{:S(2)}) copy-start(s32[256,3]{0,1:T(4,128)} %param.10) | copy-start | bytes 9220
  10.9 10.4 %copy-start.1 = (bf16[9,256,128]{2,1,0:T(8,128)(2,1)S(1)}, bf16[9,256,128]{2,1,0:T(8,128)(2,1)}, u32[]{:S(2)}) copy-start(bf16[9,256,128]{2,1,0:T(8,128)(2,1)} %w_q.3) | copy-start | bytes 1769476
  11.0 8.7 %collective-permute-start.5 = (bf16[2,10,64,128]{3,2,1,0:T(8,128)(2,1)S(1)}, bf16[2,10,64,128]{3,2,1,0:T(8,128)(2,1)S(1)}, u32[]{:S(2)}, u32[]{:S(2)}) collective-permute-start(bf16[2,10,64,128]{3,2,1,0:T(8,128)(2,1)S(1)} %slice_dynamic-update-slice_fusion.2.h0), channel_id=1, source_target_pairs={{0,1},{1,0},{2,3},{3,2},{4,8},{5,9},{6,10},{7,11},{8,4},{9,5},{10,... | collective-permute-start | bytes 983048 | tf_op jit(solution)/shard_map/feature_window/ppermute | solution.py:295
  14.8 5.1 %collective-permute-start.6 = (bf16[2,10,64,128]{3,2,1,0:T(8,128)(2,1)S(1)}, bf16[2,10,64,128]{3,2,1,0:T(8,128)(2,1)S(1)}, u32[]{:S(2)}, u32[]{:S(2)}) collective-permute-start(bf16[2,10,64,128]{3,2,1,0:T(8,128)(2,1)S(1)} %slice_dynamic-update-slice_fusion.2.h0), channel_id=1, source_target_pairs={{0,4},{4,0},{8,12},{12,8},{16,20},{20,16},{24,28},{28,24},{32,36},... | collective-permute-start | bytes 983048 | tf_op jit(solution)/shard_map/feature_window/ppermute | solution.py:292
  14.9 6.5 %copy-start.2 = (bf16[256,256]{1,0:T(8,128)(2,1)S(1)}, bf16[256,256]{1,0:T(8,128)(2,1)}, u32[]{:S(2)}) copy-start(bf16[256,256]{1,0:T(8,128)(2,1)} %w_zr.3) | copy-start | bytes 393220
  14.9 6.5 %copy-start.3 = (bf16[128,256]{1,0:T(8,128)(2,1)S(1)}, bf16[128,256]{1,0:T(8,128)(2,1)}, u32[]{:S(2)}) copy-start(bf16[128,256]{1,0:T(8,128)(2,1)} %w_msg.3) | copy-start | bytes 196612
  14.9 6.4 %copy-start.4 = (bf16[49,128]{1,0:T(8,128)(2,1)S(1)}, bf16[49,128]{1,0:T(8,128)(2,1)}, u32[]{:S(2)}) copy-start(bf16[49,128]{1,0:T(8,128)(2,1)} %w_corr.1) | copy-start | bytes 37636
  15.0 4.9 %collective-permute-start.4 = (bf16[4,6,64,128]{3,2,1,0:T(8,128)(2,1)S(1)}, bf16[4,6,64,128]{3,2,1,0:T(8,128)(2,1)S(1)}, u32[]{:S(2)}, u32[]{:S(2)}) collective-permute-start(bf16[4,6,64,128]{3,2,1,0:T(8,128)(2,1)S(1)} %pad_maximum_fusion), channel_id=1, source_target_pairs={{0,4},{4,0},{8,12},{12,8},{16,20},{20,16},{24,28},{28,24},{32,36},... | collective-permute-start | bytes 1179656 | tf_op jit(solution)/shard_map/feature_window/ppermute | solution.py:292
  19.7 1.6 %collective-permute-start.7 = (bf16[2,10,64,128]{3,2,1,0:T(8,128)(2,1)S(1)}, bf16[2,10,64,128]{3,2,1,0:T(8,128)(2,1)S(1)}, u32[]{:S(2)}, u32[]{:S(2)}) collective-permute-start(bf16[2,10,64,128]{3,2,1,0:T(8,128)(2,1)S(1)} %collective-permute-done.5.h1), channel_id=1, source_target_pairs={{0,4},{4,0},{8,12},{12,8},{16,20},{20,16},{24,28},{28,24},{32,36},... | collective-permute-start | bytes 983048 | tf_op jit(solution)/shard_map/feature_window/ppermute | solution.py:292
  25.5 8.9 %copy-start.5 = (bf16[8,320,128]{2,1,0:T(8,128)(2,1)}, bf16[8,320,128]{2,1,0:T(8,128)(2,1)S(1)}, u32[]{:S(2)}) copy-start(bf16[8,320,128]{2,1,0:T(8,128)(2,1)S(1)} %get-tuple-element.23.motion) | copy-start | bytes 1966084
  25.5 1.5 %collective-permute-start.8 = (bf16[4,192,128]{2,1,0:T(8,128)(2,1)S(1)}, bf16[4,192,128]{2,1,0:T(8,128)(2,1)S(1)}, u32[]{:S(2)}, u32[]{:S(2)}) collective-permute-start(bf16[4,192,128]{2,1,0:T(8,128)(2,1)S(1)} %get-tuple-element.20), channel_id=1, source_target_pairs={{0,4},{4,0},{8,12},{12,8},{16,20},{20,16},{24,28},{28,24},{32,36},... | collective-permute-start | bytes 589832 | tf_op jit(solution)/shard_map/first_sums/ppermute | solution.py:292
  27.1 7.3 %collective-permute-start.9 = (bf16[4,192,128]{2,1,0:T(8,128)(2,1)S(1)}, bf16[4,192,128]{2,1,0:T(8,128)(2,1)S(1)}, u32[]{:S(2)}, u32[]{:S(2)}) collective-permute-start(bf16[4,192,128]{2,1,0:T(8,128)(2,1)S(1)} %fusion.2), channel_id=1, source_target_pairs={{0,1},{1,0},{2,3},{3,2},{4,8},{5,9},{6,10},{7,11},{8,4},{9,5},{10,... | collective-permute-start | bytes 589832 | tf_op jit(solution)/shard_map/first_sums/ppermute | solution.py:295
  34.5 8.7 %copy-start = (bf16[9,128,128]{2,1,0:T(8,128)(2,1)S(1)}, bf16[9,128,128]{2,1,0:T(8,128)(2,1)}, u32[]{:S(2)}) copy-start(bf16[9,128,128]{2,1,0:T(8,128)(2,1)} %w_res.3) | copy-start | bytes 884740
  34.6 6.6 %collective-permute-start.10 = (bf16[16,64,128]{2,1,0:T(8,128)(2,1)S(1)}, bf16[16,64,128]{2,1,0:T(8,128)(2,1)S(1)}, u32[]{:S(2)}, u32[]{:S(2)}) collective-permute-start(bf16[16,64,128]{2,1,0:T(8,128)(2,1)S(1)} %get-tuple-element.28), channel_id=1, source_target_pairs={{0,1},{1,0},{2,3},{3,2},{4,5},{5,4},{6,7},{7,6},{8,9},{9,8},{10,11... | collective-permute-start | bytes 786440 | tf_op jit(solution)/shard_map/update_rows/ppermute | solution.py:287
  35.5 7.6 %collective-permute-start.11 = (bf16[16,64,128]{2,1,0:T(8,128)(2,1)S(1)}, bf16[16,64,128]{2,1,0:T(8,128)(2,1)S(1)}, u32[]{:S(2)}, u32[]{:S(2)}) collective-permute-start(bf16[16,64,128]{2,1,0:T(8,128)(2,1)S(1)} %get-tuple-element.27), channel_id=1, source_target_pairs={{0,3},{1,2},{2,1},{3,0},{4,7},{5,6},{6,5},{7,4},{8,11},{9,10},{10,... | collective-permute-start | bytes 786440 | tf_op jit(solution)/shard_map/update_rows/ppermute | solution.py:288
  44.0 1.7 %collective-permute-start.12 = (bf16[4,5,64,128]{3,2,1,0:T(8,128)(2,1)S(1)}, bf16[4,5,64,128]{3,2,1,0:T(8,128)(2,1)S(1)}, u32[]{:S(2)}, u32[]{:S(2)}) collective-permute-start(bf16[4,5,64,128]{3,2,1,0:T(8,128)(2,1)S(1)} %first_state.1.s0.state), channel_id=1, source_target_pairs={{0,4},{4,0},{8,12},{12,8},{16,20},{20,16},{24,28},{28,24},{32,36},... | collective-permute-start | bytes 983048 | tf_op jit(solution)/shard_map/first_state/ppermute | solution.py:292
  47.7 1.5 %collective-permute-start.13 = (bf16[4,192,128]{2,1,0:T(8,128)(2,1)S(1)}, bf16[4,192,128]{2,1,0:T(8,128)(2,1)S(1)}, u32[]{:S(2)}, u32[]{:S(2)}) collective-permute-start(bf16[4,192,128]{2,1,0:T(8,128)(2,1)S(1)} %get-tuple-element.26), channel_id=1, source_target_pairs={{0,4},{4,0},{8,12},{12,8},{16,20},{20,16},{24,28},{28,24},{32,36},... | collective-permute-start | bytes 589832 | tf_op jit(solution)/shard_map/second_sums/ppermute | solution.py:292
  49.3 6.2 %collective-permute-start.14 = (bf16[2,192,128]{2,1,0:T(8,128)(2,1)S(1)}, bf16[2,192,128]{2,1,0:T(8,128)(2,1)S(1)}, u32[]{:S(2)}, u32[]{:S(2)}) collective-permute-start(bf16[2,192,128]{2,1,0:T(8,128)(2,1)S(1)} %slice.108), channel_id=1, source_target_pairs={{0,1},{1,0},{2,3},{3,2},{4,8},{5,9},{6,10},{7,11},{8,4},{9,5},{10,... | collective-permute-start | bytes 294920 | tf_op jit(solution)/shard_map/second_sums/ppermute | solution.py:295
  55.6 4.0 %collective-permute-start.15 = (bf16[2,1,64,128]{3,2,1,0:T(8,128)(2,1)S(1)}, bf16[2,1,64,128]{3,2,1,0:T(8,128)(2,1)S(1)}, u32[]{:S(2)}, u32[]{:S(2)}) collective-permute-start(bf16[2,1,64,128]{3,2,1,0:T(8,128)(2,1)S(1)} %get-tuple-element.38), channel_id=1, source_target_pairs={{0,1},{1,0},{2,3},{3,2},{4,5},{5,4},{6,7},{7,6},{8,9},{9,8},{10,11... | collective-permute-start | bytes 98312 | tf_op jit(solution)/shard_map/second_sums/ppermute | solution.py:287
  55.7 5.2 %collective-permute-start.16 = (bf16[2,1,64,128]{3,2,1,0:T(8,128)(2,1)S(1)}, bf16[2,1,64,128]{3,2,1,0:T(8,128)(2,1)S(1)}, u32[]{:S(2)}, u32[]{:S(2)}) collective-permute-start(bf16[2,1,64,128]{3,2,1,0:T(8,128)(2,1)S(1)} %get-tuple-element.37), channel_id=1, source_target_pairs={{0,3},{1,2},{2,1},{3,0},{4,7},{5,6},{6,5},{7,4},{8,11},{9,10},{10,... | collective-permute-start | bytes 98312 | tf_op jit(solution)/shard_map/second_sums/ppermute | solution.py:288
  (3 other events, 4.3 us)

commit v8 on v7

--- a/solution.py
+++ b/solution.py
@@ -6,6 +6,7 @@
 from jax.sharding import PartitionSpec as P
 
 SLOTS = 8
+GROUP = 4
 ROWS = 3
 WIDTH = 64
 CHANS = 128
@@ -111,7 +112,7 @@
     place = (lax.broadcasted_iota(jnp.int32, (WIDTH, CHANS), 1) & (WIDTH - 1)) - 4
 
     def body(i, carry):
-        slots = [2 * i + j for j in range(2)]
+        slots = [GROUP * i + j for j in range(GROUP)]
         for j, s in enumerate(slots):
             code = jnp.maximum(idx[s], 0)
             source, target = code // SLOTS, code % SLOTS
@@ -131,10 +132,10 @@
                     rim[j, 4:7] = center[first + frame, 0:3]
                     rim[j, 7:11] = halo[frame, 4:8]
 
-        rows = [(j, y) for j in range(2) for y in range(5)]
+        rows = [(j, y) for j in range(GROUP) for y in range(5)]
         turned = dot(flip[...], jnp.concatenate([feat[j, y] for j, y in rows], axis=1)).astype(BF16)
         corr = []
-        for j in range(2):
+        for j in range(GROUP):
             near = [turned[:, (5 * j + y) * CHANS : (5 * j + y + 1) * CHANS] for y in range(5)]
             totals = [None] * 5
             for t in range(10):
@@ -150,8 +151,8 @@
         turned = dot(flip[...], jnp.concatenate(corr, axis=1)).astype(BF16)
         corr = jnp.concatenate([turned[:, k * CHANS : (k + 1) * CHANS] for k in range(len(rows))])
         motion = jnp.maximum(dot(corr, spread[...]), 0.0).astype(BF16)
-        motion = [motion[j * WIDE : (j + 1) * WIDE] for j in range(2)]
-        state = [ctx[j].reshape(WIDE, CHANS).astype(F32) for j in range(2)]
+        motion = [motion[j * WIDE : (j + 1) * WIDE] for j in range(GROUP)]
+        state = [ctx[j].reshape(WIDE, CHANS).astype(F32) for j in range(GROUP)]
         xin = [(m.astype(F32) + c).astype(BF16) for m, c in zip(motion, state)]
         hidden = gru([jnp.tanh(c) for c in state], xin, w_zr[...], side_by_side(w_q))
         for s, m, h in zip(slots, motion, hidden):
@@ -162,7 +163,7 @@
         add_messages(acc, idx, slots, hidden, w_msg[...])
         return carry
 
-    lax.fori_loop(0, (count + 1) // 2, body, 0)
+    lax.fori_loop(0, (count + GROUP - 1) // GROUP, body, 0)
     give_sums(acc, part, part_other)
 
 
@@ -174,7 +175,7 @@
     acc[...] = jnp.zeros_like(acc)
 
     def body(i, carry):
-        slots = [2 * i + j for j in range(2)]
+        slots = [GROUP * i + j for j in range(GROUP)]
         for j, s in enumerate(slots):
             source = jnp.maximum(idx[s], 0) // SLOTS
             for k, piece in enumerate((s0, s1)):
@@ -183,7 +184,7 @@
                 def _():
                     state_buf[j] = piece[source % 4]
 
-        state = [state_buf[j].reshape(WIDE, CHANS).astype(F32) for j in range(2)]
+        state = [state_buf[j].reshape(WIDE, CHANS).astype(F32) for j in range(GROUP)]
         xin = [(motion[s].astype(F32) + c).astype(BF16) for s, c in zip(slots, state)]
         hidden = []
         for s in slots:
@@ -193,7 +194,7 @@
         add_messages(acc, idx, slots, hidden, w_msg[...])
         return carry
 
-    lax.fori_loop(0, (count + 1) // 2, body, 0)
+    lax.fori_loop(0, (count + GROUP - 1) // GROUP, body, 0)
     give_sums(acc, part, part_other)
 
 
@@ -337,9 +338,9 @@
                 jax.ShapeDtypeStruct((4, 5, WIDTH, CHANS), BF16),
             ],
             [
-                pltpu.VMEM((2, 5, WIDTH, CHANS), BF16),
-                pltpu.VMEM((2, 11, WIDTH, CHANS), BF16),
-                pltpu.VMEM((2, 5, WIDTH, CHANS), BF16),
+                pltpu.VMEM((GROUP, 5, WIDTH, CHANS), BF16),
+                pltpu.VMEM((GROUP, 11, WIDTH, CHANS), BF16),
+                pltpu.VMEM((GROUP, 5, WIDTH, CHANS), BF16),
                 pltpu.VMEM((SLOTS, OWN, CHANS), F32),
                 pltpu.VMEM((WIDTH, WIDTH), BF16),
                 pltpu.VMEM((CHANS, CHANS), BF16),
@@ -375,7 +376,7 @@
             second_kernel,
             sums,
             [
-                pltpu.VMEM((2, 5, WIDTH, CHANS), BF16),
+                pltpu.VMEM((GROUP, 5, WIDTH, CHANS), BF16),
                 pltpu.VMEM((SLOTS, OWN, CHANS), F32),
                 pltpu.SMEM((SLOTS,), jnp.int32),
             ],

time: 62 us -> 61.2 us (0.987)
  Pallas kernels: 7.84 us -> 6.99 us
    pallas_call x4, Pallas kernels: 7.84 us -> 6.99 us  [call(): pl.pallas_call(kernel, out_shape=outs, in_specs=[VM] * len(args), out_spe...]
where the time goes in v8:
time: 61.2 us; the launch traced here: 61 us
  starting transfers between devices  27.5 us (45%)
  waiting for transfers between devices  24.2 us (40%)
  Pallas kernels  6.99 us (11%)
  local copies, waits for them, and re-layouts  1.25 us (2%)
  other arithmetic  0.76 us (1%)
    ppermute x4, starting transfers between devices, swap_chip(): return lax.ppermute(x, ('frames', 'rows'), chip_swap)  16.3 us
    ppermute x4, waiting for transfers between devices, swap_chip(): return lax.ppermute(x, ('frames', 'rows'), chip_swap)  10.2 us
    pallas_call x4, Pallas kernels, call(): pl.pallas_call(kernel, out_shape=outs, in_specs=[VM] * len(args), out_spe...  6.99 us
    ppermute x3, starting transfers between devices, rows_swaps(): second = lax.ppermute(jnp.where(odd, to_below, to_above), 'rows', odd_swap)  6.62 us
    ppermute x6, waiting for transfers between devices, swap_core(): return lax.ppermute(x, 'frames', core_swap)  5.66 us
    ppermute x3, waiting for transfers between devices, rows_swaps(): first = lax.ppermute(jnp.where(odd, to_above, to_below), 'rows', even_swap)  5.14 us
    ppermute x3, waiting for transfers between devices, rows_swaps(): second = lax.ppermute(jnp.where(odd, to_below, to_above), 'rows', odd_swap)  3.21 us
    ppermute x3, starting transfers between devices, rows_swaps(): first = lax.ppermute(jnp.where(odd, to_above, to_below), 'rows', even_swap)  2.7 us
  transfers between devices with their start and end apart: 17, of which 11 were waited for; matrix products, arithmetic and copies ran while one was open for 1% of the time, Pallas kernels for 0%

profile of v8, /device:TPU:6, one launch (start us, length us, event | category | flops | bytes accessed | tf_op | source)
XLA Modules:
  0.0 61.0 jit_solution(14811212031548286936)
XLA Ops:
  0.9 1.7 %collective-permute-start.1 = (bf16[2,4,64,128]{3,2,1,0:T(8,128)(2,1)S(1)}, bf16[2,4,64,128]{3,2,1,0:T(8,128)(2,1)S(1)}, u32[]{:S(2)}, u32[]{:S(2)}) collective-permute-start(bf16[2,4,64,128]{3,2,1,0:T(8,128)(2,1)S(1)} %get-tuple-element.36), channel_id=1, source_target_pairs={{0,1},{1,0},{2,3},{3,2},{4,5},{5,4},{6,7},{7,6},{8,9},{9,8},{10,11... | collective-permute-start | bytes 393224 | tf_op jit(solution)/shard_map/feature_rows/ppermute | solution.py:288
  2.6 2.2 %collective-permute-start.2 = (bf16[2,4,64,128]{3,2,1,0:T(8,128)(2,1)S(1)}, bf16[2,4,64,128]{3,2,1,0:T(8,128)(2,1)S(1)}, u32[]{:S(2)}, u32[]{:S(2)}) collective-permute-start(bf16[2,4,64,128]{3,2,1,0:T(8,128)(2,1)S(1)} %get-tuple-element.35), channel_id=1, source_target_pairs={{0,3},{1,2},{2,1},{3,0},{4,7},{5,6},{6,5},{7,4},{8,11},{9,10},{10,... | collective-permute-start | bytes 393224 | tf_op jit(solution)/shard_map/feature_rows/ppermute | solution.py:289
  4.8 0.8 %collective-permute-start = (bf16[2,1,64,128]{3,2,1,0:T(8,128)(2,1)S(1)}, bf16[2,1,64,128]{3,2,1,0:T(8,128)(2,1)S(1)}, u32[]{:S(2)}, u32[]{:S(2)}) collective-permute-start(bf16[2,1,64,128]{3,2,1,0:T(8,128)(2,1)S(1)} %slice_select_fusion), channel_id=1, source_target_pairs={{0,2},{1,3},{2,0},{3,1},{4,6},{5,7},{6,4},{7,5},{8,10},{9,11},{10,... | collective-permute-start | bytes 98312 | tf_op jit(solution)/shard_map/feature_rows/ppermute | solution.py:301
  5.7 5.1 %collective-permute-start.3 = (bf16[2,6,64,128]{3,2,1,0:T(8,128)(2,1)S(1)}, bf16[2,6,64,128]{3,2,1,0:T(8,128)(2,1)S(1)}, u32[]{:S(2)}, u32[]{:S(2)}) collective-permute-start(bf16[2,6,64,128]{3,2,1,0:T(8,128)(2,1)S(1)} %constant_dynamic-update-slice_fusion.c0), channel_id=1, source_target_pairs={{0,1},{1,0},{2,3},{3,2},{4,8},{5,9},{6,10},{7,11},{8,4},{9,5},{10,... | collective-permute-start | bytes 589832 | tf_op jit(solution)/shard_map/feature_rows/ppermute | solution.py:296
  11.0 3.8 %collective-permute-start.5 = (bf16[2,10,64,128]{3,2,1,0:T(8,128)(2,1)S(1)}, bf16[2,10,64,128]{3,2,1,0:T(8,128)(2,1)S(1)}, u32[]{:S(2)}, u32[]{:S(2)}) collective-permute-start(bf16[2,10,64,128]{3,2,1,0:T(8,128)(2,1)S(1)} %slice_dynamic-update-slice_fusion.2.h0), channel_id=1, source_target_pairs={{0,1},{1,0},{2,3},{3,2},{4,8},{5,9},{6,10},{7,11},{8,4},{9,5},{10,... | collective-permute-start | bytes 983048 | tf_op jit(solution)/shard_map/feature_window/ppermute | solution.py:296
  15.7 4.0 %collective-permute-done.5.h1 = bf16[2,10,64,128]{3,2,1,0:T(8,128)(2,1)S(1)} collective-permute-done((bf16[2,10,64,128]{3,2,1,0:T(8,128)(2,1)S(1)}, bf16[2,10,64,128]{3,2,1,0:T(8,128)(2,1)S(1)}, u32[]{:S(2)}, u32[]{:S(2)}) %collective-permute-start.5) | collective-permute-done | bytes 327712 | tf_op jit(solution)/shard_map/feature_window/ppermute | solution.py:296
  19.9 1.4 %collective-permute-done.7.h3 = bf16[2,10,64,128]{3,2,1,0:T(8,128)(2,1)S(1)} collective-permute-done((bf16[2,10,64,128]{3,2,1,0:T(8,128)(2,1)S(1)}, bf16[2,10,64,128]{3,2,1,0:T(8,128)(2,1)S(1)}, u32[]{:S(2)}, u32[]{:S(2)}) %collective-permute-start.7) | collective-permute-done | bytes 327712 | tf_op jit(solution)/shard_map/feature_window/ppermute | solution.py:293
  21.3 3.3 %first_iteration.1 = (bf16[4,192,128]{2,1,0:T(8,128)(2,1)S(1)}, bf16[4,192,128]{2,1,0:T(8,128)(2,1)S(1)}, f32[8,192,128]{2,1,0:T(8,128)S(1)}, bf16[8,64,128]{2,1...) custom-call(s32[1,8]{1,0:T(1,128)S(1)} %add_bitcast_fusion.table, ...), custom_call_target="tpu_custom_call" | custom-call | flops 2000000000 | bytes 2896160 | tf_op jit(solution)/shard_map/first_iteration/pallas_call | solution.py:234
  24.9 1.3 %collective-permute-done.8 = bf16[4,192,128]{2,1,0:T(8,128)(2,1)S(1)} collective-permute-done((bf16[4,192,128]{2,1,0:T(8,128)(2,1)S(1)}, bf16[4,192,128]{2,1,0:T(8,128)(2,1)S(1)}, u32[]{:S(2)}, u32[]{:S(2)}) %collective-permute-start.8) | collective-permute-done | bytes 196640 | tf_op jit(solution)/shard_map/first_sums/ppermute | solution.py:293
  26.3 3.8 %collective-permute-start.9 = (bf16[4,192,128]{2,1,0:T(8,128)(2,1)S(1)}, bf16[4,192,128]{2,1,0:T(8,128)(2,1)S(1)}, u32[]{:S(2)}, u32[]{:S(2)}) collective-permute-start(bf16[4,192,128]{2,1,0:T(8,128)(2,1)S(1)} %fusion.2), channel_id=1, source_target_pairs={{0,1},{1,0},{2,3},{3,2},{4,8},{5,9},{6,10},{7,11},{8,4},{9,5},{10,... | collective-permute-start | bytes 589832 | tf_op jit(solution)/shard_map/first_sums/ppermute | solution.py:296
  30.1 3.5 %collective-permute-done.9 = bf16[4,192,128]{2,1,0:T(8,128)(2,1)S(1)} collective-permute-done((bf16[4,192,128]{2,1,0:T(8,128)(2,1)S(1)}, bf16[4,192,128]{2,1,0:T(8,128)(2,1)S(1)}, u32[]{:S(2)}, u32[]{:S(2)}) %collective-permute-start.9) | collective-permute-done | bytes 196640 | tf_op jit(solution)/shard_map/first_sums/ppermute | solution.py:296
  33.8 0.9 %collective-permute-start.10 = (bf16[16,64,128]{2,1,0:T(8,128)(2,1)S(1)}, bf16[16,64,128]{2,1,0:T(8,128)(2,1)S(1)}, u32[]{:S(2)}, u32[]{:S(2)}) collective-permute-start(bf16[16,64,128]{2,1,0:T(8,128)(2,1)S(1)} %get-tuple-element.28), channel_id=1, source_target_pairs={{0,1},{1,0},{2,3},{3,2},{4,5},{5,4},{6,7},{7,6},{8,9},{9,8},{10,11... | collective-permute-start | bytes 786440 | tf_op jit(solution)/shard_map/update_rows/ppermute | solution.py:288
  34.7 2.2 %collective-permute-start.11 = (bf16[16,64,128]{2,1,0:T(8,128)(2,1)S(1)}, bf16[16,64,128]{2,1,0:T(8,128)(2,1)S(1)}, u32[]{:S(2)}, u32[]{:S(2)}) collective-permute-start(bf16[16,64,128]{2,1,0:T(8,128)(2,1)S(1)} %get-tuple-element.27), channel_id=1, source_target_pairs={{0,3},{1,2},{2,1},{3,0},{4,7},{5,6},{6,5},{7,4},{8,11},{9,10},{10,... | collective-permute-start | bytes 786440 | tf_op jit(solution)/shard_map/update_rows/ppermute | solution.py:289
  36.9 3.5 %collective-permute-done.10.first = bf16[16,64,128]{2,1,0:T(8,128)(2,1)S(1)} collective-permute-done((bf16[16,64,128]{2,1,0:T(8,128)(2,1)S(1)}, bf16[16,64,128]{2,1,0:T(8,128)(2,1)S(1)}, u32[]{:S(2)}, u32[]{:S(2)}) %collective-permute-start.10) | collective-permute-done | bytes 262176 | tf_op jit(solution)/shard_map/update_rows/ppermute | solution.py:288
  40.4 1.9 %collective-permute-done.11.second = bf16[16,64,128]{2,1,0:T(8,128)(2,1)S(1)} collective-permute-done((bf16[16,64,128]{2,1,0:T(8,128)(2,1)S(1)}, bf16[16,64,128]{2,1,0:T(8,128)(2,1)S(1)}, u32[]{:S(2)}, u32[]{:S(2)}) %collective-permute-start.11) | collective-permute-done | bytes 262176 | tf_op jit(solution)/shard_map/update_rows/ppermute | solution.py:289
  43.3 1.6 %collective-permute-done.12.s1 = bf16[4,5,64,128]{3,2,1,0:T(8,128)(2,1)S(1)} collective-permute-done((bf16[4,5,64,128]{3,2,1,0:T(8,128)(2,1)S(1)}, bf16[4,5,64,128]{3,2,1,0:T(8,128)(2,1)S(1)}, u32[]{:S(2)}, u32[]{:S(2)}) %collective-permute-start.12) | collective-permute-done | bytes 327712 | tf_op jit(solution)/shard_map/first_state/ppermute | solution.py:293
  44.9 1.9 %second_iteration.1 = (bf16[4,192,128]{2,1,0:T(8,128)(2,1)S(1)}, bf16[4,192,128]{2,1,0:T(8,128)(2,1)S(1)}) custom-call(s32[1,8]{1,0:T(1,128)S(1)} %add_bitcast_fusion.table, f32[8,128]{1,0:T(8,128)S(1)} %iota.34.flags, bf16[4,5,64,128]{3,2,1,0:T(8,128)(2,1)S(1)} %first_state.1.s0.state, bf16[4,5,64,128]{3,2,1,0:T(8,128)(2,1)S(1)} %collective-permute-done.12.s1, ...), custom_call_target="tpu_custom_call" | custom-call | flops 1500000000 | bytes 3412000 | tf_op jit(solution)/shard_map/second_iteration/pallas_call | solution.py:234
  47.1 1.3 %collective-permute-done.13 = bf16[4,192,128]{2,1,0:T(8,128)(2,1)S(1)} collective-permute-done((bf16[4,192,128]{2,1,0:T(8,128)(2,1)S(1)}, bf16[4,192,128]{2,1,0:T(8,128)(2,1)S(1)}, u32[]{:S(2)}, u32[]{:S(2)}) %collective-permute-start.13) | collective-permute-done | bytes 196640 | tf_op jit(solution)/shard_map/second_sums/ppermute | solution.py:293
  48.4 3.5 %collective-permute-start.14 = (bf16[2,192,128]{2,1,0:T(8,128)(2,1)S(1)}, bf16[2,192,128]{2,1,0:T(8,128)(2,1)S(1)}, u32[]{:S(2)}, u32[]{:S(2)}) collective-permute-start(bf16[2,192,128]{2,1,0:T(8,128)(2,1)S(1)} %slice.108), channel_id=1, source_target_pairs={{0,1},{1,0},{2,3},{3,2},{4,8},{5,9},{6,10},{7,11},{8,4},{9,5},{10,... | collective-permute-start | bytes 294920 | tf_op jit(solution)/shard_map/second_sums/ppermute | solution.py:296
  52.0 2.7 %collective-permute-done.14 = bf16[2,192,128]{2,1,0:T(8,128)(2,1)S(1)} collective-permute-done((bf16[2,192,128]{2,1,0:T(8,128)(2,1)S(1)}, bf16[2,192,128]{2,1,0:T(8,128)(2,1)S(1)}, u32[]{:S(2)}, u32[]{:S(2)}) %collective-permute-start.14) | collective-permute-done | bytes 98336 | tf_op jit(solution)/shard_map/second_sums/ppermute | solution.py:296
  54.8 2.3 %collective-permute-start.16 = (bf16[2,1,64,128]{3,2,1,0:T(8,128)(2,1)S(1)}, bf16[2,1,64,128]{3,2,1,0:T(8,128)(2,1)S(1)}, u32[]{:S(2)}, u32[]{:S(2)}) collective-permute-start(bf16[2,1,64,128]{3,2,1,0:T(8,128)(2,1)S(1)} %get-tuple-element.37), channel_id=1, source_target_pairs={{0,3},{1,2},{2,1},{3,0},{4,7},{5,6},{6,5},{7,4},{8,11},{9,10},{10,... | collective-permute-start | bytes 98312 | tf_op jit(solution)/shard_map/second_sums/ppermute | solution.py:289
  57.1 1.6 %collective-permute-done.15.first = bf16[2,1,64,128]{3,2,1,0:T(8,128)(2,1)S(1)} collective-permute-done((bf16[2,1,64,128]{3,2,1,0:T(8,128)(2,1)S(1)}, bf16[2,1,64,128]{3,2,1,0:T(8,128)(2,1)S(1)}, u32[]{:S(2)}, u32[]{:S(2)}) %collective-permute-start.15) | collective-permute-done | bytes 32800 | tf_op jit(solution)/shard_map/second_sums/ppermute | solution.py:288
  58.7 1.3 %collective-permute-done.16.second = bf16[2,1,64,128]{3,2,1,0:T(8,128)(2,1)S(1)} collective-permute-done((bf16[2,1,64,128]{3,2,1,0:T(8,128)(2,1)S(1)}, bf16[2,1,64,128]{3,2,1,0:T(8,128)(2,1)S(1)}, u32[]{:S(2)}, u32[]{:S(2)}) %collective-permute-start.16) | collective-permute-done | bytes 32800 | tf_op jit(solution)/shard_map/second_sums/ppermute | solution.py:289
  60.0 1.0 %last_state.1 = bf16[2,3,64,128]{3,2,1,0:T(8,128)(2,1)} custom-call(f32[8,128]{1,0:T(8,128)S(1)} %iota.34.flags, bf16[4,5,64,128]{3,2,1,0:T(8,128)(2,1)S(1)} %first_state.1.s0.state, bf16[2,3,64,128]{3,2,1,0:T(8,128)(2,1)S(1)} %bitcast.10, bf16[2,1,64,128]{3,2,1,0:T(8,128)(2,1)S(1)} %collective-permute-done.15.first, ...), custom_call_target="tpu_custom_call" | custom-call | flops 120000000 | bytes 790528 | tf_op jit(solution)/shard_map/last_state/pallas_call | solution.py:234
  (64 shorter events, 4.0 us)
Async XLA Ops:
  0.9 9.9 %collective-permute-start.1 = (bf16[2,4,64,128]{3,2,1,0:T(8,128)(2,1)S(1)}, bf16[2,4,64,128]{3,2,1,0:T(8,128)(2,1)S(1)}, u32[]{:S(2)}, u32[]{:S(2)}) collective-permute-start(bf16[2,4,64,128]{3,2,1,0:T(8,128)(2,1)S(1)} %get-tuple-element.36), channel_id=1, source_target_pairs={{0,1},{1,0},{2,3},{3,2},{4,5},{5,4},{6,7},{7,6},{8,9},{9,8},{10,11... | collective-permute-start | bytes 393224 | tf_op jit(solution)/shard_map/feature_rows/ppermute | solution.py:288
  2.6 8.2 %collective-permute-start.2 = (bf16[2,4,64,128]{3,2,1,0:T(8,128)(2,1)S(1)}, bf16[2,4,64,128]{3,2,1,0:T(8,128)(2,1)S(1)}, u32[]{:S(2)}, u32[]{:S(2)}) collective-permute-start(bf16[2,4,64,128]{3,2,1,0:T(8,128)(2,1)S(1)} %get-tuple-element.35), channel_id=1, source_target_pairs={{0,3},{1,2},{2,1},{3,0},{4,7},{5,6},{6,5},{7,4},{8,11},{9,10},{10,... | collective-permute-start | bytes 393224 | tf_op jit(solution)/shard_map/feature_rows/ppermute | solution.py:289
  4.8 6.0 %collective-permute-start = (bf16[2,1,64,128]{3,2,1,0:T(8,128)(2,1)S(1)}, bf16[2,1,64,128]{3,2,1,0:T(8,128)(2,1)S(1)}, u32[]{:S(2)}, u32[]{:S(2)}) collective-permute-start(bf16[2,1,64,128]{3,2,1,0:T(8,128)(2,1)S(1)} %slice_select_fusion), channel_id=1, source_target_pairs={{0,2},{1,3},{2,0},{3,1},{4,6},{5,7},{6,4},{7,5},{8,10},{9,11},{10,... | collective-permute-start | bytes 98312 | tf_op jit(solution)/shard_map/feature_rows/ppermute | solution.py:301
  5.7 9.2 %collective-permute-start.3 = (bf16[2,6,64,128]{3,2,1,0:T(8,128)(2,1)S(1)}, bf16[2,6,64,128]{3,2,1,0:T(8,128)(2,1)S(1)}, u32[]{:S(2)}, u32[]{:S(2)}) collective-permute-start(bf16[2,6,64,128]{3,2,1,0:T(8,128)(2,1)S(1)} %constant_dynamic-update-slice_fusion.c0), channel_id=1, source_target_pairs={{0,1},{1,0},{2,3},{3,2},{4,8},{5,9},{6,10},{7,11},{8,4},{9,5},{10,... | collective-permute-start | bytes 589832 | tf_op jit(solution)/shard_map/feature_rows/ppermute | solution.py:296
  10.9 4.0 %copy-start.9 = (s32[256,3]{0,1:T(4,128)S(1)}, s32[256,3]{0,1:T(4,128)}, u32[]{:S(2)}) copy-start(s32[256,3]{0,1:T(4,128)} %param.10) | copy-start | bytes 9220
  10.9 10.4 %copy-start.1 = (bf16[9,256,128]{2,1,0:T(8,128)(2,1)S(1)}, bf16[9,256,128]{2,1,0:T(8,128)(2,1)}, u32[]{:S(2)}) copy-start(bf16[9,256,128]{2,1,0:T(8,128)(2,1)} %w_q.3) | copy-start | bytes 1769476
  11.0 8.7 %collective-permute-start.5 = (bf16[2,10,64,128]{3,2,1,0:T(8,128)(2,1)S(1)}, bf16[2,10,64,128]{3,2,1,0:T(8,128)(2,1)S(1)}, u32[]{:S(2)}, u32[]{:S(2)}) collective-permute-start(bf16[2,10,64,128]{3,2,1,0:T(8,128)(2,1)S(1)} %slice_dynamic-update-slice_fusion.2.h0), channel_id=1, source_target_pairs={{0,1},{1,0},{2,3},{3,2},{4,8},{5,9},{6,10},{7,11},{8,4},{9,5},{10,... | collective-permute-start | bytes 983048 | tf_op jit(solution)/shard_map/feature_window/ppermute | solution.py:296
  14.8 5.1 %collective-permute-start.6 = (bf16[2,10,64,128]{3,2,1,0:T(8,128)(2,1)S(1)}, bf16[2,10,64,128]{3,2,1,0:T(8,128)(2,1)S(1)}, u32[]{:S(2)}, u32[]{:S(2)}) collective-permute-start(bf16[2,10,64,128]{3,2,1,0:T(8,128)(2,1)S(1)} %slice_dynamic-update-slice_fusion.2.h0), channel_id=1, source_target_pairs={{0,4},{4,0},{8,12},{12,8},{16,20},{20,16},{24,28},{28,24},{32,36},... | collective-permute-start | bytes 983048 | tf_op jit(solution)/shard_map/feature_window/ppermute | solution.py:293
  14.9 6.5 %copy-start.2 = (bf16[256,256]{1,0:T(8,128)(2,1)S(1)}, bf16[256,256]{1,0:T(8,128)(2,1)}, u32[]{:S(2)}) copy-start(bf16[256,256]{1,0:T(8,128)(2,1)} %w_zr.3) | copy-start | bytes 393220
  14.9 6.5 %copy-start.3 = (bf16[128,256]{1,0:T(8,128)(2,1)S(1)}, bf16[128,256]{1,0:T(8,128)(2,1)}, u32[]{:S(2)}) copy-start(bf16[128,256]{1,0:T(8,128)(2,1)} %w_msg.3) | copy-start | bytes 196612
  14.9 6.4 %copy-start.4 = (bf16[49,128]{1,0:T(8,128)(2,1)S(1)}, bf16[49,128]{1,0:T(8,128)(2,1)}, u32[]{:S(2)}) copy-start(bf16[49,128]{1,0:T(8,128)(2,1)} %w_corr.1) | copy-start | bytes 37636
  15.0 4.9 %collective-permute-start.4 = (bf16[4,6,64,128]{3,2,1,0:T(8,128)(2,1)S(1)}, bf16[4,6,64,128]{3,2,1,0:T(8,128)(2,1)S(1)}, u32[]{:S(2)}, u32[]{:S(2)}) collective-permute-start(bf16[4,6,64,128]{3,2,1,0:T(8,128)(2,1)S(1)} %pad_maximum_fusion), channel_id=1, source_target_pairs={{0,4},{4,0},{8,12},{12,8},{16,20},{20,16},{24,28},{28,24},{32,36},... | collective-permute-start | bytes 1179656 | tf_op jit(solution)/shard_map/feature_window/ppermute | solution.py:293
  19.7 1.6 %collective-permute-start.7 = (bf16[2,10,64,128]{3,2,1,0:T(8,128)(2,1)S(1)}, bf16[2,10,64,128]{3,2,1,0:T(8,128)(2,1)S(1)}, u32[]{:S(2)}, u32[]{:S(2)}) collective-permute-start(bf16[2,10,64,128]{3,2,1,0:T(8,128)(2,1)S(1)} %collective-permute-done.5.h1), channel_id=1, source_target_pairs={{0,4},{4,0},{8,12},{12,8},{16,20},{20,16},{24,28},{28,24},{32,36},... | collective-permute-start | bytes 983048 | tf_op jit(solution)/shard_map/feature_window/ppermute | solution.py:293
  24.7 8.9 %copy-start.5 = (bf16[8,320,128]{2,1,0:T(8,128)(2,1)}, bf16[8,320,128]{2,1,0:T(8,128)(2,1)S(1)}, u32[]{:S(2)}) copy-start(bf16[8,320,128]{2,1,0:T(8,128)(2,1)S(1)} %get-tuple-element.23.motion) | copy-start | bytes 1966084
  24.7 1.5 %collective-permute-start.8 = (bf16[4,192,128]{2,1,0:T(8,128)(2,1)S(1)}, bf16[4,192,128]{2,1,0:T(8,128)(2,1)S(1)}, u32[]{:S(2)}, u32[]{:S(2)}) collective-permute-start(bf16[4,192,128]{2,1,0:T(8,128)(2,1)S(1)} %get-tuple-element.20), channel_id=1, source_target_pairs={{0,4},{4,0},{8,12},{12,8},{16,20},{20,16},{24,28},{28,24},{32,36},... | collective-permute-start | bytes 589832 | tf_op jit(solution)/shard_map/first_sums/ppermute | solution.py:293
  26.3 7.3 %collective-permute-start.9 = (bf16[4,192,128]{2,1,0:T(8,128)(2,1)S(1)}, bf16[4,192,128]{2,1,0:T(8,128)(2,1)S(1)}, u32[]{:S(2)}, u32[]{:S(2)}) collective-permute-start(bf16[4,192,128]{2,1,0:T(8,128)(2,1)S(1)} %fusion.2), channel_id=1, source_target_pairs={{0,1},{1,0},{2,3},{3,2},{4,8},{5,9},{6,10},{7,11},{8,4},{9,5},{10,... | collective-permute-start | bytes 589832 | tf_op jit(solution)/shard_map/first_sums/ppermute | solution.py:296
  33.7 8.7 %copy-start = (bf16[9,128,128]{2,1,0:T(8,128)(2,1)S(1)}, bf16[9,128,128]{2,1,0:T(8,128)(2,1)}, u32[]{:S(2)}) copy-start(bf16[9,128,128]{2,1,0:T(8,128)(2,1)} %w_res.3) | copy-start | bytes 884740
  33.8 6.6 %collective-permute-start.10 = (bf16[16,64,128]{2,1,0:T(8,128)(2,1)S(1)}, bf16[16,64,128]{2,1,0:T(8,128)(2,1)S(1)}, u32[]{:S(2)}, u32[]{:S(2)}) collective-permute-start(bf16[16,64,128]{2,1,0:T(8,128)(2,1)S(1)} %get-tuple-element.28), channel_id=1, source_target_pairs={{0,1},{1,0},{2,3},{3,2},{4,5},{5,4},{6,7},{7,6},{8,9},{9,8},{10,11... | collective-permute-start | bytes 786440 | tf_op jit(solution)/shard_map/update_rows/ppermute | solution.py:288
  34.7 7.6 %collective-permute-start.11 = (bf16[16,64,128]{2,1,0:T(8,128)(2,1)S(1)}, bf16[16,64,128]{2,1,0:T(8,128)(2,1)S(1)}, u32[]{:S(2)}, u32[]{:S(2)}) collective-permute-start(bf16[16,64,128]{2,1,0:T(8,128)(2,1)S(1)} %get-tuple-element.27), channel_id=1, source_target_pairs={{0,3},{1,2},{2,1},{3,0},{4,7},{5,6},{6,5},{7,4},{8,11},{9,10},{10,... | collective-permute-start | bytes 786440 | tf_op jit(solution)/shard_map/update_rows/ppermute | solution.py:289
  43.2 1.7 %collective-permute-start.12 = (bf16[4,5,64,128]{3,2,1,0:T(8,128)(2,1)S(1)}, bf16[4,5,64,128]{3,2,1,0:T(8,128)(2,1)S(1)}, u32[]{:S(2)}, u32[]{:S(2)}) collective-permute-start(bf16[4,5,64,128]{3,2,1,0:T(8,128)(2,1)S(1)} %first_state.1.s0.state), channel_id=1, source_target_pairs={{0,4},{4,0},{8,12},{12,8},{16,20},{20,16},{24,28},{28,24},{32,36},... | collective-permute-start | bytes 983048 | tf_op jit(solution)/shard_map/first_state/ppermute | solution.py:293
  46.8 1.5 %collective-permute-start.13 = (bf16[4,192,128]{2,1,0:T(8,128)(2,1)S(1)}, bf16[4,192,128]{2,1,0:T(8,128)(2,1)S(1)}, u32[]{:S(2)}, u32[]{:S(2)}) collective-permute-start(bf16[4,192,128]{2,1,0:T(8,128)(2,1)S(1)} %get-tuple-element.26), channel_id=1, source_target_pairs={{0,4},{4,0},{8,12},{12,8},{16,20},{20,16},{24,28},{28,24},{32,36},... | collective-permute-start | bytes 589832 | tf_op jit(solution)/shard_map/second_sums/ppermute | solution.py:293
  48.4 6.2 %collective-permute-start.14 = (bf16[2,192,128]{2,1,0:T(8,128)(2,1)S(1)}, bf16[2,192,128]{2,1,0:T(8,128)(2,1)S(1)}, u32[]{:S(2)}, u32[]{:S(2)}) collective-permute-start(bf16[2,192,128]{2,1,0:T(8,128)(2,1)S(1)} %slice.108), channel_id=1, source_target_pairs={{0,1},{1,0},{2,3},{3,2},{4,8},{5,9},{6,10},{7,11},{8,4},{9,5},{10,... | collective-permute-start | bytes 294920 | tf_op jit(solution)/shard_map/second_sums/ppermute | solution.py:296
  54.7 4.0 %collective-permute-start.15 = (bf16[2,1,64,128]{3,2,1,0:T(8,128)(2,1)S(1)}, bf16[2,1,64,128]{3,2,1,0:T(8,128)(2,1)S(1)}, u32[]{:S(2)}, u32[]{:S(2)}) collective-permute-start(bf16[2,1,64,128]{3,2,1,0:T(8,128)(2,1)S(1)} %get-tuple-element.38), channel_id=1, source_target_pairs={{0,1},{1,0},{2,3},{3,2},{4,5},{5,4},{6,7},{7,6},{8,9},{9,8},{10,11... | collective-permute-start | bytes 98312 | tf_op jit(solution)/shard_map/second_sums/ppermute | solution.py:288
  54.8 5.2 %collective-permute-start.16 = (bf16[2,1,64,128]{3,2,1,0:T(8,128)(2,1)S(1)}, bf16[2,1,64,128]{3,2,1,0:T(8,128)(2,1)S(1)}, u32[]{:S(2)}, u32[]{:S(2)}) collective-permute-start(bf16[2,1,64,128]{3,2,1,0:T(8,128)(2,1)S(1)} %get-tuple-element.37), channel_id=1, source_target_pairs={{0,3},{1,2},{2,1},{3,0},{4,7},{5,6},{6,5},{7,4},{8,11},{9,10},{10,... | collective-permute-start | bytes 98312 | tf_op jit(solution)/shard_map/second_sums/ppermute | solution.py:289
  (3 other events, 4.3 us)

commit v9 on v8

--- a/solution.py
+++ b/solution.py
@@ -84,17 +84,7 @@
     part_other[...] = acc[4:].astype(BF16)
 
 
-def first_kernel(
-    table, c0, c1, c23, h0, h1, h2, h3, w_corr, w_zr, w_q, w_msg,
-    part, part_other, hid, hid_first, hid_last, motion_out, base,
-    feat, rim, ctx, acc, flip, spread, edge, idx,
-):
-    pieces = ((c0, 0, h0), (c1, 0, h1), (c23, 0, h2), (c23, 2, h3))
-    count = read_table(table, idx)
-    acc[...] = jnp.zeros_like(acc)
-    for half, (center, _, halo) in enumerate(pieces[:2]):
-        frames = pl.ds(2 * half, 2)
-        base[frames, 0], base[frames, 1:4], base[frames, 4] = halo[:, 8], center[:, 3:6], halo[:, 9]
+def tables_kernel(w_corr, flip, spread, edge):
     ends = [lax.broadcasted_iota(jnp.int32, (WIDTH, WIDTH), k) for k in range(2)]
     flip[...] = jnp.where(ends[0] + ends[1] == WIDTH - 1, 1.0, 0.0).astype(BF16)
     lane, tap = [lax.broadcasted_iota(jnp.int32, (CHANS, SPAN * SPAN), k) for k in range(2)]
@@ -109,6 +99,19 @@
     inside = (place >= 0) & (place < 32) & ((place & 7) < SPAN) & (at >= 0) & (at < WIDTH)
     inside = inside & ((place < 24) | (lane >= WIDTH))
     edge[...] = jnp.where(inside, 1.0 / CHANS**0.5, 0.0)
+
+
+def first_kernel(
+    table, c0, c1, c23, h0, h1, h2, h3, flip, spread, edge, w_zr, w_q, w_msg,
+    part, part_other, hid, hid_first, hid_last, motion_out, base,
+    feat, rim, ctx, acc, idx,
+):
+    pieces = ((c0, 0, h0), (c1, 0, h1), (c23, 0, h2), (c23, 2, h3))
+    count = read_table(table, idx)
+    acc[...] = jnp.zeros_like(acc)
+    for half, (center, _, halo) in enumerate(pieces[:2]):
+        frames = pl.ds(2 * half, 2)
+        base[frames, 0], base[frames, 1:4], base[frames, 4] = halo[:, 8], center[:, 3:6], halo[:, 9]
     place = (lax.broadcasted_iota(jnp.int32, (WIDTH, CHANS), 1) & (WIDTH - 1)) - 4
 
     def body(i, carry):
@@ -317,8 +320,19 @@
             ],
             axis=1,
         )
-    halo, pairs = lax.optimization_barrier((halo, pairs))
+    halo, pairs, w_corr = lax.optimization_barrier((halo, pairs, w_corr))
     idx, flags = slot_table(pairs, index), row_flags(row)
+    tables = call(
+        tables_kernel,
+        [
+            jax.ShapeDtypeStruct((WIDTH, WIDTH), BF16),
+            jax.ShapeDtypeStruct((CHANS, CHANS), BF16),
+            jax.ShapeDtypeStruct((WIDTH, CHANS), F32),
+        ],
+        [],
+        2_000_000,
+        w_corr,
+    )
     with jax.named_scope("feature_window"):
         near_halo = swap_chip(halo)
         halo_other = swap_core(halo)
@@ -342,13 +356,10 @@
                 pltpu.VMEM((GROUP, 11, WIDTH, CHANS), BF16),
                 pltpu.VMEM((GROUP, 5, WIDTH, CHANS), BF16),
                 pltpu.VMEM((SLOTS, OWN, CHANS), F32),
-                pltpu.VMEM((WIDTH, WIDTH), BF16),
-                pltpu.VMEM((CHANS, CHANS), BF16),
-                pltpu.VMEM((WIDTH, CHANS), F32),
                 pltpu.SMEM((SLOTS,), jnp.int32),
             ],
             2_000_000_000,
-            idx, center, near_center, center_other, halo, near_halo, halo_other, near_halo_other, w_corr, w_zr, w_q, w_msg,
+            idx, center, near_center, center_other, halo, near_halo, halo_other, near_halo_other, *tables, w_zr, w_q, w_msg,
         )
 
     with jax.named_scope("first_sums"):

time: 61.2 us -> 61.1 us (level)
    pallas_call x4 -> x5, Pallas kernels: 6.99 us -> 7.08 us  [call(): pl.pallas_call(kernel, out_shape=outs, in_specs=[VM] * len(args), out_spe...]
where the time goes in v9:
time: 61.1 us; the launch traced here: 60.9 us
  starting transfers between devices  27.5 us (45%)
  waiting for transfers between devices  24 us (39%)
  Pallas kernels  7.08 us (12%)
  local copies, waits for them, and re-layouts  1.25 us (2%)
  other arithmetic  0.76 us (1%)
    ppermute x4, starting transfers between devices, swap_chip(): return lax.ppermute(x, ('frames', 'rows'), chip_swap)  16.3 us
    ppermute x4, waiting for transfers between devices, swap_chip(): return lax.ppermute(x, ('frames', 'rows'), chip_swap)  10 us
    pallas_call x5, Pallas kernels, call(): pl.pallas_call(kernel, out_shape=outs, in_specs=[VM] * len(args), out_spe...  7.08 us
    ppermute x3, starting transfers between devices, rows_swaps(): second = lax.ppermute(jnp.where(odd, to_below, to_above), 'rows', odd_swap)  6.63 us
    ppermute x6, waiting for transfers between devices, swap_core(): return lax.ppermute(x, 'frames', core_swap)  5.66 us
    ppermute x3, waiting for transfers between devices, rows_swaps(): first = lax.ppermute(jnp.where(odd, to_above, to_below), 'rows', even_swap)  5.12 us
    ppermute x3, waiting for transfers between devices, rows_swaps(): second = lax.ppermute(jnp.where(odd, to_below, to_above), 'rows', odd_swap)  3.21 us
    ppermute x3, starting transfers between devices, rows_swaps(): first = lax.ppermute(jnp.where(odd, to_above, to_below), 'rows', even_swap)  2.7 us
  transfers between devices with their start and end apart: 17, of which 11 were waited for; matrix products, arithmetic and copies ran while one was open for 1% of the time, Pallas kernels for 0%

profile of v9, /device:TPU:6, one launch (start us, length us, event | category | flops | bytes accessed | tf_op | source)
XLA Modules:
  0.0 60.9 jit_solution(8609868770026325935)
XLA Ops:
  0.9 1.7 %collective-permute-start.1 = (bf16[2,4,64,128]{3,2,1,0:T(8,128)(2,1)S(1)}, bf16[2,4,64,128]{3,2,1,0:T(8,128)(2,1)S(1)}, u32[]{:S(2)}, u32[]{:S(2)}) collective-permute-start(bf16[2,4,64,128]{3,2,1,0:T(8,128)(2,1)S(1)} %get-tuple-element.44), channel_id=1, source_target_pairs={{0,1},{1,0},{2,3},{3,2},{4,5},{5,4},{6,7},{7,6},{8,9},{9,8},{10,11... | collective-permute-start | bytes 393224 | tf_op jit(solution)/shard_map/feature_rows/ppermute | solution.py:291
  2.6 2.2 %collective-permute-start.2 = (bf16[2,4,64,128]{3,2,1,0:T(8,128)(2,1)S(1)}, bf16[2,4,64,128]{3,2,1,0:T(8,128)(2,1)S(1)}, u32[]{:S(2)}, u32[]{:S(2)}) collective-permute-start(bf16[2,4,64,128]{3,2,1,0:T(8,128)(2,1)S(1)} %get-tuple-element.43), channel_id=1, source_target_pairs={{0,3},{1,2},{2,1},{3,0},{4,7},{5,6},{6,5},{7,4},{8,11},{9,10},{10,... | collective-permute-start | bytes 393224 | tf_op jit(solution)/shard_map/feature_rows/ppermute | solution.py:292
  4.8 0.8 %collective-permute-start = (bf16[2,1,64,128]{3,2,1,0:T(8,128)(2,1)S(1)}, bf16[2,1,64,128]{3,2,1,0:T(8,128)(2,1)S(1)}, u32[]{:S(2)}, u32[]{:S(2)}) collective-permute-start(bf16[2,1,64,128]{3,2,1,0:T(8,128)(2,1)S(1)} %slice_select_fusion), channel_id=1, source_target_pairs={{0,2},{1,3},{2,0},{3,1},{4,6},{5,7},{6,4},{7,5},{8,10},{9,11},{10,... | collective-permute-start | bytes 98312 | tf_op jit(solution)/shard_map/feature_rows/ppermute | solution.py:304
  5.7 5.1 %collective-permute-start.3 = (bf16[2,6,64,128]{3,2,1,0:T(8,128)(2,1)S(1)}, bf16[2,6,64,128]{3,2,1,0:T(8,128)(2,1)S(1)}, u32[]{:S(2)}, u32[]{:S(2)}) collective-permute-start(bf16[2,6,64,128]{3,2,1,0:T(8,128)(2,1)S(1)} %constant_dynamic-update-slice_fusion.c0), channel_id=1, source_target_pairs={{0,1},{1,0},{2,3},{3,2},{4,8},{5,9},{6,10},{7,11},{8,4},{9,5},{10,... | collective-permute-start | bytes 589832 | tf_op jit(solution)/shard_map/feature_rows/ppermute | solution.py:299
  11.0 3.8 %collective-permute-start.5 = (bf16[2,10,64,128]{3,2,1,0:T(8,128)(2,1)S(1)}, bf16[2,10,64,128]{3,2,1,0:T(8,128)(2,1)S(1)}, u32[]{:S(2)}, u32[]{:S(2)}) collective-permute-start(bf16[2,10,64,128]{3,2,1,0:T(8,128)(2,1)S(1)} %slice_dynamic-update-slice_fusion.2.h0), channel_id=1, source_target_pairs={{0,1},{1,0},{2,3},{3,2},{4,8},{5,9},{6,10},{7,11},{8,4},{9,5},{10,... | collective-permute-start | bytes 983048 | tf_op jit(solution)/shard_map/feature_window/ppermute | solution.py:299
  15.8 3.9 %collective-permute-done.5.h1 = bf16[2,10,64,128]{3,2,1,0:T(8,128)(2,1)S(1)} collective-permute-done((bf16[2,10,64,128]{3,2,1,0:T(8,128)(2,1)S(1)}, bf16[2,10,64,128]{3,2,1,0:T(8,128)(2,1)S(1)}, u32[]{:S(2)}, u32[]{:S(2)}) %collective-permute-start.5) | collective-permute-done | bytes 327712 | tf_op jit(solution)/shard_map/feature_window/ppermute | solution.py:299
  19.9 1.4 %collective-permute-done.7.h3 = bf16[2,10,64,128]{3,2,1,0:T(8,128)(2,1)S(1)} collective-permute-done((bf16[2,10,64,128]{3,2,1,0:T(8,128)(2,1)S(1)}, bf16[2,10,64,128]{3,2,1,0:T(8,128)(2,1)S(1)}, u32[]{:S(2)}, u32[]{:S(2)}) %collective-permute-start.7) | collective-permute-done | bytes 327712 | tf_op jit(solution)/shard_map/feature_window/ppermute | solution.py:296
  21.3 3.2 %first_iteration.1 = (bf16[4,192,128]{2,1,0:T(8,128)(2,1)S(1)}, bf16[4,192,128]{2,1,0:T(8,128)(2,1)S(1)}, f32[8,192,128]{2,1,0:T(8,128)S(1)}, bf16[8,64,128]{2,1...) custom-call(s32[1,8]{1,0:T(1,128)S(1)} %add_bitcast_fusion.table, ...), custom_call_target="tpu_custom_call" | custom-call | flops 2000000000 | bytes 2957344 | tf_op jit(solution)/shard_map/first_iteration/pallas_call | solution.py:237
  24.8 1.3 %collective-permute-done.8 = bf16[4,192,128]{2,1,0:T(8,128)(2,1)S(1)} collective-permute-done((bf16[4,192,128]{2,1,0:T(8,128)(2,1)S(1)}, bf16[4,192,128]{2,1,0:T(8,128)(2,1)S(1)}, u32[]{:S(2)}, u32[]{:S(2)}) %collective-permute-start.8) | collective-permute-done | bytes 196640 | tf_op jit(solution)/shard_map/first_sums/ppermute | solution.py:296
  26.2 3.8 %collective-permute-start.9 = (bf16[4,192,128]{2,1,0:T(8,128)(2,1)S(1)}, bf16[4,192,128]{2,1,0:T(8,128)(2,1)S(1)}, u32[]{:S(2)}, u32[]{:S(2)}) collective-permute-start(bf16[4,192,128]{2,1,0:T(8,128)(2,1)S(1)} %fusion.2), channel_id=1, source_target_pairs={{0,1},{1,0},{2,3},{3,2},{4,8},{5,9},{6,10},{7,11},{8,4},{9,5},{10,... | collective-permute-start | bytes 589832 | tf_op jit(solution)/shard_map/first_sums/ppermute | solution.py:299
  30.0 3.5 %collective-permute-done.9 = bf16[4,192,128]{2,1,0:T(8,128)(2,1)S(1)} collective-permute-done((bf16[4,192,128]{2,1,0:T(8,128)(2,1)S(1)}, bf16[4,192,128]{2,1,0:T(8,128)(2,1)S(1)}, u32[]{:S(2)}, u32[]{:S(2)}) %collective-permute-start.9) | collective-permute-done | bytes 196640 | tf_op jit(solution)/shard_map/first_sums/ppermute | solution.py:299
  33.7 0.9 %collective-permute-start.10 = (bf16[16,64,128]{2,1,0:T(8,128)(2,1)S(1)}, bf16[16,64,128]{2,1,0:T(8,128)(2,1)S(1)}, u32[]{:S(2)}, u32[]{:S(2)}) collective-permute-start(bf16[16,64,128]{2,1,0:T(8,128)(2,1)S(1)} %get-tuple-element.36), channel_id=1, source_target_pairs={{0,1},{1,0},{2,3},{3,2},{4,5},{5,4},{6,7},{7,6},{8,9},{9,8},{10,11... | collective-permute-start | bytes 786440 | tf_op jit(solution)/shard_map/update_rows/ppermute | solution.py:291
  34.6 2.2 %collective-permute-start.11 = (bf16[16,64,128]{2,1,0:T(8,128)(2,1)S(1)}, bf16[16,64,128]{2,1,0:T(8,128)(2,1)S(1)}, u32[]{:S(2)}, u32[]{:S(2)}) collective-permute-start(bf16[16,64,128]{2,1,0:T(8,128)(2,1)S(1)} %get-tuple-element.35), channel_id=1, source_target_pairs={{0,3},{1,2},{2,1},{3,0},{4,7},{5,6},{6,5},{7,4},{8,11},{9,10},{10,... | collective-permute-start | bytes 786440 | tf_op jit(solution)/shard_map/update_rows/ppermute | solution.py:292
  36.8 3.5 %collective-permute-done.10.first = bf16[16,64,128]{2,1,0:T(8,128)(2,1)S(1)} collective-permute-done((bf16[16,64,128]{2,1,0:T(8,128)(2,1)S(1)}, bf16[16,64,128]{2,1,0:T(8,128)(2,1)S(1)}, u32[]{:S(2)}, u32[]{:S(2)}) %collective-permute-start.10) | collective-permute-done | bytes 262176 | tf_op jit(solution)/shard_map/update_rows/ppermute | solution.py:291
  40.3 1.9 %collective-permute-done.11.second = bf16[16,64,128]{2,1,0:T(8,128)(2,1)S(1)} collective-permute-done((bf16[16,64,128]{2,1,0:T(8,128)(2,1)S(1)}, bf16[16,64,128]{2,1,0:T(8,128)(2,1)S(1)}, u32[]{:S(2)}, u32[]{:S(2)}) %collective-permute-start.11) | collective-permute-done | bytes 262176 | tf_op jit(solution)/shard_map/update_rows/ppermute | solution.py:292
  43.2 1.6 %collective-permute-done.12.s1 = bf16[4,5,64,128]{3,2,1,0:T(8,128)(2,1)S(1)} collective-permute-done((bf16[4,5,64,128]{3,2,1,0:T(8,128)(2,1)S(1)}, bf16[4,5,64,128]{3,2,1,0:T(8,128)(2,1)S(1)}, u32[]{:S(2)}, u32[]{:S(2)}) %collective-permute-start.12) | collective-permute-done | bytes 327712 | tf_op jit(solution)/shard_map/first_state/ppermute | solution.py:296
  44.8 1.9 %second_iteration.1 = (bf16[4,192,128]{2,1,0:T(8,128)(2,1)S(1)}, bf16[4,192,128]{2,1,0:T(8,128)(2,1)S(1)}) custom-call(s32[1,8]{1,0:T(1,128)S(1)} %add_bitcast_fusion.table, f32[8,128]{1,0:T(8,128)S(1)} %iota.34.flags, bf16[4,5,64,128]{3,2,1,0:T(8,128)(2,1)S(1)} %first_state.1.s0.state, bf16[4,5,64,128]{3,2,1,0:T(8,128)(2,1)S(1)} %collective-permute-done.12.s1, ...), custom_call_target="tpu_custom_call" | custom-call | flops 1500000000 | bytes 3412000 | tf_op jit(solution)/shard_map/second_iteration/pallas_call | solution.py:237
  47.0 1.3 %collective-permute-done.13 = bf16[4,192,128]{2,1,0:T(8,128)(2,1)S(1)} collective-permute-done((bf16[4,192,128]{2,1,0:T(8,128)(2,1)S(1)}, bf16[4,192,128]{2,1,0:T(8,128)(2,1)S(1)}, u32[]{:S(2)}, u32[]{:S(2)}) %collective-permute-start.13) | collective-permute-done | bytes 196640 | tf_op jit(solution)/shard_map/second_sums/ppermute | solution.py:296
  48.4 3.6 %collective-permute-start.14 = (bf16[2,192,128]{2,1,0:T(8,128)(2,1)S(1)}, bf16[2,192,128]{2,1,0:T(8,128)(2,1)S(1)}, u32[]{:S(2)}, u32[]{:S(2)}) collective-permute-start(bf16[2,192,128]{2,1,0:T(8,128)(2,1)S(1)} %slice.108), channel_id=1, source_target_pairs={{0,1},{1,0},{2,3},{3,2},{4,8},{5,9},{6,10},{7,11},{8,4},{9,5},{10,... | collective-permute-start | bytes 294920 | tf_op jit(solution)/shard_map/second_sums/ppermute | solution.py:299
  51.9 2.7 %collective-permute-done.14 = bf16[2,192,128]{2,1,0:T(8,128)(2,1)S(1)} collective-permute-done((bf16[2,192,128]{2,1,0:T(8,128)(2,1)S(1)}, bf16[2,192,128]{2,1,0:T(8,128)(2,1)S(1)}, u32[]{:S(2)}, u32[]{:S(2)}) %collective-permute-start.14) | collective-permute-done | bytes 98336 | tf_op jit(solution)/shard_map/second_sums/ppermute | solution.py:299
  54.7 2.3 %collective-permute-start.16 = (bf16[2,1,64,128]{3,2,1,0:T(8,128)(2,1)S(1)}, bf16[2,1,64,128]{3,2,1,0:T(8,128)(2,1)S(1)}, u32[]{:S(2)}, u32[]{:S(2)}) collective-permute-start(bf16[2,1,64,128]{3,2,1,0:T(8,128)(2,1)S(1)} %get-tuple-element.45), channel_id=1, source_target_pairs={{0,3},{1,2},{2,1},{3,0},{4,7},{5,6},{6,5},{7,4},{8,11},{9,10},{10,... | collective-permute-start | bytes 98312 | tf_op jit(solution)/shard_map/second_sums/ppermute | solution.py:292
  57.0 1.6 %collective-permute-done.15.first = bf16[2,1,64,128]{3,2,1,0:T(8,128)(2,1)S(1)} collective-permute-done((bf16[2,1,64,128]{3,2,1,0:T(8,128)(2,1)S(1)}, bf16[2,1,64,128]{3,2,1,0:T(8,128)(2,1)S(1)}, u32[]{:S(2)}, u32[]{:S(2)}) %collective-permute-start.15) | collective-permute-done | bytes 32800 | tf_op jit(solution)/shard_map/second_sums/ppermute | solution.py:291
  58.6 1.3 %collective-permute-done.16.second = bf16[2,1,64,128]{3,2,1,0:T(8,128)(2,1)S(1)} collective-permute-done((bf16[2,1,64,128]{3,2,1,0:T(8,128)(2,1)S(1)}, bf16[2,1,64,128]{3,2,1,0:T(8,128)(2,1)S(1)}, u32[]{:S(2)}, u32[]{:S(2)}) %collective-permute-start.16) | collective-permute-done | bytes 32800 | tf_op jit(solution)/shard_map/second_sums/ppermute | solution.py:292
  60.0 1.0 %last_state.1 = bf16[2,3,64,128]{3,2,1,0:T(8,128)(2,1)} custom-call(f32[8,128]{1,0:T(8,128)S(1)} %iota.34.flags, bf16[4,5,64,128]{3,2,1,0:T(8,128)(2,1)S(1)} %first_state.1.s0.state, bf16[2,3,64,128]{3,2,1,0:T(8,128)(2,1)S(1)} %bitcast.10, bf16[2,1,64,128]{3,2,1,0:T(8,128)(2,1)S(1)} %collective-permute-done.15.first, ...), custom_call_target="tpu_custom_call" | custom-call | flops 120000000 | bytes 790528 | tf_op jit(solution)/shard_map/last_state/pallas_call | solution.py:237
  (65 shorter events, 4.2 us)
Async XLA Ops:
  0.9 9.9 %collective-permute-start.1 = (bf16[2,4,64,128]{3,2,1,0:T(8,128)(2,1)S(1)}, bf16[2,4,64,128]{3,2,1,0:T(8,128)(2,1)S(1)}, u32[]{:S(2)}, u32[]{:S(2)}) collective-permute-start(bf16[2,4,64,128]{3,2,1,0:T(8,128)(2,1)S(1)} %get-tuple-element.44), channel_id=1, source_target_pairs={{0,1},{1,0},{2,3},{3,2},{4,5},{5,4},{6,7},{7,6},{8,9},{9,8},{10,11... | collective-permute-start | bytes 393224 | tf_op jit(solution)/shard_map/feature_rows/ppermute | solution.py:291
  2.6 8.2 %collective-permute-start.2 = (bf16[2,4,64,128]{3,2,1,0:T(8,128)(2,1)S(1)}, bf16[2,4,64,128]{3,2,1,0:T(8,128)(2,1)S(1)}, u32[]{:S(2)}, u32[]{:S(2)}) collective-permute-start(bf16[2,4,64,128]{3,2,1,0:T(8,128)(2,1)S(1)} %get-tuple-element.43), channel_id=1, source_target_pairs={{0,3},{1,2},{2,1},{3,0},{4,7},{5,6},{6,5},{7,4},{8,11},{9,10},{10,... | collective-permute-start | bytes 393224 | tf_op jit(solution)/shard_map/feature_rows/ppermute | solution.py:292
  4.8 6.0 %collective-permute-start = (bf16[2,1,64,128]{3,2,1,0:T(8,128)(2,1)S(1)}, bf16[2,1,64,128]{3,2,1,0:T(8,128)(2,1)S(1)}, u32[]{:S(2)}, u32[]{:S(2)}) collective-permute-start(bf16[2,1,64,128]{3,2,1,0:T(8,128)(2,1)S(1)} %slice_select_fusion), channel_id=1, source_target_pairs={{0,2},{1,3},{2,0},{3,1},{4,6},{5,7},{6,4},{7,5},{8,10},{9,11},{10,... | collective-permute-start | bytes 98312 | tf_op jit(solution)/shard_map/feature_rows/ppermute | solution.py:304
  5.7 9.2 %collective-permute-start.3 = (bf16[2,6,64,128]{3,2,1,0:T(8,128)(2,1)S(1)}, bf16[2,6,64,128]{3,2,1,0:T(8,128)(2,1)S(1)}, u32[]{:S(2)}, u32[]{:S(2)}) collective-permute-start(bf16[2,6,64,128]{3,2,1,0:T(8,128)(2,1)S(1)} %constant_dynamic-update-slice_fusion.c0), channel_id=1, source_target_pairs={{0,1},{1,0},{2,3},{3,2},{4,8},{5,9},{6,10},{7,11},{8,4},{9,5},{10,... | collective-permute-start | bytes 589832 | tf_op jit(solution)/shard_map/feature_rows/ppermute | solution.py:299
  10.9 4.0 %copy-start.9 = (s32[256,3]{0,1:T(4,128)S(1)}, s32[256,3]{0,1:T(4,128)}, u32[]{:S(2)}) copy-start(s32[256,3]{0,1:T(4,128)} %param.10) | copy-start | bytes 9220
  10.9 10.4 %copy-start.2 = (bf16[9,256,128]{2,1,0:T(8,128)(2,1)S(1)}, bf16[9,256,128]{2,1,0:T(8,128)(2,1)}, u32[]{:S(2)}) copy-start(bf16[9,256,128]{2,1,0:T(8,128)(2,1)} %w_q.3) | copy-start | bytes 1769476
  11.0 8.7 %collective-permute-start.5 = (bf16[2,10,64,128]{3,2,1,0:T(8,128)(2,1)S(1)}, bf16[2,10,64,128]{3,2,1,0:T(8,128)(2,1)S(1)}, u32[]{:S(2)}, u32[]{:S(2)}) collective-permute-start(bf16[2,10,64,128]{3,2,1,0:T(8,128)(2,1)S(1)} %slice_dynamic-update-slice_fusion.2.h0), channel_id=1, source_target_pairs={{0,1},{1,0},{2,3},{3,2},{4,8},{5,9},{6,10},{7,11},{8,4},{9,5},{10,... | collective-permute-start | bytes 983048 | tf_op jit(solution)/shard_map/feature_window/ppermute | solution.py:299
  14.8 5.1 %collective-permute-start.6 = (bf16[2,10,64,128]{3,2,1,0:T(8,128)(2,1)S(1)}, bf16[2,10,64,128]{3,2,1,0:T(8,128)(2,1)S(1)}, u32[]{:S(2)}, u32[]{:S(2)}) collective-permute-start(bf16[2,10,64,128]{3,2,1,0:T(8,128)(2,1)S(1)} %slice_dynamic-update-slice_fusion.2.h0), channel_id=1, source_target_pairs={{0,4},{4,0},{8,12},{12,8},{16,20},{20,16},{24,28},{28,24},{32,36},... | collective-permute-start | bytes 983048 | tf_op jit(solution)/shard_map/feature_window/ppermute | solution.py:296
  14.9 6.5 %copy-start.3 = (bf16[256,256]{1,0:T(8,128)(2,1)S(1)}, bf16[256,256]{1,0:T(8,128)(2,1)}, u32[]{:S(2)}) copy-start(bf16[256,256]{1,0:T(8,128)(2,1)} %w_zr.3) | copy-start | bytes 393220
  14.9 6.4 %copy-start.4 = (bf16[128,256]{1,0:T(8,128)(2,1)S(1)}, bf16[128,256]{1,0:T(8,128)(2,1)}, u32[]{:S(2)}) copy-start(bf16[128,256]{1,0:T(8,128)(2,1)} %w_msg.3) | copy-start | bytes 196612
  15.0 4.9 %collective-permute-start.4 = (bf16[4,6,64,128]{3,2,1,0:T(8,128)(2,1)S(1)}, bf16[4,6,64,128]{3,2,1,0:T(8,128)(2,1)S(1)}, u32[]{:S(2)}, u32[]{:S(2)}) collective-permute-start(bf16[4,6,64,128]{3,2,1,0:T(8,128)(2,1)S(1)} %pad_maximum_fusion), channel_id=1, source_target_pairs={{0,4},{4,0},{8,12},{12,8},{16,20},{20,16},{24,28},{28,24},{32,36},... | collective-permute-start | bytes 1179656 | tf_op jit(solution)/shard_map/feature_window/ppermute | solution.py:296
  19.7 1.6 %collective-permute-start.7 = (bf16[2,10,64,128]{3,2,1,0:T(8,128)(2,1)S(1)}, bf16[2,10,64,128]{3,2,1,0:T(8,128)(2,1)S(1)}, u32[]{:S(2)}, u32[]{:S(2)}) collective-permute-start(bf16[2,10,64,128]{3,2,1,0:T(8,128)(2,1)S(1)} %collective-permute-done.5.h1), channel_id=1, source_target_pairs={{0,4},{4,0},{8,12},{12,8},{16,20},{20,16},{24,28},{28,24},{32,36},... | collective-permute-start | bytes 983048 | tf_op jit(solution)/shard_map/feature_window/ppermute | solution.py:296
  24.6 8.9 %copy-start.5 = (bf16[8,320,128]{2,1,0:T(8,128)(2,1)}, bf16[8,320,128]{2,1,0:T(8,128)(2,1)S(1)}, u32[]{:S(2)}) copy-start(bf16[8,320,128]{2,1,0:T(8,128)(2,1)S(1)} %get-tuple-element.31.motion) | copy-start | bytes 1966084
  24.6 1.5 %collective-permute-start.8 = (bf16[4,192,128]{2,1,0:T(8,128)(2,1)S(1)}, bf16[4,192,128]{2,1,0:T(8,128)(2,1)S(1)}, u32[]{:S(2)}, u32[]{:S(2)}) collective-permute-start(bf16[4,192,128]{2,1,0:T(8,128)(2,1)S(1)} %get-tuple-element.28), channel_id=1, source_target_pairs={{0,4},{4,0},{8,12},{12,8},{16,20},{20,16},{24,28},{28,24},{32,36},... | collective-permute-start | bytes 589832 | tf_op jit(solution)/shard_map/first_sums/ppermute | solution.py:296
  26.2 7.3 %collective-permute-start.9 = (bf16[4,192,128]{2,1,0:T(8,128)(2,1)S(1)}, bf16[4,192,128]{2,1,0:T(8,128)(2,1)S(1)}, u32[]{:S(2)}, u32[]{:S(2)}) collective-permute-start(bf16[4,192,128]{2,1,0:T(8,128)(2,1)S(1)} %fusion.2), channel_id=1, source_target_pairs={{0,1},{1,0},{2,3},{3,2},{4,8},{5,9},{6,10},{7,11},{8,4},{9,5},{10,... | collective-permute-start | bytes 589832 | tf_op jit(solution)/shard_map/first_sums/ppermute | solution.py:299
  33.6 8.7 %copy-start = (bf16[9,128,128]{2,1,0:T(8,128)(2,1)S(1)}, bf16[9,128,128]{2,1,0:T(8,128)(2,1)}, u32[]{:S(2)}) copy-start(bf16[9,128,128]{2,1,0:T(8,128)(2,1)} %w_res.3) | copy-start | bytes 884740
  33.7 6.6 %collective-permute-start.10 = (bf16[16,64,128]{2,1,0:T(8,128)(2,1)S(1)}, bf16[16,64,128]{2,1,0:T(8,128)(2,1)S(1)}, u32[]{:S(2)}, u32[]{:S(2)}) collective-permute-start(bf16[16,64,128]{2,1,0:T(8,128)(2,1)S(1)} %get-tuple-element.36), channel_id=1, source_target_pairs={{0,1},{1,0},{2,3},{3,2},{4,5},{5,4},{6,7},{7,6},{8,9},{9,8},{10,11... | collective-permute-start | bytes 786440 | tf_op jit(solution)/shard_map/update_rows/ppermute | solution.py:291
  34.6 7.6 %collective-permute-start.11 = (bf16[16,64,128]{2,1,0:T(8,128)(2,1)S(1)}, bf16[16,64,128]{2,1,0:T(8,128)(2,1)S(1)}, u32[]{:S(2)}, u32[]{:S(2)}) collective-permute-start(bf16[16,64,128]{2,1,0:T(8,128)(2,1)S(1)} %get-tuple-element.35), channel_id=1, source_target_pairs={{0,3},{1,2},{2,1},{3,0},{4,7},{5,6},{6,5},{7,4},{8,11},{9,10},{10,... | collective-permute-start | bytes 786440 | tf_op jit(solution)/shard_map/update_rows/ppermute | solution.py:292
  42.3 2.5 %copy-start.6 = (bf16[8,320,128]{2,1,0:T(8,128)(2,1)S(1)}, bf16[8,320,128]{2,1,0:T(8,128)(2,1)}, u32[]{:S(2)}) copy-start(bf16[8,320,128]{2,1,0:T(8,128)(2,1)} %copy-done.5) | copy-start | bytes 1966084
  43.1 1.7 %collective-permute-start.12 = (bf16[4,5,64,128]{3,2,1,0:T(8,128)(2,1)S(1)}, bf16[4,5,64,128]{3,2,1,0:T(8,128)(2,1)S(1)}, u32[]{:S(2)}, u32[]{:S(2)}) collective-permute-start(bf16[4,5,64,128]{3,2,1,0:T(8,128)(2,1)S(1)} %first_state.1.s0.state), channel_id=1, source_target_pairs={{0,4},{4,0},{8,12},{12,8},{16,20},{20,16},{24,28},{28,24},{32,36},... | collective-permute-start | bytes 983048 | tf_op jit(solution)/shard_map/first_state/ppermute | solution.py:296
  46.8 1.5 %collective-permute-start.13 = (bf16[4,192,128]{2,1,0:T(8,128)(2,1)S(1)}, bf16[4,192,128]{2,1,0:T(8,128)(2,1)S(1)}, u32[]{:S(2)}, u32[]{:S(2)}) collective-permute-start(bf16[4,192,128]{2,1,0:T(8,128)(2,1)S(1)} %get-tuple-element.34), channel_id=1, source_target_pairs={{0,4},{4,0},{8,12},{12,8},{16,20},{20,16},{24,28},{28,24},{32,36},... | collective-permute-start | bytes 589832 | tf_op jit(solution)/shard_map/second_sums/ppermute | solution.py:296
  48.4 6.2 %collective-permute-start.14 = (bf16[2,192,128]{2,1,0:T(8,128)(2,1)S(1)}, bf16[2,192,128]{2,1,0:T(8,128)(2,1)S(1)}, u32[]{:S(2)}, u32[]{:S(2)}) collective-permute-start(bf16[2,192,128]{2,1,0:T(8,128)(2,1)S(1)} %slice.108), channel_id=1, source_target_pairs={{0,1},{1,0},{2,3},{3,2},{4,8},{5,9},{6,10},{7,11},{8,4},{9,5},{10,... | collective-permute-start | bytes 294920 | tf_op jit(solution)/shard_map/second_sums/ppermute | solution.py:299
  54.6 4.0 %collective-permute-start.15 = (bf16[2,1,64,128]{3,2,1,0:T(8,128)(2,1)S(1)}, bf16[2,1,64,128]{3,2,1,0:T(8,128)(2,1)S(1)}, u32[]{:S(2)}, u32[]{:S(2)}) collective-permute-start(bf16[2,1,64,128]{3,2,1,0:T(8,128)(2,1)S(1)} %get-tuple-element.46), channel_id=1, source_target_pairs={{0,1},{1,0},{2,3},{3,2},{4,5},{5,4},{6,7},{7,6},{8,9},{9,8},{10,11... | collective-permute-start | bytes 98312 | tf_op jit(solution)/shard_map/second_sums/ppermute | solution.py:291
  54.7 5.2 %collective-permute-start.16 = (bf16[2,1,64,128]{3,2,1,0:T(8,128)(2,1)S(1)}, bf16[2,1,64,128]{3,2,1,0:T(8,128)(2,1)S(1)}, u32[]{:S(2)}, u32[]{:S(2)}) collective-permute-start(bf16[2,1,64,128]{3,2,1,0:T(8,128)(2,1)S(1)} %get-tuple-element.45), channel_id=1, source_target_pairs={{0,3},{1,2},{2,1},{3,0},{4,7},{5,6},{6,5},{7,4},{8,11},{9,10},{10,... | collective-permute-start | bytes 98312 | tf_op jit(solution)/shard_map/second_sums/ppermute | solution.py:292
  (3 other events, 2.6 us)

commit v10 on v9

--- a/solution.py
+++ b/solution.py
@@ -207,17 +207,16 @@
 
 
 def state_kernel(flags, base, upd, first, second, w_res, out):
-    for half in range(2):
-        fields = []
-        for frame in (2 * half, 2 * half + 1):
-            rows = pl.ds(2 * frame, 2)
-            above, below = arrived(flags, first[rows].reshape(2 * WIDTH, CHANS), second[rows].reshape(2 * WIDTH, CHANS))
-            fields.append(jnp.concatenate([above, upd[frame].reshape(OWN, CHANS), below]))
-        new = conv_rows(fields, side_by_side(w_res), 5).reshape(2, 5, WIDTH, CHANS)
-        new = (base[2 * half : 2 * half + 2].astype(F32) + new).astype(BF16)
-        out[2 * half : 2 * half + 2, 1:4] = new[:, 1:4]
-        out[2 * half : 2 * half + 2, 0] = new[:, 0] * flags[4:5].astype(BF16)
-        out[2 * half : 2 * half + 2, 4] = new[:, 4] * flags[5:6].astype(BF16)
+    fields = []
+    for frame in range(4):
+        rows = pl.ds(2 * frame, 2)
+        above, below = arrived(flags, first[rows].reshape(2 * WIDTH, CHANS), second[rows].reshape(2 * WIDTH, CHANS))
+        fields.append(jnp.concatenate([above, upd[frame].reshape(OWN, CHANS), below]))
+    new = conv_rows(fields, side_by_side(w_res), 5).reshape(4, 5, WIDTH, CHANS)
+    new = (base[...].astype(F32) + new).astype(BF16)
+    out[:, 1:4] = new[:, 1:4]
+    out[:, 0] = new[:, 0] * flags[4:5].astype(BF16)
+    out[:, 4] = new[:, 4] * flags[5:6].astype(BF16)
 
 
 def last_kernel(flags, state, upd, first, second, w_res, out):

time: 61.1 us -> 61.1 us (level)
  no operation moved by 1% of the time
where the time goes in v10:
time: 61.1 us; the launch traced here: 61 us
  starting transfers between devices  27.7 us (45%)
  waiting for transfers between devices  24 us (39%)
  Pallas kernels  6.91 us (11%)
  local copies, waits for them, and re-layouts  1.25 us (2%)
  other arithmetic  0.76 us (1%)
    ppermute x4, starting transfers between devices, swap_chip(): return lax.ppermute(x, ('frames', 'rows'), chip_swap)  16.3 us
    ppermute x4, waiting for transfers between devices, swap_chip(): return lax.ppermute(x, ('frames', 'rows'), chip_swap)  10 us
    pallas_call x5, Pallas kernels, call(): pl.pallas_call(kernel, out_shape=outs, in_specs=[VM] * len(args), out_spe...  6.91 us
    ppermute x3, starting transfers between devices, rows_swaps(): second = lax.ppermute(jnp.where(odd, to_below, to_above), 'rows', odd_swap)  6.64 us
    ppermute x6, waiting for transfers between devices, swap_core(): return lax.ppermute(x, 'frames', core_swap)  5.65 us
    ppermute x3, waiting for transfers between devices, rows_swaps(): first = lax.ppermute(jnp.where(odd, to_above, to_below), 'rows', even_swap)  5.12 us
    ppermute x3, waiting for transfers between devices, rows_swaps(): second = lax.ppermute(jnp.where(odd, to_below, to_above), 'rows', odd_swap)  3.21 us
    ppermute x3, starting transfers between devices, rows_swaps(): first = lax.ppermute(jnp.where(odd, to_above, to_below), 'rows', even_swap)  2.7 us
  transfers between devices with their start and end apart: 17, of which 11 were waited for; matrix products, arithmetic and copies ran while one was open for 1% of the time, Pallas kernels for 0%

profile of v10, /device:TPU:6, one launch (start us, length us, event | category | flops | bytes accessed | tf_op | source)
XLA Modules:
  0.0 61.0 jit_solution(14718776871881070968)
XLA Ops:
  0.9 1.7 %collective-permute-start.1 = (bf16[2,4,64,128]{3,2,1,0:T(8,128)(2,1)S(1)}, bf16[2,4,64,128]{3,2,1,0:T(8,128)(2,1)S(1)}, u32[]{:S(2)}, u32[]{:S(2)}) collective-permute-start(bf16[2,4,64,128]{3,2,1,0:T(8,128)(2,1)S(1)} %get-tuple-element.44), channel_id=1, source_target_pairs={{0,1},{1,0},{2,3},{3,2},{4,5},{5,4},{6,7},{7,6},{8,9},{9,8},{10,11... | collective-permute-start | bytes 393224 | tf_op jit(solution)/shard_map/feature_rows/ppermute | solution.py:290
  2.6 2.2 %collective-permute-start.2 = (bf16[2,4,64,128]{3,2,1,0:T(8,128)(2,1)S(1)}, bf16[2,4,64,128]{3,2,1,0:T(8,128)(2,1)S(1)}, u32[]{:S(2)}, u32[]{:S(2)}) collective-permute-start(bf16[2,4,64,128]{3,2,1,0:T(8,128)(2,1)S(1)} %get-tuple-element.43), channel_id=1, source_target_pairs={{0,3},{1,2},{2,1},{3,0},{4,7},{5,6},{6,5},{7,4},{8,11},{9,10},{10,... | collective-permute-start | bytes 393224 | tf_op jit(solution)/shard_map/feature_rows/ppermute | solution.py:291
  4.8 0.8 %collective-permute-start = (bf16[2,1,64,128]{3,2,1,0:T(8,128)(2,1)S(1)}, bf16[2,1,64,128]{3,2,1,0:T(8,128)(2,1)S(1)}, u32[]{:S(2)}, u32[]{:S(2)}) collective-permute-start(bf16[2,1,64,128]{3,2,1,0:T(8,128)(2,1)S(1)} %slice_select_fusion), channel_id=1, source_target_pairs={{0,2},{1,3},{2,0},{3,1},{4,6},{5,7},{6,4},{7,5},{8,10},{9,11},{10,... | collective-permute-start | bytes 98312 | tf_op jit(solution)/shard_map/feature_rows/ppermute | solution.py:303
  5.7 5.1 %collective-permute-start.3 = (bf16[2,6,64,128]{3,2,1,0:T(8,128)(2,1)S(1)}, bf16[2,6,64,128]{3,2,1,0:T(8,128)(2,1)S(1)}, u32[]{:S(2)}, u32[]{:S(2)}) collective-permute-start(bf16[2,6,64,128]{3,2,1,0:T(8,128)(2,1)S(1)} %constant_dynamic-update-slice_fusion.c0), channel_id=1, source_target_pairs={{0,1},{1,0},{2,3},{3,2},{4,8},{5,9},{6,10},{7,11},{8,4},{9,5},{10,... | collective-permute-start | bytes 589832 | tf_op jit(solution)/shard_map/feature_rows/ppermute | solution.py:298
  11.0 3.8 %collective-permute-start.5 = (bf16[2,10,64,128]{3,2,1,0:T(8,128)(2,1)S(1)}, bf16[2,10,64,128]{3,2,1,0:T(8,128)(2,1)S(1)}, u32[]{:S(2)}, u32[]{:S(2)}) collective-permute-start(bf16[2,10,64,128]{3,2,1,0:T(8,128)(2,1)S(1)} %slice_dynamic-update-slice_fusion.2.h0), channel_id=1, source_target_pairs={{0,1},{1,0},{2,3},{3,2},{4,8},{5,9},{6,10},{7,11},{8,4},{9,5},{10,... | collective-permute-start | bytes 983048 | tf_op jit(solution)/shard_map/feature_window/ppermute | solution.py:298
  15.8 3.9 %collective-permute-done.5.h1 = bf16[2,10,64,128]{3,2,1,0:T(8,128)(2,1)S(1)} collective-permute-done((bf16[2,10,64,128]{3,2,1,0:T(8,128)(2,1)S(1)}, bf16[2,10,64,128]{3,2,1,0:T(8,128)(2,1)S(1)}, u32[]{:S(2)}, u32[]{:S(2)}) %collective-permute-start.5) | collective-permute-done | bytes 327712 | tf_op jit(solution)/shard_map/feature_window/ppermute | solution.py:298
  19.9 1.4 %collective-permute-done.7.h3 = bf16[2,10,64,128]{3,2,1,0:T(8,128)(2,1)S(1)} collective-permute-done((bf16[2,10,64,128]{3,2,1,0:T(8,128)(2,1)S(1)}, bf16[2,10,64,128]{3,2,1,0:T(8,128)(2,1)S(1)}, u32[]{:S(2)}, u32[]{:S(2)}) %collective-permute-start.7) | collective-permute-done | bytes 327712 | tf_op jit(solution)/shard_map/feature_window/ppermute | solution.py:295
  21.3 3.2 %first_iteration.1 = (bf16[4,192,128]{2,1,0:T(8,128)(2,1)S(1)}, bf16[4,192,128]{2,1,0:T(8,128)(2,1)S(1)}, f32[8,192,128]{2,1,0:T(8,128)S(1)}, bf16[8,64,128]{2,1...) custom-call(s32[1,8]{1,0:T(1,128)S(1)} %add_bitcast_fusion.table, ...), custom_call_target="tpu_custom_call" | custom-call | flops 2000000000 | bytes 2957344 | tf_op jit(solution)/shard_map/first_iteration/pallas_call | solution.py:236
  24.8 1.3 %collective-permute-done.8 = bf16[4,192,128]{2,1,0:T(8,128)(2,1)S(1)} collective-permute-done((bf16[4,192,128]{2,1,0:T(8,128)(2,1)S(1)}, bf16[4,192,128]{2,1,0:T(8,128)(2,1)S(1)}, u32[]{:S(2)}, u32[]{:S(2)}) %collective-permute-start.8) | collective-permute-done | bytes 196640 | tf_op jit(solution)/shard_map/first_sums/ppermute | solution.py:295
  26.2 3.8 %collective-permute-start.9 = (bf16[4,192,128]{2,1,0:T(8,128)(2,1)S(1)}, bf16[4,192,128]{2,1,0:T(8,128)(2,1)S(1)}, u32[]{:S(2)}, u32[]{:S(2)}) collective-permute-start(bf16[4,192,128]{2,1,0:T(8,128)(2,1)S(1)} %fusion.2), channel_id=1, source_target_pairs={{0,1},{1,0},{2,3},{3,2},{4,8},{5,9},{6,10},{7,11},{8,4},{9,5},{10,... | collective-permute-start | bytes 589832 | tf_op jit(solution)/shard_map/first_sums/ppermute | solution.py:298
  30.0 3.5 %collective-permute-done.9 = bf16[4,192,128]{2,1,0:T(8,128)(2,1)S(1)} collective-permute-done((bf16[4,192,128]{2,1,0:T(8,128)(2,1)S(1)}, bf16[4,192,128]{2,1,0:T(8,128)(2,1)S(1)}, u32[]{:S(2)}, u32[]{:S(2)}) %collective-permute-start.9) | collective-permute-done | bytes 196640 | tf_op jit(solution)/shard_map/first_sums/ppermute | solution.py:298
  33.7 0.9 %collective-permute-start.10 = (bf16[16,64,128]{2,1,0:T(8,128)(2,1)S(1)}, bf16[16,64,128]{2,1,0:T(8,128)(2,1)S(1)}, u32[]{:S(2)}, u32[]{:S(2)}) collective-permute-start(bf16[16,64,128]{2,1,0:T(8,128)(2,1)S(1)} %get-tuple-element.36), channel_id=1, source_target_pairs={{0,1},{1,0},{2,3},{3,2},{4,5},{5,4},{6,7},{7,6},{8,9},{9,8},{10,11... | collective-permute-start | bytes 786440 | tf_op jit(solution)/shard_map/update_rows/ppermute | solution.py:290
  34.6 2.2 %collective-permute-start.11 = (bf16[16,64,128]{2,1,0:T(8,128)(2,1)S(1)}, bf16[16,64,128]{2,1,0:T(8,128)(2,1)S(1)}, u32[]{:S(2)}, u32[]{:S(2)}) collective-permute-start(bf16[16,64,128]{2,1,0:T(8,128)(2,1)S(1)} %get-tuple-element.35), channel_id=1, source_target_pairs={{0,3},{1,2},{2,1},{3,0},{4,7},{5,6},{6,5},{7,4},{8,11},{9,10},{10,... | collective-permute-start | bytes 786440 | tf_op jit(solution)/shard_map/update_rows/ppermute | solution.py:291
  36.8 3.5 %collective-permute-done.10.first = bf16[16,64,128]{2,1,0:T(8,128)(2,1)S(1)} collective-permute-done((bf16[16,64,128]{2,1,0:T(8,128)(2,1)S(1)}, bf16[16,64,128]{2,1,0:T(8,128)(2,1)S(1)}, u32[]{:S(2)}, u32[]{:S(2)}) %collective-permute-start.10) | collective-permute-done | bytes 262176 | tf_op jit(solution)/shard_map/update_rows/ppermute | solution.py:290
  40.3 1.9 %collective-permute-done.11.second = bf16[16,64,128]{2,1,0:T(8,128)(2,1)S(1)} collective-permute-done((bf16[16,64,128]{2,1,0:T(8,128)(2,1)S(1)}, bf16[16,64,128]{2,1,0:T(8,128)(2,1)S(1)}, u32[]{:S(2)}, u32[]{:S(2)}) %collective-permute-start.11) | collective-permute-done | bytes 262176 | tf_op jit(solution)/shard_map/update_rows/ppermute | solution.py:291
  43.4 1.6 %collective-permute-done.12.s1 = bf16[4,5,64,128]{3,2,1,0:T(8,128)(2,1)S(1)} collective-permute-done((bf16[4,5,64,128]{3,2,1,0:T(8,128)(2,1)S(1)}, bf16[4,5,64,128]{3,2,1,0:T(8,128)(2,1)S(1)}, u32[]{:S(2)}, u32[]{:S(2)}) %collective-permute-start.12) | collective-permute-done | bytes 327712 | tf_op jit(solution)/shard_map/first_state/ppermute | solution.py:295
  45.0 1.8 %second_iteration.1 = (bf16[4,192,128]{2,1,0:T(8,128)(2,1)S(1)}, bf16[4,192,128]{2,1,0:T(8,128)(2,1)S(1)}) custom-call(s32[1,8]{1,0:T(1,128)S(1)} %add_bitcast_fusion.table, f32[8,128]{1,0:T(8,128)S(1)} %iota.34.flags, bf16[4,5,64,128]{3,2,1,0:T(8,128)(2,1)S(1)} %first_state.1.s0.state, bf16[4,5,64,128]{3,2,1,0:T(8,128)(2,1)S(1)} %collective-permute-done.12.s1, ...), custom_call_target="tpu_custom_call" | custom-call | flops 1500000000 | bytes 3412000 | tf_op jit(solution)/shard_map/second_iteration/pallas_call | solution.py:236
  47.0 1.3 %collective-permute-done.13 = bf16[4,192,128]{2,1,0:T(8,128)(2,1)S(1)} collective-permute-done((bf16[4,192,128]{2,1,0:T(8,128)(2,1)S(1)}, bf16[4,192,128]{2,1,0:T(8,128)(2,1)S(1)}, u32[]{:S(2)}, u32[]{:S(2)}) %collective-permute-start.13) | collective-permute-done | bytes 196640 | tf_op jit(solution)/shard_map/second_sums/ppermute | solution.py:295
  48.4 3.6 %collective-permute-start.14 = (bf16[2,192,128]{2,1,0:T(8,128)(2,1)S(1)}, bf16[2,192,128]{2,1,0:T(8,128)(2,1)S(1)}, u32[]{:S(2)}, u32[]{:S(2)}) collective-permute-start(bf16[2,192,128]{2,1,0:T(8,128)(2,1)S(1)} %slice.108), channel_id=1, source_target_pairs={{0,1},{1,0},{2,3},{3,2},{4,8},{5,9},{6,10},{7,11},{8,4},{9,5},{10,... | collective-permute-start | bytes 294920 | tf_op jit(solution)/shard_map/second_sums/ppermute | solution.py:298
  51.9 2.7 %collective-permute-done.14 = bf16[2,192,128]{2,1,0:T(8,128)(2,1)S(1)} collective-permute-done((bf16[2,192,128]{2,1,0:T(8,128)(2,1)S(1)}, bf16[2,192,128]{2,1,0:T(8,128)(2,1)S(1)}, u32[]{:S(2)}, u32[]{:S(2)}) %collective-permute-start.14) | collective-permute-done | bytes 98336 | tf_op jit(solution)/shard_map/second_sums/ppermute | solution.py:298
  54.8 2.3 %collective-permute-start.16 = (bf16[2,1,64,128]{3,2,1,0:T(8,128)(2,1)S(1)}, bf16[2,1,64,128]{3,2,1,0:T(8,128)(2,1)S(1)}, u32[]{:S(2)}, u32[]{:S(2)}) collective-permute-start(bf16[2,1,64,128]{3,2,1,0:T(8,128)(2,1)S(1)} %get-tuple-element.45), channel_id=1, source_target_pairs={{0,3},{1,2},{2,1},{3,0},{4,7},{5,6},{6,5},{7,4},{8,11},{9,10},{10,... | collective-permute-start | bytes 98312 | tf_op jit(solution)/shard_map/second_sums/ppermute | solution.py:291
  57.0 1.6 %collective-permute-done.15.first = bf16[2,1,64,128]{3,2,1,0:T(8,128)(2,1)S(1)} collective-permute-done((bf16[2,1,64,128]{3,2,1,0:T(8,128)(2,1)S(1)}, bf16[2,1,64,128]{3,2,1,0:T(8,128)(2,1)S(1)}, u32[]{:S(2)}, u32[]{:S(2)}) %collective-permute-start.15) | collective-permute-done | bytes 32800 | tf_op jit(solution)/shard_map/second_sums/ppermute | solution.py:290
  58.7 1.3 %collective-permute-done.16.second = bf16[2,1,64,128]{3,2,1,0:T(8,128)(2,1)S(1)} collective-permute-done((bf16[2,1,64,128]{3,2,1,0:T(8,128)(2,1)S(1)}, bf16[2,1,64,128]{3,2,1,0:T(8,128)(2,1)S(1)}, u32[]{:S(2)}, u32[]{:S(2)}) %collective-permute-start.16) | collective-permute-done | bytes 32800 | tf_op jit(solution)/shard_map/second_sums/ppermute | solution.py:291
  60.0 1.0 %last_state.1 = bf16[2,3,64,128]{3,2,1,0:T(8,128)(2,1)} custom-call(f32[8,128]{1,0:T(8,128)S(1)} %iota.34.flags, bf16[4,5,64,128]{3,2,1,0:T(8,128)(2,1)S(1)} %first_state.1.s0.state, bf16[2,3,64,128]{3,2,1,0:T(8,128)(2,1)S(1)} %bitcast.10, bf16[2,1,64,128]{3,2,1,0:T(8,128)(2,1)S(1)} %collective-permute-done.15.first, ...), custom_call_target="tpu_custom_call" | custom-call | flops 120000000 | bytes 790528 | tf_op jit(solution)/shard_map/last_state/pallas_call | solution.py:236
  (65 shorter events, 4.4 us)
Async XLA Ops:
  0.9 9.9 %collective-permute-start.1 = (bf16[2,4,64,128]{3,2,1,0:T(8,128)(2,1)S(1)}, bf16[2,4,64,128]{3,2,1,0:T(8,128)(2,1)S(1)}, u32[]{:S(2)}, u32[]{:S(2)}) collective-permute-start(bf16[2,4,64,128]{3,2,1,0:T(8,128)(2,1)S(1)} %get-tuple-element.44), channel_id=1, source_target_pairs={{0,1},{1,0},{2,3},{3,2},{4,5},{5,4},{6,7},{7,6},{8,9},{9,8},{10,11... | collective-permute-start | bytes 393224 | tf_op jit(solution)/shard_map/feature_rows/ppermute | solution.py:290
  2.6 8.2 %collective-permute-start.2 = (bf16[2,4,64,128]{3,2,1,0:T(8,128)(2,1)S(1)}, bf16[2,4,64,128]{3,2,1,0:T(8,128)(2,1)S(1)}, u32[]{:S(2)}, u32[]{:S(2)}) collective-permute-start(bf16[2,4,64,128]{3,2,1,0:T(8,128)(2,1)S(1)} %get-tuple-element.43), channel_id=1, source_target_pairs={{0,3},{1,2},{2,1},{3,0},{4,7},{5,6},{6,5},{7,4},{8,11},{9,10},{10,... | collective-permute-start | bytes 393224 | tf_op jit(solution)/shard_map/feature_rows/ppermute | solution.py:291
  4.8 6.0 %collective-permute-start = (bf16[2,1,64,128]{3,2,1,0:T(8,128)(2,1)S(1)}, bf16[2,1,64,128]{3,2,1,0:T(8,128)(2,1)S(1)}, u32[]{:S(2)}, u32[]{:S(2)}) collective-permute-start(bf16[2,1,64,128]{3,2,1,0:T(8,128)(2,1)S(1)} %slice_select_fusion), channel_id=1, source_target_pairs={{0,2},{1,3},{2,0},{3,1},{4,6},{5,7},{6,4},{7,5},{8,10},{9,11},{10,... | collective-permute-start | bytes 98312 | tf_op jit(solution)/shard_map/feature_rows/ppermute | solution.py:303
  5.7 9.2 %collective-permute-start.3 = (bf16[2,6,64,128]{3,2,1,0:T(8,128)(2,1)S(1)}, bf16[2,6,64,128]{3,2,1,0:T(8,128)(2,1)S(1)}, u32[]{:S(2)}, u32[]{:S(2)}) collective-permute-start(bf16[2,6,64,128]{3,2,1,0:T(8,128)(2,1)S(1)} %constant_dynamic-update-slice_fusion.c0), channel_id=1, source_target_pairs={{0,1},{1,0},{2,3},{3,2},{4,8},{5,9},{6,10},{7,11},{8,4},{9,5},{10,... | collective-permute-start | bytes 589832 | tf_op jit(solution)/shard_map/feature_rows/ppermute | solution.py:298
  10.9 4.0 %copy-start.9 = (s32[256,3]{0,1:T(4,128)S(1)}, s32[256,3]{0,1:T(4,128)}, u32[]{:S(2)}) copy-start(s32[256,3]{0,1:T(4,128)} %param.10) | copy-start | bytes 9220
  10.9 10.4 %copy-start.2 = (bf16[9,256,128]{2,1,0:T(8,128)(2,1)S(1)}, bf16[9,256,128]{2,1,0:T(8,128)(2,1)}, u32[]{:S(2)}) copy-start(bf16[9,256,128]{2,1,0:T(8,128)(2,1)} %w_q.3) | copy-start | bytes 1769476
  11.0 8.7 %collective-permute-start.5 = (bf16[2,10,64,128]{3,2,1,0:T(8,128)(2,1)S(1)}, bf16[2,10,64,128]{3,2,1,0:T(8,128)(2,1)S(1)}, u32[]{:S(2)}, u32[]{:S(2)}) collective-permute-start(bf16[2,10,64,128]{3,2,1,0:T(8,128)(2,1)S(1)} %slice_dynamic-update-slice_fusion.2.h0), channel_id=1, source_target_pairs={{0,1},{1,0},{2,3},{3,2},{4,8},{5,9},{6,10},{7,11},{8,4},{9,5},{10,... | collective-permute-start | bytes 983048 | tf_op jit(solution)/shard_map/feature_window/ppermute | solution.py:298
  14.8 5.1 %collective-permute-start.6 = (bf16[2,10,64,128]{3,2,1,0:T(8,128)(2,1)S(1)}, bf16[2,10,64,128]{3,2,1,0:T(8,128)(2,1)S(1)}, u32[]{:S(2)}, u32[]{:S(2)}) collective-permute-start(bf16[2,10,64,128]{3,2,1,0:T(8,128)(2,1)S(1)} %slice_dynamic-update-slice_fusion.2.h0), channel_id=1, source_target_pairs={{0,4},{4,0},{8,12},{12,8},{16,20},{20,16},{24,28},{28,24},{32,36},... | collective-permute-start | bytes 983048 | tf_op jit(solution)/shard_map/feature_window/ppermute | solution.py:295
  14.9 6.5 %copy-start.3 = (bf16[256,256]{1,0:T(8,128)(2,1)S(1)}, bf16[256,256]{1,0:T(8,128)(2,1)}, u32[]{:S(2)}) copy-start(bf16[256,256]{1,0:T(8,128)(2,1)} %w_zr.3) | copy-start | bytes 393220
  14.9 6.4 %copy-start.4 = (bf16[128,256]{1,0:T(8,128)(2,1)S(1)}, bf16[128,256]{1,0:T(8,128)(2,1)}, u32[]{:S(2)}) copy-start(bf16[128,256]{1,0:T(8,128)(2,1)} %w_msg.3) | copy-start | bytes 196612
  15.0 4.9 %collective-permute-start.4 = (bf16[4,6,64,128]{3,2,1,0:T(8,128)(2,1)S(1)}, bf16[4,6,64,128]{3,2,1,0:T(8,128)(2,1)S(1)}, u32[]{:S(2)}, u32[]{:S(2)}) collective-permute-start(bf16[4,6,64,128]{3,2,1,0:T(8,128)(2,1)S(1)} %pad_maximum_fusion), channel_id=1, source_target_pairs={{0,4},{4,0},{8,12},{12,8},{16,20},{20,16},{24,28},{28,24},{32,36},... | collective-permute-start | bytes 1179656 | tf_op jit(solution)/shard_map/feature_window/ppermute | solution.py:295
  19.7 1.6 %collective-permute-start.7 = (bf16[2,10,64,128]{3,2,1,0:T(8,128)(2,1)S(1)}, bf16[2,10,64,128]{3,2,1,0:T(8,128)(2,1)S(1)}, u32[]{:S(2)}, u32[]{:S(2)}) collective-permute-start(bf16[2,10,64,128]{3,2,1,0:T(8,128)(2,1)S(1)} %collective-permute-done.5.h1), channel_id=1, source_target_pairs={{0,4},{4,0},{8,12},{12,8},{16,20},{20,16},{24,28},{28,24},{32,36},... | collective-permute-start | bytes 983048 | tf_op jit(solution)/shard_map/feature_window/ppermute | solution.py:295
  24.6 8.9 %copy-start.5 = (bf16[8,320,128]{2,1,0:T(8,128)(2,1)}, bf16[8,320,128]{2,1,0:T(8,128)(2,1)S(1)}, u32[]{:S(2)}) copy-start(bf16[8,320,128]{2,1,0:T(8,128)(2,1)S(1)} %get-tuple-element.31.motion) | copy-start | bytes 1966084
  24.6 1.5 %collective-permute-start.8 = (bf16[4,192,128]{2,1,0:T(8,128)(2,1)S(1)}, bf16[4,192,128]{2,1,0:T(8,128)(2,1)S(1)}, u32[]{:S(2)}, u32[]{:S(2)}) collective-permute-start(bf16[4,192,128]{2,1,0:T(8,128)(2,1)S(1)} %get-tuple-element.28), channel_id=1, source_target_pairs={{0,4},{4,0},{8,12},{12,8},{16,20},{20,16},{24,28},{28,24},{32,36},... | collective-permute-start | bytes 589832 | tf_op jit(solution)/shard_map/first_sums/ppermute | solution.py:295
  26.2 7.3 %collective-permute-start.9 = (bf16[4,192,128]{2,1,0:T(8,128)(2,1)S(1)}, bf16[4,192,128]{2,1,0:T(8,128)(2,1)S(1)}, u32[]{:S(2)}, u32[]{:S(2)}) collective-permute-start(bf16[4,192,128]{2,1,0:T(8,128)(2,1)S(1)} %fusion.2), channel_id=1, source_target_pairs={{0,1},{1,0},{2,3},{3,2},{4,8},{5,9},{6,10},{7,11},{8,4},{9,5},{10,... | collective-permute-start | bytes 589832 | tf_op jit(solution)/shard_map/first_sums/ppermute | solution.py:298
  33.6 8.7 %copy-start = (bf16[9,128,128]{2,1,0:T(8,128)(2,1)S(1)}, bf16[9,128,128]{2,1,0:T(8,128)(2,1)}, u32[]{:S(2)}) copy-start(bf16[9,128,128]{2,1,0:T(8,128)(2,1)} %w_res.3) | copy-start | bytes 884740
  33.7 6.6 %collective-permute-start.10 = (bf16[16,64,128]{2,1,0:T(8,128)(2,1)S(1)}, bf16[16,64,128]{2,1,0:T(8,128)(2,1)S(1)}, u32[]{:S(2)}, u32[]{:S(2)}) collective-permute-start(bf16[16,64,128]{2,1,0:T(8,128)(2,1)S(1)} %get-tuple-element.36), channel_id=1, source_target_pairs={{0,1},{1,0},{2,3},{3,2},{4,5},{5,4},{6,7},{7,6},{8,9},{9,8},{10,11... | collective-permute-start | bytes 786440 | tf_op jit(solution)/shard_map/update_rows/ppermute | solution.py:290
  34.6 7.6 %collective-permute-start.11 = (bf16[16,64,128]{2,1,0:T(8,128)(2,1)S(1)}, bf16[16,64,128]{2,1,0:T(8,128)(2,1)S(1)}, u32[]{:S(2)}, u32[]{:S(2)}) collective-permute-start(bf16[16,64,128]{2,1,0:T(8,128)(2,1)S(1)} %get-tuple-element.35), channel_id=1, source_target_pairs={{0,3},{1,2},{2,1},{3,0},{4,7},{5,6},{6,5},{7,4},{8,11},{9,10},{10,... | collective-permute-start | bytes 786440 | tf_op jit(solution)/shard_map/update_rows/ppermute | solution.py:291
  42.3 2.7 %copy-start.6 = (bf16[8,320,128]{2,1,0:T(8,128)(2,1)S(1)}, bf16[8,320,128]{2,1,0:T(8,128)(2,1)}, u32[]{:S(2)}) copy-start(bf16[8,320,128]{2,1,0:T(8,128)(2,1)} %copy-done.5) | copy-start | bytes 1966084
  43.1 1.9 %collective-permute-start.12 = (bf16[4,5,64,128]{3,2,1,0:T(8,128)(2,1)S(1)}, bf16[4,5,64,128]{3,2,1,0:T(8,128)(2,1)S(1)}, u32[]{:S(2)}, u32[]{:S(2)}) collective-permute-start(bf16[4,5,64,128]{3,2,1,0:T(8,128)(2,1)S(1)} %first_state.1.s0.state), channel_id=1, source_target_pairs={{0,4},{4,0},{8,12},{12,8},{16,20},{20,16},{24,28},{28,24},{32,36},... | collective-permute-start | bytes 983048 | tf_op jit(solution)/shard_map/first_state/ppermute | solution.py:295
  46.8 1.5 %collective-permute-start.13 = (bf16[4,192,128]{2,1,0:T(8,128)(2,1)S(1)}, bf16[4,192,128]{2,1,0:T(8,128)(2,1)S(1)}, u32[]{:S(2)}, u32[]{:S(2)}) collective-permute-start(bf16[4,192,128]{2,1,0:T(8,128)(2,1)S(1)} %get-tuple-element.34), channel_id=1, source_target_pairs={{0,4},{4,0},{8,12},{12,8},{16,20},{20,16},{24,28},{28,24},{32,36},... | collective-permute-start | bytes 589832 | tf_op jit(solution)/shard_map/second_sums/ppermute | solution.py:295
  48.4 6.2 %collective-permute-start.14 = (bf16[2,192,128]{2,1,0:T(8,128)(2,1)S(1)}, bf16[2,192,128]{2,1,0:T(8,128)(2,1)S(1)}, u32[]{:S(2)}, u32[]{:S(2)}) collective-permute-start(bf16[2,192,128]{2,1,0:T(8,128)(2,1)S(1)} %slice.108), channel_id=1, source_target_pairs={{0,1},{1,0},{2,3},{3,2},{4,8},{5,9},{6,10},{7,11},{8,4},{9,5},{10,... | collective-permute-start | bytes 294920 | tf_op jit(solution)/shard_map/second_sums/ppermute | solution.py:298
  54.7 4.0 %collective-permute-start.15 = (bf16[2,1,64,128]{3,2,1,0:T(8,128)(2,1)S(1)}, bf16[2,1,64,128]{3,2,1,0:T(8,128)(2,1)S(1)}, u32[]{:S(2)}, u32[]{:S(2)}) collective-permute-start(bf16[2,1,64,128]{3,2,1,0:T(8,128)(2,1)S(1)} %get-tuple-element.46), channel_id=1, source_target_pairs={{0,1},{1,0},{2,3},{3,2},{4,5},{5,4},{6,7},{7,6},{8,9},{9,8},{10,11... | collective-permute-start | bytes 98312 | tf_op jit(solution)/shard_map/second_sums/ppermute | solution.py:290
  54.8 5.2 %collective-permute-start.16 = (bf16[2,1,64,128]{3,2,1,0:T(8,128)(2,1)S(1)}, bf16[2,1,64,128]{3,2,1,0:T(8,128)(2,1)S(1)}, u32[]{:S(2)}, u32[]{:S(2)}) collective-permute-start(bf16[2,1,64,128]{3,2,1,0:T(8,128)(2,1)S(1)} %get-tuple-element.45), channel_id=1, source_target_pairs={{0,3},{1,2},{2,1},{3,0},{4,7},{5,6},{6,5},{7,4},{8,11},{9,10},{10,... | collective-permute-start | bytes 98312 | tf_op jit(solution)/shard_map/second_sums/ppermute | solution.py:291
  (3 other events, 2.6 us)
